TPU v7x, 32 devices: a whole 2x2x4 slice. The times are simulated.
32 devices in a mesh: grp: 2 (over x), vel: 16 (over z, y, core).
Axes of the slice: x: 2, y: 2, z: 4, core: 2. Of those that a mesh axis runs over, the one named last changes fastest.
Arguments:
- discrete_lattice_vectors: float32 [3, 2048], P(None, 'vel'), may hold values from -7.5 to 7.5, as said below
- initial_compactness: float32 [16384], P('grp'), parts along dimension 0, may hold values from 0.5 to 2
- initial_flow_vector: float32 [3, 16384], P(None, 'grp'), parts along dimension 1, may hold values from -3 to 3
- initial_thermal_level: float32 [16384], P('grp'), parts along dimension 0, may hold values from 0.6 to 1.5
- initial_deviation: float32 [2048, 16384], P('vel', 'grp'), parts along dimension 1, may hold values from -0.5 to 0.5
Outputs:
- distribution: float32 [2048, 16384], P('vel', 'grp'), parts along dimension 1
- macro_profile: float32 [8, 16384], P(None, 'grp'), parts along dimension 1
There are 2 independent parts, one for each index of `grp`. A program takes and returns all parts, laid end to end along the dimension named above; an argument that names none is the same for every part. Nothing has to cross between parts.
Inputs may be any that keep to these rules, and one draw needn't show every extreme that they name: `discrete_lattice_vectors`: velocity components, drawn independently with a spread of about 1.5.
All inputs are finite; a program needn't handle non-finite values.
Results may differ from a plain program's by a relative error of at most 0.0003.
Values sent between devices are 32-bit elements; how exact they have to be, the bound alone decides.
No kernel may reach another device: no remote copies, remote signals or barrier semaphores. Data moves between devices by JAX's collectives and lax.ppermute only.
A program may use at most 128 MiB of HBM per device.

v0:
```python
import functools

import jax
import jax.numpy as jnp
from jax import lax
from jax.experimental import pallas as pl
from jax.experimental.pallas import tpu as pltpu
from jax.sharding import PartitionSpec as P

ITERS = 2

ADIABATIC_INDEX = 5.0 / 3.0
CONDUCTIVE_SHARE = 2.0 / 3.0
SHEAR_EXPONENT = 0.81
SHEAR_REFERENCE = 0.05
KINETIC_STEP = 0.05
COURANT = 0.4
SPREAD_SCALE = 1.5

LOG2E = 1.4426950408889634
LANES = 128
TILE = 256
BASIS = 16
SENT = 14
COEF = 24
DAMP = 13
CHUNKS = 8
VMEM_BYTES = 24 * 1024 * 1024

WHOLE = pl.BlockSpec(memory_space=pltpu.VMEM)
OUTSIDE = pl.BlockSpec(memory_space=pltpu.HBM)
PARAMS = pltpu.CompilerParams(vmem_limit_bytes=VMEM_BYTES)


def dot(left, right):
    return jnp.dot(left, right, preferred_element_type=jnp.float32)


def rounded(values):
    return values.astype(jnp.bfloat16).astype(jnp.float32)


def phi_rows(velocities):
    vx, vy, vz = velocities[0:1], velocities[1:2], velocities[2:3]
    sq = vx * vx + vy * vy + vz * vz
    zero = jnp.zeros_like(vx)
    rows = [
        jnp.ones_like(vx), vx, vy, vz, sq, vx * vx, vx * vy, vx * vz, vy * vy, vy * vz,
        vx * sq, vy * sq, vz * sq, zero, zero, zero,
    ]
    return jnp.concatenate(rows, axis=0), sq


def make_tables(velocities, total_count):
    phi, sq = phi_rows(velocities)
    high = rounded(phi)
    middle = rounded(phi - high)
    low = phi - high - middle
    stacked = jnp.concatenate(
        [high, high, high, middle, middle, low, jnp.zeros((32, phi.shape[1]), jnp.float32)], axis=0
    )
    basis = stacked.T.astype(jnp.bfloat16)
    weighted = phi * (SPREAD_SCALE**3 * jnp.exp(sq / (2.0 * SPREAD_SCALE**2)) / total_count)
    top = rounded(weighted)
    rest = weighted - top
    moments = jnp.concatenate(
        [
            jnp.concatenate([top, top], axis=1),
            jnp.concatenate([rest, jnp.zeros_like(rest)], axis=1),
        ],
        axis=0,
    ).astype(jnp.bfloat16)
    return basis, moments


def expand(coefficients):
    high = coefficients.astype(jnp.bfloat16)
    rest = coefficients - high.astype(jnp.float32)
    middle = rest.astype(jnp.bfloat16)
    low = (rest - middle.astype(jnp.float32)).astype(jnp.bfloat16)
    zero = jnp.zeros((32, coefficients.shape[1]), jnp.bfloat16)
    return jnp.concatenate([high, middle, low, high, middle, high, zero], axis=0)


def store_moments(moments_ref, table, values, tile, blocks):
    high = values.astype(jnp.bfloat16)
    low = (values - high.astype(jnp.float32)).astype(jnp.bfloat16)
    both = dot(table, jnp.concatenate([high, low], axis=0))
    sums = both[:BASIS] + both[BASIS:]
    per_tile = TILE // LANES
    for part in range(per_tile):
        block = tile * per_tile + part
        moments_ref[pl.ds(block, SENT, stride=blocks), :] = sums[
            :SENT, part * LANES : (part + 1) * LANES
        ]


def start_kernel(
    total_count,
    vel_ref, density_ref, flow_ref, thermal_ref, deviation_ref,
    f_ref, moments_ref, basis_ref, table_ref,
    held, sems,
):
    cells = f_ref.shape[1]
    width = cells // CHUNKS
    copies = [
        pltpu.make_async_copy(
            deviation_ref.at[:, pl.ds(chunk * width, width)],
            held.at[:, pl.ds(chunk * width, width)],
            sems.at[chunk],
        )
        for chunk in range(CHUNKS)
    ]
    for copy in copies:
        copy.start()
    basis, table = make_tables(vel_ref[...], total_count)
    basis_ref[...] = basis
    table_ref[...] = table
    for chunk in range(CHUNKS):
        copies[chunk].wait()

        def step(local, carry, chunk=chunk):
            tile = chunk * (width // TILE) + local
            here = pl.ds(pl.multiple_of(tile * TILE, TILE), TILE)
            density, flow, thermal = density_ref[:, here], flow_ref[:, here], thermal_ref[:, here]
            rate = (0.5 * LOG2E) / thermal
            speed_sq = flow[0:1] * flow[0:1] + flow[1:2] * flow[1:2] + flow[2:3] * flow[2:3]
            rows = [-rate * speed_sq, 2.0 * rate * flow, -rate, jnp.zeros((11, TILE), jnp.float32)]
            exponent = dot(basis_ref[...], expand(jnp.concatenate(rows, axis=0)))
            scale = density / (thermal * jnp.sqrt(thermal))
            values = jnp.exp2(exponent) * (scale * (1.0 + held[:, here]))
            f_ref[:, here] = values
            store_moments(moments_ref, table_ref[...], values, tile, cells // LANES)
            return carry

        lax.fori_loop(0, width // TILE, step, 0, unroll=True)


def start_call(velocities, density, flow, thermal, deviation, total_count):
    local, cells = deviation.shape
    return pl.pallas_call(
        functools.partial(start_kernel, total_count),
        out_shape=(
            pltpu.VMEM((local, cells), jnp.float32),
            pltpu.VMEM((SENT * cells // LANES, LANES), jnp.float32),
            pltpu.VMEM((local, 128), jnp.bfloat16),
            pltpu.VMEM((2 * BASIS, 2 * local), jnp.bfloat16),
        ),
        in_specs=[WHOLE, WHOLE, WHOLE, WHOLE, OUTSIDE],
        out_specs=(WHOLE, WHOLE, WHOLE, WHOLE),
        scratch_shapes=[
            pltpu.VMEM((local, cells), jnp.float32),
            pltpu.SemaphoreType.DMA((CHUNKS,)),
        ],
        compiler_params=PARAMS,
        name="start",
    )(velocities, density.reshape(1, cells), flow, thermal.reshape(1, cells), deviation)


def transport_kernel(stream_ref, f_ref, g_ref):
    rows, cells = f_ref.shape
    chunk = min(1024, cells)
    blocks = cells // LANES
    per_chunk = chunk // LANES

    def row_step(row_tile, carry):
        here = pl.ds(pl.multiple_of(row_tile * 8, 8), 8)
        stream = jnp.broadcast_to(stream_ref[here, :], (8, LANES))
        rate = jnp.tile(KINETIC_STEP * jnp.abs(stream), (1, per_chunk + 2))
        half = jnp.tile(jnp.where(stream > 0, 0.5, -0.5), (1, per_chunk + 2))
        upward = half > 0
        for part in range(cells // chunk):
            first = part * per_chunk
            before = ((first - 1) % blocks) * LANES
            after = ((first + per_chunk) % blocks) * LANES
            x = jnp.concatenate(
                [
                    f_ref[here, before : before + LANES],
                    f_ref[here, part * chunk : (part + 1) * chunk],
                    f_ref[here, after : after + LANES],
                ],
                axis=1,
            )
            wide = x.shape[1]
            rise = x - pltpu.roll(x, 1, 1)
            ahead = pltpu.roll(rise, wide - 1, 1)
            slope = jnp.maximum(jnp.minimum(rise, ahead), 0.0) + jnp.minimum(
                jnp.maximum(rise, ahead), 0.0
            )
            face = x + half * slope
            other = jnp.where(upward, pltpu.roll(face, 1, 1), pltpu.roll(face, wide - 1, 1))
            moved = x - rate * (face - other)
            g_ref[here, part * chunk : (part + 1) * chunk] = moved[:, LANES : LANES + chunk]
        return carry

    lax.fori_loop(0, rows // 8, row_step, 0)


def transport_call(stream, f):
    return pl.pallas_call(
        transport_kernel,
        out_shape=pltpu.VMEM(f.shape, jnp.float32),
        in_specs=[WHOLE, WHOLE],
        out_specs=WHOLE,
        compiler_params=PARAMS,
        name="transport",
    )(stream, f)


def fluid_kernel(moments_ref, coef_ref, macro_ref):
    blocks = moments_ref.shape[0] // SENT
    m = [moments_ref[row * blocks : (row + 1) * blocks, :] for row in range(13)]
    lane = lax.broadcasted_iota(jnp.int32, (blocks, LANES), 1)

    def following(x):
        turned = pltpu.roll(x, LANES - 1, 1)
        return jnp.where(lane == LANES - 1, pltpu.roll(turned, blocks - 1, 0), turned)

    def preceding(x):
        turned = pltpu.roll(x, 1, 1)
        return jnp.where(lane == 0, pltpu.roll(turned, 1, 0), turned)

    def power(x, exponent):
        return jnp.exp2(exponent * jnp.log2(x))

    def primitives(w):
        inverse = 1.0 / w[0]
        u = [w[1] * inverse, w[2] * inverse, w[3] * inverse]
        uu = u[0] * u[0] + u[1] * u[1] + u[2] * u[2]
        t = (2.0 * w[4] * inverse - uu) * (1.0 / 3.0)
        return u, uu, t

    n = m[0]
    w = [n, m[1], m[2], m[3], 0.5 * m[4]]
    u, uu, t = primitives(w)
    p = n * t
    second = [[m[5], m[6], m[7]], [m[6], m[8], m[9]], [m[7], m[9], m[4] - m[5] - m[8]]]
    stress = [m[5] - m[1] * u[0] - p, m[6] - m[1] * u[1], m[7] - m[1] * u[2]]
    q = []
    for i in range(3):
        along = second[i][0] * u[0] + second[i][1] * u[1] + second[i][2] * u[2]
        q.append(0.5 * (m[10 + i] - u[i] * m[4] - 2.0 * along + 2.0 * n * u[i] * uu))

    shear = SHEAR_REFERENCE * power(t, SHEAR_EXPONENT)
    high_order = [
        stress[i] + ((4.0 / 3.0 if i == 0 else 1.0) * 0.5) * shear * (following(u[i]) - preceding(u[i]))
        for i in range(3)
    ]
    high_order.append(q[0] + (3.75 * 0.5) * shear * (following(t) - preceding(t)))
    half_order = [0.5 * h for h in high_order]
    face_order = [h + following(h) for h in half_order]

    def sweep(w, u, t, shear):
        rates = jnp.abs(u[0]) + jnp.sqrt(ADIABATIC_INDEX * t)
        signal = jnp.max(jnp.max(rates, axis=0, keepdims=True), axis=1, keepdims=True)
        step = COURANT / signal
        p = w[0] * t
        euler = [w[1], w[1] * u[0] + p, w[1] * u[1], w[1] * u[2], (w[4] + p) * u[0]]
        next_u = [following(x) for x in u]
        half_shear = 0.5 * shear
        face_shear = half_shear + following(half_shear)
        sxx = face_order[0] - (4.0 / 3.0) * face_shear * (next_u[0] - u[0])
        sxy = face_order[1] - face_shear * (next_u[1] - u[1])
        sxz = face_order[2] - face_shear * (next_u[2] - u[2])
        heat = face_order[3] - 3.75 * face_shear * (following(t) - t)
        work = 0.5 * (
            sxx * (u[0] + next_u[0]) + sxy * (u[1] + next_u[1]) + sxz * (u[2] + next_u[2])
        )
        viscous = [None, sxx, sxy, sxz, work + heat]
        out = []
        for i in range(5):
            spread = signal * w[i]
            total = 0.5 * ((euler[i] + spread) + following(euler[i] - spread))
            if viscous[i] is not None:
                total = total + viscous[i]
            out.append(w[i] - step * (total - preceding(total)))
        return out

    w = sweep(w, u, t, shear)
    u, uu, t = primitives(w)
    w = sweep(w, u, t, SHEAR_REFERENCE * power(t, SHEAR_EXPONENT))
    u, uu, t = primitives(w)
    n = w[0]

    for row, field in enumerate([n, u[0], u[1], u[2], t, q[0], q[1], q[2]]):
        macro_ref[pl.ds(row, blocks, stride=8), :] = field

    inverse = 1.0 / t
    relax = n * power(t, 1.0 - SHEAR_EXPONENT)
    damp = 1.0 / (1.0 + relax)
    scale = n * inverse * lax.rsqrt(t) * relax * damp
    beta = scale * ((1.0 - CONDUCTIVE_SHARE) / 5.0) * inverse * inverse / n
    cubic = beta * inverse
    qu = q[0] * u[0] + q[1] * u[1] + q[2] * u[2]
    offset = beta * (uu * inverse - 5.0)
    twice = 2.0 * cubic
    zz = q[2] * u[2]
    polynomial = [
        scale - qu * offset,
        offset * q[0] + twice * qu * u[0],
        offset * q[1] + twice * qu * u[1],
        offset * q[2] + twice * qu * u[2],
        -cubic * (qu + 2.0 * zz),
        -twice * (q[0] * u[0] - zz),
        -twice * (q[0] * u[1] + q[1] * u[0]),
        -twice * (q[0] * u[2] + q[2] * u[0]),
        -twice * (q[1] * u[1] - zz),
        -twice * (q[1] * u[2] + q[2] * u[1]),
        cubic * q[0],
        cubic * q[1],
        cubic * q[2],
    ]
    zero = jnp.zeros_like(n)
    rate = (0.5 * LOG2E) * inverse
    exponent = [-rate * uu, 2.0 * rate * u[0], 2.0 * rate * u[1], 2.0 * rate * u[2], -rate]
    rows = polynomial + [damp, zero, zero] + exponent + [zero, zero, zero]
    for row, field in enumerate(rows):
        coef_ref[pl.ds(row, blocks, stride=COEF), :] = field


def fluid_call(moments):
    blocks = moments.shape[0] // SENT
    return pl.pallas_call(
        fluid_kernel,
        out_shape=(
            pltpu.VMEM((blocks * COEF, LANES), jnp.float32),
            pltpu.VMEM((blocks * 8, LANES), jnp.float32),
        ),
        in_specs=[WHOLE],
        out_specs=(WHOLE, WHOLE),
        compiler_params=PARAMS,
        name="fluid",
    )(moments)


def relaxed(g, coef_ref, basis, tile):
    per_tile = TILE // LANES
    parts = [
        coef_ref[pl.ds(pl.multiple_of((tile * per_tile + part) * COEF, 8), COEF), :]
        for part in range(per_tile)
    ]
    coefficients = jnp.concatenate(parts, axis=1)
    polynomial = dot(basis, expand(coefficients[:BASIS]))
    rows = jnp.concatenate([coefficients[BASIS:], jnp.zeros((8, TILE), jnp.float32)], axis=0)
    exponent = dot(basis, expand(rows))
    return g * coefficients[DAMP : DAMP + 1] + jnp.exp2(exponent) * polynomial


def update_kernel(g_ref, coef_ref, basis_ref, table_ref, f_ref, moments_ref):
    cells = f_ref.shape[1]

    def step(tile, carry):
        here = pl.ds(pl.multiple_of(tile * TILE, TILE), TILE)
        values = relaxed(g_ref[:, here], coef_ref, basis_ref[...], tile)
        f_ref[:, here] = values
        store_moments(moments_ref, table_ref[...], values, tile, cells // LANES)
        return carry

    lax.fori_loop(0, cells // TILE, step, 0, unroll=4)


def update_call(g, coefficients, basis, table):
    cells = g.shape[1]
    return pl.pallas_call(
        update_kernel,
        out_shape=(
            pltpu.VMEM(g.shape, jnp.float32),
            pltpu.VMEM((SENT * cells // LANES, LANES), jnp.float32),
        ),
        in_specs=[WHOLE] * 4,
        out_specs=(WHOLE, WHOLE),
        compiler_params=PARAMS,
        name="update",
    )(g, coefficients, basis, table)


def finish_kernel(g_ref, coef_ref, macro_ref, basis_ref, f_ref, fields_ref, held, sems):
    cells = g_ref.shape[1]
    width = cells // CHUNKS
    copies = []
    for chunk in range(CHUNKS):

        def step(local, carry, chunk=chunk):
            tile = chunk * (width // TILE) + local
            here = pl.ds(pl.multiple_of(tile * TILE, TILE), TILE)
            held[:, here] = relaxed(g_ref[:, here], coef_ref, basis_ref[...], tile)
            for part in range(TILE // LANES):
                block = tile * (TILE // LANES) + part
                fields_ref[:, pl.ds(pl.multiple_of(block * LANES, LANES), LANES)] = macro_ref[
                    pl.ds(pl.multiple_of(block * 8, 8), 8), :
                ]
            return carry

        lax.fori_loop(0, width // TILE, step, 0, unroll=True)
        there = pl.ds(chunk * width, width)
        copy = pltpu.make_async_copy(held.at[:, there], f_ref.at[:, there], sems.at[chunk])
        copy.start()
        copies.append(copy)
    for copy in copies:
        copy.wait()


def finish_call(g, coefficients, macro, basis):
    cells = g.shape[1]
    return pl.pallas_call(
        finish_kernel,
        out_shape=(
            jax.ShapeDtypeStruct(g.shape, jnp.float32),
            jax.ShapeDtypeStruct((8, cells), jnp.float32),
        ),
        in_specs=[WHOLE] * 4,
        out_specs=(OUTSIDE, WHOLE),
        scratch_shapes=[
            pltpu.VMEM(g.shape, jnp.float32),
            pltpu.SemaphoreType.DMA((CHUNKS,)),
        ],
        compiler_params=PARAMS,
        name="finish",
    )(g, coefficients, macro, basis)


def stages(count):
    sizes = []
    for size in (2, 2):
        if count > 1 and count % size == 0:
            sizes.append(size)
            count //= size
    while count % 4 == 0:
        sizes.append(4)
        count //= 4
    while count % 2 == 0:
        sizes.append(2)
        count //= 2
    return sizes


def pairs(count, stride, size, shift):
    out = []
    for device in range(count):
        rank = device // stride % size
        out.append((device, device + ((rank ^ shift) - rank) * stride))
    return out


def staged_sum(values, count, beside):
    index = lax.axis_index("vel")
    stride, trail = 1, []
    block = values
    aside = None
    for number, size in enumerate(stages(count)):
        if number == 1:
            block, aside = beside(block)
        rank = index // stride % size
        width = block.shape[0] // size
        total = lax.dynamic_slice_in_dim(block, rank * width, width, 0)
        for shift in range(1, size):
            piece = lax.dynamic_slice_in_dim(block, (rank ^ shift) * width, width, 0)
            total = total + lax.ppermute(piece, "vel", pairs(count, stride, size, shift))
        if number == 1:
            total, aside = lax.optimization_barrier((total, aside))
        trail.append((size, stride, rank, width))
        block = total
        stride *= size
    for size, stride, rank, width in reversed(trail):
        whole = jnp.zeros((width * size, block.shape[1]), block.dtype)
        whole = lax.dynamic_update_slice_in_dim(whole, block, rank * width, 0)
        for shift in range(1, size):
            piece = lax.ppermute(block, "vel", pairs(count, stride, size, shift))
            whole = lax.dynamic_update_slice_in_dim(whole, piece, (rank ^ shift) * width, 0)
        block = whole
    return block, aside


def on_device(velocities, density, flow, thermal, deviation):
    count = lax.axis_size("vel")
    f, moments, basis, table = start_call(
        velocities, density, flow, thermal, deviation, velocities.shape[1] * count
    )
    stream = velocities[0][:, None]
    for iteration in range(ITERS):

        def beside(block):
            block, held = lax.optimization_barrier((block, f))
            return block, transport_call(stream, held)

        summed, g = staged_sum(moments, count, beside)
        coefficients, macro = fluid_call(summed)
        if iteration < ITERS - 1:
            f, moments = update_call(g, coefficients, basis, table)
    return finish_call(g, coefficients, macro, basis)


def solution(mesh):
    return jax.shard_map(
        on_device,
        mesh=mesh,
        in_specs=(P(None, "vel"), P("grp"), P(None, "grp"), P("grp"), P("vel", "grp")),
        out_specs=(P("vel", "grp"), P(None, "grp")),
        check_vma=False,
    )
```

profile of v0, /device:TPU:0, one launch (start us, length us, event | category | flops | bytes accessed | tf_op | source)
XLA Modules:
  0.0 108.0 jit_solution(4588885928006770883)
XLA Ops:
  0.7 2.2 %copy-done.2 = f32[128,8192]{1,0:T(8,128)S(1)} copy-done((f32[128,8192]{1,0:T(8,128)S(1)}, f32[128,8192]{1,0:T(8,128)}, u32[]{:S(2)}) %copy-start.2) | copy-done | bytes 4194328
  5.9 4.0 %start.1 = (f32[128,8192]{1,0:T(8,128)S(1)}, f32[896,128]{1,0:T(8,128)S(1)}, bf16[128,128]{1,0:T(8,128)(2,1)S(1)}, bf16[32,256]{1,0:T(8,128)(2,1)S(1)}) custom-call(f32[3,128]{1,0:T(4,128)S(1)} %copy-done.8, f32[1,8192]{1,0:T(1,128)S(1)} %bitcast.4, f32[3,8192]{1,0:T(4,128)S(1)} %copy-done.5, f32[1,8192]{1,0:T(1,128)S(1)} %bitcast.5, f32[128,8192]{1,0:T(8,128)S(1)} %copy-done.2), custom_call_target="tpu_custom_call" | custom-call | tf_op jit(solution)/shard_map/start/pallas_call | solution.py:141
  9.9 2.0 %copy-done.3 = f32[128,8192]{1,0:T(8,128)} copy-done((f32[128,8192]{1,0:T(8,128)}, f32[128,8192]{1,0:T(8,128)S(1)}, u32[]{:S(2)}) %copy-start.3) | copy-done | bytes 4194328
  13.6 3.0 %collective-permute-start.1 = (f32[224,128]{1,0:T(8,128)S(1)}, f32[224,128]{1,0:T(8,128)S(1)}, u32[]{:S(2)}, u32[]{:S(2)}) collective-permute-start(f32[224,128]{1,0:T(8,128)S(1)} %constant_dynamic-slice_fusion.8), channel_id=1, source_target_pairs={{0,2},{1,3},{2,0},{3,1},{4,6},{5,7},{6,4},{7,5},{8,10},{9,11},{10,... | collective-permute-start | bytes 344072 | tf_op jit(solution)/shard_map/ppermute | solution.py:458
  17.4 2.2 %copy-done.4 = f32[128,8192]{1,0:T(8,128)S(1)} copy-done((f32[128,8192]{1,0:T(8,128)S(1)}, f32[128,8192]{1,0:T(8,128)}, u32[]{:S(2)}) %copy-start.4) | copy-done | bytes 4194328
  19.6 11.5 %transport.2.g_ref = f32[128,8192]{1,0:T(8,128)S(1)} custom-call(f32[128,1]{1,0:T(8,128)S(1)} %copy.7.stream_ref, f32[128,8192]{1,0:T(8,128)S(1)} %copy-done.4), custom_call_target="tpu_custom_call" | custom-call | tf_op jit(solution)/shard_map/transport/pallas_call | solution.py:200
  31.1 2.0 %copy-done = f32[128,8192]{1,0:T(8,128)} copy-done((f32[128,8192]{1,0:T(8,128)}, f32[128,8192]{1,0:T(8,128)S(1)}, u32[]{:S(2)}) %copy-start) | copy-done | bytes 4194328
  33.2 1.6 %collective-permute-start.2 = (f32[56,128]{1,0:T(8,128)S(1)}, f32[56,128]{1,0:T(8,128)S(1)}, u32[]{:S(2)}, u32[]{:S(2)}) collective-permute-start(f32[56,128]{1,0:T(8,128)S(1)} %get-tuple-element.43), channel_id=1, source_target_pairs={{0,4},{1,5},{2,6},{3,7},{4,0},{5,1},{6,2},{7,3},{8,12},{9,13},{10,... | collective-permute-start | bytes 86024 | tf_op jit(solution)/shard_map/ppermute | solution.py:458
  34.8 2.6 %collective-permute-start.3 = (f32[56,128]{1,0:T(8,128)S(1)}, f32[56,128]{1,0:T(8,128)S(1)}, u32[]{:S(2)}, u32[]{:S(2)}) collective-permute-start(f32[56,128]{1,0:T(8,128)S(1)} %get-tuple-element.45), channel_id=1, source_target_pairs={{0,8},{1,9},{2,10},{3,11},{4,12},{5,13},{6,14},{7,15},{8,0},{9,1},... | collective-permute-start | bytes 86024 | tf_op jit(solution)/shard_map/ppermute | solution.py:458
  37.6 2.5 %collective-permute-done.3 = f32[56,128]{1,0:T(8,128)S(1)} collective-permute-done((f32[56,128]{1,0:T(8,128)S(1)}, f32[56,128]{1,0:T(8,128)S(1)}, u32[]{:S(2)}, u32[]{:S(2)}) %collective-permute-start.3) | collective-permute-done | bytes 28704 | tf_op jit(solution)/shard_map/ppermute | solution.py:458
  40.1 3.3 %collective-permute-done.4 = f32[56,128]{1,0:T(8,128)S(1)} collective-permute-done((f32[56,128]{1,0:T(8,128)S(1)}, f32[56,128]{1,0:T(8,128)S(1)}, u32[]{:S(2)}, u32[]{:S(2)}) %collective-permute-start.4) | collective-permute-done | bytes 28704 | tf_op jit(solution)/shard_map/ppermute | solution.py:458
  44.1 3.8 %collective-permute-start.7 = (f32[56,128]{1,0:T(8,128)S(1)}, f32[56,128]{1,0:T(8,128)S(1)}, u32[]{:S(2)}, u32[]{:S(2)}) collective-permute-start(f32[56,128]{1,0:T(8,128)S(1)} %get-tuple-element.39), channel_id=1, source_target_pairs={{0,12},{1,13},{2,14},{3,15},{4,8},{5,9},{6,10},{7,11},{8,4},{9,5},... | collective-permute-start | bytes 86024 | tf_op jit(solution)/shard_map/ppermute | solution.py:468
  48.3 1.7 %collective-permute-done.7 = f32[56,128]{1,0:T(8,128)S(1)} collective-permute-done((f32[56,128]{1,0:T(8,128)S(1)}, f32[56,128]{1,0:T(8,128)S(1)}, u32[]{:S(2)}, u32[]{:S(2)}) %collective-permute-start.7) | collective-permute-done | bytes 28704 | tf_op jit(solution)/shard_map/ppermute | solution.py:468
  50.6 4.2 %collective-permute-done.8 = f32[224,128]{1,0:T(8,128)S(1)} collective-permute-done((f32[224,128]{1,0:T(8,128)S(1)}, f32[224,128]{1,0:T(8,128)S(1)}, u32[]{:S(2)}, u32[]{:S(2)}) %collective-permute-start.8) | collective-permute-done | bytes 114720 | tf_op jit(solution)/shard_map/ppermute | solution.py:468
  57.9 2.2 %copy-done.1 = f32[128,8192]{1,0:T(8,128)S(1)} copy-done((f32[128,8192]{1,0:T(8,128)S(1)}, f32[128,8192]{1,0:T(8,128)}, u32[]{:S(2)}) %copy-start.1) | copy-done | bytes 4194328
  60.1 7.1 %update.1 = (f32[128,8192]{1,0:T(8,128)S(1)}, f32[896,128]{1,0:T(8,128)S(1)}) custom-call(f32[128,8192]{1,0:T(8,128)S(1)} %copy-done.1, f32[1536,128]{1,0:T(8,128)S(1)} %get-tuple-element.25.coef_ref, bf16[128,128]{1,0:T(8,128)(2,1)S(1)} %get-tuple-element.26.basis_ref, bf16[32,256]{1,0:T(8,128)(2,1)S(1)} %get-tuple-element.27.table_ref), custom_call_target="tpu_custom_call" | custom-call | tf_op jit(solution)/shard_map/update/pallas_call | solution.py:364
  69.4 11.5 %transport.3.g_ref = f32[128,8192]{1,0:T(8,128)S(1)} custom-call(f32[128,1]{1,0:T(8,128)S(1)} %copy.7.stream_ref, f32[128,8192]{1,0:T(8,128)S(1)} %get-tuple-element.31.f_ref), custom_call_target="tpu_custom_call" | custom-call | tf_op jit(solution)/shard_map/transport/pallas_call | solution.py:200
  81.4 3.7 %collective-permute-start.13 = (f32[56,128]{1,0:T(8,128)S(1)}, f32[56,128]{1,0:T(8,128)S(1)}, u32[]{:S(2)}, u32[]{:S(2)}) collective-permute-start(f32[56,128]{1,0:T(8,128)S(1)} %get-tuple-element.42), channel_id=1, source_target_pairs={{0,8},{1,9},{2,10},{3,11},{4,12},{5,13},{6,14},{7,15},{8,0},{9,1},... | collective-permute-start | bytes 86024 | tf_op jit(solution)/shard_map/ppermute | solution.py:458
  85.5 2.0 %collective-permute-done.13 = f32[56,128]{1,0:T(8,128)S(1)} collective-permute-done((f32[56,128]{1,0:T(8,128)S(1)}, f32[56,128]{1,0:T(8,128)S(1)}, u32[]{:S(2)}, u32[]{:S(2)}) %collective-permute-start.13) | collective-permute-done | bytes 28704 | tf_op jit(solution)/shard_map/ppermute | solution.py:458
  87.5 3.6 %collective-permute-done.14 = f32[56,128]{1,0:T(8,128)S(1)} collective-permute-done((f32[56,128]{1,0:T(8,128)S(1)}, f32[56,128]{1,0:T(8,128)S(1)}, u32[]{:S(2)}, u32[]{:S(2)}) %collective-permute-start.14) | collective-permute-done | bytes 28704 | tf_op jit(solution)/shard_map/ppermute | solution.py:458
  91.8 3.8 %collective-permute-start.17 = (f32[56,128]{1,0:T(8,128)S(1)}, f32[56,128]{1,0:T(8,128)S(1)}, u32[]{:S(2)}, u32[]{:S(2)}) collective-permute-start(f32[56,128]{1,0:T(8,128)S(1)} %get-tuple-element.37), channel_id=1, source_target_pairs={{0,12},{1,13},{2,14},{3,15},{4,8},{5,9},{6,10},{7,11},{8,4},{9,5},... | collective-permute-start | bytes 86024 | tf_op jit(solution)/shard_map/ppermute | solution.py:468
  96.0 1.7 %collective-permute-done.17 = f32[56,128]{1,0:T(8,128)S(1)} collective-permute-done((f32[56,128]{1,0:T(8,128)S(1)}, f32[56,128]{1,0:T(8,128)S(1)}, u32[]{:S(2)}, u32[]{:S(2)}) %collective-permute-start.17) | collective-permute-done | bytes 28704 | tf_op jit(solution)/shard_map/ppermute | solution.py:468
  99.3 3.2 %collective-permute-done.18 = f32[224,128]{1,0:T(8,128)S(1)} collective-permute-done((f32[224,128]{1,0:T(8,128)S(1)}, f32[224,128]{1,0:T(8,128)S(1)}, u32[]{:S(2)}, u32[]{:S(2)}) %collective-permute-start.18) | collective-permute-done | bytes 114720 | tf_op jit(solution)/shard_map/ppermute | solution.py:468
  105.0 3.1 %finish.1 = (f32[128,8192]{1,0:T(8,128)}, f32[8,8192]{1,0:T(8,128)}) custom-call(f32[128,8192]{1,0:T(8,128)S(1)} %transport.3.g_ref, f32[1536,128]{1,0:T(8,128)S(1)} %get-tuple-element.34.coef_ref, f32[512,128]{1,0:T(8,128)S(1)} %get-tuple-element.35.macro_ref, bf16[128,128]{1,0:T(8,128)(2,1)S(1)} %get-tuple-element.26.basis_ref), custom_call_target="tpu_custom_call" | custom-call | tf_op jit(solution)/shard_map/finish/pallas_call | solution.py:405
  (75 shorter events, 18.7 us)
Async XLA Ops:
  0.7 2.2 %copy-start.2 = (f32[128,8192]{1,0:T(8,128)S(1)}, f32[128,8192]{1,0:T(8,128)}, u32[]{:S(2)}) copy-start(f32[128,8192]{1,0:T(8,128)} %deviation_ref.1) | copy-start | bytes 12582916
  11.9 1.6 %collective-permute-start = (f32[448,128]{1,0:T(8,128)S(1)}, f32[448,128]{1,0:T(8,128)S(1)}, u32[]{:S(2)}, u32[]{:S(2)}) collective-permute-start(f32[448,128]{1,0:T(8,128)S(1)} %constant_dynamic-slice_fusion.9), channel_id=1, source_target_pairs={{0,1},{1,0},{2,3},{3,2},{4,5},{5,4},{6,7},{7,6},{8,9},{9,8},{10,11... | collective-permute-start | bytes 688136 | tf_op jit(solution)/shard_map/ppermute | solution.py:458
  13.6 19.5 %collective-permute-start.1 = (f32[224,128]{1,0:T(8,128)S(1)}, f32[224,128]{1,0:T(8,128)S(1)}, u32[]{:S(2)}, u32[]{:S(2)}) collective-permute-start(f32[224,128]{1,0:T(8,128)S(1)} %constant_dynamic-slice_fusion.8), channel_id=1, source_target_pairs={{0,2},{1,3},{2,0},{3,1},{4,6},{5,7},{6,4},{7,5},{8,10},{9,11},{10,... | collective-permute-start | bytes 344072 | tf_op jit(solution)/shard_map/ppermute | solution.py:458
  17.4 2.2 %copy-start.4 = (f32[128,8192]{1,0:T(8,128)S(1)}, f32[128,8192]{1,0:T(8,128)}, u32[]{:S(2)}) copy-start(f32[128,8192]{1,0:T(8,128)} %copy-done.3) | copy-start | bytes 12582916
  31.1 2.0 %copy-start = (f32[128,8192]{1,0:T(8,128)}, f32[128,8192]{1,0:T(8,128)S(1)}, u32[]{:S(2)}) copy-start(f32[128,8192]{1,0:T(8,128)S(1)} %transport.2.g_ref) | copy-start | bytes 12582916
  33.2 4.5 %collective-permute-start.2 = (f32[56,128]{1,0:T(8,128)S(1)}, f32[56,128]{1,0:T(8,128)S(1)}, u32[]{:S(2)}, u32[]{:S(2)}) collective-permute-start(f32[56,128]{1,0:T(8,128)S(1)} %get-tuple-element.43), channel_id=1, source_target_pairs={{0,4},{1,5},{2,6},{3,7},{4,0},{5,1},{6,2},{7,3},{8,12},{9,13},{10,... | collective-permute-start | bytes 86024 | tf_op jit(solution)/shard_map/ppermute | solution.py:458
  34.8 5.3 %collective-permute-start.3 = (f32[56,128]{1,0:T(8,128)S(1)}, f32[56,128]{1,0:T(8,128)S(1)}, u32[]{:S(2)}, u32[]{:S(2)}) collective-permute-start(f32[56,128]{1,0:T(8,128)S(1)} %get-tuple-element.45), channel_id=1, source_target_pairs={{0,8},{1,9},{2,10},{3,11},{4,12},{5,13},{6,14},{7,15},{8,0},{9,1},... | collective-permute-start | bytes 86024 | tf_op jit(solution)/shard_map/ppermute | solution.py:458
  37.4 6.0 %collective-permute-start.4 = (f32[56,128]{1,0:T(8,128)S(1)}, f32[56,128]{1,0:T(8,128)S(1)}, u32[]{:S(2)}, u32[]{:S(2)}) collective-permute-start(f32[56,128]{1,0:T(8,128)S(1)} %get-tuple-element.44), channel_id=1, source_target_pairs={{0,12},{1,13},{2,14},{3,15},{4,8},{5,9},{6,10},{7,11},{8,4},{9,5},... | collective-permute-start | bytes 86024 | tf_op jit(solution)/shard_map/ppermute | solution.py:458
  43.4 4.5 %collective-permute-start.5 = (f32[56,128]{1,0:T(8,128)S(1)}, f32[56,128]{1,0:T(8,128)S(1)}, u32[]{:S(2)}, u32[]{:S(2)}) collective-permute-start(f32[56,128]{1,0:T(8,128)S(1)} %get-tuple-element.39), channel_id=1, source_target_pairs={{0,4},{1,5},{2,6},{3,7},{4,0},{5,1},{6,2},{7,3},{8,12},{9,13},{10,... | collective-permute-start | bytes 86024 | tf_op jit(solution)/shard_map/ppermute | solution.py:468
  43.5 4.8 %collective-permute-start.6 = (f32[56,128]{1,0:T(8,128)S(1)}, f32[56,128]{1,0:T(8,128)S(1)}, u32[]{:S(2)}, u32[]{:S(2)}) collective-permute-start(f32[56,128]{1,0:T(8,128)S(1)} %get-tuple-element.39), channel_id=1, source_target_pairs={{0,8},{1,9},{2,10},{3,11},{4,12},{5,13},{6,14},{7,15},{8,0},{9,1},... | collective-permute-start | bytes 86024 | tf_op jit(solution)/shard_map/ppermute | solution.py:468
  44.1 6.0 %collective-permute-start.7 = (f32[56,128]{1,0:T(8,128)S(1)}, f32[56,128]{1,0:T(8,128)S(1)}, u32[]{:S(2)}, u32[]{:S(2)}) collective-permute-start(f32[56,128]{1,0:T(8,128)S(1)} %get-tuple-element.39), channel_id=1, source_target_pairs={{0,12},{1,13},{2,14},{3,15},{4,8},{5,9},{6,10},{7,11},{8,4},{9,5},... | collective-permute-start | bytes 86024 | tf_op jit(solution)/shard_map/ppermute | solution.py:468
  50.0 4.8 %collective-permute-start.8 = (f32[224,128]{1,0:T(8,128)S(1)}, f32[224,128]{1,0:T(8,128)S(1)}, u32[]{:S(2)}, u32[]{:S(2)}) collective-permute-start(f32[224,128]{1,0:T(8,128)S(1)} %constant_dynamic-update-slice_fusion.12), channel_id=1, source_target_pairs={{0,2},{1,3},{2,0},{3,1},{4,6},{5,7},{6,4},{7,5},{8,10},{9,11},{10,... | collective-permute-start | bytes 344072 | tf_op jit(solution)/shard_map/ppermute | solution.py:468
  54.8 1.6 %collective-permute-start.9 = (f32[448,128]{1,0:T(8,128)S(1)}, f32[448,128]{1,0:T(8,128)S(1)}, u32[]{:S(2)}, u32[]{:S(2)}) collective-permute-start(f32[448,128]{1,0:T(8,128)S(1)} %constant_dynamic-update-slice_fusion.10), channel_id=1, source_target_pairs={{0,1},{1,0},{2,3},{3,2},{4,5},{5,4},{6,7},{7,6},{8,9},{9,8},{10,11... | collective-permute-start | bytes 688136 | tf_op jit(solution)/shard_map/ppermute | solution.py:468
  57.9 2.2 %copy-start.1 = (f32[128,8192]{1,0:T(8,128)S(1)}, f32[128,8192]{1,0:T(8,128)}, u32[]{:S(2)}) copy-start(f32[128,8192]{1,0:T(8,128)} %copy-done) | copy-start | bytes 12582916
  67.3 1.6 %collective-permute-start.10 = (f32[448,128]{1,0:T(8,128)S(1)}, f32[448,128]{1,0:T(8,128)S(1)}, u32[]{:S(2)}, u32[]{:S(2)}) collective-permute-start(f32[448,128]{1,0:T(8,128)S(1)} %constant_dynamic-slice_fusion.4), channel_id=1, source_target_pairs={{0,1},{1,0},{2,3},{3,2},{4,5},{5,4},{6,7},{7,6},{8,9},{9,8},{10,11... | collective-permute-start | bytes 688136 | tf_op jit(solution)/shard_map/ppermute | solution.py:458
  68.9 12.1 %collective-permute-start.11 = (f32[224,128]{1,0:T(8,128)S(1)}, f32[224,128]{1,0:T(8,128)S(1)}, u32[]{:S(2)}, u32[]{:S(2)}) collective-permute-start(f32[224,128]{1,0:T(8,128)S(1)} %constant_dynamic-slice_fusion.3), channel_id=1, source_target_pairs={{0,2},{1,3},{2,0},{3,1},{4,6},{5,7},{6,4},{7,5},{8,10},{9,11},{10,... | collective-permute-start | bytes 344072 | tf_op jit(solution)/shard_map/ppermute | solution.py:458
  81.0 4.5 %collective-permute-start.12 = (f32[56,128]{1,0:T(8,128)S(1)}, f32[56,128]{1,0:T(8,128)S(1)}, u32[]{:S(2)}, u32[]{:S(2)}) collective-permute-start(f32[56,128]{1,0:T(8,128)S(1)} %get-tuple-element.40), channel_id=1, source_target_pairs={{0,4},{1,5},{2,6},{3,7},{4,0},{5,1},{6,2},{7,3},{8,12},{9,13},{10,... | collective-permute-start | bytes 86024 | tf_op jit(solution)/shard_map/ppermute | solution.py:458
  81.4 6.0 %collective-permute-start.13 = (f32[56,128]{1,0:T(8,128)S(1)}, f32[56,128]{1,0:T(8,128)S(1)}, u32[]{:S(2)}, u32[]{:S(2)}) collective-permute-start(f32[56,128]{1,0:T(8,128)S(1)} %get-tuple-element.42), channel_id=1, source_target_pairs={{0,8},{1,9},{2,10},{3,11},{4,12},{5,13},{6,14},{7,15},{8,0},{9,1},... | collective-permute-start | bytes 86024 | tf_op jit(solution)/shard_map/ppermute | solution.py:458
  85.2 5.9 %collective-permute-start.14 = (f32[56,128]{1,0:T(8,128)S(1)}, f32[56,128]{1,0:T(8,128)S(1)}, u32[]{:S(2)}, u32[]{:S(2)}) collective-permute-start(f32[56,128]{1,0:T(8,128)S(1)} %get-tuple-element.41), channel_id=1, source_target_pairs={{0,12},{1,13},{2,14},{3,15},{4,8},{5,9},{6,10},{7,11},{8,4},{9,5},... | collective-permute-start | bytes 86024 | tf_op jit(solution)/shard_map/ppermute | solution.py:458
  91.1 4.5 %collective-permute-start.15 = (f32[56,128]{1,0:T(8,128)S(1)}, f32[56,128]{1,0:T(8,128)S(1)}, u32[]{:S(2)}, u32[]{:S(2)}) collective-permute-start(f32[56,128]{1,0:T(8,128)S(1)} %get-tuple-element.37), channel_id=1, source_target_pairs={{0,4},{1,5},{2,6},{3,7},{4,0},{5,1},{6,2},{7,3},{8,12},{9,13},{10,... | collective-permute-start | bytes 86024 | tf_op jit(solution)/shard_map/ppermute | solution.py:468
  91.2 4.8 %collective-permute-start.16 = (f32[56,128]{1,0:T(8,128)S(1)}, f32[56,128]{1,0:T(8,128)S(1)}, u32[]{:S(2)}, u32[]{:S(2)}) collective-permute-start(f32[56,128]{1,0:T(8,128)S(1)} %get-tuple-element.37), channel_id=1, source_target_pairs={{0,8},{1,9},{2,10},{3,11},{4,12},{5,13},{6,14},{7,15},{8,0},{9,1},... | collective-permute-start | bytes 86024 | tf_op jit(solution)/shard_map/ppermute | solution.py:468
  91.8 5.9 %collective-permute-start.17 = (f32[56,128]{1,0:T(8,128)S(1)}, f32[56,128]{1,0:T(8,128)S(1)}, u32[]{:S(2)}, u32[]{:S(2)}) collective-permute-start(f32[56,128]{1,0:T(8,128)S(1)} %get-tuple-element.37), channel_id=1, source_target_pairs={{0,12},{1,13},{2,14},{3,15},{4,8},{5,9},{6,10},{7,11},{8,4},{9,5},... | collective-permute-start | bytes 86024 | tf_op jit(solution)/shard_map/ppermute | solution.py:468
  97.7 4.8 %collective-permute-start.18 = (f32[224,128]{1,0:T(8,128)S(1)}, f32[224,128]{1,0:T(8,128)S(1)}, u32[]{:S(2)}, u32[]{:S(2)}) collective-permute-start(f32[224,128]{1,0:T(8,128)S(1)} %constant_dynamic-update-slice_fusion.4), channel_id=1, source_target_pairs={{0,2},{1,3},{2,0},{3,1},{4,6},{5,7},{6,4},{7,5},{8,10},{9,11},{10,... | collective-permute-start | bytes 344072 | tf_op jit(solution)/shard_map/ppermute | solution.py:468
  102.5 1.6 %collective-permute-start.19 = (f32[448,128]{1,0:T(8,128)S(1)}, f32[448,128]{1,0:T(8,128)S(1)}, u32[]{:S(2)}, u32[]{:S(2)}) collective-permute-start(f32[448,128]{1,0:T(8,128)S(1)} %constant_dynamic-update-slice_fusion.2), channel_id=1, source_target_pairs={{0,1},{1,0},{2,3},{3,2},{4,5},{5,4},{6,7},{7,6},{8,9},{9,8},{10,11... | collective-permute-start | bytes 688136 | tf_op jit(solution)/shard_map/ppermute | solution.py:468
  (5 other events, 5.1 us)
where the time goes:
time: 108 us
  Pallas kernels  39.5 us (37%)
  waiting for transfers between devices  28.4 us (26%)
  starting transfers between devices  24.2 us (22%)
  local copies, waits for them, and re-layouts  14.8 us (14%)
    pallas_call x2, Pallas kernels, transport_call(): pl.pallas_call(transport_kernel, out_shape=pltpu.VMEM(f.shape, jnp.float3...  23 us
    ppermute x10, waiting for transfers between devices, staged_sum(): piece = lax.ppermute(block, 'vel', pairs(count, stride, size, shift))  14.6 us
    ppermute x10, waiting for transfers between devices, staged_sum(): lax.ppermute(piece, 'vel', pairs(count, stride, size, shift))  13.8 us
    unnamed x18, local copies, waits for them, and re-layouts  13.7 us
    ppermute x10, starting transfers between devices, staged_sum(): lax.ppermute(piece, 'vel', pairs(count, stride, size, shift))  13.2 us
    ppermute x10, starting transfers between devices, staged_sum(): piece = lax.ppermute(block, 'vel', pairs(count, stride, size, shift))  11.1 us
    pallas_call x1, Pallas kernels, update_call(): pl.pallas_call(update_kernel, out_shape=(pltpu.VMEM(g.shape, jnp.float32)...  7.12 us
    pallas_call x1, Pallas kernels, start_call(): pl.pallas_call(functools.partial(start_kernel, total_count), out_shape=(p...  3.96 us
  transfers between devices with their start and end apart: 20, of which 14 were waited for; matrix products, arithmetic and copies ran while one was open for 1% of the time, Pallas kernels for 21%

commit v1 on v0

--- a/solution.py
+++ b/solution.py
@@ -19,17 +19,29 @@
 
 LOG2E = 1.4426950408889634
 LANES = 128
-TILE = 256
+TILE = 512
 BASIS = 16
 SENT = 14
 COEF = 24
 DAMP = 13
 CHUNKS = 8
-VMEM_BYTES = 24 * 1024 * 1024
+PARTS = 4
+MIB = 1024 * 1024
 
 WHOLE = pl.BlockSpec(memory_space=pltpu.VMEM)
 OUTSIDE = pl.BlockSpec(memory_space=pltpu.HBM)
-PARAMS = pltpu.CompilerParams(vmem_limit_bytes=VMEM_BYTES)
+
+
+def params(mebibytes):
+    return pltpu.CompilerParams(vmem_limit_bytes=mebibytes * MIB)
+
+
+def near(values):
+    return pltpu.with_memory_space_constraint(values, pltpu.VMEM)
+
+
+def far(values):
+    return pltpu.with_memory_space_constraint(values, pltpu.HBM)
 
 
 def dot(left, right):
@@ -97,25 +109,42 @@
 
 def start_kernel(
     total_count,
-    vel_ref, density_ref, flow_ref, thermal_ref, deviation_ref,
-    f_ref, moments_ref, basis_ref, table_ref,
-    held, sems,
+    vel_hbm, density_hbm, flow_hbm, thermal_hbm, deviation_hbm,
+    f_ref, moments_ref, basis_ref, table_ref, stream_ref,
+    vel_ref, density_ref, flow_ref, thermal_ref, deviation_ref, small_sems, sems,
 ):
     cells = f_ref.shape[1]
     width = cells // CHUNKS
+    small = [
+        pltpu.make_async_copy(source, target, small_sems.at[number])
+        for number, (source, target) in enumerate(
+            [
+                (vel_hbm, vel_ref),
+                (density_hbm, density_ref),
+                (flow_hbm, flow_ref),
+                (thermal_hbm, thermal_ref),
+            ]
+        )
+    ]
+    for copy in small:
+        copy.start()
     copies = [
         pltpu.make_async_copy(
+            deviation_hbm.at[:, pl.ds(chunk * width, width)],
             deviation_ref.at[:, pl.ds(chunk * width, width)],
-            held.at[:, pl.ds(chunk * width, width)],
             sems.at[chunk],
         )
         for chunk in range(CHUNKS)
     ]
     for copy in copies:
         copy.start()
+    small[0].wait()
     basis, table = make_tables(vel_ref[...], total_count)
     basis_ref[...] = basis
     table_ref[...] = table
+    stream_ref[...] = jnp.broadcast_to(vel_ref[0:1, :], (LANES, vel_ref.shape[1])).T
+    for copy in small[1:]:
+        copy.wait()
     for chunk in range(CHUNKS):
         copies[chunk].wait()
 
@@ -128,7 +157,7 @@
             rows = [-rate * speed_sq, 2.0 * rate * flow, -rate, jnp.zeros((11, TILE), jnp.float32)]
             exponent = dot(basis_ref[...], expand(jnp.concatenate(rows, axis=0)))
             scale = density / (thermal * jnp.sqrt(thermal))
-            values = jnp.exp2(exponent) * (scale * (1.0 + held[:, here]))
+            values = jnp.exp2(exponent) * (scale * (1.0 + deviation_ref[:, here]))
             f_ref[:, here] = values
             store_moments(moments_ref, table_ref[...], values, tile, cells // LANES)
             return carry
@@ -145,66 +174,97 @@
             pltpu.VMEM((SENT * cells // LANES, LANES), jnp.float32),
             pltpu.VMEM((local, 128), jnp.bfloat16),
             pltpu.VMEM((2 * BASIS, 2 * local), jnp.bfloat16),
+            pltpu.VMEM((local, LANES), jnp.float32),
         ),
-        in_specs=[WHOLE, WHOLE, WHOLE, WHOLE, OUTSIDE],
-        out_specs=(WHOLE, WHOLE, WHOLE, WHOLE),
+        in_specs=[OUTSIDE] * 5,
+        out_specs=(WHOLE,) * 5,
         scratch_shapes=[
+            pltpu.VMEM((3, local), jnp.float32),
+            pltpu.VMEM((1, cells), jnp.float32),
+            pltpu.VMEM((3, cells), jnp.float32),
+            pltpu.VMEM((1, cells), jnp.float32),
             pltpu.VMEM((local, cells), jnp.float32),
+            pltpu.SemaphoreType.DMA((4,)),
             pltpu.SemaphoreType.DMA((CHUNKS,)),
         ],
-        compiler_params=PARAMS,
+        compiler_params=params(16),
         name="start",
-    )(velocities, density.reshape(1, cells), flow, thermal.reshape(1, cells), deviation)
-
-
-def transport_kernel(stream_ref, f_ref, g_ref):
-    rows, cells = f_ref.shape
-    chunk = min(1024, cells)
+    )(
+        far(velocities),
+        far(density.reshape(1, cells)),
+        far(flow),
+        far(thermal.reshape(1, cells)),
+        far(deviation),
+    )
+
+
+def transport_kernel(first_row, stream_ref, f_ref, g_ref):
+    rows, cells = g_ref.shape
     blocks = cells // LANES
-    per_chunk = chunk // LANES
+    lane = lax.broadcasted_iota(jnp.int32, (8, LANES), 1)
+    at_first, at_last = lane == 0, lane == LANES - 1
+    lag = 4
 
     def row_step(row_tile, carry):
-        here = pl.ds(pl.multiple_of(row_tile * 8, 8), 8)
-        stream = jnp.broadcast_to(stream_ref[here, :], (8, LANES))
-        rate = jnp.tile(KINETIC_STEP * jnp.abs(stream), (1, per_chunk + 2))
-        half = jnp.tile(jnp.where(stream > 0, 0.5, -0.5), (1, per_chunk + 2))
-        upward = half > 0
-        for part in range(cells // chunk):
-            first = part * per_chunk
-            before = ((first - 1) % blocks) * LANES
-            after = ((first + per_chunk) % blocks) * LANES
-            x = jnp.concatenate(
-                [
-                    f_ref[here, before : before + LANES],
-                    f_ref[here, part * chunk : (part + 1) * chunk],
-                    f_ref[here, after : after + LANES],
-                ],
-                axis=1,
+        source = pl.ds(pl.multiple_of(first_row + row_tile * 8, 8), 8)
+        target = pl.ds(pl.multiple_of(row_tile * 8, 8), 8)
+        stream = stream_ref[source, :]
+        upward = stream > 0
+        rate = KINETIC_STEP * jnp.abs(stream)
+        half = jnp.where(upward, 0.5, -0.5)
+        x, up, rise, down, face, face_up, face_down = {}, {}, {}, {}, {}, {}, {}
+
+        def load(b):
+            at = (b % blocks) * LANES
+            x[b] = f_ref[source, at : at + LANES]
+            up[b] = pltpu.roll(x[b], 1, 1)
+
+        def slope_in(b):
+            rise[b] = x[b] - jnp.where(at_first, up[b - 1], up[b])
+            down[b] = pltpu.roll(rise[b], LANES - 1, 1)
+
+        def reconstruct(b):
+            ahead = jnp.where(at_last, down[b + 1], down[b])
+            slope = jnp.maximum(jnp.minimum(rise[b], ahead), 0.0) + jnp.minimum(
+                jnp.maximum(rise[b], ahead), 0.0
             )
-            wide = x.shape[1]
-            rise = x - pltpu.roll(x, 1, 1)
-            ahead = pltpu.roll(rise, wide - 1, 1)
-            slope = jnp.maximum(jnp.minimum(rise, ahead), 0.0) + jnp.minimum(
-                jnp.maximum(rise, ahead), 0.0
+            face[b] = x[b] + half * slope
+            face_up[b] = pltpu.roll(face[b], 1, 1)
+            face_down[b] = pltpu.roll(face[b], LANES - 1, 1)
+
+        def store(b):
+            other = jnp.where(
+                upward,
+                jnp.where(at_first, face_up[b - 1], face_up[b]),
+                jnp.where(at_last, face_down[b + 1], face_down[b]),
             )
-            face = x + half * slope
-            other = jnp.where(upward, pltpu.roll(face, 1, 1), pltpu.roll(face, wide - 1, 1))
-            moved = x - rate * (face - other)
-            g_ref[here, part * chunk : (part + 1) * chunk] = moved[:, LANES : LANES + chunk]
+            g_ref[target, b * LANES : (b + 1) * LANES] = x[b] - rate * (face[b] - other)
+
+        for k in range(-2, blocks + 3 * lag + 4):
+            for act, behind, low, high in (
+                (load, 0, -2, blocks + 1),
+                (slope_in, lag, -1, blocks + 1),
+                (reconstruct, 2 * lag + 1, -1, blocks),
+                (store, 3 * lag + 2, 0, blocks - 1),
+            ):
+                if low <= k - behind <= high:
+                    act(k - behind)
         return carry
 
     lax.fori_loop(0, rows // 8, row_step, 0)
 
 
-def transport_call(stream, f):
+def transport_call(stream, f, part):
+    local, cells = f.shape
+    rows = local // PARTS
     return pl.pallas_call(
-        transport_kernel,
-        out_shape=pltpu.VMEM(f.shape, jnp.float32),
+        functools.partial(transport_kernel, part * rows),
+        out_shape=pltpu.VMEM((rows, cells), jnp.float32),
         in_specs=[WHOLE, WHOLE],
         out_specs=WHOLE,
-        compiler_params=PARAMS,
+        compiler_params=params(4),
         name="transport",
-    )(stream, f)
+    )(near(stream), near(f))
 
 
 def fluid_kernel(moments_ref, coef_ref, macro_ref):
@@ -328,7 +388,7 @@
         ),
         in_specs=[WHOLE],
         out_specs=(WHOLE, WHOLE),
-        compiler_params=PARAMS,
+        compiler_params=params(8),
         name="fluid",
     )(moments)
 
@@ -346,12 +406,18 @@
     return g * coefficients[DAMP : DAMP + 1] + jnp.exp2(exponent) * polynomial
 
 
-def update_kernel(g_ref, coef_ref, basis_ref, table_ref, f_ref, moments_ref):
+def gathered(g_refs, here):
+    return jnp.concatenate([ref[:, here] for ref in g_refs], axis=0)
+
+
+def update_kernel(*refs):
+    g_refs = refs[:PARTS]
+    coef_ref, basis_ref, table_ref, f_ref, moments_ref = refs[PARTS:]
     cells = f_ref.shape[1]
 
     def step(tile, carry):
         here = pl.ds(pl.multiple_of(tile * TILE, TILE), TILE)
-        values = relaxed(g_ref[:, here], coef_ref, basis_ref[...], tile)
+        values = relaxed(gathered(g_refs, here), coef_ref, basis_ref[...], tile)
         f_ref[:, here] = values
         store_moments(moments_ref, table_ref[...], values, tile, cells // LANES)
         return carry
@@ -360,22 +426,24 @@
 
 
 def update_call(g, coefficients, basis, table):
-    cells = g.shape[1]
+    rows, cells = g[0].shape
     return pl.pallas_call(
         update_kernel,
         out_shape=(
-            pltpu.VMEM(g.shape, jnp.float32),
+            pltpu.VMEM((rows * PARTS, cells), jnp.float32),
             pltpu.VMEM((SENT * cells // LANES, LANES), jnp.float32),
         ),
-        in_specs=[WHOLE] * 4,
+        in_specs=[WHOLE] * (PARTS + 3),
         out_specs=(WHOLE, WHOLE),
-        compiler_params=PARAMS,
+        compiler_params=params(8),
         name="update",
-    )(g, coefficients, basis, table)
-
-
-def finish_kernel(g_ref, coef_ref, macro_ref, basis_ref, f_ref, fields_ref, held, sems):
-    cells = g_ref.shape[1]
+    )(*[near(part) for part in g], near(coefficients), near(basis), near(table))
+
+
+def finish_kernel(*refs):
+    g_refs = refs[:PARTS]
+    coef_ref, macro_ref, basis_ref, f_ref, fields_ref, held, sems = refs[PARTS:]
+    cells = held.shape[1]
     width = cells // CHUNKS
     copies = []
     for chunk in range(CHUNKS):
@@ -383,7 +451,7 @@
         def step(local, carry, chunk=chunk):
             tile = chunk * (width // TILE) + local
             here = pl.ds(pl.multiple_of(tile * TILE, TILE), TILE)
-            held[:, here] = relaxed(g_ref[:, here], coef_ref, basis_ref[...], tile)
+            held[:, here] = relaxed(gathered(g_refs, here), coef_ref, basis_ref[...], tile)
             for part in range(TILE // LANES):
                 block = tile * (TILE // LANES) + part
                 fields_ref[:, pl.ds(pl.multiple_of(block * LANES, LANES), LANES)] = macro_ref[
@@ -401,22 +469,22 @@
 
 
 def finish_call(g, coefficients, macro, basis):
-    cells = g.shape[1]
+    rows, cells = g[0].shape
     return pl.pallas_call(
         finish_kernel,
         out_shape=(
-            jax.ShapeDtypeStruct(g.shape, jnp.float32),
+            jax.ShapeDtypeStruct((rows * PARTS, cells), jnp.float32),
             jax.ShapeDtypeStruct((8, cells), jnp.float32),
         ),
-        in_specs=[WHOLE] * 4,
+        in_specs=[WHOLE] * (PARTS + 3),
         out_specs=(OUTSIDE, WHOLE),
         scratch_shapes=[
-            pltpu.VMEM(g.shape, jnp.float32),
+            pltpu.VMEM((rows * PARTS, cells), jnp.float32),
             pltpu.SemaphoreType.DMA((CHUNKS,)),
         ],
-        compiler_params=PARAMS,
+        compiler_params=params(16),
         name="finish",
-    )(g, coefficients, macro, basis)
+    )(*[near(part) for part in g], near(coefficients), near(macro), near(basis))
 
 
 def stages(count):
@@ -442,48 +510,58 @@
     return out
 
 
-def staged_sum(values, count, beside):
+def staged_sum(values, count, f, tasks):
     index = lax.axis_index("vel")
-    stride, trail = 1, []
+    stride, trail, results = 1, [], []
     block = values
-    aside = None
-    for number, size in enumerate(stages(count)):
-        if number == 1:
-            block, aside = beside(block)
+    number = 0
+
+    def before(block):
+        if 0 < number <= len(tasks):
+            block, held = lax.optimization_barrier((block, f))
+            results.append(tasks[number - 1](held))
+        return block
+
+    def after(block):
+        if 0 < number <= len(tasks):
+            block, results[-1] = lax.optimization_barrier((block, results[-1]))
+        return block
+
+    for size in stages(count):
+        block = before(block)
         rank = index // stride % size
         width = block.shape[0] // size
         total = lax.dynamic_slice_in_dim(block, rank * width, width, 0)
         for shift in range(1, size):
             piece = lax.dynamic_slice_in_dim(block, (rank ^ shift) * width, width, 0)
             total = total + lax.ppermute(piece, "vel", pairs(count, stride, size, shift))
-        if number == 1:
-            total, aside = lax.optimization_barrier((total, aside))
         trail.append((size, stride, rank, width))
-        block = total
+        block = after(total)
         stride *= size
+        number += 1
     for size, stride, rank, width in reversed(trail):
+        block = before(block)
         whole = jnp.zeros((width * size, block.shape[1]), block.dtype)
         whole = lax.dynamic_update_slice_in_dim(whole, block, rank * width, 0)
         for shift in range(1, size):
             piece = lax.ppermute(block, "vel", pairs(count, stride, size, shift))
             whole = lax.dynamic_update_slice_in_dim(whole, piece, (rank ^ shift) * width, 0)
-        block = whole
-    return block, aside
+        block = after(whole)
+        number += 1
+    return block, results
 
 
 def on_device(velocities, density, flow, thermal, deviation):
     count = lax.axis_size("vel")
-    f, moments, basis, table = start_call(
+    f, moments, basis, table, stream = start_call(
         velocities, density, flow, thermal, deviation, velocities.shape[1] * count
     )
-    stream = velocities[0][:, None]
     for iteration in range(ITERS):
-
-        def beside(block):
-            block, held = lax.optimization_barrier((block, f))
-            return block, transport_call(stream, held)
-
-        summed, g = staged_sum(moments, count, beside)
+        tasks = [
+            functools.partial(lambda held, part: transport_call(stream, held, part), part=part)
+            for part in range(PARTS)
+        ]
+        summed, g = staged_sum(moments, count, f, tasks)
         coefficients, macro = fluid_call(summed)
         if iteration < ITERS - 1:
             f, moments = update_call(g, coefficients, basis, table)

time: 108 us -> 87.1 us (0.81)
  local copies, waits for them, and re-layouts: 14.8 us -> 6.81 us
  Pallas kernels: 39.5 us -> 32.3 us
  waiting for transfers between devices: 28.4 us -> 21.8 us
    pallas_call x4 -> x10, Pallas kernels: 33.2 us -> 23.5 us  [the longest x8 15.9 us: transport_call(): pl.pallas_call(functools.partial(transport_kernel, part * rows), out_shap...]
    unnamed x18 -> x8, local copies, waits for them, and re-layouts: 13.7 us -> 6.39 us
    ppermute x10, waiting for transfers between devices: 13.8 us -> 7.18 us  [staged_sum(): lax.ppermute(piece, 'vel', pairs(count, stride, size, shift))]
    pallas_call x1, Pallas kernels: 3.96 us -> 6.46 us  [start_call(): pl.pallas_call(functools.partial(start_kernel, total_count), out_shape=(p...]
  transfers between devices with their start and end apart: 20 -> 20, of which waited for: 14 -> 11; matrix products, arithmetic and copies ran while one was open for 1% -> 0% of each run, Pallas kernels for 21% -> 14%
where the time goes in v1:
time: 87.1 us; the launch traced here: 86.9 us
  Pallas kernels  32.3 us (37%)
  starting transfers between devices  24.8 us (28%)
  waiting for transfers between devices  21.8 us (25%)
  local copies, waits for them, and re-layouts  6.81 us (8%)
  between operations  1.07 us (1%)
    pallas_call x8, Pallas kernels, transport_call(): pl.pallas_call(functools.partial(transport_kernel, part * rows), out_shap...  15.9 us
    ppermute x10, waiting for transfers between devices, staged_sum(): piece = lax.ppermute(block, 'vel', pairs(count, stride, size, shift))  14.6 us
    ppermute x10, starting transfers between devices, staged_sum(): lax.ppermute(piece, 'vel', pairs(count, stride, size, shift))  13.6 us
    ppermute x10, starting transfers between devices, staged_sum(): piece = lax.ppermute(block, 'vel', pairs(count, stride, size, shift))  11.1 us
    ppermute x10, waiting for transfers between devices, staged_sum(): lax.ppermute(piece, 'vel', pairs(count, stride, size, shift))  7.18 us
    pallas_call x1, Pallas kernels, start_call(): pl.pallas_call(functools.partial(start_kernel, total_count), out_shape=(p...  6.46 us
    unnamed x8, local copies, waits for them, and re-layouts  6.39 us
    pallas_call x1, Pallas kernels, update_call(): pl.pallas_call(update_kernel, out_shape=(pltpu.VMEM((rows * PARTS, cells)...  4.48 us
  transfers between devices with their start and end apart: 20, of which 11 were waited for; matrix products, arithmetic and copies ran while one was open for 0% of the time, Pallas kernels for 14%

profile of v1, /device:TPU:0, one launch (start us, length us, event | category | flops | bytes accessed | tf_op | source)
XLA Modules:
  0.0 86.9 jit_solution(11767792314028591356)
XLA Ops:
  0.7 6.5 %start.1 = (f32[128,8192]{1,0:T(8,128)S(1)}, f32[896,128]{1,0:T(8,128)S(1)}, bf16[128,128]{1,0:T(8,128)(2,1)S(1)}, bf16[32,256]{1,0:T(8,128)(2,1)S(1)}, f32[128,128]{1,0:T(8,128)S(1)}) custom-call(f32[3,128]{1,0:T(4,128)} %vel_hbm.1, f32[1,8192]{1,0:T(1,128)} %bitcast.2, f32[3,8192]{1,0:T(4,128)} %flow_hbm.1, f32[1,8192]{1,0:T(1,128)} %bitcast.3, ...), custom_call_target="tpu_custom_call" | custom-call | tf_op jit(solution)/shard_map/start/pallas_call | solution.py:170
  7.1 2.0 %copy-done = f32[128,8192]{1,0:T(8,128)} copy-done((f32[128,8192]{1,0:T(8,128)}, f32[128,8192]{1,0:T(8,128)S(1)}, u32[]{:S(2)}) %copy-start) | copy-done | bytes 4194328
  10.8 3.0 %collective-permute-start.1 = (f32[224,128]{1,0:T(8,128)S(1)}, f32[224,128]{1,0:T(8,128)S(1)}, u32[]{:S(2)}, u32[]{:S(2)}) collective-permute-start(f32[224,128]{1,0:T(8,128)S(1)} %constant_dynamic-slice_fusion.8), channel_id=1, source_target_pairs={{0,2},{1,3},{2,0},{3,1},{4,6},{5,7},{6,4},{7,5},{8,10},{9,11},{10,... | collective-permute-start | bytes 344072 | tf_op jit(solution)/shard_map/ppermute | solution.py:537
  13.8 2.2 %copy-done.1 = f32[128,8192]{1,0:T(8,128)S(1)} copy-done((f32[128,8192]{1,0:T(8,128)S(1)}, f32[128,8192]{1,0:T(8,128)}, u32[]{:S(2)}) %copy-start.1) | copy-done | bytes 4194328
  16.0 2.0 %transport.8.refs_0_ = f32[32,8192]{1,0:T(8,128)S(1)} custom-call(f32[128,128]{1,0:T(8,128)S(1)} %get-tuple-element.47.stream_ref, f32[128,8192]{1,0:T(8,128)S(1)} %copy-done.1), custom_call_target="tpu_custom_call" | custom-call | tf_op jit(solution)/shard_map/transport/pallas_call | solution.py:260
  19.7 2.6 %collective-permute-start.3 = (f32[56,128]{1,0:T(8,128)S(1)}, f32[56,128]{1,0:T(8,128)S(1)}, u32[]{:S(2)}, u32[]{:S(2)}) collective-permute-start(f32[56,128]{1,0:T(8,128)S(1)} %get-tuple-element.91), channel_id=1, source_target_pairs={{0,8},{1,9},{2,10},{3,11},{4,12},{5,13},{6,14},{7,15},{8,0},{9,1},... | collective-permute-start | bytes 86024 | tf_op jit(solution)/shard_map/ppermute | solution.py:537
  22.5 2.2 %copy-done.2 = f32[128,8192]{1,0:T(8,128)S(1)} copy-done((f32[128,8192]{1,0:T(8,128)S(1)}, f32[128,8192]{1,0:T(8,128)}, u32[]{:S(2)}) %copy-start.2) | copy-done | bytes 4194328
  24.7 2.0 %transport.9.refs_1_ = f32[32,8192]{1,0:T(8,128)S(1)} custom-call(f32[128,128]{1,0:T(8,128)S(1)} %get-tuple-element.47.stream_ref, f32[128,8192]{1,0:T(8,128)S(1)} %copy-done.2), custom_call_target="tpu_custom_call" | custom-call | tf_op jit(solution)/shard_map/transport/pallas_call | solution.py:260
  28.0 2.9 %collective-permute-start.6 = (f32[56,128]{1,0:T(8,128)S(1)}, f32[56,128]{1,0:T(8,128)S(1)}, u32[]{:S(2)}, u32[]{:S(2)}) collective-permute-start(f32[56,128]{1,0:T(8,128)S(1)} %add_add_fusion.1), channel_id=1, source_target_pairs={{0,8},{1,9},{2,10},{3,11},{4,12},{5,13},{6,14},{7,15},{8,0},{9,1},... | collective-permute-start | bytes 86024 | tf_op jit(solution)/shard_map/ppermute | solution.py:547
  32.5 2.0 %transport.10.refs_2_ = f32[32,8192]{1,0:T(8,128)S(1)} custom-call(f32[128,128]{1,0:T(8,128)S(1)} %get-tuple-element.47.stream_ref, f32[128,8192]{1,0:T(8,128)S(1)} %copy-done.3), custom_call_target="tpu_custom_call" | custom-call | tf_op jit(solution)/shard_map/transport/pallas_call | solution.py:260
  34.5 2.1 %collective-permute-done.7 = f32[56,128]{1,0:T(8,128)S(1)} collective-permute-done((f32[56,128]{1,0:T(8,128)S(1)}, f32[56,128]{1,0:T(8,128)S(1)}, u32[]{:S(2)}, u32[]{:S(2)}) %collective-permute-start.7) | collective-permute-done | bytes 28704 | tf_op jit(solution)/shard_map/ppermute | solution.py:547
  36.7 2.0 %transport.11.refs_3_ = f32[32,8192]{1,0:T(8,128)S(1)} custom-call(f32[128,128]{1,0:T(8,128)S(1)} %get-tuple-element.47.stream_ref, f32[128,8192]{1,0:T(8,128)S(1)} %copy-done.3), custom_call_target="tpu_custom_call" | custom-call | tf_op jit(solution)/shard_map/transport/pallas_call | solution.py:260
  39.7 3.8 %collective-permute-done.8 = f32[224,128]{1,0:T(8,128)S(1)} collective-permute-done((f32[224,128]{1,0:T(8,128)S(1)}, f32[224,128]{1,0:T(8,128)S(1)}, u32[]{:S(2)}, u32[]{:S(2)}) %collective-permute-start.8) | collective-permute-done | bytes 114720 | tf_op jit(solution)/shard_map/ppermute | solution.py:547
  46.6 4.5 %update.1 = (f32[128,8192]{1,0:T(8,128)S(1)}, f32[896,128]{1,0:T(8,128)S(1)}) custom-call(f32[32,8192]{1,0:T(8,128)S(1)} %transport.8.refs_0_, f32[32,8192]{1,0:T(8,128)S(1)} %transport.9.refs_1_, f32[32,8192]{1,0:T(8,128)S(1)} %transport.10.refs_2_, f32[32,8192]{1,0:T(8,128)S(1)} %transport.11.refs_3_, f32[1536,128]{1,0:T(8,128)S(1)} %get-tuple-element.63.refs_4_, ...), custom_call_target="tpu_custom_call" | custom-call | tf_op jit(solution)/shard_map/update/pallas_call | solution.py:430
  53.8 2.0 %transport.12.refs_0_ = f32[32,8192]{1,0:T(8,128)S(1)} custom-call(f32[128,128]{1,0:T(8,128)S(1)} %get-tuple-element.47.stream_ref, f32[128,8192]{1,0:T(8,128)S(1)} %get-tuple-element.81.f_ref), custom_call_target="tpu_custom_call" | custom-call | tf_op jit(solution)/shard_map/transport/pallas_call | solution.py:260
  55.8 2.2 %collective-permute-done.11 = f32[224,128]{1,0:T(8,128)S(1)} collective-permute-done((f32[224,128]{1,0:T(8,128)S(1)}, f32[224,128]{1,0:T(8,128)S(1)}, u32[]{:S(2)}, u32[]{:S(2)}) %collective-permute-start.11) | collective-permute-done | bytes 114720 | tf_op jit(solution)/shard_map/ppermute | solution.py:537
  60.1 2.4 %collective-permute-start.14 = (f32[56,128]{1,0:T(8,128)S(1)}, f32[56,128]{1,0:T(8,128)S(1)}, u32[]{:S(2)}, u32[]{:S(2)}) collective-permute-start(f32[56,128]{1,0:T(8,128)S(1)} %get-tuple-element.87), channel_id=1, source_target_pairs={{0,12},{1,13},{2,14},{3,15},{4,8},{5,9},{6,10},{7,11},{8,4},{9,5},... | collective-permute-start | bytes 86024 | tf_op jit(solution)/shard_map/ppermute | solution.py:537
  62.5 2.0 %transport.13.refs_1_ = f32[32,8192]{1,0:T(8,128)S(1)} custom-call(f32[128,128]{1,0:T(8,128)S(1)} %get-tuple-element.47.stream_ref, f32[128,8192]{1,0:T(8,128)S(1)} %get-tuple-element.81.f_ref), custom_call_target="tpu_custom_call" | custom-call | tf_op jit(solution)/shard_map/transport/pallas_call | solution.py:260
  65.9 2.9 %collective-permute-start.16 = (f32[56,128]{1,0:T(8,128)S(1)}, f32[56,128]{1,0:T(8,128)S(1)}, u32[]{:S(2)}, u32[]{:S(2)}) collective-permute-start(f32[56,128]{1,0:T(8,128)S(1)} %add_add_fusion), channel_id=1, source_target_pairs={{0,8},{1,9},{2,10},{3,11},{4,12},{5,13},{6,14},{7,15},{8,0},{9,1},... | collective-permute-start | bytes 86024 | tf_op jit(solution)/shard_map/ppermute | solution.py:547
  70.3 2.0 %transport.14.refs_2_ = f32[32,8192]{1,0:T(8,128)S(1)} custom-call(f32[128,128]{1,0:T(8,128)S(1)} %get-tuple-element.47.stream_ref, f32[128,8192]{1,0:T(8,128)S(1)} %get-tuple-element.81.f_ref), custom_call_target="tpu_custom_call" | custom-call | tf_op jit(solution)/shard_map/transport/pallas_call | solution.py:260
  72.3 2.1 %collective-permute-done.17 = f32[56,128]{1,0:T(8,128)S(1)} collective-permute-done((f32[56,128]{1,0:T(8,128)S(1)}, f32[56,128]{1,0:T(8,128)S(1)}, u32[]{:S(2)}, u32[]{:S(2)}) %collective-permute-start.17) | collective-permute-done | bytes 28704 | tf_op jit(solution)/shard_map/ppermute | solution.py:547
  74.5 2.0 %transport.15.refs_3_ = f32[32,8192]{1,0:T(8,128)S(1)} custom-call(f32[128,128]{1,0:T(8,128)S(1)} %get-tuple-element.47.stream_ref, f32[128,8192]{1,0:T(8,128)S(1)} %get-tuple-element.81.f_ref), custom_call_target="tpu_custom_call" | custom-call | tf_op jit(solution)/shard_map/transport/pallas_call | solution.py:260
  77.6 3.8 %collective-permute-done.18 = f32[224,128]{1,0:T(8,128)S(1)} collective-permute-done((f32[224,128]{1,0:T(8,128)S(1)}, f32[224,128]{1,0:T(8,128)S(1)}, u32[]{:S(2)}, u32[]{:S(2)}) %collective-permute-start.18) | collective-permute-done | bytes 114720 | tf_op jit(solution)/shard_map/ppermute | solution.py:547
  83.8 3.1 %finish.1 = (f32[128,8192]{1,0:T(8,128)}, f32[8,8192]{1,0:T(8,128)}) custom-call(f32[32,8192]{1,0:T(8,128)S(1)} %transport.12.refs_0_, f32[32,8192]{1,0:T(8,128)S(1)} %transport.13.refs_1_, f32[32,8192]{1,0:T(8,128)S(1)} %transport.14.refs_2_, f32[32,8192]{1,0:T(8,128)S(1)} %transport.15.refs_3_, f32[1536,128]{1,0:T(8,128)S(1)} %get-tuple-element.84.refs_4_, ...), custom_call_target="tpu_custom_call" | custom-call | tf_op jit(solution)/shard_map/finish/pallas_call | solution.py:473
  (71 shorter events, 21.7 us)
Async XLA Ops:
  7.1 2.0 %copy-start = (f32[128,8192]{1,0:T(8,128)}, f32[128,8192]{1,0:T(8,128)S(1)}, u32[]{:S(2)}) copy-start(f32[128,8192]{1,0:T(8,128)S(1)} %get-tuple-element.60.f_ref) | copy-start | bytes 12582916
  9.2 1.6 %collective-permute-start = (f32[448,128]{1,0:T(8,128)S(1)}, f32[448,128]{1,0:T(8,128)S(1)}, u32[]{:S(2)}, u32[]{:S(2)}) collective-permute-start(f32[448,128]{1,0:T(8,128)S(1)} %constant_dynamic-slice_fusion.9), channel_id=1, source_target_pairs={{0,1},{1,0},{2,3},{3,2},{4,5},{5,4},{6,7},{7,6},{8,9},{9,8},{10,11... | collective-permute-start | bytes 688136 | tf_op jit(solution)/shard_map/ppermute | solution.py:537
  10.8 7.1 %collective-permute-start.1 = (f32[224,128]{1,0:T(8,128)S(1)}, f32[224,128]{1,0:T(8,128)S(1)}, u32[]{:S(2)}, u32[]{:S(2)}) collective-permute-start(f32[224,128]{1,0:T(8,128)S(1)} %constant_dynamic-slice_fusion.8), channel_id=1, source_target_pairs={{0,2},{1,3},{2,0},{3,1},{4,6},{5,7},{6,4},{7,5},{8,10},{9,11},{10,... | collective-permute-start | bytes 344072 | tf_op jit(solution)/shard_map/ppermute | solution.py:537
  13.8 2.2 %copy-start.1 = (f32[128,8192]{1,0:T(8,128)S(1)}, f32[128,8192]{1,0:T(8,128)}, u32[]{:S(2)}) copy-start(f32[128,8192]{1,0:T(8,128)} %copy-done) | copy-start | bytes 12582916
  18.1 8.6 %collective-permute-start.2 = (f32[56,128]{1,0:T(8,128)S(1)}, f32[56,128]{1,0:T(8,128)S(1)}, u32[]{:S(2)}, u32[]{:S(2)}) collective-permute-start(f32[56,128]{1,0:T(8,128)S(1)} %get-tuple-element.89), channel_id=1, source_target_pairs={{0,4},{1,5},{2,6},{3,7},{4,0},{5,1},{6,2},{7,3},{8,12},{9,13},{10,... | collective-permute-start | bytes 86024 | tf_op jit(solution)/shard_map/ppermute | solution.py:537
  19.7 7.0 %collective-permute-start.3 = (f32[56,128]{1,0:T(8,128)S(1)}, f32[56,128]{1,0:T(8,128)S(1)}, u32[]{:S(2)}, u32[]{:S(2)}) collective-permute-start(f32[56,128]{1,0:T(8,128)S(1)} %get-tuple-element.91), channel_id=1, source_target_pairs={{0,8},{1,9},{2,10},{3,11},{4,12},{5,13},{6,14},{7,15},{8,0},{9,1},... | collective-permute-start | bytes 86024 | tf_op jit(solution)/shard_map/ppermute | solution.py:537
  22.3 5.7 %collective-permute-start.4 = (f32[56,128]{1,0:T(8,128)S(1)}, f32[56,128]{1,0:T(8,128)S(1)}, u32[]{:S(2)}, u32[]{:S(2)}) collective-permute-start(f32[56,128]{1,0:T(8,128)S(1)} %get-tuple-element.90), channel_id=1, source_target_pairs={{0,12},{1,13},{2,14},{3,15},{4,8},{5,9},{6,10},{7,11},{8,4},{9,5},... | collective-permute-start | bytes 86024 | tf_op jit(solution)/shard_map/ppermute | solution.py:537
  22.5 2.2 %copy-start.2 = (f32[128,8192]{1,0:T(8,128)S(1)}, f32[128,8192]{1,0:T(8,128)}, u32[]{:S(2)}) copy-start(f32[128,8192]{1,0:T(8,128)} %copy-done) | copy-start | bytes 12582916
  24.7 7.8 %copy-start.3 = (f32[128,8192]{1,0:T(8,128)S(1)}, f32[128,8192]{1,0:T(8,128)}, u32[]{:S(2)}) copy-start(f32[128,8192]{1,0:T(8,128)} %copy-done) | copy-start | bytes 12582916
  28.0 6.5 %collective-permute-start.5 = (f32[56,128]{1,0:T(8,128)S(1)}, f32[56,128]{1,0:T(8,128)S(1)}, u32[]{:S(2)}, u32[]{:S(2)}) collective-permute-start(f32[56,128]{1,0:T(8,128)S(1)} %add_add_fusion.1), channel_id=1, source_target_pairs={{0,4},{1,5},{2,6},{3,7},{4,0},{5,1},{6,2},{7,3},{8,12},{9,13},{10,... | collective-permute-start | bytes 86024 | tf_op jit(solution)/shard_map/ppermute | solution.py:547
  28.0 6.4 %collective-permute-start.6 = (f32[56,128]{1,0:T(8,128)S(1)}, f32[56,128]{1,0:T(8,128)S(1)}, u32[]{:S(2)}, u32[]{:S(2)}) collective-permute-start(f32[56,128]{1,0:T(8,128)S(1)} %add_add_fusion.1), channel_id=1, source_target_pairs={{0,8},{1,9},{2,10},{3,11},{4,12},{5,13},{6,14},{7,15},{8,0},{9,1},... | collective-permute-start | bytes 86024 | tf_op jit(solution)/shard_map/ppermute | solution.py:547
  31.0 5.7 %collective-permute-start.7 = (f32[56,128]{1,0:T(8,128)S(1)}, f32[56,128]{1,0:T(8,128)S(1)}, u32[]{:S(2)}, u32[]{:S(2)}) collective-permute-start(f32[56,128]{1,0:T(8,128)S(1)} %add_add_fusion.1), channel_id=1, source_target_pairs={{0,12},{1,13},{2,14},{3,15},{4,8},{5,9},{6,10},{7,11},{8,4},{9,5},... | collective-permute-start | bytes 86024 | tf_op jit(solution)/shard_map/ppermute | solution.py:547
  38.7 4.9 %collective-permute-start.8 = (f32[224,128]{1,0:T(8,128)S(1)}, f32[224,128]{1,0:T(8,128)S(1)}, u32[]{:S(2)}, u32[]{:S(2)}) collective-permute-start(f32[224,128]{1,0:T(8,128)S(1)} %constant_dynamic-update-slice_fusion.12), channel_id=1, source_target_pairs={{0,2},{1,3},{2,0},{3,1},{4,6},{5,7},{6,4},{7,5},{8,10},{9,11},{10,... | collective-permute-start | bytes 344072 | tf_op jit(solution)/shard_map/ppermute | solution.py:547
  43.5 1.6 %collective-permute-start.9 = (f32[448,128]{1,0:T(8,128)S(1)}, f32[448,128]{1,0:T(8,128)S(1)}, u32[]{:S(2)}, u32[]{:S(2)}) collective-permute-start(f32[448,128]{1,0:T(8,128)S(1)} %constant_dynamic-update-slice_fusion.10), channel_id=1, source_target_pairs={{0,1},{1,0},{2,3},{3,2},{4,5},{5,4},{6,7},{7,6},{8,9},{9,8},{10,11... | collective-permute-start | bytes 688136 | tf_op jit(solution)/shard_map/ppermute | solution.py:547
  51.1 1.6 %collective-permute-start.10 = (f32[448,128]{1,0:T(8,128)S(1)}, f32[448,128]{1,0:T(8,128)S(1)}, u32[]{:S(2)}, u32[]{:S(2)}) collective-permute-start(f32[448,128]{1,0:T(8,128)S(1)} %constant_dynamic-slice_fusion.4), channel_id=1, source_target_pairs={{0,1},{1,0},{2,3},{3,2},{4,5},{5,4},{6,7},{7,6},{8,9},{9,8},{10,11... | collective-permute-start | bytes 688136 | tf_op jit(solution)/shard_map/ppermute | solution.py:537
  52.7 5.3 %collective-permute-start.11 = (f32[224,128]{1,0:T(8,128)S(1)}, f32[224,128]{1,0:T(8,128)S(1)}, u32[]{:S(2)}, u32[]{:S(2)}) collective-permute-start(f32[224,128]{1,0:T(8,128)S(1)} %constant_dynamic-slice_fusion.3), channel_id=1, source_target_pairs={{0,2},{1,3},{2,0},{3,1},{4,6},{5,7},{6,4},{7,5},{8,10},{9,11},{10,... | collective-permute-start | bytes 344072 | tf_op jit(solution)/shard_map/ppermute | solution.py:537
  58.0 6.5 %collective-permute-start.12 = (f32[56,128]{1,0:T(8,128)S(1)}, f32[56,128]{1,0:T(8,128)S(1)}, u32[]{:S(2)}, u32[]{:S(2)}) collective-permute-start(f32[56,128]{1,0:T(8,128)S(1)} %get-tuple-element.86), channel_id=1, source_target_pairs={{0,4},{1,5},{2,6},{3,7},{4,0},{5,1},{6,2},{7,3},{8,12},{9,13},{10,... | collective-permute-start | bytes 86024 | tf_op jit(solution)/shard_map/ppermute | solution.py:537
  58.1 6.4 %collective-permute-start.13 = (f32[56,128]{1,0:T(8,128)S(1)}, f32[56,128]{1,0:T(8,128)S(1)}, u32[]{:S(2)}, u32[]{:S(2)}) collective-permute-start(f32[56,128]{1,0:T(8,128)S(1)} %get-tuple-element.88), channel_id=1, source_target_pairs={{0,8},{1,9},{2,10},{3,11},{4,12},{5,13},{6,14},{7,15},{8,0},{9,1},... | collective-permute-start | bytes 86024 | tf_op jit(solution)/shard_map/ppermute | solution.py:537
  60.1 5.7 %collective-permute-start.14 = (f32[56,128]{1,0:T(8,128)S(1)}, f32[56,128]{1,0:T(8,128)S(1)}, u32[]{:S(2)}, u32[]{:S(2)}) collective-permute-start(f32[56,128]{1,0:T(8,128)S(1)} %get-tuple-element.87), channel_id=1, source_target_pairs={{0,12},{1,13},{2,14},{3,15},{4,8},{5,9},{6,10},{7,11},{8,4},{9,5},... | collective-permute-start | bytes 86024 | tf_op jit(solution)/shard_map/ppermute | solution.py:537
  65.8 6.5 %collective-permute-start.15 = (f32[56,128]{1,0:T(8,128)S(1)}, f32[56,128]{1,0:T(8,128)S(1)}, u32[]{:S(2)}, u32[]{:S(2)}) collective-permute-start(f32[56,128]{1,0:T(8,128)S(1)} %add_add_fusion), channel_id=1, source_target_pairs={{0,4},{1,5},{2,6},{3,7},{4,0},{5,1},{6,2},{7,3},{8,12},{9,13},{10,... | collective-permute-start | bytes 86024 | tf_op jit(solution)/shard_map/ppermute | solution.py:547
  65.9 6.4 %collective-permute-start.16 = (f32[56,128]{1,0:T(8,128)S(1)}, f32[56,128]{1,0:T(8,128)S(1)}, u32[]{:S(2)}, u32[]{:S(2)}) collective-permute-start(f32[56,128]{1,0:T(8,128)S(1)} %add_add_fusion), channel_id=1, source_target_pairs={{0,8},{1,9},{2,10},{3,11},{4,12},{5,13},{6,14},{7,15},{8,0},{9,1},... | collective-permute-start | bytes 86024 | tf_op jit(solution)/shard_map/ppermute | solution.py:547
  68.8 5.7 %collective-permute-start.17 = (f32[56,128]{1,0:T(8,128)S(1)}, f32[56,128]{1,0:T(8,128)S(1)}, u32[]{:S(2)}, u32[]{:S(2)}) collective-permute-start(f32[56,128]{1,0:T(8,128)S(1)} %add_add_fusion), channel_id=1, source_target_pairs={{0,12},{1,13},{2,14},{3,15},{4,8},{5,9},{6,10},{7,11},{8,4},{9,5},... | collective-permute-start | bytes 86024 | tf_op jit(solution)/shard_map/ppermute | solution.py:547
  76.5 4.9 %collective-permute-start.18 = (f32[224,128]{1,0:T(8,128)S(1)}, f32[224,128]{1,0:T(8,128)S(1)}, u32[]{:S(2)}, u32[]{:S(2)}) collective-permute-start(f32[224,128]{1,0:T(8,128)S(1)} %constant_dynamic-update-slice_fusion.4), channel_id=1, source_target_pairs={{0,2},{1,3},{2,0},{3,1},{4,6},{5,7},{6,4},{7,5},{8,10},{9,11},{10,... | collective-permute-start | bytes 344072 | tf_op jit(solution)/shard_map/ppermute | solution.py:547
  81.4 1.6 %collective-permute-start.19 = (f32[448,128]{1,0:T(8,128)S(1)}, f32[448,128]{1,0:T(8,128)S(1)}, u32[]{:S(2)}, u32[]{:S(2)}) collective-permute-start(f32[448,128]{1,0:T(8,128)S(1)} %constant_dynamic-update-slice_fusion.2), channel_id=1, source_target_pairs={{0,1},{1,0},{2,3},{3,2},{4,5},{5,4},{6,7},{7,6},{8,9},{9,8},{10,11... | collective-permute-start | bytes 688136 | tf_op jit(solution)/shard_map/ppermute | solution.py:547

commit v2 on v1

--- a/solution.py
+++ b/solution.py
@@ -487,72 +487,45 @@
     )(*[near(part) for part in g], near(coefficients), near(macro), near(basis))
 
 
-def stages(count):
-    sizes = []
-    for size in (2, 2):
-        if count > 1 and count % size == 0:
-            sizes.append(size)
-            count //= size
-    while count % 4 == 0:
-        sizes.append(4)
-        count //= 4
-    while count % 2 == 0:
-        sizes.append(2)
-        count //= 2
-    return sizes
-
-
-def pairs(count, stride, size, shift):
-    out = []
-    for device in range(count):
-        rank = device // stride % size
-        out.append((device, device + ((rank ^ shift) - rank) * stride))
-    return out
-
-
-def staged_sum(values, count, f, tasks):
-    index = lax.axis_index("vel")
-    stride, trail, results = 1, [], []
-    block = values
-    number = 0
-
-    def before(block):
-        if 0 < number <= len(tasks):
-            block, held = lax.optimization_barrier((block, f))
-            results.append(tasks[number - 1](held))
-        return block
-
-    def after(block):
-        if 0 < number <= len(tasks):
-            block, results[-1] = lax.optimization_barrier((block, results[-1]))
-        return block
-
-    for size in stages(count):
-        block = before(block)
-        rank = index // stride % size
-        width = block.shape[0] // size
-        total = lax.dynamic_slice_in_dim(block, rank * width, width, 0)
-        for shift in range(1, size):
-            piece = lax.dynamic_slice_in_dim(block, (rank ^ shift) * width, width, 0)
-            total = total + lax.ppermute(piece, "vel", pairs(count, stride, size, shift))
-        trail.append((size, stride, rank, width))
-        block = after(total)
-        stride *= size
-        number += 1
-    for size, stride, rank, width in reversed(trail):
-        block = before(block)
-        whole = jnp.zeros((width * size, block.shape[1]), block.dtype)
-        whole = lax.dynamic_update_slice_in_dim(whole, block, rank * width, 0)
-        for shift in range(1, size):
-            piece = lax.ppermute(block, "vel", pairs(count, stride, size, shift))
-            whole = lax.dynamic_update_slice_in_dim(whole, piece, (rank ^ shift) * width, 0)
-        block = after(whole)
-        number += 1
-    return block, results
+def swap(values, count):
+    return lax.ppermute(values, "vel", [(device, device ^ 1) for device in range(count)])
+
+
+def staged_sum(values, count, offsets, f, tasks):
+    chips = count // 2
+    groups = [list(range(part, count, 2)) for part in range(2)]
+    rows, lanes = values.shape
+    half, width = rows // 2, rows // count
+    results = []
+
+    def exchange(block, some):
+        block, held = lax.optimization_barrier((block, f))
+        made = [task(held) for task in some]
+        out = lax.all_to_all(block, "vel", 0, 0, axis_index_groups=groups, tiled=True)
+        out, made = lax.optimization_barrier((out, made))
+        results.extend(made)
+        return out
+
+    own = lax.dynamic_slice_in_dim(values, offsets[0], half, 0, allow_negative_indices=False)
+    other = lax.dynamic_slice_in_dim(values, offsets[1], half, 0, allow_negative_indices=False)
+    block = own + swap(other, count)
+    block = jnp.sum(exchange(block.reshape(chips, width, lanes), tasks[: PARTS // 2]), axis=0)
+    copies = jnp.broadcast_to(block[None], (chips, width, lanes))
+    block = exchange(copies, tasks[PARTS // 2 :]).reshape(half, lanes)
+    whole = jnp.zeros((rows, lanes), values.dtype)
+    for part, offset in ((block, offsets[0]), (swap(block, count), offsets[1])):
+        whole = lax.dynamic_update_slice(
+            whole, part, (offset, 0), allow_negative_indices=(False, False)
+        )
+    return whole, results
 
 
 def on_device(velocities, density, flow, thermal, deviation):
     count = lax.axis_size("vel")
+    half = SENT * density.shape[0] // LANES // 2
+    mine = (lax.axis_index("vel") & 1) * half
+    offsets = (mine, half - mine)
+    velocities, offsets = lax.optimization_barrier((velocities, offsets))
     f, moments, basis, table, stream = start_call(
         velocities, density, flow, thermal, deviation, velocities.shape[1] * count
     )
@@ -561,7 +534,7 @@
             functools.partial(lambda held, part: transport_call(stream, held, part), part=part)
             for part in range(PARTS)
         ]
-        summed, g = staged_sum(moments, count, f, tasks)
+        summed, g = staged_sum(moments, count, offsets, f, tasks)
         coefficients, macro = fluid_call(summed)
         if iteration < ITERS - 1:
             f, moments = update_call(g, coefficients, basis, table)

time: 87.1 us -> 95 us (1.091)
  local copies, waits for them, and re-layouts: 6.81 us -> 29.5 us
  waiting for transfers between devices: 21.8 us -> 9.78 us
  starting transfers between devices: 24.8 us -> 20.2 us
  other arithmetic: 0.11 us -> 1.47 us
    ppermute x20 -> x4, starting transfers between devices: 24.8 us -> 1.09 us  [swap(): lax.ppermute(values, 'vel', [(device, device ^ 1) for device in range(cou...]
    ppermute x20 -> x4, waiting for transfers between devices: 21.8 us -> 2.24 us  [swap(): lax.ppermute(values, 'vel', [(device, device ^ 1) for device in range(cou...]
    all_to_all x0 -> x4, starting transfers between devices: none -> 19.1 us  [exchange(): lax.all_to_all(block, 'vel', 0, 0, axis_index_groups=groups, tiled=True)]
    unnamed x8 -> x24, local copies, waits for them, and re-layouts: 6.39 us -> 19.2 us
    all_to_all x0 -> x4, waiting for transfers between devices: none -> 7.55 us  [exchange(): lax.all_to_all(block, 'vel', 0, 0, axis_index_groups=groups, tiled=True)]
    dynamic_update_slice x16 -> x4, local copies, waits for them, and re-layouts: 0.21 us -> 7.27 us  [staged_sum(): lax.dynamic_update_slice(whole, part, (offset, 0), allow_negative_indices...]
    another operation x6 -> x2, local copies, waits for them, and re-layouts: 0.11 us -> 1.61 us
    broadcast_in_dim x0 -> x2, local copies, waits for them, and re-layouts: none -> 1.41 us  [staged_sum(): copies = jnp.broadcast_to(block[None], (chips, width, lanes))]
  transfers between devices with their start and end apart: 20 -> 8, of which waited for: 11 -> 6; matrix products, arithmetic and copies ran while one was open for 0% -> 6% of each run, Pallas kernels for 14% -> 17%
where the time goes in v2:
time: 95 us; the launch traced here: 94.1 us
  Pallas kernels  32.3 us (34%)
  local copies, waits for them, and re-layouts  29.5 us (31%)
  starting transfers between devices  20.2 us (21%)
  waiting for transfers between devices  9.78 us (10%)
  other arithmetic  1.47 us (2%)
    unnamed x24, local copies, waits for them, and re-layouts  19.2 us
    all_to_all x4, starting transfers between devices, exchange(): lax.all_to_all(block, 'vel', 0, 0, axis_index_groups=groups, tiled=True)  19.1 us
    pallas_call x8, Pallas kernels, transport_call(): pl.pallas_call(functools.partial(transport_kernel, part * rows), out_shap...  16 us
    all_to_all x4, waiting for transfers between devices, exchange(): lax.all_to_all(block, 'vel', 0, 0, axis_index_groups=groups, tiled=True)  7.55 us
    dynamic_update_slice x4, local copies, waits for them, and re-layouts, staged_sum(): lax.dynamic_update_slice(whole, part, (offset, 0), allow_negative_indices...  7.27 us
    pallas_call x1, Pallas kernels, start_call(): pl.pallas_call(functools.partial(start_kernel, total_count), out_shape=(p...  6.46 us
    pallas_call x1, Pallas kernels, update_call(): pl.pallas_call(update_kernel, out_shape=(pltpu.VMEM((rows * PARTS, cells)...  4.48 us
    pallas_call x1, Pallas kernels, finish_call(): pl.pallas_call(finish_kernel, out_shape=(jax.ShapeDtypeStruct((rows * PAR...  3.06 us
  transfers between devices with their start and end apart: 8, of which 6 were waited for; matrix products, arithmetic and copies ran while one was open for 6% of the time, Pallas kernels for 17%

profile of v2, /device:TPU:0, one launch (start us, length us, event | category | flops | bytes accessed | tf_op | source)
XLA Modules:
  0.0 94.1 jit_solution(17602609377517580744)
XLA Ops:
  0.6 6.5 %start.1 = (f32[128,8192]{1,0:T(8,128)S(1)}, f32[896,128]{1,0:T(8,128)S(1)}, bf16[128,128]{1,0:T(8,128)(2,1)S(1)}, bf16[32,256]{1,0:T(8,128)(2,1)S(1)}, f32[128,128]{1,0:T(8,128)S(1)}) custom-call(f32[3,128]{1,0:T(4,128)} %vel_hbm, f32[1,8192]{1,0:T(1,128)} %bitcast.10, f32[3,8192]{1,0:T(4,128)} %flow_hbm.1, f32[1,8192]{1,0:T(1,128)} %bitcast.11, ...), custom_call_target="tpu_custom_call" | custom-call | tf_op jit(solution)/shard_map/start/pallas_call | solution.py:170
  7.1 2.0 %copy-done.3 = f32[128,8192]{1,0:T(8,128)} copy-done((f32[128,8192]{1,0:T(8,128)}, f32[128,8192]{1,0:T(8,128)S(1)}, u32[]{:S(2)}) %copy-start.3) | copy-done | bytes 4194328
  11.5 7.2 %all-to-all-start = ((f32[8,56,128]{2,1,0:T(8,128)}), f32[8,56,128]{2,1,0:T(8,128)S(1)}, u32[]{:S(2)}, u32[]{:S(2)}) async-start(f32[8,56,128]{2,1,0:T(8,128)} %bitcast.2), calls=%async_computation | async-start | bytes 458752 | tf_op jit(solution)/shard_map/all_to_all | solution.py:504
  18.7 2.2 %copy-done.4 = f32[128,8192]{1,0:T(8,128)S(1)} copy-done((f32[128,8192]{1,0:T(8,128)S(1)}, f32[128,8192]{1,0:T(8,128)}, u32[]{:S(2)}) %copy-start.4) | copy-done | bytes 4194328
  20.9 2.0 %transport.9.refs_1_ = f32[32,8192]{1,0:T(8,128)S(1)} custom-call(f32[128,128]{1,0:T(8,128)S(1)} %get-tuple-element.41.stream_ref, f32[128,8192]{1,0:T(8,128)S(1)} %copy-done.4), custom_call_target="tpu_custom_call" | custom-call | tf_op jit(solution)/shard_map/transport/pallas_call | solution.py:260
  22.9 2.0 %transport.8.refs_0_ = f32[32,8192]{1,0:T(8,128)S(1)} custom-call(f32[128,128]{1,0:T(8,128)S(1)} %get-tuple-element.41.stream_ref, f32[128,8192]{1,0:T(8,128)S(1)} %copy-done.4), custom_call_target="tpu_custom_call" | custom-call | tf_op jit(solution)/shard_map/transport/pallas_call | solution.py:260
  24.9 2.5 %all-to-all-done = f32[8,56,128]{2,1,0:T(8,128)S(1)} async-done(((f32[8,56,128]{2,1,0:T(8,128)}), f32[8,56,128]{2,1,0:T(8,128)S(1)}, u32[]{:S(2)}, u32[]{:S(2)}) %all-to-all-start) | async-done | bytes 229408 | tf_op jit(solution)/shard_map/all_to_all | solution.py:504
  28.2 3.5 %all-to-all-start.1 = ((f32[8,56,128]{2,1,0:T(8,128)}), f32[8,56,128]{2,1,0:T(8,128)S(1)}, u32[]{:S(2)}, u32[]{:S(2)}) async-start(f32[8,56,128]{2,1,0:T(8,128)} %broadcast_in_dim.4), calls=%async_computation.1 | async-start | bytes 458752 | tf_op jit(solution)/shard_map/all_to_all | solution.py:504
  31.6 2.2 %copy-done.5 = f32[128,8192]{1,0:T(8,128)S(1)} copy-done((f32[128,8192]{1,0:T(8,128)S(1)}, f32[128,8192]{1,0:T(8,128)}, u32[]{:S(2)}) %copy-start.5) | copy-done | bytes 4194328
  33.8 2.0 %transport.11.refs_3_ = f32[32,8192]{1,0:T(8,128)S(1)} custom-call(f32[128,128]{1,0:T(8,128)S(1)} %get-tuple-element.41.stream_ref, f32[128,8192]{1,0:T(8,128)S(1)} %copy-done.5), custom_call_target="tpu_custom_call" | custom-call | tf_op jit(solution)/shard_map/transport/pallas_call | solution.py:260
  35.8 2.0 %transport.10.refs_2_ = f32[32,8192]{1,0:T(8,128)S(1)} custom-call(f32[128,128]{1,0:T(8,128)S(1)} %get-tuple-element.41.stream_ref, f32[128,8192]{1,0:T(8,128)S(1)} %copy-done.5), custom_call_target="tpu_custom_call" | custom-call | tf_op jit(solution)/shard_map/transport/pallas_call | solution.py:260
  40.6 1.8 %dynamic_update_slice.12 = f32[896,128]{1,0:T(8,128)} dynamic-update-slice(f32[896,128]{1,0:T(8,128)} %broadcast.5.clone, f32[448,128]{1,0:T(8,128)S(1)} %bitcast.9, s32[]{:T(128)S(6)} %mul.3, s32[]{:T(128)} %constant.2.clone.1) | dynamic-update-slice | bytes 458756 | tf_op jit(solution)/shard_map/dynamic_update_slice | solution.py:517
  48.0 4.5 %update.1 = (f32[128,8192]{1,0:T(8,128)S(1)}, f32[896,128]{1,0:T(8,128)S(1)}) custom-call(f32[32,8192]{1,0:T(8,128)S(1)} %transport.8.refs_0_, f32[32,8192]{1,0:T(8,128)S(1)} %transport.9.refs_1_, f32[32,8192]{1,0:T(8,128)S(1)} %copy-done.9, f32[32,8192]{1,0:T(8,128)S(1)} %transport.11.refs_3_, f32[1536,128]{1,0:T(8,128)S(1)} %get-tuple-element.51.refs_4_, ...), custom_call_target="tpu_custom_call" | custom-call | tf_op jit(solution)/shard_map/update/pallas_call | solution.py:430
  52.5 2.0 %copy-done = f32[128,8192]{1,0:T(8,128)} copy-done((f32[128,8192]{1,0:T(8,128)}, f32[128,8192]{1,0:T(8,128)S(1)}, u32[]{:S(2)}) %copy-start) | copy-done | bytes 4194328
  56.9 5.0 %all-to-all-start.2 = ((f32[8,56,128]{2,1,0:T(8,128)}), f32[8,56,128]{2,1,0:T(8,128)S(1)}, u32[]{:S(2)}, u32[]{:S(2)}) async-start(f32[8,56,128]{2,1,0:T(8,128)} %bitcast.4), calls=%async_computation.2 | async-start | bytes 458752 | tf_op jit(solution)/shard_map/all_to_all | solution.py:504
  61.9 2.2 %copy-done.1 = f32[128,8192]{1,0:T(8,128)S(1)} copy-done((f32[128,8192]{1,0:T(8,128)S(1)}, f32[128,8192]{1,0:T(8,128)}, u32[]{:S(2)}) %copy-start.1) | copy-done | bytes 4194328
  64.1 2.0 %transport.13.refs_1_ = f32[32,8192]{1,0:T(8,128)S(1)} custom-call(f32[128,128]{1,0:T(8,128)S(1)} %get-tuple-element.41.stream_ref, f32[128,8192]{1,0:T(8,128)S(1)} %copy-done.1), custom_call_target="tpu_custom_call" | custom-call | tf_op jit(solution)/shard_map/transport/pallas_call | solution.py:260
  66.1 2.0 %transport.12.refs_0_ = f32[32,8192]{1,0:T(8,128)S(1)} custom-call(f32[128,128]{1,0:T(8,128)S(1)} %get-tuple-element.41.stream_ref, f32[128,8192]{1,0:T(8,128)S(1)} %copy-done.1), custom_call_target="tpu_custom_call" | custom-call | tf_op jit(solution)/shard_map/transport/pallas_call | solution.py:260
  68.1 2.8 %all-to-all-done.2 = f32[8,56,128]{2,1,0:T(8,128)S(1)} async-done(((f32[8,56,128]{2,1,0:T(8,128)}), f32[8,56,128]{2,1,0:T(8,128)S(1)}, u32[]{:S(2)}, u32[]{:S(2)}) %all-to-all-start.2) | async-done | bytes 229408 | tf_op jit(solution)/shard_map/all_to_all | solution.py:504
  71.6 3.4 %all-to-all-start.3 = ((f32[8,56,128]{2,1,0:T(8,128)}), f32[8,56,128]{2,1,0:T(8,128)S(1)}, u32[]{:S(2)}, u32[]{:S(2)}) async-start(f32[8,56,128]{2,1,0:T(8,128)} %broadcast_in_dim.5), calls=%async_computation.3 | async-start | bytes 458752 | tf_op jit(solution)/shard_map/all_to_all | solution.py:504
  75.0 2.2 %copy-done.2 = f32[128,8192]{1,0:T(8,128)S(1)} copy-done((f32[128,8192]{1,0:T(8,128)S(1)}, f32[128,8192]{1,0:T(8,128)}, u32[]{:S(2)}) %copy-start.2) | copy-done | bytes 4194328
  77.2 2.0 %transport.15.refs_3_ = f32[32,8192]{1,0:T(8,128)S(1)} custom-call(f32[128,128]{1,0:T(8,128)S(1)} %get-tuple-element.41.stream_ref, f32[128,8192]{1,0:T(8,128)S(1)} %copy-done.2), custom_call_target="tpu_custom_call" | custom-call | tf_op jit(solution)/shard_map/transport/pallas_call | solution.py:260
  79.2 2.0 %transport.14.refs_2_ = f32[32,8192]{1,0:T(8,128)S(1)} custom-call(f32[128,128]{1,0:T(8,128)S(1)} %get-tuple-element.41.stream_ref, f32[128,8192]{1,0:T(8,128)S(1)} %copy-done.2), custom_call_target="tpu_custom_call" | custom-call | tf_op jit(solution)/shard_map/transport/pallas_call | solution.py:260
  91.0 3.1 %finish.1 = (f32[128,8192]{1,0:T(8,128)}, f32[8,8192]{1,0:T(8,128)}) custom-call(f32[32,8192]{1,0:T(8,128)S(1)} %transport.12.refs_0_, f32[32,8192]{1,0:T(8,128)S(1)} %transport.13.refs_1_, f32[32,8192]{1,0:T(8,128)S(1)} %copy-done.7, f32[32,8192]{1,0:T(8,128)S(1)} %transport.15.refs_3_, f32[1536,128]{1,0:T(8,128)S(1)} %get-tuple-element.66.refs_4_, ...), custom_call_target="tpu_custom_call" | custom-call | tf_op jit(solution)/shard_map/finish/pallas_call | solution.py:473
  (43 shorter events, 24.3 us)
Async XLA Ops:
  7.1 2.0 %copy-start.3 = (f32[128,8192]{1,0:T(8,128)}, f32[128,8192]{1,0:T(8,128)S(1)}, u32[]{:S(2)}) copy-start(f32[128,8192]{1,0:T(8,128)S(1)} %get-tuple-element.47.f_ref) | copy-start | bytes 12582916
  9.2 1.6 %collective-permute-start = (f32[448,128]{1,0:T(8,128)S(1)}, f32[448,128]{1,0:T(8,128)S(1)}, u32[]{:S(2)}, u32[]{:S(2)}) collective-permute-start(f32[448,128]{1,0:T(8,128)S(1)} %constant_dynamic-slice_fusion.1), channel_id=1, source_target_pairs={{0,1},{1,0},{2,3},{3,2},{4,5},{5,4},{6,7},{7,6},{8,9},{9,8},{10,11... | collective-permute-start | bytes 688136 | tf_op jit(solution)/shard_map/ppermute | solution.py:491
  11.5 15.9 %all-to-all-start = ((f32[8,56,128]{2,1,0:T(8,128)}), f32[8,56,128]{2,1,0:T(8,128)S(1)}, u32[]{:S(2)}, u32[]{:S(2)}) async-start(f32[8,56,128]{2,1,0:T(8,128)} %bitcast.2), calls=%async_computation | async-start | bytes 458752 | tf_op jit(solution)/shard_map/all_to_all | solution.py:504
  18.7 2.2 %copy-start.4 = (f32[128,8192]{1,0:T(8,128)S(1)}, f32[128,8192]{1,0:T(8,128)}, u32[]{:S(2)}) copy-start(f32[128,8192]{1,0:T(8,128)} %copy-done.3) | copy-start | bytes 12582916
  28.2 11.6 %all-to-all-start.1 = ((f32[8,56,128]{2,1,0:T(8,128)}), f32[8,56,128]{2,1,0:T(8,128)S(1)}, u32[]{:S(2)}, u32[]{:S(2)}) async-start(f32[8,56,128]{2,1,0:T(8,128)} %broadcast_in_dim.4), calls=%async_computation.1 | async-start | bytes 458752 | tf_op jit(solution)/shard_map/all_to_all | solution.py:504
  31.6 2.2 %copy-start.5 = (f32[128,8192]{1,0:T(8,128)S(1)}, f32[128,8192]{1,0:T(8,128)}, u32[]{:S(2)}) copy-start(f32[128,8192]{1,0:T(8,128)} %copy-done.3) | copy-start | bytes 12582916
  37.8 1.0 %copy-start.8 = (f32[32,8192]{1,0:T(8,128)}, f32[32,8192]{1,0:T(8,128)S(1)}, u32[]{:S(2)}) copy-start(f32[32,8192]{1,0:T(8,128)S(1)} %transport.10.refs_2_) | copy-start | bytes 3145732
  39.8 2.6 %collective-permute-start.1 = (f32[448,128]{1,0:T(8,128)S(1)}, f32[448,128]{1,0:T(8,128)}, u32[]{:S(2)}, u32[]{:S(2)}) collective-permute-start(f32[448,128]{1,0:T(8,128)S(1)} %bitcast.8), channel_id=1, source_target_pairs={{0,1},{1,0},{2,3},{3,2},{4,5},{5,4},{6,7},{7,6},{8,9},{9,8},{10,11... | collective-permute-start | bytes 688136 | tf_op jit(solution)/shard_map/ppermute | solution.py:491
  44.3 1.0 %copy-start.11 = (f32[896,128]{1,0:T(8,128)S(1)}, f32[896,128]{1,0:T(8,128)}, u32[]{:S(2)}) copy-start(f32[896,128]{1,0:T(8,128)} %dynamic_update_slice.13.moments_ref) | copy-start | bytes 1376260
  46.8 1.2 %copy-start.9 = (f32[32,8192]{1,0:T(8,128)S(1)}, f32[32,8192]{1,0:T(8,128)}, u32[]{:S(2)}) copy-start(f32[32,8192]{1,0:T(8,128)} %copy-done.8) | copy-start | bytes 3145732
  52.5 2.0 %copy-start = (f32[128,8192]{1,0:T(8,128)}, f32[128,8192]{1,0:T(8,128)S(1)}, u32[]{:S(2)}) copy-start(f32[128,8192]{1,0:T(8,128)S(1)} %get-tuple-element.62.f_ref) | copy-start | bytes 12582916
  54.5 1.7 %collective-permute-start.2 = (f32[448,128]{1,0:T(8,128)S(1)}, f32[448,128]{1,0:T(8,128)S(1)}, u32[]{:S(2)}, u32[]{:S(2)}) collective-permute-start(f32[448,128]{1,0:T(8,128)S(1)} %constant_dynamic-slice_fusion), channel_id=1, source_target_pairs={{0,1},{1,0},{2,3},{3,2},{4,5},{5,4},{6,7},{7,6},{8,9},{9,8},{10,11... | collective-permute-start | bytes 688136 | tf_op jit(solution)/shard_map/ppermute | solution.py:491
  56.9 14.0 %all-to-all-start.2 = ((f32[8,56,128]{2,1,0:T(8,128)}), f32[8,56,128]{2,1,0:T(8,128)S(1)}, u32[]{:S(2)}, u32[]{:S(2)}) async-start(f32[8,56,128]{2,1,0:T(8,128)} %bitcast.4), calls=%async_computation.2 | async-start | bytes 458752 | tf_op jit(solution)/shard_map/all_to_all | solution.py:504
  61.9 2.2 %copy-start.1 = (f32[128,8192]{1,0:T(8,128)S(1)}, f32[128,8192]{1,0:T(8,128)}, u32[]{:S(2)}) copy-start(f32[128,8192]{1,0:T(8,128)} %copy-done) | copy-start | bytes 12582916
  71.6 11.8 %all-to-all-start.3 = ((f32[8,56,128]{2,1,0:T(8,128)}), f32[8,56,128]{2,1,0:T(8,128)S(1)}, u32[]{:S(2)}, u32[]{:S(2)}) async-start(f32[8,56,128]{2,1,0:T(8,128)} %broadcast_in_dim.5), calls=%async_computation.3 | async-start | bytes 458752 | tf_op jit(solution)/shard_map/all_to_all | solution.py:504
  75.0 2.2 %copy-start.2 = (f32[128,8192]{1,0:T(8,128)S(1)}, f32[128,8192]{1,0:T(8,128)}, u32[]{:S(2)}) copy-start(f32[128,8192]{1,0:T(8,128)} %copy-done) | copy-start | bytes 12582916
  81.2 1.0 %copy-start.6 = (f32[32,8192]{1,0:T(8,128)}, f32[32,8192]{1,0:T(8,128)S(1)}, u32[]{:S(2)}) copy-start(f32[32,8192]{1,0:T(8,128)S(1)} %transport.14.refs_2_) | copy-start | bytes 3145732
  83.4 2.6 %collective-permute-start.3 = (f32[448,128]{1,0:T(8,128)S(1)}, f32[448,128]{1,0:T(8,128)}, u32[]{:S(2)}, u32[]{:S(2)}) collective-permute-start(f32[448,128]{1,0:T(8,128)S(1)} %bitcast.6), channel_id=1, source_target_pairs={{0,1},{1,0},{2,3},{3,2},{4,5},{5,4},{6,7},{7,6},{8,9},{9,8},{10,11... | collective-permute-start | bytes 688136 | tf_op jit(solution)/shard_map/ppermute | solution.py:491
  87.9 1.0 %copy-start.10 = (f32[896,128]{1,0:T(8,128)S(1)}, f32[896,128]{1,0:T(8,128)}, u32[]{:S(2)}) copy-start(f32[896,128]{1,0:T(8,128)} %dynamic_update_slice.15.moments_ref) | copy-start | bytes 1376260
  89.8 1.2 %copy-start.7 = (f32[32,8192]{1,0:T(8,128)S(1)}, f32[32,8192]{1,0:T(8,128)}, u32[]{:S(2)}) copy-start(f32[32,8192]{1,0:T(8,128)} %copy-done.6) | copy-start | bytes 3145732

commit v3 on v2

--- a/solution.py
+++ b/solution.py
@@ -19,9 +19,9 @@
 
 LOG2E = 1.4426950408889634
 LANES = 128
-TILE = 512
+TILE = 256
 BASIS = 16
-SENT = 14
+SENT = 13
 COEF = 24
 DAMP = 13
 CHUNKS = 8
@@ -396,7 +396,7 @@
 def relaxed(g, coef_ref, basis, tile):
     per_tile = TILE // LANES
     parts = [
-        coef_ref[pl.ds(pl.multiple_of((tile * per_tile + part) * COEF, 8), COEF), :]
+        coef_ref[pl.ds((tile * per_tile + part) * COEF, COEF), :]
         for part in range(per_tile)
     ]
     coefficients = jnp.concatenate(parts, axis=1)
@@ -415,14 +415,20 @@
     coef_ref, basis_ref, table_ref, f_ref, moments_ref = refs[PARTS:]
     cells = f_ref.shape[1]
 
-    def step(tile, carry):
-        here = pl.ds(pl.multiple_of(tile * TILE, TILE), TILE)
-        values = relaxed(gathered(g_refs, here), coef_ref, basis_ref[...], tile)
-        f_ref[:, here] = values
+    def front(tile):
+        here = pl.ds(tile * TILE, TILE)
+        return relaxed(gathered(g_refs, here), coef_ref, basis_ref[...], tile)
+
+    def back(tile, values):
+        f_ref[:, tile * TILE : (tile + 1) * TILE] = values
         store_moments(moments_ref, table_ref[...], values, tile, cells // LANES)
-        return carry
-
-    lax.fori_loop(0, cells // TILE, step, 0, unroll=4)
+
+    values = front(0)
+    for tile in range(1, cells // TILE):
+        upcoming = front(tile)
+        back(tile - 1, values)
+        values = upcoming
+    back(cells // TILE - 1, values)
 
 
 def update_call(g, coefficients, basis, table):
@@ -447,19 +453,12 @@
     width = cells // CHUNKS
     copies = []
     for chunk in range(CHUNKS):
-
-        def step(local, carry, chunk=chunk):
+        for local in range(width // TILE):
             tile = chunk * (width // TILE) + local
-            here = pl.ds(pl.multiple_of(tile * TILE, TILE), TILE)
+            here = pl.ds(tile * TILE, TILE)
             held[:, here] = relaxed(gathered(g_refs, here), coef_ref, basis_ref[...], tile)
-            for part in range(TILE // LANES):
-                block = tile * (TILE // LANES) + part
-                fields_ref[:, pl.ds(pl.multiple_of(block * LANES, LANES), LANES)] = macro_ref[
-                    pl.ds(pl.multiple_of(block * 8, 8), 8), :
-                ]
-            return carry
-
-        lax.fori_loop(0, width // TILE, step, 0, unroll=True)
+            for block in range(tile * TILE // LANES, (tile + 1) * TILE // LANES):
+                fields_ref[:, pl.ds(block * LANES, LANES)] = macro_ref[pl.ds(block * 8, 8), :]
         there = pl.ds(chunk * width, width)
         copy = pltpu.make_async_copy(held.at[:, there], f_ref.at[:, there], sems.at[chunk])
         copy.start()
@@ -487,45 +486,67 @@
     )(*[near(part) for part in g], near(coefficients), near(macro), near(basis))
 
 
-def swap(values, count):
-    return lax.ppermute(values, "vel", [(device, device ^ 1) for device in range(count)])
-
-
-def staged_sum(values, count, offsets, f, tasks):
-    chips = count // 2
-    groups = [list(range(part, count, 2)) for part in range(2)]
-    rows, lanes = values.shape
-    half, width = rows // 2, rows // count
-    results = []
-
-    def exchange(block, some):
-        block, held = lax.optimization_barrier((block, f))
-        made = [task(held) for task in some]
-        out = lax.all_to_all(block, "vel", 0, 0, axis_index_groups=groups, tiled=True)
-        out, made = lax.optimization_barrier((out, made))
-        results.extend(made)
-        return out
-
-    own = lax.dynamic_slice_in_dim(values, offsets[0], half, 0, allow_negative_indices=False)
-    other = lax.dynamic_slice_in_dim(values, offsets[1], half, 0, allow_negative_indices=False)
-    block = own + swap(other, count)
-    block = jnp.sum(exchange(block.reshape(chips, width, lanes), tasks[: PARTS // 2]), axis=0)
-    copies = jnp.broadcast_to(block[None], (chips, width, lanes))
-    block = exchange(copies, tasks[PARTS // 2 :]).reshape(half, lanes)
-    whole = jnp.zeros((rows, lanes), values.dtype)
-    for part, offset in ((block, offsets[0]), (swap(block, count), offsets[1])):
-        whole = lax.dynamic_update_slice(
-            whole, part, (offset, 0), allow_negative_indices=(False, False)
-        )
-    return whole, results
+def add_kernel(left_ref, right_ref, out_ref):
+    out_ref[...] = left_ref[...] + right_ref[...]
+
+
+def add_call(left, right):
+    return pl.pallas_call(
+        add_kernel,
+        out_shape=pltpu.VMEM(left.shape, left.dtype),
+        in_specs=[WHOLE, WHOLE],
+        out_specs=WHOLE,
+        compiler_params=params(1),
+        name="add",
+    )(near(left), near(right))
+
+
+def plan(count):
+    strides = [1 << bit for bit in range(count.bit_length() - 1)]
+    return strides[:2], strides[2:]
+
+
+def swap(values, count, stride):
+    return lax.ppermute(values, "vel", [(device, device ^ stride) for device in range(count)])
+
+
+def staged_sum(values, count, sides, f, tasks):
+    splits, sums = plan(count)
+    results, waiting = [], list(tasks)
+
+    def exchange(block, stride, sent):
+        if stride == 1 or not waiting:
+            return block, swap(sent, count, stride)
+        block, sent, held = lax.optimization_barrier((block, sent, f))
+        made = waiting.pop(0)(held)
+        block, got, made = lax.optimization_barrier((block, swap(sent, count, stride), made))
+        results.append(made)
+        return block, got
+
+    block = values
+    for stride, lower_side in zip(splits, sides):
+        half = block.shape[0] // 2
+        first, second = block[:half], block[half:]
+        kept, sent = jnp.where(lower_side, first, second), jnp.where(lower_side, second, first)
+        kept, got = exchange(kept, stride, sent)
+        block = kept + got
+    for stride in sums:
+        block, got = exchange(block, stride, block)
+        block = add_call(block, got)
+    for stride, lower_side in reversed(list(zip(splits, sides))):
+        block, got = exchange(block, stride, block)
+        lower, upper = jnp.where(lower_side, block, got), jnp.where(lower_side, got, block)
+        block = jnp.concatenate([lower, upper], axis=0)
+    for task in waiting:
+        results.append(task(f))
+    return block, results
 
 
 def on_device(velocities, density, flow, thermal, deviation):
     count = lax.axis_size("vel")
-    half = SENT * density.shape[0] // LANES // 2
-    mine = (lax.axis_index("vel") & 1) * half
-    offsets = (mine, half - mine)
-    velocities, offsets = lax.optimization_barrier((velocities, offsets))
+    place = lax.axis_index("vel")
+    sides = [place & stride == 0 for stride in plan(count)[0]]
+    velocities, sides = lax.optimization_barrier((velocities, sides))
     f, moments, basis, table, stream = start_call(
         velocities, density, flow, thermal, deviation, velocities.shape[1] * count
     )
@@ -534,7 +555,7 @@
             functools.partial(lambda held, part: transport_call(stream, held, part), part=part)
             for part in range(PARTS)
         ]
-        summed, g = staged_sum(moments, count, offsets, f, tasks)
+        summed, g = staged_sum(moments, count, sides, f, tasks)
         coefficients, macro = fluid_call(summed)
         if iteration < ITERS - 1:
             f, moments = update_call(g, coefficients, basis, table)

time: 95 us -> 65.9 us (0.69)
  local copies, waits for them, and re-layouts: 29.5 us -> 0 us
  waiting for transfers between devices: 9.78 us -> 15.5 us
  Pallas kernels: 32.3 us -> 30.2 us
  starting transfers between devices: 20.2 us -> 18.7 us
  other arithmetic: 1.47 us -> 0.39 us
    unnamed x24 -> x0, local copies, waits for them, and re-layouts: 19.2 us -> none
    all_to_all x4 -> x0, starting transfers between devices: 19.1 us -> none  [exchange(): lax.all_to_all(block, 'vel', 0, 0, axis_index_groups=groups, tiled=True)]
    ppermute x4 -> x12, starting transfers between devices: 1.09 us -> 18.7 us  [swap(): lax.ppermute(values, 'vel', [(device, device ^ stride) for device in rang...]
    ppermute x4 -> x12, waiting for transfers between devices: 2.24 us -> 15.5 us  [swap(): lax.ppermute(values, 'vel', [(device, device ^ stride) for device in rang...]
    all_to_all x4 -> x0, waiting for transfers between devices: 7.55 us -> none  [exchange(): lax.all_to_all(block, 'vel', 0, 0, axis_index_groups=groups, tiled=True)]
    dynamic_update_slice x4 -> x0, local copies, waits for them, and re-layouts: 7.27 us -> none  [staged_sum(): lax.dynamic_update_slice(whole, part, (offset, 0), allow_negative_indices...]
    another operation x2 -> x0, local copies, waits for them, and re-layouts: 1.61 us -> none
    broadcast_in_dim x2 -> x0, local copies, waits for them, and re-layouts: 1.41 us -> none  [staged_sum(): copies = jnp.broadcast_to(block[None], (chips, width, lanes))]
  transfers between devices with their start and end apart: 8 -> 12, of which waited for: 6 -> 12; matrix products, arithmetic and copies ran while one was open for 6% -> 0% of each run, Pallas kernels for 17% -> 24%
where the time goes in v3:
time: 65.9 us; the launch traced here: 65.8 us
  Pallas kernels  30.2 us (46%)
  starting transfers between devices  18.7 us (28%)
  waiting for transfers between devices  15.5 us (24%)
  between operations  1.01 us (2%)
    ppermute x12, starting transfers between devices, swap(): lax.ppermute(values, 'vel', [(device, device ^ stride) for device in rang...  18.7 us
    pallas_call x8, Pallas kernels, transport_call(): pl.pallas_call(functools.partial(transport_kernel, part * rows), out_shap...  15.9 us
    ppermute x12, waiting for transfers between devices, swap(): lax.ppermute(values, 'vel', [(device, device ^ stride) for device in rang...  15.5 us
    pallas_call x1, Pallas kernels, start_call(): pl.pallas_call(functools.partial(start_kernel, total_count), out_shape=(p...  5.54 us
    pallas_call x1, Pallas kernels, update_call(): pl.pallas_call(update_kernel, out_shape=(pltpu.VMEM((rows * PARTS, cells)...  3.23 us
    pallas_call x1, Pallas kernels, finish_call(): pl.pallas_call(finish_kernel, out_shape=(jax.ShapeDtypeStruct((rows * PAR...  3.06 us
    pallas_call x2, Pallas kernels, fluid_call(): pl.pallas_call(fluid_kernel, out_shape=(pltpu.VMEM((blocks * COEF, LANES)...  2.37 us
  transfers between devices with their start and end apart: 12, of which 12 were waited for; matrix products, arithmetic and copies ran while one was open for 0% of the time, Pallas kernels for 24%

profile of v3, /device:TPU:0, one launch (start us, length us, event | category | flops | bytes accessed | tf_op | source)
XLA Modules:
  0.0 65.8 jit_solution(856784655806813831)
XLA Ops:
  0.6 5.5 %start.1 = (f32[128,8192]{1,0:T(8,128)S(1)}, f32[832,128]{1,0:T(8,128)S(1)}, bf16[128,128]{1,0:T(8,128)(2,1)S(1)}, bf16[32,256]{1,0:T(8,128)(2,1)S(1)}, f32[128,128]{1,0:T(8,128)S(1)}) custom-call(f32[3,128]{1,0:T(4,128)} %vel_hbm, f32[1,8192]{1,0:T(1,128)} %bitcast.2, f32[3,8192]{1,0:T(4,128)} %flow_hbm.1, f32[1,8192]{1,0:T(1,128)} %bitcast.3, ...), custom_call_target="tpu_custom_call" | custom-call | tf_op jit(solution)/shard_map/start/pallas_call | solution.py:170
  7.9 3.0 %collective-permute-start.1 = (f32[208,128]{1,0:T(8,128)S(1)}, f32[208,128]{1,0:T(8,128)S(1)}, u32[]{:S(2)}, u32[]{:S(2)}) collective-permute-start(f32[208,128]{1,0:T(8,128)S(1)} %get-tuple-element.69), channel_id=1, source_target_pairs={{0,2},{1,3},{2,0},{3,1},{4,6},{5,7},{6,4},{7,5},{8,10},{9,11},{10,... | collective-permute-start | bytes 319496 | tf_op jit(solution)/shard_map/ppermute | solution.py:510
  10.8 2.0 %transport.8.refs_0_ = f32[32,8192]{1,0:T(8,128)S(1)} custom-call(f32[128,128]{1,0:T(8,128)S(1)} %get-tuple-element.70.stream_ref, f32[128,8192]{1,0:T(8,128)S(1)} %get-tuple-element.89.f_ref), custom_call_target="tpu_custom_call" | custom-call | tf_op jit(solution)/shard_map/transport/pallas_call | solution.py:260
  14.1 1.9 %collective-permute-start.2 = (f32[208,128]{1,0:T(8,128)S(1)}, f32[208,128]{1,0:T(8,128)S(1)}, u32[]{:S(2)}, u32[]{:S(2)}) collective-permute-start(f32[208,128]{1,0:T(8,128)S(1)} %add.17.left_ref), channel_id=1, source_target_pairs={{0,4},{1,5},{2,6},{3,7},{4,0},{5,1},{6,2},{7,3},{8,12},{9,13},{10,... | collective-permute-start | bytes 319496 | tf_op jit(solution)/shard_map/ppermute | solution.py:510
  16.0 2.0 %transport.9.refs_1_ = f32[32,8192]{1,0:T(8,128)S(1)} custom-call(f32[128,128]{1,0:T(8,128)S(1)} %get-tuple-element.70.stream_ref, f32[128,8192]{1,0:T(8,128)S(1)} %get-tuple-element.89.f_ref), custom_call_target="tpu_custom_call" | custom-call | tf_op jit(solution)/shard_map/transport/pallas_call | solution.py:260
  18.9 2.9 %collective-permute-start.3 = (f32[208,128]{1,0:T(8,128)S(1)}, f32[208,128]{1,0:T(8,128)S(1)}, u32[]{:S(2)}, u32[]{:S(2)}) collective-permute-start(f32[208,128]{1,0:T(8,128)S(1)} %add.22.left_ref), channel_id=1, source_target_pairs={{0,8},{1,9},{2,10},{3,11},{4,12},{5,13},{6,14},{7,15},{8,0},{9,1},... | collective-permute-start | bytes 319496 | tf_op jit(solution)/shard_map/ppermute | solution.py:510
  21.8 2.0 %transport.10.refs_2_ = f32[32,8192]{1,0:T(8,128)S(1)} custom-call(f32[128,128]{1,0:T(8,128)S(1)} %get-tuple-element.70.stream_ref, f32[128,8192]{1,0:T(8,128)S(1)} %get-tuple-element.89.f_ref), custom_call_target="tpu_custom_call" | custom-call | tf_op jit(solution)/shard_map/transport/pallas_call | solution.py:260
  24.6 2.9 %collective-permute-start.4 = (f32[208,128]{1,0:T(8,128)S(1)}, f32[208,128]{1,0:T(8,128)S(1)}, u32[]{:S(2)}, u32[]{:S(2)}) collective-permute-start(f32[208,128]{1,0:T(8,128)S(1)} %add.23), channel_id=1, source_target_pairs={{0,2},{1,3},{2,0},{3,1},{4,6},{5,7},{6,4},{7,5},{8,10},{9,11},{10,... | collective-permute-start | bytes 319496 | tf_op jit(solution)/shard_map/ppermute | solution.py:510
  27.6 2.0 %transport.11.refs_3_ = f32[32,8192]{1,0:T(8,128)S(1)} custom-call(f32[128,128]{1,0:T(8,128)S(1)} %get-tuple-element.70.stream_ref, f32[128,8192]{1,0:T(8,128)S(1)} %get-tuple-element.89.f_ref), custom_call_target="tpu_custom_call" | custom-call | tf_op jit(solution)/shard_map/transport/pallas_call | solution.py:260
  30.4 1.5 %collective-permute-done.5 = f32[416,128]{1,0:T(8,128)S(1)} collective-permute-done((f32[416,128]{1,0:T(8,128)S(1)}, f32[416,128]{1,0:T(8,128)S(1)}, u32[]{:S(2)}, u32[]{:S(2)}) %collective-permute-start.5) | collective-permute-done | bytes 213024 | tf_op jit(solution)/shard_map/ppermute | solution.py:510
  31.9 1.5 %fluid.2 = (f32[1536,128]{1,0:T(8,128)S(1)}, f32[512,128]{1,0:T(8,128)}) custom-call(f32[832,128]{1,0:T(8,128)S(1)} %pad_maximum_fusion.moments_ref), custom_call_target="tpu_custom_call" | custom-call | tf_op jit(solution)/shard_map/fluid/pallas_call | solution.py:383
  33.4 3.2 %update.1 = (f32[128,8192]{1,0:T(8,128)S(1)}, f32[832,128]{1,0:T(8,128)S(1)}) custom-call(f32[32,8192]{1,0:T(8,128)S(1)} %transport.8.refs_0_, f32[32,8192]{1,0:T(8,128)S(1)} %transport.9.refs_1_, f32[32,8192]{1,0:T(8,128)S(1)} %transport.10.refs_2_, f32[32,8192]{1,0:T(8,128)S(1)} %transport.11.refs_3_, f32[1536,128]{1,0:T(8,128)S(1)} %get-tuple-element.93.refs_4_, ...), custom_call_target="tpu_custom_call" | custom-call | tf_op jit(solution)/shard_map/update/pallas_call | solution.py:436
  36.9 1.3 %collective-permute-done.6 = f32[416,128]{1,0:T(8,128)S(1)} collective-permute-done((f32[416,128]{1,0:T(8,128)S(1)}, f32[416,128]{1,0:T(8,128)S(1)}, u32[]{:S(2)}, u32[]{:S(2)}) %collective-permute-start.6) | collective-permute-done | bytes 213024 | tf_op jit(solution)/shard_map/ppermute | solution.py:510
  38.3 2.1 %collective-permute-start.7 = (f32[208,128]{1,0:T(8,128)S(1)}, f32[208,128]{1,0:T(8,128)S(1)}, u32[]{:S(2)}, u32[]{:S(2)}) collective-permute-start(f32[208,128]{1,0:T(8,128)S(1)} %get-tuple-element.99), channel_id=1, source_target_pairs={{0,2},{1,3},{2,0},{3,1},{4,6},{5,7},{6,4},{7,5},{8,10},{9,11},{10,... | collective-permute-start | bytes 319496 | tf_op jit(solution)/shard_map/ppermute | solution.py:510
  40.4 2.0 %transport.12.refs_0_ = f32[32,8192]{1,0:T(8,128)S(1)} custom-call(f32[128,128]{1,0:T(8,128)S(1)} %get-tuple-element.70.stream_ref, f32[128,8192]{1,0:T(8,128)S(1)} %get-tuple-element.118.f_ref), custom_call_target="tpu_custom_call" | custom-call | tf_op jit(solution)/shard_map/transport/pallas_call | solution.py:260
  44.6 2.0 %transport.13.refs_1_ = f32[32,8192]{1,0:T(8,128)S(1)} custom-call(f32[128,128]{1,0:T(8,128)S(1)} %get-tuple-element.70.stream_ref, f32[128,8192]{1,0:T(8,128)S(1)} %get-tuple-element.118.f_ref), custom_call_target="tpu_custom_call" | custom-call | tf_op jit(solution)/shard_map/transport/pallas_call | solution.py:260
  46.6 1.8 %collective-permute-done.8.right_ref = f32[208,128]{1,0:T(8,128)S(1)} collective-permute-done((f32[208,128]{1,0:T(8,128)S(1)}, f32[208,128]{1,0:T(8,128)S(1)}, u32[]{:S(2)}, u32[]{:S(2)}) %collective-permute-start.8) | collective-permute-done | bytes 106528 | tf_op jit(solution)/shard_map/ppermute | solution.py:510
  48.4 2.3 %collective-permute-start.9 = (f32[208,128]{1,0:T(8,128)S(1)}, f32[208,128]{1,0:T(8,128)S(1)}, u32[]{:S(2)}, u32[]{:S(2)}) collective-permute-start(f32[208,128]{1,0:T(8,128)S(1)} %add.24.left_ref), channel_id=1, source_target_pairs={{0,8},{1,9},{2,10},{3,11},{4,12},{5,13},{6,14},{7,15},{8,0},{9,1},... | collective-permute-start | bytes 319496 | tf_op jit(solution)/shard_map/ppermute | solution.py:510
  50.8 2.0 %transport.14.refs_2_ = f32[32,8192]{1,0:T(8,128)S(1)} custom-call(f32[128,128]{1,0:T(8,128)S(1)} %get-tuple-element.70.stream_ref, f32[128,8192]{1,0:T(8,128)S(1)} %get-tuple-element.118.f_ref), custom_call_target="tpu_custom_call" | custom-call | tf_op jit(solution)/shard_map/transport/pallas_call | solution.py:260
  52.8 2.5 %collective-permute-done.9.right_ref = f32[208,128]{1,0:T(8,128)S(1)} collective-permute-done((f32[208,128]{1,0:T(8,128)S(1)}, f32[208,128]{1,0:T(8,128)S(1)}, u32[]{:S(2)}, u32[]{:S(2)}) %collective-permute-start.9) | collective-permute-done | bytes 106528 | tf_op jit(solution)/shard_map/ppermute | solution.py:510
  55.3 1.8 %collective-permute-start.10 = (f32[208,128]{1,0:T(8,128)S(1)}, f32[208,128]{1,0:T(8,128)S(1)}, u32[]{:S(2)}, u32[]{:S(2)}) collective-permute-start(f32[208,128]{1,0:T(8,128)S(1)} %add.25), channel_id=1, source_target_pairs={{0,2},{1,3},{2,0},{3,1},{4,6},{5,7},{6,4},{7,5},{8,10},{9,11},{10,... | collective-permute-start | bytes 319496 | tf_op jit(solution)/shard_map/ppermute | solution.py:510
  57.1 2.0 %transport.15.refs_3_ = f32[32,8192]{1,0:T(8,128)S(1)} custom-call(f32[128,128]{1,0:T(8,128)S(1)} %get-tuple-element.70.stream_ref, f32[128,8192]{1,0:T(8,128)S(1)} %get-tuple-element.118.f_ref), custom_call_target="tpu_custom_call" | custom-call | tf_op jit(solution)/shard_map/transport/pallas_call | solution.py:260
  60.2 1.5 %collective-permute-done.11 = f32[416,128]{1,0:T(8,128)S(1)} collective-permute-done((f32[416,128]{1,0:T(8,128)S(1)}, f32[416,128]{1,0:T(8,128)S(1)}, u32[]{:S(2)}, u32[]{:S(2)}) %collective-permute-start.11) | collective-permute-done | bytes 213024 | tf_op jit(solution)/shard_map/ppermute | solution.py:510
  62.6 3.1 %finish.1 = (f32[128,8192]{1,0:T(8,128)}, f32[8,8192]{1,0:T(8,128)}) custom-call(f32[32,8192]{1,0:T(8,128)S(1)} %transport.12.refs_0_, f32[32,8192]{1,0:T(8,128)S(1)} %transport.13.refs_1_, f32[32,8192]{1,0:T(8,128)S(1)} %transport.14.refs_2_, f32[32,8192]{1,0:T(8,128)S(1)} %transport.15.refs_3_, f32[1536,128]{1,0:T(8,128)S(1)} %get-tuple-element.122.refs_4_, ...), custom_call_target="tpu_custom_call" | custom-call | tf_op jit(solution)/shard_map/finish/pallas_call | solution.py:472
  (33 shorter events, 10.1 us)
Async XLA Ops:
  6.2 1.6 %collective-permute-start = (f32[416,128]{1,0:T(8,128)S(1)}, f32[416,128]{1,0:T(8,128)S(1)}, u32[]{:S(2)}, u32[]{:S(2)}) collective-permute-start(f32[416,128]{1,0:T(8,128)S(1)} %slice_select_fusion.1), channel_id=1, source_target_pairs={{0,1},{1,0},{2,3},{3,2},{4,5},{5,4},{6,7},{7,6},{8,9},{9,8},{10,11... | collective-permute-start | bytes 638984 | tf_op jit(solution)/shard_map/ppermute | solution.py:510
  7.9 6.2 %collective-permute-start.1 = (f32[208,128]{1,0:T(8,128)S(1)}, f32[208,128]{1,0:T(8,128)S(1)}, u32[]{:S(2)}, u32[]{:S(2)}) collective-permute-start(f32[208,128]{1,0:T(8,128)S(1)} %get-tuple-element.69), channel_id=1, source_target_pairs={{0,2},{1,3},{2,0},{3,1},{4,6},{5,7},{6,4},{7,5},{8,10},{9,11},{10,... | collective-permute-start | bytes 319496 | tf_op jit(solution)/shard_map/ppermute | solution.py:510
  14.1 4.8 %collective-permute-start.2 = (f32[208,128]{1,0:T(8,128)S(1)}, f32[208,128]{1,0:T(8,128)S(1)}, u32[]{:S(2)}, u32[]{:S(2)}) collective-permute-start(f32[208,128]{1,0:T(8,128)S(1)} %add.17.left_ref), channel_id=1, source_target_pairs={{0,4},{1,5},{2,6},{3,7},{4,0},{5,1},{6,2},{7,3},{8,12},{9,13},{10,... | collective-permute-start | bytes 319496 | tf_op jit(solution)/shard_map/ppermute | solution.py:510
  18.9 5.7 %collective-permute-start.3 = (f32[208,128]{1,0:T(8,128)S(1)}, f32[208,128]{1,0:T(8,128)S(1)}, u32[]{:S(2)}, u32[]{:S(2)}) collective-permute-start(f32[208,128]{1,0:T(8,128)S(1)} %add.22.left_ref), channel_id=1, source_target_pairs={{0,8},{1,9},{2,10},{3,11},{4,12},{5,13},{6,14},{7,15},{8,0},{9,1},... | collective-permute-start | bytes 319496 | tf_op jit(solution)/shard_map/ppermute | solution.py:510
  24.6 5.6 %collective-permute-start.4 = (f32[208,128]{1,0:T(8,128)S(1)}, f32[208,128]{1,0:T(8,128)S(1)}, u32[]{:S(2)}, u32[]{:S(2)}) collective-permute-start(f32[208,128]{1,0:T(8,128)S(1)} %add.23), channel_id=1, source_target_pairs={{0,2},{1,3},{2,0},{3,1},{4,6},{5,7},{6,4},{7,5},{8,10},{9,11},{10,... | collective-permute-start | bytes 319496 | tf_op jit(solution)/shard_map/ppermute | solution.py:510
  30.3 1.5 %collective-permute-start.5 = (f32[416,128]{1,0:T(8,128)S(1)}, f32[416,128]{1,0:T(8,128)S(1)}, u32[]{:S(2)}, u32[]{:S(2)}) collective-permute-start(f32[416,128]{1,0:T(8,128)S(1)} %pad_maximum_fusion.2), channel_id=1, source_target_pairs={{0,1},{1,0},{2,3},{3,2},{4,5},{5,4},{6,7},{7,6},{8,9},{9,8},{10,11... | collective-permute-start | bytes 638984 | tf_op jit(solution)/shard_map/ppermute | solution.py:510
  36.7 1.5 %collective-permute-start.6 = (f32[416,128]{1,0:T(8,128)S(1)}, f32[416,128]{1,0:T(8,128)S(1)}, u32[]{:S(2)}, u32[]{:S(2)}) collective-permute-start(f32[416,128]{1,0:T(8,128)S(1)} %slice_select_fusion), channel_id=1, source_target_pairs={{0,1},{1,0},{2,3},{3,2},{4,5},{5,4},{6,7},{7,6},{8,9},{9,8},{10,11... | collective-permute-start | bytes 638984 | tf_op jit(solution)/shard_map/ppermute | solution.py:510
  38.3 5.4 %collective-permute-start.7 = (f32[208,128]{1,0:T(8,128)S(1)}, f32[208,128]{1,0:T(8,128)S(1)}, u32[]{:S(2)}, u32[]{:S(2)}) collective-permute-start(f32[208,128]{1,0:T(8,128)S(1)} %get-tuple-element.99), channel_id=1, source_target_pairs={{0,2},{1,3},{2,0},{3,1},{4,6},{5,7},{6,4},{7,5},{8,10},{9,11},{10,... | collective-permute-start | bytes 319496 | tf_op jit(solution)/shard_map/ppermute | solution.py:510
  43.6 4.8 %collective-permute-start.8 = (f32[208,128]{1,0:T(8,128)S(1)}, f32[208,128]{1,0:T(8,128)S(1)}, u32[]{:S(2)}, u32[]{:S(2)}) collective-permute-start(f32[208,128]{1,0:T(8,128)S(1)} %add.19.left_ref), channel_id=1, source_target_pairs={{0,4},{1,5},{2,6},{3,7},{4,0},{5,1},{6,2},{7,3},{8,12},{9,13},{10,... | collective-permute-start | bytes 319496 | tf_op jit(solution)/shard_map/ppermute | solution.py:510
  48.4 6.8 %collective-permute-start.9 = (f32[208,128]{1,0:T(8,128)S(1)}, f32[208,128]{1,0:T(8,128)S(1)}, u32[]{:S(2)}, u32[]{:S(2)}) collective-permute-start(f32[208,128]{1,0:T(8,128)S(1)} %add.24.left_ref), channel_id=1, source_target_pairs={{0,8},{1,9},{2,10},{3,11},{4,12},{5,13},{6,14},{7,15},{8,0},{9,1},... | collective-permute-start | bytes 319496 | tf_op jit(solution)/shard_map/ppermute | solution.py:510
  55.3 4.8 %collective-permute-start.10 = (f32[208,128]{1,0:T(8,128)S(1)}, f32[208,128]{1,0:T(8,128)S(1)}, u32[]{:S(2)}, u32[]{:S(2)}) collective-permute-start(f32[208,128]{1,0:T(8,128)S(1)} %add.25), channel_id=1, source_target_pairs={{0,2},{1,3},{2,0},{3,1},{4,6},{5,7},{6,4},{7,5},{8,10},{9,11},{10,... | collective-permute-start | bytes 319496 | tf_op jit(solution)/shard_map/ppermute | solution.py:510
  60.1 1.5 %collective-permute-start.11 = (f32[416,128]{1,0:T(8,128)S(1)}, f32[416,128]{1,0:T(8,128)S(1)}, u32[]{:S(2)}, u32[]{:S(2)}) collective-permute-start(f32[416,128]{1,0:T(8,128)S(1)} %pad_maximum_fusion.3), channel_id=1, source_target_pairs={{0,1},{1,0},{2,3},{3,2},{4,5},{5,4},{6,7},{7,6},{8,9},{9,8},{10,11... | collective-permute-start | bytes 638984 | tf_op jit(solution)/shard_map/ppermute | solution.py:510

commit v4 on v3

--- a/solution.py
+++ b/solution.py
@@ -25,7 +25,8 @@
 COEF = 24
 DAMP = 13
 CHUNKS = 8
-PARTS = 4
+PARTS = 8
+BESIDE = (1, 2, 1, 2, 1, 1)
 MIB = 1024 * 1024
 
 WHOLE = pl.BlockSpec(memory_space=pltpu.VMEM)
@@ -512,34 +513,52 @@
 
 def staged_sum(values, count, sides, f, tasks):
     splits, sums = plan(count)
-    results, waiting = [], list(tasks)
-
-    def exchange(block, stride, sent):
-        if stride == 1 or not waiting:
-            return block, swap(sent, count, stride)
-        block, sent, held = lax.optimization_barrier((block, sent, f))
-        made = waiting.pop(0)(held)
-        block, got, made = lax.optimization_barrier((block, swap(sent, count, stride), made))
-        results.append(made)
-        return block, got
-
-    block = values
-    for stride, lower_side in zip(splits, sides):
-        half = block.shape[0] // 2
-        first, second = block[:half], block[half:]
-        kept, sent = jnp.where(lower_side, first, second), jnp.where(lower_side, second, first)
-        kept, got = exchange(kept, stride, sent)
-        block = kept + got
+    results, waiting, portions = [], list(tasks), list(BESIDE)
+
+    def exchange(chunks, stride):
+        got = [swap(chunk, count, stride) for chunk in chunks]
+        portion = portions.pop(0) if portions else 0
+        if portion:
+            _, held = lax.optimization_barrier((chunks[-1], f))
+            made = [task(held) for task in waiting[:portion]]
+            del waiting[:portion]
+            got[0], made = lax.optimization_barrier((got[0], made))
+            results.extend(made)
+        return got
+
+    def split(chunks, stride, lower_side):
+        kept, sent = [], []
+        for chunk in chunks:
+            half = chunk.shape[0] // 2
+            first, second = chunk[:half], chunk[half:]
+            kept.append(jnp.where(lower_side, first, second))
+            sent.append(jnp.where(lower_side, second, first))
+        sent = lax.optimization_barrier(sent)
+        got = exchange(sent, stride)
+        if len(chunks) == 1:
+            return [kept[0] + got[0]]
+        return [add_call(own, other) for own, other in zip(kept, got)]
+
+    def join(chunks, stride, lower_side):
+        out = []
+        for own, got in zip(chunks, exchange(chunks, stride)):
+            lower = jnp.where(lower_side, own, got)
+            upper = jnp.where(lower_side, got, own)
+            out.append((lower, upper))
+        return out
+
+    (block,) = split([values], splits[0], sides[0])
+    half = block.shape[0] // 2
+    chunks = [block[:half], block[half:]]
+    for stride, lower_side in zip(splits[1:], sides[1:]):
+        chunks = split(chunks, stride, lower_side)
     for stride in sums:
-        block, got = exchange(block, stride, block)
-        block = add_call(block, got)
-    for stride, lower_side in reversed(list(zip(splits, sides))):
-        block, got = exchange(block, stride, block)
-        lower, upper = jnp.where(lower_side, block, got), jnp.where(lower_side, got, block)
-        block = jnp.concatenate([lower, upper], axis=0)
-    for task in waiting:
-        results.append(task(f))
-    return block, results
+        chunks = [add_call(own, got) for own, got in zip(chunks, exchange(chunks, stride))]
+    for stride, lower_side in reversed(list(zip(splits[1:], sides[1:]))):
+        chunks = [jnp.concatenate(both, axis=0) for both in join(chunks, stride, lower_side)]
+    lowers, uppers = zip(*join(chunks, splits[0], sides[0]))
+    results.extend(task(f) for task in waiting)
+    return jnp.concatenate(lowers + uppers, axis=0), results
 
 
 def on_device(velocities, density, flow, thermal, deviation):

time: 65.9 us -> 64.3 us (0.976)
  waiting for transfers between devices: 15.5 us -> 5.49 us
  starting transfers between devices: 18.7 us -> 26.8 us
    ppermute x12 -> x22, waiting for transfers between devices: 15.5 us -> 5.49 us  [swap(): lax.ppermute(values, 'vel', [(device, device ^ stride) for device in rang...]
    ppermute x12 -> x22, starting transfers between devices: 18.7 us -> 26.8 us  [swap(): lax.ppermute(values, 'vel', [(device, device ^ stride) for device in rang...]
    pallas_call x8 -> x16, Pallas kernels: 15.9 us -> 15.9 us  [transport_call(): pl.pallas_call(functools.partial(transport_kernel, part * rows), out_shap...]
  transfers between devices with their start and end apart: 12 -> 22, of which waited for: 12 -> 13; matrix products, arithmetic and copies ran while one was open for 0% -> 0% of each run, Pallas kernels for 24% -> 25%
where the time goes in v4:
time: 64.3 us; the launch traced here: 64.1 us
  Pallas kernels  30.3 us (47%)
  starting transfers between devices  26.8 us (42%)
  waiting for transfers between devices  5.49 us (9%)
  between operations  1.17 us (2%)
    ppermute x22, starting transfers between devices, swap(): lax.ppermute(values, 'vel', [(device, device ^ stride) for device in rang...  26.8 us
    pallas_call x16, Pallas kernels, transport_call(): pl.pallas_call(functools.partial(transport_kernel, part * rows), out_shap...  15.9 us
    pallas_call x1, Pallas kernels, start_call(): pl.pallas_call(functools.partial(start_kernel, total_count), out_shape=(p...  5.54 us
    ppermute x22, waiting for transfers between devices, swap(): lax.ppermute(values, 'vel', [(device, device ^ stride) for device in rang...  5.49 us
    pallas_call x1, Pallas kernels, update_call(): pl.pallas_call(update_kernel, out_shape=(pltpu.VMEM((rows * PARTS, cells)...  3.23 us
    pallas_call x1, Pallas kernels, finish_call(): pl.pallas_call(finish_kernel, out_shape=(jax.ShapeDtypeStruct((rows * PAR...  3.06 us
    pallas_call x2, Pallas kernels, fluid_call(): pl.pallas_call(fluid_kernel, out_shape=(pltpu.VMEM((blocks * COEF, LANES)...  2.37 us
  transfers between devices with their start and end apart: 22, of which 13 were waited for; matrix products, arithmetic and copies ran while one was open for 0% of the time, Pallas kernels for 25%

profile of v4, /device:TPU:0, one launch (start us, length us, event | category | flops | bytes accessed | tf_op | source)
XLA Modules:
  0.0 64.1 jit_solution(8538219475264143103)
XLA Ops:
  0.6 5.5 %start.1 = (f32[128,8192]{1,0:T(8,128)S(1)}, f32[832,128]{1,0:T(8,128)S(1)}, bf16[128,128]{1,0:T(8,128)(2,1)S(1)}, bf16[32,256]{1,0:T(8,128)(2,1)S(1)}, f32[128,128]{1,0:T(8,128)S(1)}) custom-call(f32[3,128]{1,0:T(4,128)} %vel_hbm, f32[1,8192]{1,0:T(1,128)} %bitcast.2, f32[3,8192]{1,0:T(4,128)} %flow_hbm.1, f32[1,8192]{1,0:T(1,128)} %bitcast.3, ...), custom_call_target="tpu_custom_call" | custom-call | tf_op jit(solution)/shard_map/start/pallas_call | solution.py:171
  6.7 1.0 %transport.16.refs_0_ = f32[16,8192]{1,0:T(8,128)S(1)} custom-call(f32[128,128]{1,0:T(8,128)S(1)} %get-tuple-element.62.stream_ref, f32[128,8192]{1,0:T(8,128)S(1)} %get-tuple-element.84.f_ref), custom_call_target="tpu_custom_call" | custom-call | tf_op jit(solution)/shard_map/transport/pallas_call | solution.py:261
  7.9 3.0 %collective-permute-start.1 = (f32[104,128]{1,0:T(8,128)S(1)}, f32[104,128]{1,0:T(8,128)S(1)}, u32[]{:S(2)}, u32[]{:S(2)}) collective-permute-start(f32[104,128]{1,0:T(8,128)S(1)} %get-tuple-element.68), channel_id=1, source_target_pairs={{0,2},{1,3},{2,0},{3,1},{4,6},{5,7},{6,4},{7,5},{8,10},{9,11},{10,... | collective-permute-start | bytes 159752 | tf_op jit(solution)/shard_map/ppermute | solution.py:511
  11.9 1.0 %transport.17.refs_1_ = f32[16,8192]{1,0:T(8,128)S(1)} custom-call(f32[128,128]{1,0:T(8,128)S(1)} %get-tuple-element.62.stream_ref, f32[128,8192]{1,0:T(8,128)S(1)} %get-tuple-element.84.f_ref), custom_call_target="tpu_custom_call" | custom-call | tf_op jit(solution)/shard_map/transport/pallas_call | solution.py:261
  13.0 2.4 %collective-permute-start.2 = (f32[104,128]{1,0:T(8,128)S(1)}, f32[104,128]{1,0:T(8,128)S(1)}, u32[]{:S(2)}, u32[]{:S(2)}) collective-permute-start(f32[104,128]{1,0:T(8,128)S(1)} %add.22.left_ref), channel_id=1, source_target_pairs={{0,4},{1,5},{2,6},{3,7},{4,0},{5,1},{6,2},{7,3},{8,12},{9,13},{10,... | collective-permute-start | bytes 159752 | tf_op jit(solution)/shard_map/ppermute | solution.py:511
  15.4 1.3 %collective-permute-start.5 = (f32[104,128]{1,0:T(8,128)S(1)}, f32[104,128]{1,0:T(8,128)S(1)}, u32[]{:S(2)}, u32[]{:S(2)}) collective-permute-start(f32[104,128]{1,0:T(8,128)S(1)} %add.23.left_ref), channel_id=1, source_target_pairs={{0,4},{1,5},{2,6},{3,7},{4,0},{5,1},{6,2},{7,3},{8,12},{9,13},{10,... | collective-permute-start | bytes 159752 | tf_op jit(solution)/shard_map/ppermute | solution.py:511
  17.9 2.9 %collective-permute-start.4 = (f32[104,128]{1,0:T(8,128)S(1)}, f32[104,128]{1,0:T(8,128)S(1)}, u32[]{:S(2)}, u32[]{:S(2)}) collective-permute-start(f32[104,128]{1,0:T(8,128)S(1)} %add.24.left_ref), channel_id=1, source_target_pairs={{0,8},{1,9},{2,10},{3,11},{4,12},{5,13},{6,14},{7,15},{8,0},{9,1},... | collective-permute-start | bytes 159752 | tf_op jit(solution)/shard_map/ppermute | solution.py:511
  20.8 1.6 %collective-permute-start.7 = (f32[104,128]{1,0:T(8,128)S(1)}, f32[104,128]{1,0:T(8,128)S(1)}, u32[]{:S(2)}, u32[]{:S(2)}) collective-permute-start(f32[104,128]{1,0:T(8,128)S(1)} %add.25.left_ref), channel_id=1, source_target_pairs={{0,8},{1,9},{2,10},{3,11},{4,12},{5,13},{6,14},{7,15},{8,0},{9,1},... | collective-permute-start | bytes 159752 | tf_op jit(solution)/shard_map/ppermute | solution.py:511
  23.4 1.0 %transport.20.refs_4_ = f32[16,8192]{1,0:T(8,128)S(1)} custom-call(f32[128,128]{1,0:T(8,128)S(1)} %get-tuple-element.62.stream_ref, f32[128,8192]{1,0:T(8,128)S(1)} %get-tuple-element.84.f_ref), custom_call_target="tpu_custom_call" | custom-call | tf_op jit(solution)/shard_map/transport/pallas_call | solution.py:261
  24.5 1.5 %collective-permute-start.6 = (f32[104,128]{1,0:T(8,128)S(1)}, f32[104,128]{1,0:T(8,128)S(1)}, u32[]{:S(2)}, u32[]{:S(2)}) collective-permute-start(f32[104,128]{1,0:T(8,128)S(1)} %add.26), channel_id=1, source_target_pairs={{0,2},{1,3},{2,0},{3,1},{4,6},{5,7},{6,4},{7,5},{8,10},{9,11},{10,... | collective-permute-start | bytes 159752 | tf_op jit(solution)/shard_map/ppermute | solution.py:511
  26.0 1.5 %collective-permute-start.9 = (f32[104,128]{1,0:T(8,128)S(1)}, f32[104,128]{1,0:T(8,128)S(1)}, u32[]{:S(2)}, u32[]{:S(2)}) collective-permute-start(f32[104,128]{1,0:T(8,128)S(1)} %add.27), channel_id=1, source_target_pairs={{0,2},{1,3},{2,0},{3,1},{4,6},{5,7},{6,4},{7,5},{8,10},{9,11},{10,... | collective-permute-start | bytes 159752 | tf_op jit(solution)/shard_map/ppermute | solution.py:511
  28.8 1.4 %collective-permute-done.9 = f32[104,128]{1,0:T(8,128)S(1)} collective-permute-done((f32[104,128]{1,0:T(8,128)S(1)}, f32[104,128]{1,0:T(8,128)S(1)}, u32[]{:S(2)}, u32[]{:S(2)}) %collective-permute-start.9) | collective-permute-done | bytes 53280 | tf_op jit(solution)/shard_map/ppermute | solution.py:511
  30.3 1.0 %transport.23.refs_7_ = f32[16,8192]{1,0:T(8,128)S(1)} custom-call(f32[128,128]{1,0:T(8,128)S(1)} %get-tuple-element.62.stream_ref, f32[128,8192]{1,0:T(8,128)S(1)} %get-tuple-element.84.f_ref), custom_call_target="tpu_custom_call" | custom-call | tf_op jit(solution)/shard_map/transport/pallas_call | solution.py:261
  31.7 1.5 %fluid.2 = (f32[1536,128]{1,0:T(8,128)S(1)}, f32[512,128]{1,0:T(8,128)}) custom-call(f32[832,128]{1,0:T(8,128)S(1)} %pad_maximum_fusion.moments_ref), custom_call_target="tpu_custom_call" | custom-call | tf_op jit(solution)/shard_map/fluid/pallas_call | solution.py:384
  33.2 3.2 %update.1 = (f32[128,8192]{1,0:T(8,128)S(1)}, f32[832,128]{1,0:T(8,128)S(1)}) custom-call(f32[16,8192]{1,0:T(8,128)S(1)} %transport.16.refs_0_, f32[16,8192]{1,0:T(8,128)S(1)} %transport.17.refs_1_, f32[16,8192]{1,0:T(8,128)S(1)} %transport.18.refs_2_, f32[16,8192]{1,0:T(8,128)S(1)} %transport.19.refs_3_, f32[16,8192]{1,0:T(8,128)S(1)} %transport.20.refs_4_, ...), custom_call_target="tpu_custom_call" | custom-call | tf_op jit(solution)/shard_map/update/pallas_call | solution.py:437
  38.1 1.5 %collective-permute-start.12 = (f32[104,128]{1,0:T(8,128)S(1)}, f32[104,128]{1,0:T(8,128)S(1)}, u32[]{:S(2)}, u32[]{:S(2)}) collective-permute-start(f32[104,128]{1,0:T(8,128)S(1)} %get-tuple-element.95), channel_id=1, source_target_pairs={{0,2},{1,3},{2,0},{3,1},{4,6},{5,7},{6,4},{7,5},{8,10},{9,11},{10,... | collective-permute-start | bytes 159752 | tf_op jit(solution)/shard_map/ppermute | solution.py:511
  41.2 1.0 %transport.25.refs_1_ = f32[16,8192]{1,0:T(8,128)S(1)} custom-call(f32[128,128]{1,0:T(8,128)S(1)} %get-tuple-element.62.stream_ref, f32[128,8192]{1,0:T(8,128)S(1)} %get-tuple-element.111.f_ref), custom_call_target="tpu_custom_call" | custom-call | tf_op jit(solution)/shard_map/transport/pallas_call | solution.py:261
  42.5 1.1 %collective-permute-start.13 = (f32[104,128]{1,0:T(8,128)S(1)}, f32[104,128]{1,0:T(8,128)S(1)}, u32[]{:S(2)}, u32[]{:S(2)}) collective-permute-start(f32[104,128]{1,0:T(8,128)S(1)} %add.28.left_ref), channel_id=1, source_target_pairs={{0,4},{1,5},{2,6},{3,7},{4,0},{5,1},{6,2},{7,3},{8,12},{9,13},{10,... | collective-permute-start | bytes 159752 | tf_op jit(solution)/shard_map/ppermute | solution.py:511
  43.7 1.5 %collective-permute-start.16 = (f32[104,128]{1,0:T(8,128)S(1)}, f32[104,128]{1,0:T(8,128)S(1)}, u32[]{:S(2)}, u32[]{:S(2)}) collective-permute-start(f32[104,128]{1,0:T(8,128)S(1)} %add.29.left_ref), channel_id=1, source_target_pairs={{0,4},{1,5},{2,6},{3,7},{4,0},{5,1},{6,2},{7,3},{8,12},{9,13},{10,... | collective-permute-start | bytes 159752 | tf_op jit(solution)/shard_map/ppermute | solution.py:511
  46.8 2.1 %collective-permute-start.15 = (f32[104,128]{1,0:T(8,128)S(1)}, f32[104,128]{1,0:T(8,128)S(1)}, u32[]{:S(2)}, u32[]{:S(2)}) collective-permute-start(f32[104,128]{1,0:T(8,128)S(1)} %add.30.left_ref), channel_id=1, source_target_pairs={{0,8},{1,9},{2,10},{3,11},{4,12},{5,13},{6,14},{7,15},{8,0},{9,1},... | collective-permute-start | bytes 159752 | tf_op jit(solution)/shard_map/ppermute | solution.py:511
  48.9 2.1 %collective-permute-start.18 = (f32[104,128]{1,0:T(8,128)S(1)}, f32[104,128]{1,0:T(8,128)S(1)}, u32[]{:S(2)}, u32[]{:S(2)}) collective-permute-start(f32[104,128]{1,0:T(8,128)S(1)} %add.31.left_ref), channel_id=1, source_target_pairs={{0,8},{1,9},{2,10},{3,11},{4,12},{5,13},{6,14},{7,15},{8,0},{9,1},... | collective-permute-start | bytes 159752 | tf_op jit(solution)/shard_map/ppermute | solution.py:511
  52.0 1.0 %transport.28.refs_4_ = f32[16,8192]{1,0:T(8,128)S(1)} custom-call(f32[128,128]{1,0:T(8,128)S(1)} %get-tuple-element.62.stream_ref, f32[128,8192]{1,0:T(8,128)S(1)} %get-tuple-element.111.f_ref), custom_call_target="tpu_custom_call" | custom-call | tf_op jit(solution)/shard_map/transport/pallas_call | solution.py:261
  54.0 1.7 %collective-permute-start.20 = (f32[104,128]{1,0:T(8,128)S(1)}, f32[104,128]{1,0:T(8,128)S(1)}, u32[]{:S(2)}, u32[]{:S(2)}) collective-permute-start(f32[104,128]{1,0:T(8,128)S(1)} %add.33), channel_id=1, source_target_pairs={{0,2},{1,3},{2,0},{3,1},{4,6},{5,7},{6,4},{7,5},{8,10},{9,11},{10,... | collective-permute-start | bytes 159752 | tf_op jit(solution)/shard_map/ppermute | solution.py:511
  60.9 3.1 %finish.1 = (f32[128,8192]{1,0:T(8,128)}, f32[8,8192]{1,0:T(8,128)}) custom-call(f32[16,8192]{1,0:T(8,128)S(1)} %transport.24.refs_0_, f32[16,8192]{1,0:T(8,128)S(1)} %transport.25.refs_1_, f32[16,8192]{1,0:T(8,128)S(1)} %transport.26.refs_2_, f32[16,8192]{1,0:T(8,128)S(1)} %transport.27.refs_3_, f32[16,8192]{1,0:T(8,128)S(1)} %transport.28.refs_4_, ...), custom_call_target="tpu_custom_call" | custom-call | tf_op jit(solution)/shard_map/finish/pallas_call | solution.py:473
  (72 shorter events, 18.2 us)
Async XLA Ops:
  6.2 1.6 %collective-permute-start = (f32[416,128]{1,0:T(8,128)S(1)}, f32[416,128]{1,0:T(8,128)S(1)}, u32[]{:S(2)}, u32[]{:S(2)}) collective-permute-start(f32[416,128]{1,0:T(8,128)S(1)} %slice_select_fusion.1), channel_id=1, source_target_pairs={{0,1},{1,0},{2,3},{3,2},{4,5},{5,4},{6,7},{7,6},{8,9},{9,8},{10,11... | collective-permute-start | bytes 638984 | tf_op jit(solution)/shard_map/ppermute | solution.py:511
  7.9 5.1 %collective-permute-start.1 = (f32[104,128]{1,0:T(8,128)S(1)}, f32[104,128]{1,0:T(8,128)S(1)}, u32[]{:S(2)}, u32[]{:S(2)}) collective-permute-start(f32[104,128]{1,0:T(8,128)S(1)} %get-tuple-element.68), channel_id=1, source_target_pairs={{0,2},{1,3},{2,0},{3,1},{4,6},{5,7},{6,4},{7,5},{8,10},{9,11},{10,... | collective-permute-start | bytes 159752 | tf_op jit(solution)/shard_map/ppermute | solution.py:511
  10.8 4.5 %collective-permute-start.3 = (f32[104,128]{1,0:T(8,128)S(1)}, f32[104,128]{1,0:T(8,128)S(1)}, u32[]{:S(2)}, u32[]{:S(2)}) collective-permute-start(f32[104,128]{1,0:T(8,128)S(1)} %get-tuple-element.69), channel_id=1, source_target_pairs={{0,2},{1,3},{2,0},{3,1},{4,6},{5,7},{6,4},{7,5},{8,10},{9,11},{10,... | collective-permute-start | bytes 159752 | tf_op jit(solution)/shard_map/ppermute | solution.py:511
  13.0 5.0 %collective-permute-start.2 = (f32[104,128]{1,0:T(8,128)S(1)}, f32[104,128]{1,0:T(8,128)S(1)}, u32[]{:S(2)}, u32[]{:S(2)}) collective-permute-start(f32[104,128]{1,0:T(8,128)S(1)} %add.22.left_ref), channel_id=1, source_target_pairs={{0,4},{1,5},{2,6},{3,7},{4,0},{5,1},{6,2},{7,3},{8,12},{9,13},{10,... | collective-permute-start | bytes 159752 | tf_op jit(solution)/shard_map/ppermute | solution.py:511
  15.4 5.4 %collective-permute-start.5 = (f32[104,128]{1,0:T(8,128)S(1)}, f32[104,128]{1,0:T(8,128)S(1)}, u32[]{:S(2)}, u32[]{:S(2)}) collective-permute-start(f32[104,128]{1,0:T(8,128)S(1)} %add.23.left_ref), channel_id=1, source_target_pairs={{0,4},{1,5},{2,6},{3,7},{4,0},{5,1},{6,2},{7,3},{8,12},{9,13},{10,... | collective-permute-start | bytes 159752 | tf_op jit(solution)/shard_map/ppermute | solution.py:511
  17.9 6.5 %collective-permute-start.4 = (f32[104,128]{1,0:T(8,128)S(1)}, f32[104,128]{1,0:T(8,128)S(1)}, u32[]{:S(2)}, u32[]{:S(2)}) collective-permute-start(f32[104,128]{1,0:T(8,128)S(1)} %add.24.left_ref), channel_id=1, source_target_pairs={{0,8},{1,9},{2,10},{3,11},{4,12},{5,13},{6,14},{7,15},{8,0},{9,1},... | collective-permute-start | bytes 159752 | tf_op jit(solution)/shard_map/ppermute | solution.py:511
  20.8 5.2 %collective-permute-start.7 = (f32[104,128]{1,0:T(8,128)S(1)}, f32[104,128]{1,0:T(8,128)S(1)}, u32[]{:S(2)}, u32[]{:S(2)}) collective-permute-start(f32[104,128]{1,0:T(8,128)S(1)} %add.25.left_ref), channel_id=1, source_target_pairs={{0,8},{1,9},{2,10},{3,11},{4,12},{5,13},{6,14},{7,15},{8,0},{9,1},... | collective-permute-start | bytes 159752 | tf_op jit(solution)/shard_map/ppermute | solution.py:511
  24.5 4.2 %collective-permute-start.6 = (f32[104,128]{1,0:T(8,128)S(1)}, f32[104,128]{1,0:T(8,128)S(1)}, u32[]{:S(2)}, u32[]{:S(2)}) collective-permute-start(f32[104,128]{1,0:T(8,128)S(1)} %add.26), channel_id=1, source_target_pairs={{0,2},{1,3},{2,0},{3,1},{4,6},{5,7},{6,4},{7,5},{8,10},{9,11},{10,... | collective-permute-start | bytes 159752 | tf_op jit(solution)/shard_map/ppermute | solution.py:511
  26.0 4.2 %collective-permute-start.9 = (f32[104,128]{1,0:T(8,128)S(1)}, f32[104,128]{1,0:T(8,128)S(1)}, u32[]{:S(2)}, u32[]{:S(2)}) collective-permute-start(f32[104,128]{1,0:T(8,128)S(1)} %add.27), channel_id=1, source_target_pairs={{0,2},{1,3},{2,0},{3,1},{4,6},{5,7},{6,4},{7,5},{8,10},{9,11},{10,... | collective-permute-start | bytes 159752 | tf_op jit(solution)/shard_map/ppermute | solution.py:511
  28.7 2.6 %collective-permute-start.8 = (f32[208,128]{1,0:T(8,128)S(1)}, f32[208,128]{1,0:T(8,128)S(1)}, u32[]{:S(2)}, u32[]{:S(2)}) collective-permute-start(f32[208,128]{1,0:T(8,128)S(1)} %pad_maximum_fusion.2), channel_id=1, source_target_pairs={{0,1},{1,0},{2,3},{3,2},{4,5},{5,4},{6,7},{7,6},{8,9},{9,8},{10,11... | collective-permute-start | bytes 319496 | tf_op jit(solution)/shard_map/ppermute | solution.py:511
  30.2 1.4 %collective-permute-start.10 = (f32[208,128]{1,0:T(8,128)S(1)}, f32[208,128]{1,0:T(8,128)S(1)}, u32[]{:S(2)}, u32[]{:S(2)}) collective-permute-start(f32[208,128]{1,0:T(8,128)S(1)} %pad_maximum_fusion.3), channel_id=1, source_target_pairs={{0,1},{1,0},{2,3},{3,2},{4,5},{5,4},{6,7},{7,6},{8,9},{9,8},{10,11... | collective-permute-start | bytes 319496 | tf_op jit(solution)/shard_map/ppermute | solution.py:511
  36.5 1.5 %collective-permute-start.11 = (f32[416,128]{1,0:T(8,128)S(1)}, f32[416,128]{1,0:T(8,128)S(1)}, u32[]{:S(2)}, u32[]{:S(2)}) collective-permute-start(f32[416,128]{1,0:T(8,128)S(1)} %slice_select_fusion), channel_id=1, source_target_pairs={{0,1},{1,0},{2,3},{3,2},{4,5},{5,4},{6,7},{7,6},{8,9},{9,8},{10,11... | collective-permute-start | bytes 638984 | tf_op jit(solution)/shard_map/ppermute | solution.py:511
  38.1 4.4 %collective-permute-start.12 = (f32[104,128]{1,0:T(8,128)S(1)}, f32[104,128]{1,0:T(8,128)S(1)}, u32[]{:S(2)}, u32[]{:S(2)}) collective-permute-start(f32[104,128]{1,0:T(8,128)S(1)} %get-tuple-element.95), channel_id=1, source_target_pairs={{0,2},{1,3},{2,0},{3,1},{4,6},{5,7},{6,4},{7,5},{8,10},{9,11},{10,... | collective-permute-start | bytes 159752 | tf_op jit(solution)/shard_map/ppermute | solution.py:511
  39.6 4.1 %collective-permute-start.14 = (f32[104,128]{1,0:T(8,128)S(1)}, f32[104,128]{1,0:T(8,128)S(1)}, u32[]{:S(2)}, u32[]{:S(2)}) collective-permute-start(f32[104,128]{1,0:T(8,128)S(1)} %get-tuple-element.96), channel_id=1, source_target_pairs={{0,2},{1,3},{2,0},{3,1},{4,6},{5,7},{6,4},{7,5},{8,10},{9,11},{10,... | collective-permute-start | bytes 159752 | tf_op jit(solution)/shard_map/ppermute | solution.py:511
  42.5 4.3 %collective-permute-start.13 = (f32[104,128]{1,0:T(8,128)S(1)}, f32[104,128]{1,0:T(8,128)S(1)}, u32[]{:S(2)}, u32[]{:S(2)}) collective-permute-start(f32[104,128]{1,0:T(8,128)S(1)} %add.28.left_ref), channel_id=1, source_target_pairs={{0,4},{1,5},{2,6},{3,7},{4,0},{5,1},{6,2},{7,3},{8,12},{9,13},{10,... | collective-permute-start | bytes 159752 | tf_op jit(solution)/shard_map/ppermute | solution.py:511
  43.7 5.2 %collective-permute-start.16 = (f32[104,128]{1,0:T(8,128)S(1)}, f32[104,128]{1,0:T(8,128)S(1)}, u32[]{:S(2)}, u32[]{:S(2)}) collective-permute-start(f32[104,128]{1,0:T(8,128)S(1)} %add.29.left_ref), channel_id=1, source_target_pairs={{0,4},{1,5},{2,6},{3,7},{4,0},{5,1},{6,2},{7,3},{8,12},{9,13},{10,... | collective-permute-start | bytes 159752 | tf_op jit(solution)/shard_map/ppermute | solution.py:511
  46.8 6.2 %collective-permute-start.15 = (f32[104,128]{1,0:T(8,128)S(1)}, f32[104,128]{1,0:T(8,128)S(1)}, u32[]{:S(2)}, u32[]{:S(2)}) collective-permute-start(f32[104,128]{1,0:T(8,128)S(1)} %add.30.left_ref), channel_id=1, source_target_pairs={{0,8},{1,9},{2,10},{3,11},{4,12},{5,13},{6,14},{7,15},{8,0},{9,1},... | collective-permute-start | bytes 159752 | tf_op jit(solution)/shard_map/ppermute | solution.py:511
  48.9 5.1 %collective-permute-start.18 = (f32[104,128]{1,0:T(8,128)S(1)}, f32[104,128]{1,0:T(8,128)S(1)}, u32[]{:S(2)}, u32[]{:S(2)}) collective-permute-start(f32[104,128]{1,0:T(8,128)S(1)} %add.31.left_ref), channel_id=1, source_target_pairs={{0,8},{1,9},{2,10},{3,11},{4,12},{5,13},{6,14},{7,15},{8,0},{9,1},... | collective-permute-start | bytes 159752 | tf_op jit(solution)/shard_map/ppermute | solution.py:511
  53.1 4.2 %collective-permute-start.17 = (f32[104,128]{1,0:T(8,128)S(1)}, f32[104,128]{1,0:T(8,128)S(1)}, u32[]{:S(2)}, u32[]{:S(2)}) collective-permute-start(f32[104,128]{1,0:T(8,128)S(1)} %add.32), channel_id=1, source_target_pairs={{0,2},{1,3},{2,0},{3,1},{4,6},{5,7},{6,4},{7,5},{8,10},{9,11},{10,... | collective-permute-start | bytes 159752 | tf_op jit(solution)/shard_map/ppermute | solution.py:511
  54.0 4.2 %collective-permute-start.20 = (f32[104,128]{1,0:T(8,128)S(1)}, f32[104,128]{1,0:T(8,128)S(1)}, u32[]{:S(2)}, u32[]{:S(2)}) collective-permute-start(f32[104,128]{1,0:T(8,128)S(1)} %add.33), channel_id=1, source_target_pairs={{0,2},{1,3},{2,0},{3,1},{4,6},{5,7},{6,4},{7,5},{8,10},{9,11},{10,... | collective-permute-start | bytes 159752 | tf_op jit(solution)/shard_map/ppermute | solution.py:511
  58.3 1.7 %collective-permute-start.19 = (f32[208,128]{1,0:T(8,128)S(1)}, f32[208,128]{1,0:T(8,128)S(1)}, u32[]{:S(2)}, u32[]{:S(2)}) collective-permute-start(f32[208,128]{1,0:T(8,128)S(1)} %pad_maximum_fusion.4), channel_id=1, source_target_pairs={{0,1},{1,0},{2,3},{3,2},{4,5},{5,4},{6,7},{7,6},{8,9},{9,8},{10,11... | collective-permute-start | bytes 319496 | tf_op jit(solution)/shard_map/ppermute | solution.py:511
  58.4 1.6 %collective-permute-start.21 = (f32[208,128]{1,0:T(8,128)S(1)}, f32[208,128]{1,0:T(8,128)S(1)}, u32[]{:S(2)}, u32[]{:S(2)}) collective-permute-start(f32[208,128]{1,0:T(8,128)S(1)} %pad_maximum_fusion.5), channel_id=1, source_target_pairs={{0,1},{1,0},{2,3},{3,2},{4,5},{5,4},{6,7},{7,6},{8,9},{9,8},{10,11... | collective-permute-start | bytes 319496 | tf_op jit(solution)/shard_map/ppermute | solution.py:511

commit v5 on v4

--- a/solution.py
+++ b/solution.py
@@ -507,24 +507,36 @@
     return strides[:2], strides[2:]
 
 
-def swap(values, count, stride):
-    return lax.ppermute(values, "vel", [(device, device ^ stride) for device in range(count)])
+def swap(values, count, stride, odd_only=False):
+    pairs = [(device, device ^ stride) for device in range(count) if device & 1 or not odd_only]
+    return lax.ppermute(values, "vel", pairs)
 
 
 def staged_sum(values, count, sides, f, tasks):
     splits, sums = plan(count)
     results, waiting, portions = [], list(tasks), list(BESIDE)
-
-    def exchange(chunks, stride):
-        got = [swap(chunk, count, stride) for chunk in chunks]
+    even = sides[0]
+
+    def beside(sent, got):
         portion = portions.pop(0) if portions else 0
         if portion:
-            _, held = lax.optimization_barrier((chunks[-1], f))
+            _, held = lax.optimization_barrier((sent, f))
             made = [task(held) for task in waiting[:portion]]
             del waiting[:portion]
-            got[0], made = lax.optimization_barrier((got[0], made))
+            got, made = lax.optimization_barrier((got, made))
             results.extend(made)
         return got
+
+    def exchange(chunks, stride):
+        shared, extra = chunks
+        got = swap(shared, count, stride)
+        more = swap(extra, count, stride, odd_only=True)
+        return beside(extra, got), more
+
+    def add(chunks, received):
+        shared = add_call(chunks[0], received[0])
+        shared, more = lax.optimization_barrier((shared, received[1]))
+        return [shared, add_call(chunks[1], more)]
 
     def split(chunks, stride, lower_side):
         kept, sent = [], []
@@ -534,31 +546,41 @@
             kept.append(jnp.where(lower_side, first, second))
             sent.append(jnp.where(lower_side, second, first))
         sent = lax.optimization_barrier(sent)
-        got = exchange(sent, stride)
-        if len(chunks) == 1:
-            return [kept[0] + got[0]]
-        return [add_call(own, other) for own, other in zip(kept, got)]
+        return add(kept, exchange(sent, stride))
 
     def join(chunks, stride, lower_side):
-        out = []
-        for own, got in zip(chunks, exchange(chunks, stride)):
-            lower = jnp.where(lower_side, own, got)
-            upper = jnp.where(lower_side, got, own)
-            out.append((lower, upper))
-        return out
-
-    (block,) = split([values], splits[0], sides[0])
-    half = block.shape[0] // 2
-    chunks = [block[:half], block[half:]]
+        def both(own, got):
+            return jnp.concatenate(
+                [jnp.where(lower_side, own, got), jnp.where(lower_side, got, own)], axis=0
+            )
+
+        got, more = exchange(chunks, stride)
+        shared, more = lax.optimization_barrier((both(chunks[0], got), more))
+        return [shared, both(chunks[1], more)]
+
+    portion = values.shape[0] // SENT
+    evens, odds, extra = values[: 5 * portion], values[5 * portion : 10 * portion], values[10 * portion :]
+    kept, sent = jnp.where(even, evens, odds), jnp.where(even, odds, evens)
+    to_odd = [(device, device + 1) for device in range(0, count, 2)]
+    to_even = [(device + 1, device) for device in range(0, count, 2)]
+    got, more = swap(sent, count, 1), lax.ppermute(extra, "vel", to_odd)
+    chunks = add([kept, extra], [beside(sent, got), more])
     for stride, lower_side in zip(splits[1:], sides[1:]):
         chunks = split(chunks, stride, lower_side)
     for stride in sums:
-        chunks = [add_call(own, got) for own, got in zip(chunks, exchange(chunks, stride))]
+        chunks = add(chunks, exchange(chunks, stride))
     for stride, lower_side in reversed(list(zip(splits[1:], sides[1:]))):
-        chunks = [jnp.concatenate(both, axis=0) for both in join(chunks, stride, lower_side)]
-    lowers, uppers = zip(*join(chunks, splits[0], sides[0]))
+        chunks = join(chunks, stride, lower_side)
+    shared, extra = chunks
+    got, more = swap(shared, count, 1), lax.ppermute(extra, "vel", to_even)
+    got = beside(shared, got)
     results.extend(task(f) for task in waiting)
-    return jnp.concatenate(lowers + uppers, axis=0), results
+    whole = [
+        jnp.where(even, shared, got),
+        jnp.where(even, got, shared),
+        jnp.where(even, more, extra),
+    ]
+    return jnp.concatenate(whole, axis=0), results
 
 
 def on_device(velocities, density, flow, thermal, deviation):

time: 64.3 us -> 79.7 us (1.24)
  starting transfers between devices: 26.8 us -> 34.9 us
  waiting for transfers between devices: 5.49 us -> 12.4 us
    ppermute x22 -> x24, starting transfers between devices: 26.8 us -> 34.9 us  [the longest x20 28.3 us: swap(): return lax.ppermute(values, 'vel', pairs)]
    ppermute x22 -> x24, waiting for transfers between devices: 5.49 us -> 12.4 us  [the longest x20 12.4 us: swap(): return lax.ppermute(values, 'vel', pairs)]
  transfers between devices with their start and end apart: 22 -> 24, of which waited for: 13 -> 7; matrix products, arithmetic and copies ran while one was open for 0% -> 0% of each run, Pallas kernels for 25% -> 20%
where the time goes in v5:
time: 79.7 us; the launch traced here: 79.4 us
  starting transfers between devices  34.9 us (44%)
  Pallas kernels  30.4 us (38%)
  waiting for transfers between devices  12.4 us (16%)
  between operations  1.37 us (2%)
    ppermute x20, starting transfers between devices, swap(): return lax.ppermute(values, 'vel', pairs)  28.3 us
    pallas_call x16, Pallas kernels, transport_call(): pl.pallas_call(functools.partial(transport_kernel, part * rows), out_shap...  16 us
    ppermute x20, waiting for transfers between devices, swap(): return lax.ppermute(values, 'vel', pairs)  12.4 us
    pallas_call x1, Pallas kernels, start_call(): pl.pallas_call(functools.partial(start_kernel, total_count), out_shape=(p...  5.54 us
    ppermute x2, starting transfers between devices, staged_sum(): got, more = (swap(sent, count, 1), lax.ppermute(extra, 'vel', to_odd))  4.03 us
    pallas_call x1, Pallas kernels, update_call(): pl.pallas_call(update_kernel, out_shape=(pltpu.VMEM((rows * PARTS, cells)...  3.23 us
    pallas_call x1, Pallas kernels, finish_call(): pl.pallas_call(finish_kernel, out_shape=(jax.ShapeDtypeStruct((rows * PAR...  3.07 us
    ppermute x2, starting transfers between devices, staged_sum(): got, more = (swap(shared, count, 1), lax.ppermute(extra, 'vel', to_even))  2.58 us
  transfers between devices with their start and end apart: 24, of which 7 were waited for; matrix products, arithmetic and copies ran while one was open for 0% of the time, Pallas kernels for 20%

profile of v5, /device:TPU:0, one launch (start us, length us, event | category | flops | bytes accessed | tf_op | source)
XLA Modules:
  0.0 79.4 jit_solution(10429255286660628599)
XLA Ops:
  0.6 5.5 %start.1 = (f32[128,8192]{1,0:T(8,128)S(1)}, f32[832,128]{1,0:T(8,128)S(1)}, bf16[128,128]{1,0:T(8,128)(2,1)S(1)}, bf16[32,256]{1,0:T(8,128)(2,1)S(1)}, f32[128,128]{1,0:T(8,128)S(1)}) custom-call(f32[3,128]{1,0:T(4,128)} %vel_hbm, f32[1,8192]{1,0:T(1,128)} %bitcast.2, f32[3,8192]{1,0:T(4,128)} %flow_hbm.1, f32[1,8192]{1,0:T(1,128)} %bitcast.3, ...), custom_call_target="tpu_custom_call" | custom-call | tf_op jit(solution)/shard_map/start/pallas_call | solution.py:171
  6.7 2.0 %collective-permute-start.1 = (f32[192,128]{1,0:T(8,128)S(1)}, f32[192,128]{1,0:T(8,128)S(1)}, u32[]{:S(2)}, u32[]{:S(2)}) collective-permute-start(f32[192,128]{1,0:T(8,128)S(1)} %slice.44.left_ref), channel_id=1, source_target_pairs={{0,1},{2,3},{4,5},{6,7},{8,9},{10,11},{12,13},{14,15},{16,17},{18,... | collective-permute-start | bytes 294920 | tf_op jit(solution)/shard_map/ppermute | solution.py:566
  9.8 3.0 %collective-permute-start.2 = (f32[160,128]{1,0:T(8,128)S(1)}, f32[160,128]{1,0:T(8,128)S(1)}, u32[]{:S(2)}, u32[]{:S(2)}) collective-permute-start(f32[160,128]{1,0:T(8,128)S(1)} %get-tuple-element.90), channel_id=1, source_target_pairs={{0,2},{1,3},{2,0},{3,1},{4,6},{5,7},{6,4},{7,5},{8,10},{9,11},{10,... | collective-permute-start | bytes 245768 | tf_op jit(solution)/shard_map/ppermute | solution.py:512
  13.5 1.0 %transport.18.refs_2_ = f32[16,8192]{1,0:T(8,128)S(1)} custom-call(f32[128,128]{1,0:T(8,128)S(1)} %get-tuple-element.82.stream_ref, f32[128,8192]{1,0:T(8,128)S(1)} %get-tuple-element.113.f_ref), custom_call_target="tpu_custom_call" | custom-call | tf_op jit(solution)/shard_map/transport/pallas_call | solution.py:261
  14.5 1.0 %transport.17.refs_1_ = f32[16,8192]{1,0:T(8,128)S(1)} custom-call(f32[128,128]{1,0:T(8,128)S(1)} %get-tuple-element.82.stream_ref, f32[128,8192]{1,0:T(8,128)S(1)} %get-tuple-element.113.f_ref), custom_call_target="tpu_custom_call" | custom-call | tf_op jit(solution)/shard_map/transport/pallas_call | solution.py:261
  15.7 1.9 %collective-permute-start.4 = (f32[160,128]{1,0:T(8,128)S(1)}, f32[160,128]{1,0:T(8,128)S(1)}, u32[]{:S(2)}, u32[]{:S(2)}) collective-permute-start(f32[160,128]{1,0:T(8,128)S(1)} %add.18.left_ref), channel_id=1, source_target_pairs={{0,4},{1,5},{2,6},{3,7},{4,0},{5,1},{6,2},{7,3},{8,12},{9,13},{10,... | collective-permute-start | bytes 245768 | tf_op jit(solution)/shard_map/ppermute | solution.py:512
  20.2 3.1 %collective-permute-start.6 = (f32[160,128]{1,0:T(8,128)S(1)}, f32[160,128]{1,0:T(8,128)S(1)}, u32[]{:S(2)}, u32[]{:S(2)}) collective-permute-start(f32[160,128]{1,0:T(8,128)S(1)} %add.20.left_ref), channel_id=1, source_target_pairs={{0,8},{1,9},{2,10},{3,11},{4,12},{5,13},{6,14},{7,15},{8,0},{9,1},... | collective-permute-start | bytes 245768 | tf_op jit(solution)/shard_map/ppermute | solution.py:512
  24.1 1.0 %transport.21.refs_5_ = f32[16,8192]{1,0:T(8,128)S(1)} custom-call(f32[128,128]{1,0:T(8,128)S(1)} %get-tuple-element.82.stream_ref, f32[128,8192]{1,0:T(8,128)S(1)} %get-tuple-element.113.f_ref), custom_call_target="tpu_custom_call" | custom-call | tf_op jit(solution)/shard_map/transport/pallas_call | solution.py:261
  25.1 1.0 %transport.20.refs_4_ = f32[16,8192]{1,0:T(8,128)S(1)} custom-call(f32[128,128]{1,0:T(8,128)S(1)} %get-tuple-element.82.stream_ref, f32[128,8192]{1,0:T(8,128)S(1)} %get-tuple-element.113.f_ref), custom_call_target="tpu_custom_call" | custom-call | tf_op jit(solution)/shard_map/transport/pallas_call | solution.py:261
  26.1 4.0 %collective-permute-start.8 = (f32[160,128]{1,0:T(8,128)S(1)}, f32[160,128]{1,0:T(8,128)S(1)}, u32[]{:S(2)}, u32[]{:S(2)}) collective-permute-start(f32[160,128]{1,0:T(8,128)S(1)} %add.22), channel_id=1, source_target_pairs={{0,2},{1,3},{2,0},{3,1},{4,6},{5,7},{6,4},{7,5},{8,10},{9,11},{10,... | collective-permute-start | bytes 245768 | tf_op jit(solution)/shard_map/ppermute | solution.py:512
  30.7 1.0 %transport.22.refs_6_ = f32[16,8192]{1,0:T(8,128)S(1)} custom-call(f32[128,128]{1,0:T(8,128)S(1)} %get-tuple-element.82.stream_ref, f32[128,8192]{1,0:T(8,128)S(1)} %get-tuple-element.113.f_ref), custom_call_target="tpu_custom_call" | custom-call | tf_op jit(solution)/shard_map/transport/pallas_call | solution.py:261
  32.6 1.3 %collective-permute-start.11 = (f32[192,128]{1,0:T(8,128)S(1)}, f32[192,128]{1,0:T(8,128)S(1)}, u32[]{:S(2)}, u32[]{:S(2)}) collective-permute-start(f32[192,128]{1,0:T(8,128)S(1)} %pad_maximum_fusion.4), channel_id=1, source_target_pairs={{1,0},{3,2},{5,4},{7,6},{9,8},{11,10},{13,12},{15,14},{17,16},{19,... | collective-permute-start | bytes 294920 | tf_op jit(solution)/shard_map/ppermute | solution.py:575
  33.9 5.2 %collective-permute-start.10 = (f32[320,128]{1,0:T(8,128)S(1)}, f32[320,128]{1,0:T(8,128)S(1)}, u32[]{:S(2)}, u32[]{:S(2)}) collective-permute-start(f32[320,128]{1,0:T(8,128)S(1)} %pad_maximum_fusion.2), channel_id=1, source_target_pairs={{0,1},{1,0},{2,3},{3,2},{4,5},{5,4},{6,7},{7,6},{8,9},{9,8},{10,11... | collective-permute-start | bytes 491528 | tf_op jit(solution)/shard_map/ppermute | solution.py:512
  40.2 1.5 %fluid.2 = (f32[1536,128]{1,0:T(8,128)S(1)}, f32[512,128]{1,0:T(8,128)}) custom-call(f32[832,128]{1,0:T(8,128)S(1)} %pad_maximum_fusion.moments_ref), custom_call_target="tpu_custom_call" | custom-call | tf_op jit(solution)/shard_map/fluid/pallas_call | solution.py:384
  41.7 3.2 %update.1 = (f32[128,8192]{1,0:T(8,128)S(1)}, f32[832,128]{1,0:T(8,128)S(1)}) custom-call(f32[16,8192]{1,0:T(8,128)S(1)} %transport.16.refs_0_, f32[16,8192]{1,0:T(8,128)S(1)} %transport.17.refs_1_, f32[16,8192]{1,0:T(8,128)S(1)} %transport.18.refs_2_, f32[16,8192]{1,0:T(8,128)S(1)} %transport.19.refs_3_, f32[16,8192]{1,0:T(8,128)S(1)} %transport.20.refs_4_, ...), custom_call_target="tpu_custom_call" | custom-call | tf_op jit(solution)/shard_map/update/pallas_call | solution.py:437
  45.4 2.1 %collective-permute-start.13 = (f32[192,128]{1,0:T(8,128)S(1)}, f32[192,128]{1,0:T(8,128)S(1)}, u32[]{:S(2)}, u32[]{:S(2)}) collective-permute-start(f32[192,128]{1,0:T(8,128)S(1)} %slice.51.left_ref), channel_id=1, source_target_pairs={{0,1},{2,3},{4,5},{6,7},{8,9},{10,11},{12,13},{14,15},{16,17},{18,... | collective-permute-start | bytes 294920 | tf_op jit(solution)/shard_map/ppermute | solution.py:566
  48.6 1.1 %collective-permute-start.14 = (f32[160,128]{1,0:T(8,128)S(1)}, f32[160,128]{1,0:T(8,128)S(1)}, u32[]{:S(2)}, u32[]{:S(2)}) collective-permute-start(f32[160,128]{1,0:T(8,128)S(1)} %get-tuple-element.127), channel_id=1, source_target_pairs={{0,2},{1,3},{2,0},{3,1},{4,6},{5,7},{6,4},{7,5},{8,10},{9,11},{10,... | collective-permute-start | bytes 245768 | tf_op jit(solution)/shard_map/ppermute | solution.py:512
  55.3 3.2 %collective-permute-done.16.right_ref = f32[160,128]{1,0:T(8,128)S(1)} collective-permute-done((f32[160,128]{1,0:T(8,128)S(1)}, f32[160,128]{1,0:T(8,128)S(1)}, u32[]{:S(2)}, u32[]{:S(2)}) %collective-permute-start.16) | collective-permute-done | bytes 81952 | tf_op jit(solution)/shard_map/ppermute | solution.py:512
  61.7 4.2 %collective-permute-done.18.right_ref = f32[160,128]{1,0:T(8,128)S(1)} collective-permute-done((f32[160,128]{1,0:T(8,128)S(1)}, f32[160,128]{1,0:T(8,128)S(1)}, u32[]{:S(2)}, u32[]{:S(2)}) %collective-permute-start.18) | collective-permute-done | bytes 81952 | tf_op jit(solution)/shard_map/ppermute | solution.py:512
  65.9 1.2 %collective-permute-start.20 = (f32[160,128]{1,0:T(8,128)S(1)}, f32[160,128]{1,0:T(8,128)S(1)}, u32[]{:S(2)}, u32[]{:S(2)}) collective-permute-start(f32[160,128]{1,0:T(8,128)S(1)} %add.30), channel_id=1, source_target_pairs={{0,2},{1,3},{2,0},{3,1},{4,6},{5,7},{6,4},{7,5},{8,10},{9,11},{10,... | collective-permute-start | bytes 245768 | tf_op jit(solution)/shard_map/ppermute | solution.py:512
  68.8 2.3 %collective-permute-done.20 = f32[160,128]{1,0:T(8,128)S(1)} collective-permute-done((f32[160,128]{1,0:T(8,128)S(1)}, f32[160,128]{1,0:T(8,128)S(1)}, u32[]{:S(2)}, u32[]{:S(2)}) %collective-permute-start.20) | collective-permute-done | bytes 81952 | tf_op jit(solution)/shard_map/ppermute | solution.py:512
  71.2 1.3 %collective-permute-start.23 = (f32[192,128]{1,0:T(8,128)S(1)}, f32[192,128]{1,0:T(8,128)S(1)}, u32[]{:S(2)}, u32[]{:S(2)}) collective-permute-start(f32[192,128]{1,0:T(8,128)S(1)} %pad_maximum_fusion.5), channel_id=1, source_target_pairs={{1,0},{3,2},{5,4},{7,6},{9,8},{11,10},{13,12},{15,14},{17,16},{19,... | collective-permute-start | bytes 294920 | tf_op jit(solution)/shard_map/ppermute | solution.py:575
  72.5 1.7 %collective-permute-start.22 = (f32[320,128]{1,0:T(8,128)S(1)}, f32[320,128]{1,0:T(8,128)S(1)}, u32[]{:S(2)}, u32[]{:S(2)}) collective-permute-start(f32[320,128]{1,0:T(8,128)S(1)} %pad_maximum_fusion.3), channel_id=1, source_target_pairs={{0,1},{1,0},{2,3},{3,2},{4,5},{5,4},{6,7},{7,6},{8,9},{9,8},{10,11... | collective-permute-start | bytes 491528 | tf_op jit(solution)/shard_map/ppermute | solution.py:512
  76.1 3.1 %finish.1 = (f32[128,8192]{1,0:T(8,128)}, f32[8,8192]{1,0:T(8,128)}) custom-call(f32[16,8192]{1,0:T(8,128)S(1)} %transport.24.refs_0_, f32[16,8192]{1,0:T(8,128)S(1)} %transport.25.refs_1_, f32[16,8192]{1,0:T(8,128)S(1)} %transport.26.refs_2_, f32[16,8192]{1,0:T(8,128)S(1)} %transport.27.refs_3_, f32[16,8192]{1,0:T(8,128)S(1)} %transport.28.refs_4_, ...), custom_call_target="tpu_custom_call" | custom-call | tf_op jit(solution)/shard_map/finish/pallas_call | solution.py:473
  (83 shorter events, 22.2 us)
Async XLA Ops:
  6.2 3.5 %collective-permute-start = (f32[320,128]{1,0:T(8,128)S(1)}, f32[320,128]{1,0:T(8,128)S(1)}, u32[]{:S(2)}, u32[]{:S(2)}) collective-permute-start(f32[320,128]{1,0:T(8,128)S(1)} %get-tuple-element.159), channel_id=1, source_target_pairs={{0,1},{1,0},{2,3},{3,2},{4,5},{5,4},{6,7},{7,6},{8,9},{9,8},{10,11... | collective-permute-start | bytes 491528 | tf_op jit(solution)/shard_map/ppermute | solution.py:512
  6.7 3.0 %collective-permute-start.1 = (f32[192,128]{1,0:T(8,128)S(1)}, f32[192,128]{1,0:T(8,128)S(1)}, u32[]{:S(2)}, u32[]{:S(2)}) collective-permute-start(f32[192,128]{1,0:T(8,128)S(1)} %slice.44.left_ref), channel_id=1, source_target_pairs={{0,1},{2,3},{4,5},{6,7},{8,9},{10,11},{12,13},{14,15},{16,17},{18,... | collective-permute-start | bytes 294920 | tf_op jit(solution)/shard_map/ppermute | solution.py:566
  9.8 5.9 %collective-permute-start.2 = (f32[160,128]{1,0:T(8,128)S(1)}, f32[160,128]{1,0:T(8,128)S(1)}, u32[]{:S(2)}, u32[]{:S(2)}) collective-permute-start(f32[160,128]{1,0:T(8,128)S(1)} %get-tuple-element.90), channel_id=1, source_target_pairs={{0,2},{1,3},{2,0},{3,1},{4,6},{5,7},{6,4},{7,5},{8,10},{9,11},{10,... | collective-permute-start | bytes 245768 | tf_op jit(solution)/shard_map/ppermute | solution.py:512
  12.9 2.8 %collective-permute-start.3 = (f32[96,128]{1,0:T(8,128)S(1)}, f32[96,128]{1,0:T(8,128)S(1)}, u32[]{:S(2)}, u32[]{:S(2)}) collective-permute-start(f32[96,128]{1,0:T(8,128)S(1)} %get-tuple-element.91), channel_id=1, source_target_pairs={{1,3},{3,1},{5,7},{7,5},{9,11},{11,9},{13,15},{15,13},{17,19},{19,... | collective-permute-start | bytes 147464 | tf_op jit(solution)/shard_map/ppermute | solution.py:512
  15.7 4.5 %collective-permute-start.4 = (f32[160,128]{1,0:T(8,128)S(1)}, f32[160,128]{1,0:T(8,128)S(1)}, u32[]{:S(2)}, u32[]{:S(2)}) collective-permute-start(f32[160,128]{1,0:T(8,128)S(1)} %add.18.left_ref), channel_id=1, source_target_pairs={{0,4},{1,5},{2,6},{3,7},{4,0},{5,1},{6,2},{7,3},{8,12},{9,13},{10,... | collective-permute-start | bytes 245768 | tf_op jit(solution)/shard_map/ppermute | solution.py:512
  17.6 2.7 %collective-permute-start.5 = (f32[96,128]{1,0:T(8,128)S(1)}, f32[96,128]{1,0:T(8,128)S(1)}, u32[]{:S(2)}, u32[]{:S(2)}) collective-permute-start(f32[96,128]{1,0:T(8,128)S(1)} %add.19.left_ref), channel_id=1, source_target_pairs={{1,5},{3,7},{5,1},{7,3},{9,13},{11,15},{13,9},{15,11},{17,21},{19,... | collective-permute-start | bytes 147464 | tf_op jit(solution)/shard_map/ppermute | solution.py:512
  20.2 5.8 %collective-permute-start.6 = (f32[160,128]{1,0:T(8,128)S(1)}, f32[160,128]{1,0:T(8,128)S(1)}, u32[]{:S(2)}, u32[]{:S(2)}) collective-permute-start(f32[160,128]{1,0:T(8,128)S(1)} %add.20.left_ref), channel_id=1, source_target_pairs={{0,8},{1,9},{2,10},{3,11},{4,12},{5,13},{6,14},{7,15},{8,0},{9,1},... | collective-permute-start | bytes 245768 | tf_op jit(solution)/shard_map/ppermute | solution.py:512
  23.4 2.7 %collective-permute-start.7 = (f32[96,128]{1,0:T(8,128)S(1)}, f32[96,128]{1,0:T(8,128)S(1)}, u32[]{:S(2)}, u32[]{:S(2)}) collective-permute-start(f32[96,128]{1,0:T(8,128)S(1)} %add.21.left_ref), channel_id=1, source_target_pairs={{1,9},{3,11},{5,13},{7,15},{9,1},{11,3},{13,5},{15,7},{17,25},{19,... | collective-permute-start | bytes 147464 | tf_op jit(solution)/shard_map/ppermute | solution.py:512
  26.1 6.4 %collective-permute-start.8 = (f32[160,128]{1,0:T(8,128)S(1)}, f32[160,128]{1,0:T(8,128)S(1)}, u32[]{:S(2)}, u32[]{:S(2)}) collective-permute-start(f32[160,128]{1,0:T(8,128)S(1)} %add.22), channel_id=1, source_target_pairs={{0,2},{1,3},{2,0},{3,1},{4,6},{5,7},{6,4},{7,5},{8,10},{9,11},{10,... | collective-permute-start | bytes 245768 | tf_op jit(solution)/shard_map/ppermute | solution.py:512
  30.1 2.5 %collective-permute-start.9 = (f32[96,128]{1,0:T(8,128)S(1)}, f32[96,128]{1,0:T(8,128)S(1)}, u32[]{:S(2)}, u32[]{:S(2)}) collective-permute-start(f32[96,128]{1,0:T(8,128)S(1)} %add.23), channel_id=1, source_target_pairs={{1,3},{3,1},{5,7},{7,5},{9,11},{11,9},{13,15},{15,13},{17,19},{19,... | collective-permute-start | bytes 147464 | tf_op jit(solution)/shard_map/ppermute | solution.py:512
  32.6 7.5 %collective-permute-start.11 = (f32[192,128]{1,0:T(8,128)S(1)}, f32[192,128]{1,0:T(8,128)S(1)}, u32[]{:S(2)}, u32[]{:S(2)}) collective-permute-start(f32[192,128]{1,0:T(8,128)S(1)} %pad_maximum_fusion.4), channel_id=1, source_target_pairs={{1,0},{3,2},{5,4},{7,6},{9,8},{11,10},{13,12},{15,14},{17,16},{19,... | collective-permute-start | bytes 294920 | tf_op jit(solution)/shard_map/ppermute | solution.py:575
  33.9 6.3 %collective-permute-start.10 = (f32[320,128]{1,0:T(8,128)S(1)}, f32[320,128]{1,0:T(8,128)S(1)}, u32[]{:S(2)}, u32[]{:S(2)}) collective-permute-start(f32[320,128]{1,0:T(8,128)S(1)} %pad_maximum_fusion.2), channel_id=1, source_target_pairs={{0,1},{1,0},{2,3},{3,2},{4,5},{5,4},{6,7},{7,6},{8,9},{9,8},{10,11... | collective-permute-start | bytes 491528 | tf_op jit(solution)/shard_map/ppermute | solution.py:512
  45.0 3.5 %collective-permute-start.12 = (f32[320,128]{1,0:T(8,128)S(1)}, f32[320,128]{1,0:T(8,128)S(1)}, u32[]{:S(2)}, u32[]{:S(2)}) collective-permute-start(f32[320,128]{1,0:T(8,128)S(1)} %get-tuple-element.157), channel_id=1, source_target_pairs={{0,1},{1,0},{2,3},{3,2},{4,5},{5,4},{6,7},{7,6},{8,9},{9,8},{10,11... | collective-permute-start | bytes 491528 | tf_op jit(solution)/shard_map/ppermute | solution.py:512
  45.4 3.1 %collective-permute-start.13 = (f32[192,128]{1,0:T(8,128)S(1)}, f32[192,128]{1,0:T(8,128)S(1)}, u32[]{:S(2)}, u32[]{:S(2)}) collective-permute-start(f32[192,128]{1,0:T(8,128)S(1)} %slice.51.left_ref), channel_id=1, source_target_pairs={{0,1},{2,3},{4,5},{6,7},{8,9},{10,11},{12,13},{14,15},{16,17},{18,... | collective-permute-start | bytes 294920 | tf_op jit(solution)/shard_map/ppermute | solution.py:566
  48.6 4.6 %collective-permute-start.14 = (f32[160,128]{1,0:T(8,128)S(1)}, f32[160,128]{1,0:T(8,128)S(1)}, u32[]{:S(2)}, u32[]{:S(2)}) collective-permute-start(f32[160,128]{1,0:T(8,128)S(1)} %get-tuple-element.127), channel_id=1, source_target_pairs={{0,2},{1,3},{2,0},{3,1},{4,6},{5,7},{6,4},{7,5},{8,10},{9,11},{10,... | collective-permute-start | bytes 245768 | tf_op jit(solution)/shard_map/ppermute | solution.py:512
  49.8 3.5 %collective-permute-start.15 = (f32[96,128]{1,0:T(8,128)S(1)}, f32[96,128]{1,0:T(8,128)S(1)}, u32[]{:S(2)}, u32[]{:S(2)}) collective-permute-start(f32[96,128]{1,0:T(8,128)S(1)} %get-tuple-element.128), channel_id=1, source_target_pairs={{1,3},{3,1},{5,7},{7,5},{9,11},{11,9},{13,15},{15,13},{17,19},{19,... | collective-permute-start | bytes 147464 | tf_op jit(solution)/shard_map/ppermute | solution.py:512
  53.3 5.2 %collective-permute-start.16 = (f32[160,128]{1,0:T(8,128)S(1)}, f32[160,128]{1,0:T(8,128)S(1)}, u32[]{:S(2)}, u32[]{:S(2)}) collective-permute-start(f32[160,128]{1,0:T(8,128)S(1)} %add.26.left_ref), channel_id=1, source_target_pairs={{0,4},{1,5},{2,6},{3,7},{4,0},{5,1},{6,2},{7,3},{8,12},{9,13},{10,... | collective-permute-start | bytes 245768 | tf_op jit(solution)/shard_map/ppermute | solution.py:512
  53.4 5.0 %collective-permute-start.17 = (f32[96,128]{1,0:T(8,128)S(1)}, f32[96,128]{1,0:T(8,128)S(1)}, u32[]{:S(2)}, u32[]{:S(2)}) collective-permute-start(f32[96,128]{1,0:T(8,128)S(1)} %add.27.left_ref), channel_id=1, source_target_pairs={{1,5},{3,7},{5,1},{7,3},{9,13},{11,15},{13,9},{15,11},{17,21},{19,... | collective-permute-start | bytes 147464 | tf_op jit(solution)/shard_map/ppermute | solution.py:512
  58.5 7.4 %collective-permute-start.18 = (f32[160,128]{1,0:T(8,128)S(1)}, f32[160,128]{1,0:T(8,128)S(1)}, u32[]{:S(2)}, u32[]{:S(2)}) collective-permute-start(f32[160,128]{1,0:T(8,128)S(1)} %add.28.left_ref), channel_id=1, source_target_pairs={{0,8},{1,9},{2,10},{3,11},{4,12},{5,13},{6,14},{7,15},{8,0},{9,1},... | collective-permute-start | bytes 245768 | tf_op jit(solution)/shard_map/ppermute | solution.py:512
  59.0 6.9 %collective-permute-start.19 = (f32[96,128]{1,0:T(8,128)S(1)}, f32[96,128]{1,0:T(8,128)S(1)}, u32[]{:S(2)}, u32[]{:S(2)}) collective-permute-start(f32[96,128]{1,0:T(8,128)S(1)} %add.29.left_ref), channel_id=1, source_target_pairs={{1,9},{3,11},{5,13},{7,15},{9,1},{11,3},{13,5},{15,7},{17,25},{19,... | collective-permute-start | bytes 147464 | tf_op jit(solution)/shard_map/ppermute | solution.py:512
  65.9 5.1 %collective-permute-start.20 = (f32[160,128]{1,0:T(8,128)S(1)}, f32[160,128]{1,0:T(8,128)S(1)}, u32[]{:S(2)}, u32[]{:S(2)}) collective-permute-start(f32[160,128]{1,0:T(8,128)S(1)} %add.30), channel_id=1, source_target_pairs={{0,2},{1,3},{2,0},{3,1},{4,6},{5,7},{6,4},{7,5},{8,10},{9,11},{10,... | collective-permute-start | bytes 245768 | tf_op jit(solution)/shard_map/ppermute | solution.py:512
  67.1 4.0 %collective-permute-start.21 = (f32[96,128]{1,0:T(8,128)S(1)}, f32[96,128]{1,0:T(8,128)S(1)}, u32[]{:S(2)}, u32[]{:S(2)}) collective-permute-start(f32[96,128]{1,0:T(8,128)S(1)} %add.31), channel_id=1, source_target_pairs={{1,3},{3,1},{5,7},{7,5},{9,11},{11,9},{13,15},{15,13},{17,19},{19,... | collective-permute-start | bytes 147464 | tf_op jit(solution)/shard_map/ppermute | solution.py:512
  71.2 4.0 %collective-permute-start.23 = (f32[192,128]{1,0:T(8,128)S(1)}, f32[192,128]{1,0:T(8,128)S(1)}, u32[]{:S(2)}, u32[]{:S(2)}) collective-permute-start(f32[192,128]{1,0:T(8,128)S(1)} %pad_maximum_fusion.5), channel_id=1, source_target_pairs={{1,0},{3,2},{5,4},{7,6},{9,8},{11,10},{13,12},{15,14},{17,16},{19,... | collective-permute-start | bytes 294920 | tf_op jit(solution)/shard_map/ppermute | solution.py:575
  72.5 2.7 %collective-permute-start.22 = (f32[320,128]{1,0:T(8,128)S(1)}, f32[320,128]{1,0:T(8,128)S(1)}, u32[]{:S(2)}, u32[]{:S(2)}) collective-permute-start(f32[320,128]{1,0:T(8,128)S(1)} %pad_maximum_fusion.3), channel_id=1, source_target_pairs={{0,1},{1,0},{2,3},{3,2},{4,5},{5,4},{6,7},{7,6},{8,9},{9,8},{10,11... | collective-permute-start | bytes 491528 | tf_op jit(solution)/shard_map/ppermute | solution.py:512

commit v6 on v4

--- a/solution.py
+++ b/solution.py
@@ -106,6 +106,15 @@
         moments_ref[pl.ds(block, SENT, stride=blocks), :] = sums[
             :SENT, part * LANES : (part + 1) * LANES
         ]
+
+
+def in_turn(front, back, tiles):
+    values = front(0)
+    for tile in range(1, tiles):
+        upcoming = front(tile)
+        back(tile - 1, values)
+        values = upcoming
+    back(tiles - 1, values)
 
 
 def start_kernel(
@@ -146,24 +155,26 @@
     stream_ref[...] = jnp.broadcast_to(vel_ref[0:1, :], (LANES, vel_ref.shape[1])).T
     for copy in small[1:]:
         copy.wait()
-    for chunk in range(CHUNKS):
-        copies[chunk].wait()
-
-        def step(local, carry, chunk=chunk):
-            tile = chunk * (width // TILE) + local
-            here = pl.ds(pl.multiple_of(tile * TILE, TILE), TILE)
-            density, flow, thermal = density_ref[:, here], flow_ref[:, here], thermal_ref[:, here]
-            rate = (0.5 * LOG2E) / thermal
-            speed_sq = flow[0:1] * flow[0:1] + flow[1:2] * flow[1:2] + flow[2:3] * flow[2:3]
-            rows = [-rate * speed_sq, 2.0 * rate * flow, -rate, jnp.zeros((11, TILE), jnp.float32)]
-            exponent = dot(basis_ref[...], expand(jnp.concatenate(rows, axis=0)))
-            scale = density / (thermal * jnp.sqrt(thermal))
-            values = jnp.exp2(exponent) * (scale * (1.0 + deviation_ref[:, here]))
-            f_ref[:, here] = values
-            store_moments(moments_ref, table_ref[...], values, tile, cells // LANES)
-            return carry
-
-        lax.fori_loop(0, width // TILE, step, 0, unroll=True)
+    def front(tile):
+        here = pl.ds(tile * TILE, TILE)
+        density, flow, thermal = density_ref[:, here], flow_ref[:, here], thermal_ref[:, here]
+        rate = (0.5 * LOG2E) / thermal
+        speed_sq = flow[0:1] * flow[0:1] + flow[1:2] * flow[1:2] + flow[2:3] * flow[2:3]
+        rows = [-rate * speed_sq, 2.0 * rate * flow, -rate, jnp.zeros((11, TILE), jnp.float32)]
+        exponent = dot(basis, expand(jnp.concatenate(rows, axis=0)))
+        scale = density / (thermal * jnp.sqrt(thermal))
+        return jnp.exp2(exponent) * (scale * (1.0 + deviation_ref[:, here]))
+
+    def back(tile, values):
+        f_ref[:, tile * TILE : (tile + 1) * TILE] = values
+        store_moments(moments_ref, table, values, tile, cells // LANES)
+
+    def front_when_here(tile):
+        if tile * TILE % width == 0:
+            copies[tile * TILE // width].wait()
+        return front(tile)
+
+    in_turn(front_when_here, back, cells // TILE)
 
 
 def start_call(velocities, density, flow, thermal, deviation, total_count):
@@ -268,7 +279,7 @@
     )(near(stream), near(f))
 
 
-def fluid_kernel(moments_ref, coef_ref, macro_ref):
+def fluid_kernel(moments_ref, coef_ref, macro_ref=None):
     blocks = moments_ref.shape[0] // SENT
     m = [moments_ref[row * blocks : (row + 1) * blocks, :] for row in range(13)]
     lane = lax.broadcasted_iota(jnp.int32, (blocks, LANES), 1)
@@ -343,8 +354,9 @@
     u, uu, t = primitives(w)
     n = w[0]
 
-    for row, field in enumerate([n, u[0], u[1], u[2], t, q[0], q[1], q[2]]):
-        macro_ref[pl.ds(row, blocks, stride=8), :] = field
+    if macro_ref is not None:
+        for row, field in enumerate([n, u[0], u[1], u[2], t, q[0], q[1], q[2]]):
+            macro_ref[pl.ds(row, blocks, stride=8), :] = field
 
     inverse = 1.0 / t
     relax = n * power(t, 1.0 - SHEAR_EXPONENT)
@@ -379,19 +391,19 @@
         coef_ref[pl.ds(row, blocks, stride=COEF), :] = field
 
 
-def fluid_call(moments):
+def fluid_call(moments, last):
     blocks = moments.shape[0] // SENT
+    shapes = [pltpu.VMEM((blocks * COEF, LANES), jnp.float32)]
+    if last:
+        shapes.append(pltpu.VMEM((blocks * 8, LANES), jnp.float32))
     return pl.pallas_call(
         fluid_kernel,
-        out_shape=(
-            pltpu.VMEM((blocks * COEF, LANES), jnp.float32),
-            pltpu.VMEM((blocks * 8, LANES), jnp.float32),
-        ),
+        out_shape=shapes,
         in_specs=[WHOLE],
-        out_specs=(WHOLE, WHOLE),
+        out_specs=[WHOLE] * len(shapes),
         compiler_params=params(8),
         name="fluid",
-    )(moments)
+    )(near(moments))
 
 
 def relaxed(g, coef_ref, basis, tile):
@@ -424,12 +436,7 @@
         f_ref[:, tile * TILE : (tile + 1) * TILE] = values
         store_moments(moments_ref, table_ref[...], values, tile, cells // LANES)
 
-    values = front(0)
-    for tile in range(1, cells // TILE):
-        upcoming = front(tile)
-        back(tile - 1, values)
-        values = upcoming
-    back(cells // TILE - 1, values)
+    in_turn(front, back, cells // TILE)
 
 
 def update_call(g, coefficients, basis, table):
@@ -575,10 +582,11 @@
             for part in range(PARTS)
         ]
         summed, g = staged_sum(moments, count, sides, f, tasks)
-        coefficients, macro = fluid_call(summed)
-        if iteration < ITERS - 1:
+        last = iteration == ITERS - 1
+        coefficients, *macro = fluid_call(summed, last)
+        if not last:
             f, moments = update_call(g, coefficients, basis, table)
-    return finish_call(g, coefficients, macro, basis)
+    return finish_call(g, coefficients, macro[0], basis)
 
 
 def solution(mesh):

time: 64.3 us -> 63.5 us (0.988)
  Pallas kernels: 30.3 us -> 29.5 us
    pallas_call x2, Pallas kernels: 2.37 us -> 1.71 us  [fluid_call(): pl.pallas_call(fluid_kernel, out_shape=shapes, in_specs=[WHOLE], out_spec...]
where the time goes in v6:
time: 63.5 us; the launch traced here: 63.3 us
  Pallas kernels  29.5 us (46%)
  starting transfers between devices  26.8 us (42%)
  waiting for transfers between devices  5.5 us (9%)
  between operations  1.18 us (2%)
    ppermute x22, starting transfers between devices, swap(): lax.ppermute(values, 'vel', [(device, device ^ stride) for device in rang...  26.8 us
    pallas_call x16, Pallas kernels, transport_call(): pl.pallas_call(functools.partial(transport_kernel, part * rows), out_shap...  15.9 us
    ppermute x22, waiting for transfers between devices, swap(): lax.ppermute(values, 'vel', [(device, device ^ stride) for device in rang...  5.5 us
    pallas_call x1, Pallas kernels, start_call(): pl.pallas_call(functools.partial(start_kernel, total_count), out_shape=(p...  5.39 us
    pallas_call x1, Pallas kernels, update_call(): pl.pallas_call(update_kernel, out_shape=(pltpu.VMEM((rows * PARTS, cells)...  3.24 us
    pallas_call x1, Pallas kernels, finish_call(): pl.pallas_call(finish_kernel, out_shape=(jax.ShapeDtypeStruct((rows * PAR...  3.06 us
    pallas_call x2, Pallas kernels, fluid_call(): pl.pallas_call(fluid_kernel, out_shape=shapes, in_specs=[WHOLE], out_spec...  1.71 us
  transfers between devices with their start and end apart: 22, of which 13 were waited for; matrix products, arithmetic and copies ran while one was open for 0% of the time, Pallas kernels for 25%

profile of v6, /device:TPU:0, one launch (start us, length us, event | category | flops | bytes accessed | tf_op | source)
XLA Modules:
  0.0 63.3 jit_solution(8363789748299877137)
XLA Ops:
  0.6 5.4 %start.1 = (f32[128,8192]{1,0:T(8,128)S(1)}, f32[832,128]{1,0:T(8,128)S(1)}, bf16[128,128]{1,0:T(8,128)(2,1)S(1)}, bf16[32,256]{1,0:T(8,128)(2,1)S(1)}, f32[128,128]{1,0:T(8,128)S(1)}) custom-call(f32[3,128]{1,0:T(4,128)} %vel_hbm, f32[1,8192]{1,0:T(1,128)} %bitcast.2, f32[3,8192]{1,0:T(4,128)} %flow_hbm.1, f32[1,8192]{1,0:T(1,128)} %bitcast.3, ...), custom_call_target="tpu_custom_call" | custom-call | tf_op jit(solution)/shard_map/start/pallas_call | solution.py:182
  6.6 1.0 %transport.16.refs_0_ = f32[16,8192]{1,0:T(8,128)S(1)} custom-call(f32[128,128]{1,0:T(8,128)S(1)} %get-tuple-element.61.stream_ref, f32[128,8192]{1,0:T(8,128)S(1)} %get-tuple-element.83.f_ref), custom_call_target="tpu_custom_call" | custom-call | tf_op jit(solution)/shard_map/transport/pallas_call | solution.py:272
  7.7 3.0 %collective-permute-start.1 = (f32[104,128]{1,0:T(8,128)S(1)}, f32[104,128]{1,0:T(8,128)S(1)}, u32[]{:S(2)}, u32[]{:S(2)}) collective-permute-start(f32[104,128]{1,0:T(8,128)S(1)} %get-tuple-element.67), channel_id=1, source_target_pairs={{0,2},{1,3},{2,0},{3,1},{4,6},{5,7},{6,4},{7,5},{8,10},{9,11},{10,... | collective-permute-start | bytes 159752 | tf_op jit(solution)/shard_map/ppermute | solution.py:518
  11.8 1.0 %transport.17.refs_1_ = f32[16,8192]{1,0:T(8,128)S(1)} custom-call(f32[128,128]{1,0:T(8,128)S(1)} %get-tuple-element.61.stream_ref, f32[128,8192]{1,0:T(8,128)S(1)} %get-tuple-element.83.f_ref), custom_call_target="tpu_custom_call" | custom-call | tf_op jit(solution)/shard_map/transport/pallas_call | solution.py:272
  12.8 2.4 %collective-permute-start.2 = (f32[104,128]{1,0:T(8,128)S(1)}, f32[104,128]{1,0:T(8,128)S(1)}, u32[]{:S(2)}, u32[]{:S(2)}) collective-permute-start(f32[104,128]{1,0:T(8,128)S(1)} %add.22.left_ref), channel_id=1, source_target_pairs={{0,4},{1,5},{2,6},{3,7},{4,0},{5,1},{6,2},{7,3},{8,12},{9,13},{10,... | collective-permute-start | bytes 159752 | tf_op jit(solution)/shard_map/ppermute | solution.py:518
  15.2 1.3 %collective-permute-start.5 = (f32[104,128]{1,0:T(8,128)S(1)}, f32[104,128]{1,0:T(8,128)S(1)}, u32[]{:S(2)}, u32[]{:S(2)}) collective-permute-start(f32[104,128]{1,0:T(8,128)S(1)} %add.23.left_ref), channel_id=1, source_target_pairs={{0,4},{1,5},{2,6},{3,7},{4,0},{5,1},{6,2},{7,3},{8,12},{9,13},{10,... | collective-permute-start | bytes 159752 | tf_op jit(solution)/shard_map/ppermute | solution.py:518
  16.5 1.0 %transport.19.refs_3_ = f32[16,8192]{1,0:T(8,128)S(1)} custom-call(f32[128,128]{1,0:T(8,128)S(1)} %get-tuple-element.61.stream_ref, f32[128,8192]{1,0:T(8,128)S(1)} %get-tuple-element.83.f_ref), custom_call_target="tpu_custom_call" | custom-call | tf_op jit(solution)/shard_map/transport/pallas_call | solution.py:272
  17.8 2.8 %collective-permute-start.4 = (f32[104,128]{1,0:T(8,128)S(1)}, f32[104,128]{1,0:T(8,128)S(1)}, u32[]{:S(2)}, u32[]{:S(2)}) collective-permute-start(f32[104,128]{1,0:T(8,128)S(1)} %add.24.left_ref), channel_id=1, source_target_pairs={{0,8},{1,9},{2,10},{3,11},{4,12},{5,13},{6,14},{7,15},{8,0},{9,1},... | collective-permute-start | bytes 159752 | tf_op jit(solution)/shard_map/ppermute | solution.py:518
  20.7 1.6 %collective-permute-start.7 = (f32[104,128]{1,0:T(8,128)S(1)}, f32[104,128]{1,0:T(8,128)S(1)}, u32[]{:S(2)}, u32[]{:S(2)}) collective-permute-start(f32[104,128]{1,0:T(8,128)S(1)} %add.25.left_ref), channel_id=1, source_target_pairs={{0,8},{1,9},{2,10},{3,11},{4,12},{5,13},{6,14},{7,15},{8,0},{9,1},... | collective-permute-start | bytes 159752 | tf_op jit(solution)/shard_map/ppermute | solution.py:518
  23.2 1.0 %transport.20.refs_4_ = f32[16,8192]{1,0:T(8,128)S(1)} custom-call(f32[128,128]{1,0:T(8,128)S(1)} %get-tuple-element.61.stream_ref, f32[128,8192]{1,0:T(8,128)S(1)} %get-tuple-element.83.f_ref), custom_call_target="tpu_custom_call" | custom-call | tf_op jit(solution)/shard_map/transport/pallas_call | solution.py:272
  24.3 1.5 %collective-permute-start.6 = (f32[104,128]{1,0:T(8,128)S(1)}, f32[104,128]{1,0:T(8,128)S(1)}, u32[]{:S(2)}, u32[]{:S(2)}) collective-permute-start(f32[104,128]{1,0:T(8,128)S(1)} %add.26), channel_id=1, source_target_pairs={{0,2},{1,3},{2,0},{3,1},{4,6},{5,7},{6,4},{7,5},{8,10},{9,11},{10,... | collective-permute-start | bytes 159752 | tf_op jit(solution)/shard_map/ppermute | solution.py:518
  25.9 1.5 %collective-permute-start.9 = (f32[104,128]{1,0:T(8,128)S(1)}, f32[104,128]{1,0:T(8,128)S(1)}, u32[]{:S(2)}, u32[]{:S(2)}) collective-permute-start(f32[104,128]{1,0:T(8,128)S(1)} %add.27), channel_id=1, source_target_pairs={{0,2},{1,3},{2,0},{3,1},{4,6},{5,7},{6,4},{7,5},{8,10},{9,11},{10,... | collective-permute-start | bytes 159752 | tf_op jit(solution)/shard_map/ppermute | solution.py:518
  28.7 1.4 %collective-permute-done.9 = f32[104,128]{1,0:T(8,128)S(1)} collective-permute-done((f32[104,128]{1,0:T(8,128)S(1)}, f32[104,128]{1,0:T(8,128)S(1)}, u32[]{:S(2)}, u32[]{:S(2)}) %collective-permute-start.9) | collective-permute-done | bytes 53280 | tf_op jit(solution)/shard_map/ppermute | solution.py:518
  30.2 1.0 %transport.23.refs_7_ = f32[16,8192]{1,0:T(8,128)S(1)} custom-call(f32[128,128]{1,0:T(8,128)S(1)} %get-tuple-element.61.stream_ref, f32[128,8192]{1,0:T(8,128)S(1)} %get-tuple-element.83.f_ref), custom_call_target="tpu_custom_call" | custom-call | tf_op jit(solution)/shard_map/transport/pallas_call | solution.py:272
  32.4 3.2 %update.1 = (f32[128,8192]{1,0:T(8,128)S(1)}, f32[832,128]{1,0:T(8,128)S(1)}) custom-call(f32[16,8192]{1,0:T(8,128)S(1)} %transport.16.refs_0_, f32[16,8192]{1,0:T(8,128)S(1)} %transport.17.refs_1_, f32[16,8192]{1,0:T(8,128)S(1)} %transport.18.refs_2_, f32[16,8192]{1,0:T(8,128)S(1)} %transport.19.refs_3_, f32[16,8192]{1,0:T(8,128)S(1)} %transport.20.refs_4_, ...), custom_call_target="tpu_custom_call" | custom-call | tf_op jit(solution)/shard_map/update/pallas_call | solution.py:444
  37.3 1.5 %collective-permute-start.12 = (f32[104,128]{1,0:T(8,128)S(1)}, f32[104,128]{1,0:T(8,128)S(1)}, u32[]{:S(2)}, u32[]{:S(2)}) collective-permute-start(f32[104,128]{1,0:T(8,128)S(1)} %get-tuple-element.93), channel_id=1, source_target_pairs={{0,2},{1,3},{2,0},{3,1},{4,6},{5,7},{6,4},{7,5},{8,10},{9,11},{10,... | collective-permute-start | bytes 159752 | tf_op jit(solution)/shard_map/ppermute | solution.py:518
  40.4 1.0 %transport.25.refs_1_ = f32[16,8192]{1,0:T(8,128)S(1)} custom-call(f32[128,128]{1,0:T(8,128)S(1)} %get-tuple-element.61.stream_ref, f32[128,8192]{1,0:T(8,128)S(1)} %get-tuple-element.109.f_ref), custom_call_target="tpu_custom_call" | custom-call | tf_op jit(solution)/shard_map/transport/pallas_call | solution.py:272
  41.7 1.1 %collective-permute-start.13 = (f32[104,128]{1,0:T(8,128)S(1)}, f32[104,128]{1,0:T(8,128)S(1)}, u32[]{:S(2)}, u32[]{:S(2)}) collective-permute-start(f32[104,128]{1,0:T(8,128)S(1)} %add.28.left_ref), channel_id=1, source_target_pairs={{0,4},{1,5},{2,6},{3,7},{4,0},{5,1},{6,2},{7,3},{8,12},{9,13},{10,... | collective-permute-start | bytes 159752 | tf_op jit(solution)/shard_map/ppermute | solution.py:518
  42.9 1.5 %collective-permute-start.16 = (f32[104,128]{1,0:T(8,128)S(1)}, f32[104,128]{1,0:T(8,128)S(1)}, u32[]{:S(2)}, u32[]{:S(2)}) collective-permute-start(f32[104,128]{1,0:T(8,128)S(1)} %add.29.left_ref), channel_id=1, source_target_pairs={{0,4},{1,5},{2,6},{3,7},{4,0},{5,1},{6,2},{7,3},{8,12},{9,13},{10,... | collective-permute-start | bytes 159752 | tf_op jit(solution)/shard_map/ppermute | solution.py:518
  46.0 2.1 %collective-permute-start.15 = (f32[104,128]{1,0:T(8,128)S(1)}, f32[104,128]{1,0:T(8,128)S(1)}, u32[]{:S(2)}, u32[]{:S(2)}) collective-permute-start(f32[104,128]{1,0:T(8,128)S(1)} %add.30.left_ref), channel_id=1, source_target_pairs={{0,8},{1,9},{2,10},{3,11},{4,12},{5,13},{6,14},{7,15},{8,0},{9,1},... | collective-permute-start | bytes 159752 | tf_op jit(solution)/shard_map/ppermute | solution.py:518
  48.1 2.1 %collective-permute-start.18 = (f32[104,128]{1,0:T(8,128)S(1)}, f32[104,128]{1,0:T(8,128)S(1)}, u32[]{:S(2)}, u32[]{:S(2)}) collective-permute-start(f32[104,128]{1,0:T(8,128)S(1)} %add.31.left_ref), channel_id=1, source_target_pairs={{0,8},{1,9},{2,10},{3,11},{4,12},{5,13},{6,14},{7,15},{8,0},{9,1},... | collective-permute-start | bytes 159752 | tf_op jit(solution)/shard_map/ppermute | solution.py:518
  51.2 1.0 %transport.28.refs_4_ = f32[16,8192]{1,0:T(8,128)S(1)} custom-call(f32[128,128]{1,0:T(8,128)S(1)} %get-tuple-element.61.stream_ref, f32[128,8192]{1,0:T(8,128)S(1)} %get-tuple-element.109.f_ref), custom_call_target="tpu_custom_call" | custom-call | tf_op jit(solution)/shard_map/transport/pallas_call | solution.py:272
  53.2 1.7 %collective-permute-start.20 = (f32[104,128]{1,0:T(8,128)S(1)}, f32[104,128]{1,0:T(8,128)S(1)}, u32[]{:S(2)}, u32[]{:S(2)}) collective-permute-start(f32[104,128]{1,0:T(8,128)S(1)} %add.33), channel_id=1, source_target_pairs={{0,2},{1,3},{2,0},{3,1},{4,6},{5,7},{6,4},{7,5},{8,10},{9,11},{10,... | collective-permute-start | bytes 159752 | tf_op jit(solution)/shard_map/ppermute | solution.py:518
  60.1 3.1 %finish.1 = (f32[128,8192]{1,0:T(8,128)}, f32[8,8192]{1,0:T(8,128)}) custom-call(f32[16,8192]{1,0:T(8,128)S(1)} %transport.24.refs_0_, f32[16,8192]{1,0:T(8,128)S(1)} %transport.25.refs_1_, f32[16,8192]{1,0:T(8,128)S(1)} %transport.26.refs_2_, f32[16,8192]{1,0:T(8,128)S(1)} %transport.27.refs_3_, f32[16,8192]{1,0:T(8,128)S(1)} %transport.28.refs_4_, ...), custom_call_target="tpu_custom_call" | custom-call | tf_op jit(solution)/shard_map/finish/pallas_call | solution.py:480
  (72 shorter events, 18.0 us)
Async XLA Ops:
  6.1 1.6 %collective-permute-start = (f32[416,128]{1,0:T(8,128)S(1)}, f32[416,128]{1,0:T(8,128)S(1)}, u32[]{:S(2)}, u32[]{:S(2)}) collective-permute-start(f32[416,128]{1,0:T(8,128)S(1)} %slice_select_fusion.1), channel_id=1, source_target_pairs={{0,1},{1,0},{2,3},{3,2},{4,5},{5,4},{6,7},{7,6},{8,9},{9,8},{10,11... | collective-permute-start | bytes 638984 | tf_op jit(solution)/shard_map/ppermute | solution.py:518
  7.7 5.1 %collective-permute-start.1 = (f32[104,128]{1,0:T(8,128)S(1)}, f32[104,128]{1,0:T(8,128)S(1)}, u32[]{:S(2)}, u32[]{:S(2)}) collective-permute-start(f32[104,128]{1,0:T(8,128)S(1)} %get-tuple-element.67), channel_id=1, source_target_pairs={{0,2},{1,3},{2,0},{3,1},{4,6},{5,7},{6,4},{7,5},{8,10},{9,11},{10,... | collective-permute-start | bytes 159752 | tf_op jit(solution)/shard_map/ppermute | solution.py:518
  10.7 4.5 %collective-permute-start.3 = (f32[104,128]{1,0:T(8,128)S(1)}, f32[104,128]{1,0:T(8,128)S(1)}, u32[]{:S(2)}, u32[]{:S(2)}) collective-permute-start(f32[104,128]{1,0:T(8,128)S(1)} %get-tuple-element.68), channel_id=1, source_target_pairs={{0,2},{1,3},{2,0},{3,1},{4,6},{5,7},{6,4},{7,5},{8,10},{9,11},{10,... | collective-permute-start | bytes 159752 | tf_op jit(solution)/shard_map/ppermute | solution.py:518
  12.8 5.0 %collective-permute-start.2 = (f32[104,128]{1,0:T(8,128)S(1)}, f32[104,128]{1,0:T(8,128)S(1)}, u32[]{:S(2)}, u32[]{:S(2)}) collective-permute-start(f32[104,128]{1,0:T(8,128)S(1)} %add.22.left_ref), channel_id=1, source_target_pairs={{0,4},{1,5},{2,6},{3,7},{4,0},{5,1},{6,2},{7,3},{8,12},{9,13},{10,... | collective-permute-start | bytes 159752 | tf_op jit(solution)/shard_map/ppermute | solution.py:518
  15.2 5.4 %collective-permute-start.5 = (f32[104,128]{1,0:T(8,128)S(1)}, f32[104,128]{1,0:T(8,128)S(1)}, u32[]{:S(2)}, u32[]{:S(2)}) collective-permute-start(f32[104,128]{1,0:T(8,128)S(1)} %add.23.left_ref), channel_id=1, source_target_pairs={{0,4},{1,5},{2,6},{3,7},{4,0},{5,1},{6,2},{7,3},{8,12},{9,13},{10,... | collective-permute-start | bytes 159752 | tf_op jit(solution)/shard_map/ppermute | solution.py:518
  17.8 6.5 %collective-permute-start.4 = (f32[104,128]{1,0:T(8,128)S(1)}, f32[104,128]{1,0:T(8,128)S(1)}, u32[]{:S(2)}, u32[]{:S(2)}) collective-permute-start(f32[104,128]{1,0:T(8,128)S(1)} %add.24.left_ref), channel_id=1, source_target_pairs={{0,8},{1,9},{2,10},{3,11},{4,12},{5,13},{6,14},{7,15},{8,0},{9,1},... | collective-permute-start | bytes 159752 | tf_op jit(solution)/shard_map/ppermute | solution.py:518
  20.7 5.2 %collective-permute-start.7 = (f32[104,128]{1,0:T(8,128)S(1)}, f32[104,128]{1,0:T(8,128)S(1)}, u32[]{:S(2)}, u32[]{:S(2)}) collective-permute-start(f32[104,128]{1,0:T(8,128)S(1)} %add.25.left_ref), channel_id=1, source_target_pairs={{0,8},{1,9},{2,10},{3,11},{4,12},{5,13},{6,14},{7,15},{8,0},{9,1},... | collective-permute-start | bytes 159752 | tf_op jit(solution)/shard_map/ppermute | solution.py:518
  24.3 4.2 %collective-permute-start.6 = (f32[104,128]{1,0:T(8,128)S(1)}, f32[104,128]{1,0:T(8,128)S(1)}, u32[]{:S(2)}, u32[]{:S(2)}) collective-permute-start(f32[104,128]{1,0:T(8,128)S(1)} %add.26), channel_id=1, source_target_pairs={{0,2},{1,3},{2,0},{3,1},{4,6},{5,7},{6,4},{7,5},{8,10},{9,11},{10,... | collective-permute-start | bytes 159752 | tf_op jit(solution)/shard_map/ppermute | solution.py:518
  25.9 4.2 %collective-permute-start.9 = (f32[104,128]{1,0:T(8,128)S(1)}, f32[104,128]{1,0:T(8,128)S(1)}, u32[]{:S(2)}, u32[]{:S(2)}) collective-permute-start(f32[104,128]{1,0:T(8,128)S(1)} %add.27), channel_id=1, source_target_pairs={{0,2},{1,3},{2,0},{3,1},{4,6},{5,7},{6,4},{7,5},{8,10},{9,11},{10,... | collective-permute-start | bytes 159752 | tf_op jit(solution)/shard_map/ppermute | solution.py:518
  28.6 2.6 %collective-permute-start.8 = (f32[208,128]{1,0:T(8,128)S(1)}, f32[208,128]{1,0:T(8,128)S(1)}, u32[]{:S(2)}, u32[]{:S(2)}) collective-permute-start(f32[208,128]{1,0:T(8,128)S(1)} %pad_maximum_fusion.2), channel_id=1, source_target_pairs={{0,1},{1,0},{2,3},{3,2},{4,5},{5,4},{6,7},{7,6},{8,9},{9,8},{10,11... | collective-permute-start | bytes 319496 | tf_op jit(solution)/shard_map/ppermute | solution.py:518
  30.1 1.4 %collective-permute-start.10 = (f32[208,128]{1,0:T(8,128)S(1)}, f32[208,128]{1,0:T(8,128)S(1)}, u32[]{:S(2)}, u32[]{:S(2)}) collective-permute-start(f32[208,128]{1,0:T(8,128)S(1)} %pad_maximum_fusion.3), channel_id=1, source_target_pairs={{0,1},{1,0},{2,3},{3,2},{4,5},{5,4},{6,7},{7,6},{8,9},{9,8},{10,11... | collective-permute-start | bytes 319496 | tf_op jit(solution)/shard_map/ppermute | solution.py:518
  35.7 1.5 %collective-permute-start.11 = (f32[416,128]{1,0:T(8,128)S(1)}, f32[416,128]{1,0:T(8,128)S(1)}, u32[]{:S(2)}, u32[]{:S(2)}) collective-permute-start(f32[416,128]{1,0:T(8,128)S(1)} %slice_select_fusion), channel_id=1, source_target_pairs={{0,1},{1,0},{2,3},{3,2},{4,5},{5,4},{6,7},{7,6},{8,9},{9,8},{10,11... | collective-permute-start | bytes 638984 | tf_op jit(solution)/shard_map/ppermute | solution.py:518
  37.3 4.4 %collective-permute-start.12 = (f32[104,128]{1,0:T(8,128)S(1)}, f32[104,128]{1,0:T(8,128)S(1)}, u32[]{:S(2)}, u32[]{:S(2)}) collective-permute-start(f32[104,128]{1,0:T(8,128)S(1)} %get-tuple-element.93), channel_id=1, source_target_pairs={{0,2},{1,3},{2,0},{3,1},{4,6},{5,7},{6,4},{7,5},{8,10},{9,11},{10,... | collective-permute-start | bytes 159752 | tf_op jit(solution)/shard_map/ppermute | solution.py:518
  38.8 4.1 %collective-permute-start.14 = (f32[104,128]{1,0:T(8,128)S(1)}, f32[104,128]{1,0:T(8,128)S(1)}, u32[]{:S(2)}, u32[]{:S(2)}) collective-permute-start(f32[104,128]{1,0:T(8,128)S(1)} %get-tuple-element.94), channel_id=1, source_target_pairs={{0,2},{1,3},{2,0},{3,1},{4,6},{5,7},{6,4},{7,5},{8,10},{9,11},{10,... | collective-permute-start | bytes 159752 | tf_op jit(solution)/shard_map/ppermute | solution.py:518
  41.7 4.3 %collective-permute-start.13 = (f32[104,128]{1,0:T(8,128)S(1)}, f32[104,128]{1,0:T(8,128)S(1)}, u32[]{:S(2)}, u32[]{:S(2)}) collective-permute-start(f32[104,128]{1,0:T(8,128)S(1)} %add.28.left_ref), channel_id=1, source_target_pairs={{0,4},{1,5},{2,6},{3,7},{4,0},{5,1},{6,2},{7,3},{8,12},{9,13},{10,... | collective-permute-start | bytes 159752 | tf_op jit(solution)/shard_map/ppermute | solution.py:518
  42.9 5.2 %collective-permute-start.16 = (f32[104,128]{1,0:T(8,128)S(1)}, f32[104,128]{1,0:T(8,128)S(1)}, u32[]{:S(2)}, u32[]{:S(2)}) collective-permute-start(f32[104,128]{1,0:T(8,128)S(1)} %add.29.left_ref), channel_id=1, source_target_pairs={{0,4},{1,5},{2,6},{3,7},{4,0},{5,1},{6,2},{7,3},{8,12},{9,13},{10,... | collective-permute-start | bytes 159752 | tf_op jit(solution)/shard_map/ppermute | solution.py:518
  46.0 6.2 %collective-permute-start.15 = (f32[104,128]{1,0:T(8,128)S(1)}, f32[104,128]{1,0:T(8,128)S(1)}, u32[]{:S(2)}, u32[]{:S(2)}) collective-permute-start(f32[104,128]{1,0:T(8,128)S(1)} %add.30.left_ref), channel_id=1, source_target_pairs={{0,8},{1,9},{2,10},{3,11},{4,12},{5,13},{6,14},{7,15},{8,0},{9,1},... | collective-permute-start | bytes 159752 | tf_op jit(solution)/shard_map/ppermute | solution.py:518
  48.1 5.1 %collective-permute-start.18 = (f32[104,128]{1,0:T(8,128)S(1)}, f32[104,128]{1,0:T(8,128)S(1)}, u32[]{:S(2)}, u32[]{:S(2)}) collective-permute-start(f32[104,128]{1,0:T(8,128)S(1)} %add.31.left_ref), channel_id=1, source_target_pairs={{0,8},{1,9},{2,10},{3,11},{4,12},{5,13},{6,14},{7,15},{8,0},{9,1},... | collective-permute-start | bytes 159752 | tf_op jit(solution)/shard_map/ppermute | solution.py:518
  52.3 4.2 %collective-permute-start.17 = (f32[104,128]{1,0:T(8,128)S(1)}, f32[104,128]{1,0:T(8,128)S(1)}, u32[]{:S(2)}, u32[]{:S(2)}) collective-permute-start(f32[104,128]{1,0:T(8,128)S(1)} %add.32), channel_id=1, source_target_pairs={{0,2},{1,3},{2,0},{3,1},{4,6},{5,7},{6,4},{7,5},{8,10},{9,11},{10,... | collective-permute-start | bytes 159752 | tf_op jit(solution)/shard_map/ppermute | solution.py:518
  53.2 4.2 %collective-permute-start.20 = (f32[104,128]{1,0:T(8,128)S(1)}, f32[104,128]{1,0:T(8,128)S(1)}, u32[]{:S(2)}, u32[]{:S(2)}) collective-permute-start(f32[104,128]{1,0:T(8,128)S(1)} %add.33), channel_id=1, source_target_pairs={{0,2},{1,3},{2,0},{3,1},{4,6},{5,7},{6,4},{7,5},{8,10},{9,11},{10,... | collective-permute-start | bytes 159752 | tf_op jit(solution)/shard_map/ppermute | solution.py:518
  57.5 1.7 %collective-permute-start.19 = (f32[208,128]{1,0:T(8,128)S(1)}, f32[208,128]{1,0:T(8,128)S(1)}, u32[]{:S(2)}, u32[]{:S(2)}) collective-permute-start(f32[208,128]{1,0:T(8,128)S(1)} %pad_maximum_fusion.4), channel_id=1, source_target_pairs={{0,1},{1,0},{2,3},{3,2},{4,5},{5,4},{6,7},{7,6},{8,9},{9,8},{10,11... | collective-permute-start | bytes 319496 | tf_op jit(solution)/shard_map/ppermute | solution.py:518
  57.6 1.6 %collective-permute-start.21 = (f32[208,128]{1,0:T(8,128)S(1)}, f32[208,128]{1,0:T(8,128)S(1)}, u32[]{:S(2)}, u32[]{:S(2)}) collective-permute-start(f32[208,128]{1,0:T(8,128)S(1)} %pad_maximum_fusion.5), channel_id=1, source_target_pairs={{0,1},{1,0},{2,3},{3,2},{4,5},{5,4},{6,7},{7,6},{8,9},{9,8},{10,11... | collective-permute-start | bytes 319496 | tf_op jit(solution)/shard_map/ppermute | solution.py:518

commit v7 on v6

--- a/solution.py
+++ b/solution.py
@@ -64,15 +64,20 @@
     return jnp.concatenate(rows, axis=0), sq
 
 
+def parts_of(values):
+    high = rounded(values)
+    middle = rounded(values - high)
+    return high, middle, values - high - middle
+
+
 def make_tables(velocities, total_count):
     phi, sq = phi_rows(velocities)
-    high = rounded(phi)
-    middle = rounded(phi - high)
-    low = phi - high - middle
-    stacked = jnp.concatenate(
-        [high, high, high, middle, middle, low, jnp.zeros((32, phi.shape[1]), jnp.float32)], axis=0
-    )
-    basis = stacked.T.astype(jnp.bfloat16)
+    high, middle, low = parts_of(phi)
+    three = [high[:8], high[:8], high[:8], middle[:8], middle[:8], low[:8]]
+    wide = jnp.zeros((128 - 6 * 8, phi.shape[1]), jnp.float32)
+    exponent = jnp.concatenate(three + [wide], axis=0).T[:, : 6 * 8].astype(jnp.bfloat16)
+    two = [high, high, middle]
+    polynomial = jnp.concatenate(two + [wide], axis=0).T[:, : 3 * BASIS].astype(jnp.bfloat16)
     weighted = phi * (SPREAD_SCALE**3 * jnp.exp(sq / (2.0 * SPREAD_SCALE**2)) / total_count)
     top = rounded(weighted)
     rest = weighted - top
@@ -83,16 +88,18 @@
         ],
         axis=0,
     ).astype(jnp.bfloat16)
-    return basis, moments
-
-
-def expand(coefficients):
-    high = coefficients.astype(jnp.bfloat16)
-    rest = coefficients - high.astype(jnp.float32)
-    middle = rest.astype(jnp.bfloat16)
-    low = (rest - middle.astype(jnp.float32)).astype(jnp.bfloat16)
-    zero = jnp.zeros((32, coefficients.shape[1]), jnp.bfloat16)
-    return jnp.concatenate([high, middle, low, high, middle, high, zero], axis=0)
+    return exponent, polynomial, moments
+
+
+def expand_exponent(rows):
+    high, middle, low = parts_of(rows)
+    return jnp.concatenate([high, middle, low, high, middle, high], axis=0).astype(jnp.bfloat16)
+
+
+def expand_polynomial(rows):
+    high = rows.astype(jnp.bfloat16)
+    middle = (rows - high.astype(jnp.float32)).astype(jnp.bfloat16)
+    return jnp.concatenate([high, middle, high], axis=0)
 
 
 def store_moments(moments_ref, table, values, tile, blocks):
@@ -120,7 +127,7 @@
 def start_kernel(
     total_count,
     vel_hbm, density_hbm, flow_hbm, thermal_hbm, deviation_hbm,
-    f_ref, moments_ref, basis_ref, table_ref, stream_ref,
+    f_ref, moments_ref, exponent_ref, polynomial_ref, table_ref, stream_ref,
     vel_ref, density_ref, flow_ref, thermal_ref, deviation_ref, small_sems, sems,
 ):
     cells = f_ref.shape[1]
@@ -149,8 +156,9 @@
     for copy in copies:
         copy.start()
     small[0].wait()
-    basis, table = make_tables(vel_ref[...], total_count)
-    basis_ref[...] = basis
+    exponent_table, polynomial_table, table = make_tables(vel_ref[...], total_count)
+    exponent_ref[...] = exponent_table
+    polynomial_ref[...] = polynomial_table
     table_ref[...] = table
     stream_ref[...] = jnp.broadcast_to(vel_ref[0:1, :], (LANES, vel_ref.shape[1])).T
     for copy in small[1:]:
@@ -160,8 +168,8 @@
         density, flow, thermal = density_ref[:, here], flow_ref[:, here], thermal_ref[:, here]
         rate = (0.5 * LOG2E) / thermal
         speed_sq = flow[0:1] * flow[0:1] + flow[1:2] * flow[1:2] + flow[2:3] * flow[2:3]
-        rows = [-rate * speed_sq, 2.0 * rate * flow, -rate, jnp.zeros((11, TILE), jnp.float32)]
-        exponent = dot(basis, expand(jnp.concatenate(rows, axis=0)))
+        rows = [-rate * speed_sq, 2.0 * rate * flow, -rate, jnp.zeros((3, TILE), jnp.float32)]
+        exponent = dot(exponent_table, expand_exponent(jnp.concatenate(rows, axis=0)))
         scale = density / (thermal * jnp.sqrt(thermal))
         return jnp.exp2(exponent) * (scale * (1.0 + deviation_ref[:, here]))
 
@@ -184,12 +192,13 @@
         out_shape=(
             pltpu.VMEM((local, cells), jnp.float32),
             pltpu.VMEM((SENT * cells // LANES, LANES), jnp.float32),
-            pltpu.VMEM((local, 128), jnp.bfloat16),
+            pltpu.VMEM((local, 6 * 8), jnp.bfloat16),
+            pltpu.VMEM((local, 3 * BASIS), jnp.bfloat16),
             pltpu.VMEM((2 * BASIS, 2 * local), jnp.bfloat16),
             pltpu.VMEM((local, LANES), jnp.float32),
         ),
         in_specs=[OUTSIDE] * 5,
-        out_specs=(WHOLE,) * 5,
+        out_specs=(WHOLE,) * 6,
         scratch_shapes=[
             pltpu.VMEM((3, local), jnp.float32),
             pltpu.VMEM((1, cells), jnp.float32),
@@ -406,16 +415,15 @@
     )(near(moments))
 
 
-def relaxed(g, coef_ref, basis, tile):
+def relaxed(g, coef_ref, exponent_ref, polynomial_ref, tile):
     per_tile = TILE // LANES
     parts = [
         coef_ref[pl.ds((tile * per_tile + part) * COEF, COEF), :]
         for part in range(per_tile)
     ]
     coefficients = jnp.concatenate(parts, axis=1)
-    polynomial = dot(basis, expand(coefficients[:BASIS]))
-    rows = jnp.concatenate([coefficients[BASIS:], jnp.zeros((8, TILE), jnp.float32)], axis=0)
-    exponent = dot(basis, expand(rows))
+    polynomial = dot(polynomial_ref[...], expand_polynomial(coefficients[:BASIS]))
+    exponent = dot(exponent_ref[...], expand_exponent(coefficients[BASIS:]))
     return g * coefficients[DAMP : DAMP + 1] + jnp.exp2(exponent) * polynomial
 
 
@@ -425,12 +433,12 @@
 
 def update_kernel(*refs):
     g_refs = refs[:PARTS]
-    coef_ref, basis_ref, table_ref, f_ref, moments_ref = refs[PARTS:]
+    coef_ref, exponent_ref, polynomial_ref, table_ref, f_ref, moments_ref = refs[PARTS:]
     cells = f_ref.shape[1]
 
     def front(tile):
         here = pl.ds(tile * TILE, TILE)
-        return relaxed(gathered(g_refs, here), coef_ref, basis_ref[...], tile)
+        return relaxed(gathered(g_refs, here), coef_ref, exponent_ref, polynomial_ref, tile)
 
     def back(tile, values):
         f_ref[:, tile * TILE : (tile + 1) * TILE] = values
@@ -439,7 +447,7 @@
     in_turn(front, back, cells // TILE)
 
 
-def update_call(g, coefficients, basis, table):
+def update_call(g, coefficients, tables, table):
     rows, cells = g[0].shape
     return pl.pallas_call(
         update_kernel,
@@ -447,16 +455,16 @@
             pltpu.VMEM((rows * PARTS, cells), jnp.float32),
             pltpu.VMEM((SENT * cells // LANES, LANES), jnp.float32),
         ),
-        in_specs=[WHOLE] * (PARTS + 3),
+        in_specs=[WHOLE] * (PARTS + 4),
         out_specs=(WHOLE, WHOLE),
         compiler_params=params(8),
         name="update",
-    )(*[near(part) for part in g], near(coefficients), near(basis), near(table))
+    )(*map(near, g), near(coefficients), *map(near, tables), near(table))
 
 
 def finish_kernel(*refs):
     g_refs = refs[:PARTS]
-    coef_ref, macro_ref, basis_ref, f_ref, fields_ref, held, sems = refs[PARTS:]
+    coef_ref, macro_ref, exponent_ref, polynomial_ref, f_ref, fields_ref, held, sems = refs[PARTS:]
     cells = held.shape[1]
     width = cells // CHUNKS
     copies = []
@@ -464,7 +472,7 @@
         for local in range(width // TILE):
             tile = chunk * (width // TILE) + local
             here = pl.ds(tile * TILE, TILE)
-            held[:, here] = relaxed(gathered(g_refs, here), coef_ref, basis_ref[...], tile)
+            held[:, here] = relaxed(gathered(g_refs, here), coef_ref, exponent_ref, polynomial_ref, tile)
             for block in range(tile * TILE // LANES, (tile + 1) * TILE // LANES):
                 fields_ref[:, pl.ds(block * LANES, LANES)] = macro_ref[pl.ds(block * 8, 8), :]
         there = pl.ds(chunk * width, width)
@@ -475,7 +483,7 @@
         copy.wait()
 
 
-def finish_call(g, coefficients, macro, basis):
+def finish_call(g, coefficients, macro, tables):
     rows, cells = g[0].shape
     return pl.pallas_call(
         finish_kernel,
@@ -483,7 +491,7 @@
             jax.ShapeDtypeStruct((rows * PARTS, cells), jnp.float32),
             jax.ShapeDtypeStruct((8, cells), jnp.float32),
         ),
-        in_specs=[WHOLE] * (PARTS + 3),
+        in_specs=[WHOLE] * (PARTS + 4),
         out_specs=(OUTSIDE, WHOLE),
         scratch_shapes=[
             pltpu.VMEM((rows * PARTS, cells), jnp.float32),
@@ -491,7 +499,7 @@
         ],
         compiler_params=params(16),
         name="finish",
-    )(*[near(part) for part in g], near(coefficients), near(macro), near(basis))
+    )(*map(near, g), near(coefficients), near(macro), *map(near, tables))
 
 
 def add_kernel(left_ref, right_ref, out_ref):
@@ -573,7 +581,7 @@
     place = lax.axis_index("vel")
     sides = [place & stride == 0 for stride in plan(count)[0]]
     velocities, sides = lax.optimization_barrier((velocities, sides))
-    f, moments, basis, table, stream = start_call(
+    f, moments, *tables, table, stream = start_call(
         velocities, density, flow, thermal, deviation, velocities.shape[1] * count
     )
     for iteration in range(ITERS):
@@ -585,8 +593,8 @@
         last = iteration == ITERS - 1
         coefficients, *macro = fluid_call(summed, last)
         if not last:
-            f, moments = update_call(g, coefficients, basis, table)
-    return finish_call(g, coefficients, macro[0], basis)
+            f, moments = update_call(g, coefficients, tables, table)
+    return finish_call(g, coefficients, macro[0], tables)
 
 
 def solution(mesh):

time: 63.5 us -> 63.4 us (level)
  no operation moved by 1% of the time
where the time goes in v7:
time: 63.4 us; the launch traced here: 63.3 us
  Pallas kernels  29.4 us (46%)
  starting transfers between devices  26.8 us (42%)
  waiting for transfers between devices  5.5 us (9%)
  between operations  1.18 us (2%)
    ppermute x22, starting transfers between devices, swap(): lax.ppermute(values, 'vel', [(device, device ^ stride) for device in rang...  26.8 us
    pallas_call x16, Pallas kernels, transport_call(): pl.pallas_call(functools.partial(transport_kernel, part * rows), out_shap...  15.9 us
    ppermute x22, waiting for transfers between devices, swap(): lax.ppermute(values, 'vel', [(device, device ^ stride) for device in rang...  5.5 us
    pallas_call x1, Pallas kernels, start_call(): pl.pallas_call(functools.partial(start_kernel, total_count), out_shape=(p...  5.34 us
    pallas_call x1, Pallas kernels, update_call(): pl.pallas_call(update_kernel, out_shape=(pltpu.VMEM((rows * PARTS, cells)...  3.23 us
    pallas_call x1, Pallas kernels, finish_call(): pl.pallas_call(finish_kernel, out_shape=(jax.ShapeDtypeStruct((rows * PAR...  3.06 us
    pallas_call x2, Pallas kernels, fluid_call(): pl.pallas_call(fluid_kernel, out_shape=shapes, in_specs=[WHOLE], out_spec...  1.71 us
  transfers between devices with their start and end apart: 22, of which 13 were waited for; matrix products, arithmetic and copies ran while one was open for 0% of the time, Pallas kernels for 25%

profile of v7, /device:TPU:0, one launch (start us, length us, event | category | flops | bytes accessed | tf_op | source)
XLA Modules:
  0.0 63.3 jit_solution(5047279569291325069)
XLA Ops:
  0.6 5.3 %start.1 = (f32[128,8192]{1,0:T(8,128)S(1)}, f32[832,128]{1,0:T(8,128)S(1)}, bf16[128,48]{1,0:T(8,128)(2,1)S(1)}, bf16[128,48]{1,0:T(8,128)(2,1)S(1)}, bf16[32,2...) custom-call(f32[3,128]{1,0:T(4,128)} %vel_hbm, f32[1,8192]{1,0:T(1,128)} %bitcast.2, f32[3,8192]{1,0:T(4,128)} %flow_hbm.1, ...), custom_call_target="tpu_custom_call" | custom-call | tf_op jit(solution)/shard_map/start/pallas_call | solution.py:190
  6.5 1.0 %transport.16.refs_0_ = f32[16,8192]{1,0:T(8,128)S(1)} custom-call(f32[128,128]{1,0:T(8,128)S(1)} %get-tuple-element.62.stream_ref, f32[128,8192]{1,0:T(8,128)S(1)} %get-tuple-element.84.f_ref), custom_call_target="tpu_custom_call" | custom-call | tf_op jit(solution)/shard_map/transport/pallas_call | solution.py:281
  7.7 3.0 %collective-permute-start.1 = (f32[104,128]{1,0:T(8,128)S(1)}, f32[104,128]{1,0:T(8,128)S(1)}, u32[]{:S(2)}, u32[]{:S(2)}) collective-permute-start(f32[104,128]{1,0:T(8,128)S(1)} %get-tuple-element.68), channel_id=1, source_target_pairs={{0,2},{1,3},{2,0},{3,1},{4,6},{5,7},{6,4},{7,5},{8,10},{9,11},{10,... | collective-permute-start | bytes 159752 | tf_op jit(solution)/shard_map/ppermute | solution.py:526
  11.7 1.0 %transport.17.refs_1_ = f32[16,8192]{1,0:T(8,128)S(1)} custom-call(f32[128,128]{1,0:T(8,128)S(1)} %get-tuple-element.62.stream_ref, f32[128,8192]{1,0:T(8,128)S(1)} %get-tuple-element.84.f_ref), custom_call_target="tpu_custom_call" | custom-call | tf_op jit(solution)/shard_map/transport/pallas_call | solution.py:281
  12.8 2.4 %collective-permute-start.2 = (f32[104,128]{1,0:T(8,128)S(1)}, f32[104,128]{1,0:T(8,128)S(1)}, u32[]{:S(2)}, u32[]{:S(2)}) collective-permute-start(f32[104,128]{1,0:T(8,128)S(1)} %add.22.left_ref), channel_id=1, source_target_pairs={{0,4},{1,5},{2,6},{3,7},{4,0},{5,1},{6,2},{7,3},{8,12},{9,13},{10,... | collective-permute-start | bytes 159752 | tf_op jit(solution)/shard_map/ppermute | solution.py:526
  15.2 1.3 %collective-permute-start.5 = (f32[104,128]{1,0:T(8,128)S(1)}, f32[104,128]{1,0:T(8,128)S(1)}, u32[]{:S(2)}, u32[]{:S(2)}) collective-permute-start(f32[104,128]{1,0:T(8,128)S(1)} %add.23.left_ref), channel_id=1, source_target_pairs={{0,4},{1,5},{2,6},{3,7},{4,0},{5,1},{6,2},{7,3},{8,12},{9,13},{10,... | collective-permute-start | bytes 159752 | tf_op jit(solution)/shard_map/ppermute | solution.py:526
  16.4 1.0 %transport.19.refs_3_ = f32[16,8192]{1,0:T(8,128)S(1)} custom-call(f32[128,128]{1,0:T(8,128)S(1)} %get-tuple-element.62.stream_ref, f32[128,8192]{1,0:T(8,128)S(1)} %get-tuple-element.84.f_ref), custom_call_target="tpu_custom_call" | custom-call | tf_op jit(solution)/shard_map/transport/pallas_call | solution.py:281
  17.8 2.8 %collective-permute-start.4 = (f32[104,128]{1,0:T(8,128)S(1)}, f32[104,128]{1,0:T(8,128)S(1)}, u32[]{:S(2)}, u32[]{:S(2)}) collective-permute-start(f32[104,128]{1,0:T(8,128)S(1)} %add.24.left_ref), channel_id=1, source_target_pairs={{0,8},{1,9},{2,10},{3,11},{4,12},{5,13},{6,14},{7,15},{8,0},{9,1},... | collective-permute-start | bytes 159752 | tf_op jit(solution)/shard_map/ppermute | solution.py:526
  20.6 1.6 %collective-permute-start.7 = (f32[104,128]{1,0:T(8,128)S(1)}, f32[104,128]{1,0:T(8,128)S(1)}, u32[]{:S(2)}, u32[]{:S(2)}) collective-permute-start(f32[104,128]{1,0:T(8,128)S(1)} %add.25.left_ref), channel_id=1, source_target_pairs={{0,8},{1,9},{2,10},{3,11},{4,12},{5,13},{6,14},{7,15},{8,0},{9,1},... | collective-permute-start | bytes 159752 | tf_op jit(solution)/shard_map/ppermute | solution.py:526
  23.2 1.0 %transport.20.refs_4_ = f32[16,8192]{1,0:T(8,128)S(1)} custom-call(f32[128,128]{1,0:T(8,128)S(1)} %get-tuple-element.62.stream_ref, f32[128,8192]{1,0:T(8,128)S(1)} %get-tuple-element.84.f_ref), custom_call_target="tpu_custom_call" | custom-call | tf_op jit(solution)/shard_map/transport/pallas_call | solution.py:281
  24.3 1.5 %collective-permute-start.6 = (f32[104,128]{1,0:T(8,128)S(1)}, f32[104,128]{1,0:T(8,128)S(1)}, u32[]{:S(2)}, u32[]{:S(2)}) collective-permute-start(f32[104,128]{1,0:T(8,128)S(1)} %add.26), channel_id=1, source_target_pairs={{0,2},{1,3},{2,0},{3,1},{4,6},{5,7},{6,4},{7,5},{8,10},{9,11},{10,... | collective-permute-start | bytes 159752 | tf_op jit(solution)/shard_map/ppermute | solution.py:526
  25.8 1.5 %collective-permute-start.9 = (f32[104,128]{1,0:T(8,128)S(1)}, f32[104,128]{1,0:T(8,128)S(1)}, u32[]{:S(2)}, u32[]{:S(2)}) collective-permute-start(f32[104,128]{1,0:T(8,128)S(1)} %add.27), channel_id=1, source_target_pairs={{0,2},{1,3},{2,0},{3,1},{4,6},{5,7},{6,4},{7,5},{8,10},{9,11},{10,... | collective-permute-start | bytes 159752 | tf_op jit(solution)/shard_map/ppermute | solution.py:526
  28.6 1.4 %collective-permute-done.9 = f32[104,128]{1,0:T(8,128)S(1)} collective-permute-done((f32[104,128]{1,0:T(8,128)S(1)}, f32[104,128]{1,0:T(8,128)S(1)}, u32[]{:S(2)}, u32[]{:S(2)}) %collective-permute-start.9) | collective-permute-done | bytes 53280 | tf_op jit(solution)/shard_map/ppermute | solution.py:526
  30.1 1.0 %transport.23.refs_7_ = f32[16,8192]{1,0:T(8,128)S(1)} custom-call(f32[128,128]{1,0:T(8,128)S(1)} %get-tuple-element.62.stream_ref, f32[128,8192]{1,0:T(8,128)S(1)} %get-tuple-element.84.f_ref), custom_call_target="tpu_custom_call" | custom-call | tf_op jit(solution)/shard_map/transport/pallas_call | solution.py:281
  32.3 3.2 %update.1 = (f32[128,8192]{1,0:T(8,128)S(1)}, f32[832,128]{1,0:T(8,128)S(1)}) custom-call(f32[16,8192]{1,0:T(8,128)S(1)} %transport.16.refs_0_, f32[16,8192]{1,0:T(8,128)S(1)} %transport.17.refs_1_, f32[16,8192]{1,0:T(8,128)S(1)} %transport.18.refs_2_, f32[16,8192]{1,0:T(8,128)S(1)} %transport.19.refs_3_, f32[16,8192]{1,0:T(8,128)S(1)} %transport.20.refs_4_, ...), custom_call_target="tpu_custom_call" | custom-call | tf_op jit(solution)/shard_map/update/pallas_call | solution.py:452
  37.2 1.5 %collective-permute-start.12 = (f32[104,128]{1,0:T(8,128)S(1)}, f32[104,128]{1,0:T(8,128)S(1)}, u32[]{:S(2)}, u32[]{:S(2)}) collective-permute-start(f32[104,128]{1,0:T(8,128)S(1)} %get-tuple-element.95), channel_id=1, source_target_pairs={{0,2},{1,3},{2,0},{3,1},{4,6},{5,7},{6,4},{7,5},{8,10},{9,11},{10,... | collective-permute-start | bytes 159752 | tf_op jit(solution)/shard_map/ppermute | solution.py:526
  40.3 1.0 %transport.25.refs_1_ = f32[16,8192]{1,0:T(8,128)S(1)} custom-call(f32[128,128]{1,0:T(8,128)S(1)} %get-tuple-element.62.stream_ref, f32[128,8192]{1,0:T(8,128)S(1)} %get-tuple-element.111.f_ref), custom_call_target="tpu_custom_call" | custom-call | tf_op jit(solution)/shard_map/transport/pallas_call | solution.py:281
  41.6 1.1 %collective-permute-start.13 = (f32[104,128]{1,0:T(8,128)S(1)}, f32[104,128]{1,0:T(8,128)S(1)}, u32[]{:S(2)}, u32[]{:S(2)}) collective-permute-start(f32[104,128]{1,0:T(8,128)S(1)} %add.28.left_ref), channel_id=1, source_target_pairs={{0,4},{1,5},{2,6},{3,7},{4,0},{5,1},{6,2},{7,3},{8,12},{9,13},{10,... | collective-permute-start | bytes 159752 | tf_op jit(solution)/shard_map/ppermute | solution.py:526
  42.9 1.5 %collective-permute-start.16 = (f32[104,128]{1,0:T(8,128)S(1)}, f32[104,128]{1,0:T(8,128)S(1)}, u32[]{:S(2)}, u32[]{:S(2)}) collective-permute-start(f32[104,128]{1,0:T(8,128)S(1)} %add.29.left_ref), channel_id=1, source_target_pairs={{0,4},{1,5},{2,6},{3,7},{4,0},{5,1},{6,2},{7,3},{8,12},{9,13},{10,... | collective-permute-start | bytes 159752 | tf_op jit(solution)/shard_map/ppermute | solution.py:526
  45.9 2.1 %collective-permute-start.15 = (f32[104,128]{1,0:T(8,128)S(1)}, f32[104,128]{1,0:T(8,128)S(1)}, u32[]{:S(2)}, u32[]{:S(2)}) collective-permute-start(f32[104,128]{1,0:T(8,128)S(1)} %add.30.left_ref), channel_id=1, source_target_pairs={{0,8},{1,9},{2,10},{3,11},{4,12},{5,13},{6,14},{7,15},{8,0},{9,1},... | collective-permute-start | bytes 159752 | tf_op jit(solution)/shard_map/ppermute | solution.py:526
  48.1 2.1 %collective-permute-start.18 = (f32[104,128]{1,0:T(8,128)S(1)}, f32[104,128]{1,0:T(8,128)S(1)}, u32[]{:S(2)}, u32[]{:S(2)}) collective-permute-start(f32[104,128]{1,0:T(8,128)S(1)} %add.31.left_ref), channel_id=1, source_target_pairs={{0,8},{1,9},{2,10},{3,11},{4,12},{5,13},{6,14},{7,15},{8,0},{9,1},... | collective-permute-start | bytes 159752 | tf_op jit(solution)/shard_map/ppermute | solution.py:526
  51.2 1.0 %transport.28.refs_4_ = f32[16,8192]{1,0:T(8,128)S(1)} custom-call(f32[128,128]{1,0:T(8,128)S(1)} %get-tuple-element.62.stream_ref, f32[128,8192]{1,0:T(8,128)S(1)} %get-tuple-element.111.f_ref), custom_call_target="tpu_custom_call" | custom-call | tf_op jit(solution)/shard_map/transport/pallas_call | solution.py:281
  53.2 1.7 %collective-permute-start.20 = (f32[104,128]{1,0:T(8,128)S(1)}, f32[104,128]{1,0:T(8,128)S(1)}, u32[]{:S(2)}, u32[]{:S(2)}) collective-permute-start(f32[104,128]{1,0:T(8,128)S(1)} %add.33), channel_id=1, source_target_pairs={{0,2},{1,3},{2,0},{3,1},{4,6},{5,7},{6,4},{7,5},{8,10},{9,11},{10,... | collective-permute-start | bytes 159752 | tf_op jit(solution)/shard_map/ppermute | solution.py:526
  60.0 3.1 %finish.1 = (f32[128,8192]{1,0:T(8,128)}, f32[8,8192]{1,0:T(8,128)}) custom-call(f32[16,8192]{1,0:T(8,128)S(1)} %transport.24.refs_0_, f32[16,8192]{1,0:T(8,128)S(1)} %transport.25.refs_1_, f32[16,8192]{1,0:T(8,128)S(1)} %transport.26.refs_2_, f32[16,8192]{1,0:T(8,128)S(1)} %transport.27.refs_3_, f32[16,8192]{1,0:T(8,128)S(1)} %transport.28.refs_4_, ...), custom_call_target="tpu_custom_call" | custom-call | tf_op jit(solution)/shard_map/finish/pallas_call | solution.py:488
  (72 shorter events, 18.0 us)
Async XLA Ops:
  6.0 1.6 %collective-permute-start = (f32[416,128]{1,0:T(8,128)S(1)}, f32[416,128]{1,0:T(8,128)S(1)}, u32[]{:S(2)}, u32[]{:S(2)}) collective-permute-start(f32[416,128]{1,0:T(8,128)S(1)} %slice_select_fusion.1), channel_id=1, source_target_pairs={{0,1},{1,0},{2,3},{3,2},{4,5},{5,4},{6,7},{7,6},{8,9},{9,8},{10,11... | collective-permute-start | bytes 638984 | tf_op jit(solution)/shard_map/ppermute | solution.py:526
  7.7 5.1 %collective-permute-start.1 = (f32[104,128]{1,0:T(8,128)S(1)}, f32[104,128]{1,0:T(8,128)S(1)}, u32[]{:S(2)}, u32[]{:S(2)}) collective-permute-start(f32[104,128]{1,0:T(8,128)S(1)} %get-tuple-element.68), channel_id=1, source_target_pairs={{0,2},{1,3},{2,0},{3,1},{4,6},{5,7},{6,4},{7,5},{8,10},{9,11},{10,... | collective-permute-start | bytes 159752 | tf_op jit(solution)/shard_map/ppermute | solution.py:526
  10.6 4.5 %collective-permute-start.3 = (f32[104,128]{1,0:T(8,128)S(1)}, f32[104,128]{1,0:T(8,128)S(1)}, u32[]{:S(2)}, u32[]{:S(2)}) collective-permute-start(f32[104,128]{1,0:T(8,128)S(1)} %get-tuple-element.69), channel_id=1, source_target_pairs={{0,2},{1,3},{2,0},{3,1},{4,6},{5,7},{6,4},{7,5},{8,10},{9,11},{10,... | collective-permute-start | bytes 159752 | tf_op jit(solution)/shard_map/ppermute | solution.py:526
  12.8 5.0 %collective-permute-start.2 = (f32[104,128]{1,0:T(8,128)S(1)}, f32[104,128]{1,0:T(8,128)S(1)}, u32[]{:S(2)}, u32[]{:S(2)}) collective-permute-start(f32[104,128]{1,0:T(8,128)S(1)} %add.22.left_ref), channel_id=1, source_target_pairs={{0,4},{1,5},{2,6},{3,7},{4,0},{5,1},{6,2},{7,3},{8,12},{9,13},{10,... | collective-permute-start | bytes 159752 | tf_op jit(solution)/shard_map/ppermute | solution.py:526
  15.2 5.4 %collective-permute-start.5 = (f32[104,128]{1,0:T(8,128)S(1)}, f32[104,128]{1,0:T(8,128)S(1)}, u32[]{:S(2)}, u32[]{:S(2)}) collective-permute-start(f32[104,128]{1,0:T(8,128)S(1)} %add.23.left_ref), channel_id=1, source_target_pairs={{0,4},{1,5},{2,6},{3,7},{4,0},{5,1},{6,2},{7,3},{8,12},{9,13},{10,... | collective-permute-start | bytes 159752 | tf_op jit(solution)/shard_map/ppermute | solution.py:526
  17.8 6.5 %collective-permute-start.4 = (f32[104,128]{1,0:T(8,128)S(1)}, f32[104,128]{1,0:T(8,128)S(1)}, u32[]{:S(2)}, u32[]{:S(2)}) collective-permute-start(f32[104,128]{1,0:T(8,128)S(1)} %add.24.left_ref), channel_id=1, source_target_pairs={{0,8},{1,9},{2,10},{3,11},{4,12},{5,13},{6,14},{7,15},{8,0},{9,1},... | collective-permute-start | bytes 159752 | tf_op jit(solution)/shard_map/ppermute | solution.py:526
  20.6 5.2 %collective-permute-start.7 = (f32[104,128]{1,0:T(8,128)S(1)}, f32[104,128]{1,0:T(8,128)S(1)}, u32[]{:S(2)}, u32[]{:S(2)}) collective-permute-start(f32[104,128]{1,0:T(8,128)S(1)} %add.25.left_ref), channel_id=1, source_target_pairs={{0,8},{1,9},{2,10},{3,11},{4,12},{5,13},{6,14},{7,15},{8,0},{9,1},... | collective-permute-start | bytes 159752 | tf_op jit(solution)/shard_map/ppermute | solution.py:526
  24.3 4.2 %collective-permute-start.6 = (f32[104,128]{1,0:T(8,128)S(1)}, f32[104,128]{1,0:T(8,128)S(1)}, u32[]{:S(2)}, u32[]{:S(2)}) collective-permute-start(f32[104,128]{1,0:T(8,128)S(1)} %add.26), channel_id=1, source_target_pairs={{0,2},{1,3},{2,0},{3,1},{4,6},{5,7},{6,4},{7,5},{8,10},{9,11},{10,... | collective-permute-start | bytes 159752 | tf_op jit(solution)/shard_map/ppermute | solution.py:526
  25.8 4.2 %collective-permute-start.9 = (f32[104,128]{1,0:T(8,128)S(1)}, f32[104,128]{1,0:T(8,128)S(1)}, u32[]{:S(2)}, u32[]{:S(2)}) collective-permute-start(f32[104,128]{1,0:T(8,128)S(1)} %add.27), channel_id=1, source_target_pairs={{0,2},{1,3},{2,0},{3,1},{4,6},{5,7},{6,4},{7,5},{8,10},{9,11},{10,... | collective-permute-start | bytes 159752 | tf_op jit(solution)/shard_map/ppermute | solution.py:526
  28.5 2.6 %collective-permute-start.8 = (f32[208,128]{1,0:T(8,128)S(1)}, f32[208,128]{1,0:T(8,128)S(1)}, u32[]{:S(2)}, u32[]{:S(2)}) collective-permute-start(f32[208,128]{1,0:T(8,128)S(1)} %pad_maximum_fusion.2), channel_id=1, source_target_pairs={{0,1},{1,0},{2,3},{3,2},{4,5},{5,4},{6,7},{7,6},{8,9},{9,8},{10,11... | collective-permute-start | bytes 319496 | tf_op jit(solution)/shard_map/ppermute | solution.py:526
  30.0 1.4 %collective-permute-start.10 = (f32[208,128]{1,0:T(8,128)S(1)}, f32[208,128]{1,0:T(8,128)S(1)}, u32[]{:S(2)}, u32[]{:S(2)}) collective-permute-start(f32[208,128]{1,0:T(8,128)S(1)} %pad_maximum_fusion.3), channel_id=1, source_target_pairs={{0,1},{1,0},{2,3},{3,2},{4,5},{5,4},{6,7},{7,6},{8,9},{9,8},{10,11... | collective-permute-start | bytes 319496 | tf_op jit(solution)/shard_map/ppermute | solution.py:526
  35.6 1.5 %collective-permute-start.11 = (f32[416,128]{1,0:T(8,128)S(1)}, f32[416,128]{1,0:T(8,128)S(1)}, u32[]{:S(2)}, u32[]{:S(2)}) collective-permute-start(f32[416,128]{1,0:T(8,128)S(1)} %slice_select_fusion), channel_id=1, source_target_pairs={{0,1},{1,0},{2,3},{3,2},{4,5},{5,4},{6,7},{7,6},{8,9},{9,8},{10,11... | collective-permute-start | bytes 638984 | tf_op jit(solution)/shard_map/ppermute | solution.py:526
  37.2 4.4 %collective-permute-start.12 = (f32[104,128]{1,0:T(8,128)S(1)}, f32[104,128]{1,0:T(8,128)S(1)}, u32[]{:S(2)}, u32[]{:S(2)}) collective-permute-start(f32[104,128]{1,0:T(8,128)S(1)} %get-tuple-element.95), channel_id=1, source_target_pairs={{0,2},{1,3},{2,0},{3,1},{4,6},{5,7},{6,4},{7,5},{8,10},{9,11},{10,... | collective-permute-start | bytes 159752 | tf_op jit(solution)/shard_map/ppermute | solution.py:526
  38.7 4.1 %collective-permute-start.14 = (f32[104,128]{1,0:T(8,128)S(1)}, f32[104,128]{1,0:T(8,128)S(1)}, u32[]{:S(2)}, u32[]{:S(2)}) collective-permute-start(f32[104,128]{1,0:T(8,128)S(1)} %get-tuple-element.96), channel_id=1, source_target_pairs={{0,2},{1,3},{2,0},{3,1},{4,6},{5,7},{6,4},{7,5},{8,10},{9,11},{10,... | collective-permute-start | bytes 159752 | tf_op jit(solution)/shard_map/ppermute | solution.py:526
  41.6 4.3 %collective-permute-start.13 = (f32[104,128]{1,0:T(8,128)S(1)}, f32[104,128]{1,0:T(8,128)S(1)}, u32[]{:S(2)}, u32[]{:S(2)}) collective-permute-start(f32[104,128]{1,0:T(8,128)S(1)} %add.28.left_ref), channel_id=1, source_target_pairs={{0,4},{1,5},{2,6},{3,7},{4,0},{5,1},{6,2},{7,3},{8,12},{9,13},{10,... | collective-permute-start | bytes 159752 | tf_op jit(solution)/shard_map/ppermute | solution.py:526
  42.9 5.2 %collective-permute-start.16 = (f32[104,128]{1,0:T(8,128)S(1)}, f32[104,128]{1,0:T(8,128)S(1)}, u32[]{:S(2)}, u32[]{:S(2)}) collective-permute-start(f32[104,128]{1,0:T(8,128)S(1)} %add.29.left_ref), channel_id=1, source_target_pairs={{0,4},{1,5},{2,6},{3,7},{4,0},{5,1},{6,2},{7,3},{8,12},{9,13},{10,... | collective-permute-start | bytes 159752 | tf_op jit(solution)/shard_map/ppermute | solution.py:526
  45.9 6.2 %collective-permute-start.15 = (f32[104,128]{1,0:T(8,128)S(1)}, f32[104,128]{1,0:T(8,128)S(1)}, u32[]{:S(2)}, u32[]{:S(2)}) collective-permute-start(f32[104,128]{1,0:T(8,128)S(1)} %add.30.left_ref), channel_id=1, source_target_pairs={{0,8},{1,9},{2,10},{3,11},{4,12},{5,13},{6,14},{7,15},{8,0},{9,1},... | collective-permute-start | bytes 159752 | tf_op jit(solution)/shard_map/ppermute | solution.py:526
  48.1 5.1 %collective-permute-start.18 = (f32[104,128]{1,0:T(8,128)S(1)}, f32[104,128]{1,0:T(8,128)S(1)}, u32[]{:S(2)}, u32[]{:S(2)}) collective-permute-start(f32[104,128]{1,0:T(8,128)S(1)} %add.31.left_ref), channel_id=1, source_target_pairs={{0,8},{1,9},{2,10},{3,11},{4,12},{5,13},{6,14},{7,15},{8,0},{9,1},... | collective-permute-start | bytes 159752 | tf_op jit(solution)/shard_map/ppermute | solution.py:526
  52.2 4.2 %collective-permute-start.17 = (f32[104,128]{1,0:T(8,128)S(1)}, f32[104,128]{1,0:T(8,128)S(1)}, u32[]{:S(2)}, u32[]{:S(2)}) collective-permute-start(f32[104,128]{1,0:T(8,128)S(1)} %add.32), channel_id=1, source_target_pairs={{0,2},{1,3},{2,0},{3,1},{4,6},{5,7},{6,4},{7,5},{8,10},{9,11},{10,... | collective-permute-start | bytes 159752 | tf_op jit(solution)/shard_map/ppermute | solution.py:526
  53.2 4.2 %collective-permute-start.20 = (f32[104,128]{1,0:T(8,128)S(1)}, f32[104,128]{1,0:T(8,128)S(1)}, u32[]{:S(2)}, u32[]{:S(2)}) collective-permute-start(f32[104,128]{1,0:T(8,128)S(1)} %add.33), channel_id=1, source_target_pairs={{0,2},{1,3},{2,0},{3,1},{4,6},{5,7},{6,4},{7,5},{8,10},{9,11},{10,... | collective-permute-start | bytes 159752 | tf_op jit(solution)/shard_map/ppermute | solution.py:526
  57.4 1.7 %collective-permute-start.19 = (f32[208,128]{1,0:T(8,128)S(1)}, f32[208,128]{1,0:T(8,128)S(1)}, u32[]{:S(2)}, u32[]{:S(2)}) collective-permute-start(f32[208,128]{1,0:T(8,128)S(1)} %pad_maximum_fusion.4), channel_id=1, source_target_pairs={{0,1},{1,0},{2,3},{3,2},{4,5},{5,4},{6,7},{7,6},{8,9},{9,8},{10,11... | collective-permute-start | bytes 319496 | tf_op jit(solution)/shard_map/ppermute | solution.py:526
  57.5 1.6 %collective-permute-start.21 = (f32[208,128]{1,0:T(8,128)S(1)}, f32[208,128]{1,0:T(8,128)S(1)}, u32[]{:S(2)}, u32[]{:S(2)}) collective-permute-start(f32[208,128]{1,0:T(8,128)S(1)} %pad_maximum_fusion.5), channel_id=1, source_target_pairs={{0,1},{1,0},{2,3},{3,2},{4,5},{5,4},{6,7},{7,6},{8,9},{9,8},{10,11... | collective-permute-start | bytes 319496 | tf_op jit(solution)/shard_map/ppermute | solution.py:526

commit v8 on v7

--- a/solution.py
+++ b/solution.py
@@ -24,9 +24,10 @@
 SENT = 13
 COEF = 24
 DAMP = 13
+ROWS = 64
 CHUNKS = 8
 PARTS = 8
-BESIDE = (1, 2, 1, 2, 1, 1)
+BESIDE = (1, 2, 1, 1, 2, 1)
 MIB = 1024 * 1024
 
 WHOLE = pl.BlockSpec(memory_space=pltpu.VMEM)
@@ -102,10 +103,8 @@
     return jnp.concatenate([high, middle, high], axis=0)
 
 
-def store_moments(moments_ref, table, values, tile, blocks):
-    high = values.astype(jnp.bfloat16)
-    low = (values - high.astype(jnp.float32)).astype(jnp.bfloat16)
-    both = dot(table, jnp.concatenate([high, low], axis=0))
+def store_moments(moments_ref, table, split, tile, blocks):
+    both = dot(table, split)
     sums = both[:BASIS] + both[BASIS:]
     per_tile = TILE // LANES
     for part in range(per_tile):
@@ -115,13 +114,24 @@
         ]
 
 
+def store_tile(f_ref, here, rows, values_of):
+    high, low = [], []
+    for first in range(0, rows, ROWS):
+        some = pl.ds(first, ROWS)
+        values = values_of(some)
+        f_ref[some, here] = values
+        high.append(values.astype(jnp.bfloat16))
+        low.append((values - high[-1].astype(jnp.float32)).astype(jnp.bfloat16))
+    return jnp.concatenate(high + low, axis=0)
+
+
 def in_turn(front, back, tiles):
-    values = front(0)
+    made = front(0)
     for tile in range(1, tiles):
         upcoming = front(tile)
-        back(tile - 1, values)
-        values = upcoming
-    back(tiles - 1, values)
+        back(tile - 1, made)
+        made = upcoming
+    back(tiles - 1, made)
 
 
 def start_kernel(
@@ -169,13 +179,17 @@
         rate = (0.5 * LOG2E) / thermal
         speed_sq = flow[0:1] * flow[0:1] + flow[1:2] * flow[1:2] + flow[2:3] * flow[2:3]
         rows = [-rate * speed_sq, 2.0 * rate * flow, -rate, jnp.zeros((3, TILE), jnp.float32)]
-        exponent = dot(exponent_table, expand_exponent(jnp.concatenate(rows, axis=0)))
+        spread = expand_exponent(jnp.concatenate(rows, axis=0))
         scale = density / (thermal * jnp.sqrt(thermal))
-        return jnp.exp2(exponent) * (scale * (1.0 + deviation_ref[:, here]))
-
-    def back(tile, values):
-        f_ref[:, tile * TILE : (tile + 1) * TILE] = values
-        store_moments(moments_ref, table, values, tile, cells // LANES)
+
+        def values_of(some):
+            exponent = dot(exponent_ref[some, :], spread)
+            return jnp.exp2(exponent) * (scale * (1.0 + deviation_ref[some, here]))
+
+        return store_tile(f_ref, here, f_ref.shape[0], values_of)
+
+    def back(tile, split):
+        store_moments(moments_ref, table, split, tile, cells // LANES)
 
     def front_when_here(tile):
         if tile * TILE % width == 0:
@@ -415,20 +429,25 @@
     )(near(moments))
 
 
-def relaxed(g, coef_ref, exponent_ref, polynomial_ref, tile):
+def relaxed(g_refs, here, coef_ref, exponent_ref, polynomial_ref, tile):
     per_tile = TILE // LANES
     parts = [
         coef_ref[pl.ds((tile * per_tile + part) * COEF, COEF), :]
         for part in range(per_tile)
     ]
     coefficients = jnp.concatenate(parts, axis=1)
-    polynomial = dot(polynomial_ref[...], expand_polynomial(coefficients[:BASIS]))
-    exponent = dot(exponent_ref[...], expand_exponent(coefficients[BASIS:]))
-    return g * coefficients[DAMP : DAMP + 1] + jnp.exp2(exponent) * polynomial
-
-
-def gathered(g_refs, here):
-    return jnp.concatenate([ref[:, here] for ref in g_refs], axis=0)
+    cubic = expand_polynomial(coefficients[:BASIS])
+    spread = expand_exponent(coefficients[BASIS:])
+    rows = g_refs[0].shape[0]
+
+    def values_of(some):
+        polynomial = dot(polynomial_ref[some, :], cubic)
+        exponent = dot(exponent_ref[some, :], spread)
+        refs = g_refs[some.start // rows : (some.start + some.size) // rows]
+        g = jnp.concatenate([ref[:, here] for ref in refs], axis=0)
+        return g * coefficients[DAMP : DAMP + 1] + jnp.exp2(exponent) * polynomial
+
+    return values_of
 
 
 def update_kernel(*refs):
@@ -438,11 +457,11 @@
 
     def front(tile):
         here = pl.ds(tile * TILE, TILE)
-        return relaxed(gathered(g_refs, here), coef_ref, exponent_ref, polynomial_ref, tile)
-
-    def back(tile, values):
-        f_ref[:, tile * TILE : (tile + 1) * TILE] = values
-        store_moments(moments_ref, table_ref[...], values, tile, cells // LANES)
+        values_of = relaxed(g_refs, here, coef_ref, exponent_ref, polynomial_ref, tile)
+        return store_tile(f_ref, here, f_ref.shape[0], values_of)
+
+    def back(tile, split):
+        store_moments(moments_ref, table_ref[...], split, tile, cells // LANES)
 
     in_turn(front, back, cells // TILE)
 
@@ -472,7 +491,9 @@
         for local in range(width // TILE):
             tile = chunk * (width // TILE) + local
             here = pl.ds(tile * TILE, TILE)
-            held[:, here] = relaxed(gathered(g_refs, here), coef_ref, exponent_ref, polynomial_ref, tile)
+            values_of = relaxed(g_refs, here, coef_ref, exponent_ref, polynomial_ref, tile)
+            for first in range(0, held.shape[0], ROWS):
+                held[pl.ds(first, ROWS), here] = values_of(pl.ds(first, ROWS))
             for block in range(tile * TILE // LANES, (tile + 1) * TILE // LANES):
                 fields_ref[:, pl.ds(block * LANES, LANES)] = macro_ref[pl.ds(block * 8, 8), :]
         there = pl.ds(chunk * width, width)

time: 63.4 us -> 63.5 us (level)
  transfers between devices with their start and end apart: 22 -> 22, of which waited for: 13 -> 12; matrix products, arithmetic and copies ran while one was open for 0% -> 0% of each run, Pallas kernels for 25% -> 25%
where the time goes in v8:
time: 63.5 us; the launch traced here: 63.3 us
  Pallas kernels  29.4 us (46%)
  starting transfers between devices  27 us (43%)
  waiting for transfers between devices  5.27 us (8%)
  between operations  1.18 us (2%)
    ppermute x22, starting transfers between devices, swap(): lax.ppermute(values, 'vel', [(device, device ^ stride) for device in rang...  27 us
    pallas_call x16, Pallas kernels, transport_call(): pl.pallas_call(functools.partial(transport_kernel, part * rows), out_shap...  15.9 us
    pallas_call x1, Pallas kernels, start_call(): pl.pallas_call(functools.partial(start_kernel, total_count), out_shape=(p...  5.41 us
    ppermute x22, waiting for transfers between devices, swap(): lax.ppermute(values, 'vel', [(device, device ^ stride) for device in rang...  5.27 us
    pallas_call x1, Pallas kernels, update_call(): pl.pallas_call(update_kernel, out_shape=(pltpu.VMEM((rows * PARTS, cells)...  3.2 us
    pallas_call x1, Pallas kernels, finish_call(): pl.pallas_call(finish_kernel, out_shape=(jax.ShapeDtypeStruct((rows * PAR...  3.06 us
    pallas_call x2, Pallas kernels, fluid_call(): pl.pallas_call(fluid_kernel, out_shape=shapes, in_specs=[WHOLE], out_spec...  1.71 us
  transfers between devices with their start and end apart: 22, of which 12 were waited for; matrix products, arithmetic and copies ran while one was open for 0% of the time, Pallas kernels for 25%

profile of v8, /device:TPU:0, one launch (start us, length us, event | category | flops | bytes accessed | tf_op | source)
XLA Modules:
  0.0 63.3 jit_solution(15321333824777632334)
XLA Ops:
  0.6 5.4 %start.1 = (f32[128,8192]{1,0:T(8,128)S(1)}, f32[832,128]{1,0:T(8,128)S(1)}, bf16[128,48]{1,0:T(8,128)(2,1)S(1)}, bf16[128,48]{1,0:T(8,128)(2,1)S(1)}, bf16[32,2...) custom-call(f32[3,128]{1,0:T(4,128)} %vel_hbm, f32[1,8192]{1,0:T(1,128)} %bitcast.2, f32[3,8192]{1,0:T(4,128)} %flow_hbm.1, ...), custom_call_target="tpu_custom_call" | custom-call | tf_op jit(solution)/shard_map/start/pallas_call | solution.py:204
  6.6 1.0 %transport.16.refs_0_ = f32[16,8192]{1,0:T(8,128)S(1)} custom-call(f32[128,128]{1,0:T(8,128)S(1)} %get-tuple-element.62.stream_ref, f32[128,8192]{1,0:T(8,128)S(1)} %get-tuple-element.84.f_ref), custom_call_target="tpu_custom_call" | custom-call | tf_op jit(solution)/shard_map/transport/pallas_call | solution.py:295
  7.8 3.0 %collective-permute-start.1 = (f32[104,128]{1,0:T(8,128)S(1)}, f32[104,128]{1,0:T(8,128)S(1)}, u32[]{:S(2)}, u32[]{:S(2)}) collective-permute-start(f32[104,128]{1,0:T(8,128)S(1)} %get-tuple-element.68), channel_id=1, source_target_pairs={{0,2},{1,3},{2,0},{3,1},{4,6},{5,7},{6,4},{7,5},{8,10},{9,11},{10,... | collective-permute-start | bytes 159752 | tf_op jit(solution)/shard_map/ppermute | solution.py:547
  11.8 1.0 %transport.17.refs_1_ = f32[16,8192]{1,0:T(8,128)S(1)} custom-call(f32[128,128]{1,0:T(8,128)S(1)} %get-tuple-element.62.stream_ref, f32[128,8192]{1,0:T(8,128)S(1)} %get-tuple-element.84.f_ref), custom_call_target="tpu_custom_call" | custom-call | tf_op jit(solution)/shard_map/transport/pallas_call | solution.py:295
  12.9 2.4 %collective-permute-start.2 = (f32[104,128]{1,0:T(8,128)S(1)}, f32[104,128]{1,0:T(8,128)S(1)}, u32[]{:S(2)}, u32[]{:S(2)}) collective-permute-start(f32[104,128]{1,0:T(8,128)S(1)} %add.22.left_ref), channel_id=1, source_target_pairs={{0,4},{1,5},{2,6},{3,7},{4,0},{5,1},{6,2},{7,3},{8,12},{9,13},{10,... | collective-permute-start | bytes 159752 | tf_op jit(solution)/shard_map/ppermute | solution.py:547
  15.2 1.3 %collective-permute-start.5 = (f32[104,128]{1,0:T(8,128)S(1)}, f32[104,128]{1,0:T(8,128)S(1)}, u32[]{:S(2)}, u32[]{:S(2)}) collective-permute-start(f32[104,128]{1,0:T(8,128)S(1)} %add.23.left_ref), channel_id=1, source_target_pairs={{0,4},{1,5},{2,6},{3,7},{4,0},{5,1},{6,2},{7,3},{8,12},{9,13},{10,... | collective-permute-start | bytes 159752 | tf_op jit(solution)/shard_map/ppermute | solution.py:547
  16.5 1.0 %transport.19.refs_3_ = f32[16,8192]{1,0:T(8,128)S(1)} custom-call(f32[128,128]{1,0:T(8,128)S(1)} %get-tuple-element.62.stream_ref, f32[128,8192]{1,0:T(8,128)S(1)} %get-tuple-element.84.f_ref), custom_call_target="tpu_custom_call" | custom-call | tf_op jit(solution)/shard_map/transport/pallas_call | solution.py:295
  17.8 2.8 %collective-permute-start.4 = (f32[104,128]{1,0:T(8,128)S(1)}, f32[104,128]{1,0:T(8,128)S(1)}, u32[]{:S(2)}, u32[]{:S(2)}) collective-permute-start(f32[104,128]{1,0:T(8,128)S(1)} %add.24.left_ref), channel_id=1, source_target_pairs={{0,8},{1,9},{2,10},{3,11},{4,12},{5,13},{6,14},{7,15},{8,0},{9,1},... | collective-permute-start | bytes 159752 | tf_op jit(solution)/shard_map/ppermute | solution.py:547
  20.7 1.6 %collective-permute-start.7 = (f32[104,128]{1,0:T(8,128)S(1)}, f32[104,128]{1,0:T(8,128)S(1)}, u32[]{:S(2)}, u32[]{:S(2)}) collective-permute-start(f32[104,128]{1,0:T(8,128)S(1)} %add.25.left_ref), channel_id=1, source_target_pairs={{0,8},{1,9},{2,10},{3,11},{4,12},{5,13},{6,14},{7,15},{8,0},{9,1},... | collective-permute-start | bytes 159752 | tf_op jit(solution)/shard_map/ppermute | solution.py:547
  23.2 1.1 %collective-permute-done.4.right_ref = f32[104,128]{1,0:T(8,128)S(1)} collective-permute-done((f32[104,128]{1,0:T(8,128)S(1)}, f32[104,128]{1,0:T(8,128)S(1)}, u32[]{:S(2)}, u32[]{:S(2)}) %collective-permute-start.4) | collective-permute-done | bytes 53280 | tf_op jit(solution)/shard_map/ppermute | solution.py:547
  24.4 1.5 %collective-permute-start.6 = (f32[104,128]{1,0:T(8,128)S(1)}, f32[104,128]{1,0:T(8,128)S(1)}, u32[]{:S(2)}, u32[]{:S(2)}) collective-permute-start(f32[104,128]{1,0:T(8,128)S(1)} %add.26), channel_id=1, source_target_pairs={{0,2},{1,3},{2,0},{3,1},{4,6},{5,7},{6,4},{7,5},{8,10},{9,11},{10,... | collective-permute-start | bytes 159752 | tf_op jit(solution)/shard_map/ppermute | solution.py:547
  25.9 1.5 %collective-permute-start.9 = (f32[104,128]{1,0:T(8,128)S(1)}, f32[104,128]{1,0:T(8,128)S(1)}, u32[]{:S(2)}, u32[]{:S(2)}) collective-permute-start(f32[104,128]{1,0:T(8,128)S(1)} %add.27), channel_id=1, source_target_pairs={{0,2},{1,3},{2,0},{3,1},{4,6},{5,7},{6,4},{7,5},{8,10},{9,11},{10,... | collective-permute-start | bytes 159752 | tf_op jit(solution)/shard_map/ppermute | solution.py:547
  28.4 1.0 %transport.21.refs_5_ = f32[16,8192]{1,0:T(8,128)S(1)} custom-call(f32[128,128]{1,0:T(8,128)S(1)} %get-tuple-element.62.stream_ref, f32[128,8192]{1,0:T(8,128)S(1)} %get-tuple-element.84.f_ref), custom_call_target="tpu_custom_call" | custom-call | tf_op jit(solution)/shard_map/transport/pallas_call | solution.py:295
  30.2 1.0 %transport.23.refs_7_ = f32[16,8192]{1,0:T(8,128)S(1)} custom-call(f32[128,128]{1,0:T(8,128)S(1)} %get-tuple-element.62.stream_ref, f32[128,8192]{1,0:T(8,128)S(1)} %get-tuple-element.84.f_ref), custom_call_target="tpu_custom_call" | custom-call | tf_op jit(solution)/shard_map/transport/pallas_call | solution.py:295
  32.4 3.2 %update.1 = (f32[128,8192]{1,0:T(8,128)S(1)}, f32[832,128]{1,0:T(8,128)S(1)}) custom-call(f32[16,8192]{1,0:T(8,128)S(1)} %transport.16.refs_0_, f32[16,8192]{1,0:T(8,128)S(1)} %transport.17.refs_1_, f32[16,8192]{1,0:T(8,128)S(1)} %transport.18.refs_2_, f32[16,8192]{1,0:T(8,128)S(1)} %transport.19.refs_3_, f32[16,8192]{1,0:T(8,128)S(1)} %transport.20.refs_4_, ...), custom_call_target="tpu_custom_call" | custom-call | tf_op jit(solution)/shard_map/update/pallas_call | solution.py:471
  37.2 1.5 %collective-permute-start.12 = (f32[104,128]{1,0:T(8,128)S(1)}, f32[104,128]{1,0:T(8,128)S(1)}, u32[]{:S(2)}, u32[]{:S(2)}) collective-permute-start(f32[104,128]{1,0:T(8,128)S(1)} %get-tuple-element.95), channel_id=1, source_target_pairs={{0,2},{1,3},{2,0},{3,1},{4,6},{5,7},{6,4},{7,5},{8,10},{9,11},{10,... | collective-permute-start | bytes 159752 | tf_op jit(solution)/shard_map/ppermute | solution.py:547
  40.3 1.0 %transport.25.refs_1_ = f32[16,8192]{1,0:T(8,128)S(1)} custom-call(f32[128,128]{1,0:T(8,128)S(1)} %get-tuple-element.62.stream_ref, f32[128,8192]{1,0:T(8,128)S(1)} %get-tuple-element.111.f_ref), custom_call_target="tpu_custom_call" | custom-call | tf_op jit(solution)/shard_map/transport/pallas_call | solution.py:295
  41.6 1.2 %collective-permute-start.13 = (f32[104,128]{1,0:T(8,128)S(1)}, f32[104,128]{1,0:T(8,128)S(1)}, u32[]{:S(2)}, u32[]{:S(2)}) collective-permute-start(f32[104,128]{1,0:T(8,128)S(1)} %add.28.left_ref), channel_id=1, source_target_pairs={{0,4},{1,5},{2,6},{3,7},{4,0},{5,1},{6,2},{7,3},{8,12},{9,13},{10,... | collective-permute-start | bytes 159752 | tf_op jit(solution)/shard_map/ppermute | solution.py:547
  42.9 1.5 %collective-permute-start.16 = (f32[104,128]{1,0:T(8,128)S(1)}, f32[104,128]{1,0:T(8,128)S(1)}, u32[]{:S(2)}, u32[]{:S(2)}) collective-permute-start(f32[104,128]{1,0:T(8,128)S(1)} %add.29.left_ref), channel_id=1, source_target_pairs={{0,4},{1,5},{2,6},{3,7},{4,0},{5,1},{6,2},{7,3},{8,12},{9,13},{10,... | collective-permute-start | bytes 159752 | tf_op jit(solution)/shard_map/ppermute | solution.py:547
  46.0 2.1 %collective-permute-start.15 = (f32[104,128]{1,0:T(8,128)S(1)}, f32[104,128]{1,0:T(8,128)S(1)}, u32[]{:S(2)}, u32[]{:S(2)}) collective-permute-start(f32[104,128]{1,0:T(8,128)S(1)} %add.30.left_ref), channel_id=1, source_target_pairs={{0,8},{1,9},{2,10},{3,11},{4,12},{5,13},{6,14},{7,15},{8,0},{9,1},... | collective-permute-start | bytes 159752 | tf_op jit(solution)/shard_map/ppermute | solution.py:547
  48.1 2.1 %collective-permute-start.18 = (f32[104,128]{1,0:T(8,128)S(1)}, f32[104,128]{1,0:T(8,128)S(1)}, u32[]{:S(2)}, u32[]{:S(2)}) collective-permute-start(f32[104,128]{1,0:T(8,128)S(1)} %add.31.left_ref), channel_id=1, source_target_pairs={{0,8},{1,9},{2,10},{3,11},{4,12},{5,13},{6,14},{7,15},{8,0},{9,1},... | collective-permute-start | bytes 159752 | tf_op jit(solution)/shard_map/ppermute | solution.py:547
  53.2 1.7 %collective-permute-start.20 = (f32[104,128]{1,0:T(8,128)S(1)}, f32[104,128]{1,0:T(8,128)S(1)}, u32[]{:S(2)}, u32[]{:S(2)}) collective-permute-start(f32[104,128]{1,0:T(8,128)S(1)} %add.33), channel_id=1, source_target_pairs={{0,2},{1,3},{2,0},{3,1},{4,6},{5,7},{6,4},{7,5},{8,10},{9,11},{10,... | collective-permute-start | bytes 159752 | tf_op jit(solution)/shard_map/ppermute | solution.py:547
  55.9 1.0 %transport.29.refs_5_ = f32[16,8192]{1,0:T(8,128)S(1)} custom-call(f32[128,128]{1,0:T(8,128)S(1)} %get-tuple-element.62.stream_ref, f32[128,8192]{1,0:T(8,128)S(1)} %get-tuple-element.111.f_ref), custom_call_target="tpu_custom_call" | custom-call | tf_op jit(solution)/shard_map/transport/pallas_call | solution.py:295
  60.1 3.1 %finish.1 = (f32[128,8192]{1,0:T(8,128)}, f32[8,8192]{1,0:T(8,128)}) custom-call(f32[16,8192]{1,0:T(8,128)S(1)} %transport.24.refs_0_, f32[16,8192]{1,0:T(8,128)S(1)} %transport.25.refs_1_, f32[16,8192]{1,0:T(8,128)S(1)} %transport.26.refs_2_, f32[16,8192]{1,0:T(8,128)S(1)} %transport.27.refs_3_, f32[16,8192]{1,0:T(8,128)S(1)} %transport.28.refs_4_, ...), custom_call_target="tpu_custom_call" | custom-call | tf_op jit(solution)/shard_map/finish/pallas_call | solution.py:509
  (72 shorter events, 18.3 us)
Async XLA Ops:
  6.1 1.6 %collective-permute-start = (f32[416,128]{1,0:T(8,128)S(1)}, f32[416,128]{1,0:T(8,128)S(1)}, u32[]{:S(2)}, u32[]{:S(2)}) collective-permute-start(f32[416,128]{1,0:T(8,128)S(1)} %slice_select_fusion.1), channel_id=1, source_target_pairs={{0,1},{1,0},{2,3},{3,2},{4,5},{5,4},{6,7},{7,6},{8,9},{9,8},{10,11... | collective-permute-start | bytes 638984 | tf_op jit(solution)/shard_map/ppermute | solution.py:547
  7.8 5.1 %collective-permute-start.1 = (f32[104,128]{1,0:T(8,128)S(1)}, f32[104,128]{1,0:T(8,128)S(1)}, u32[]{:S(2)}, u32[]{:S(2)}) collective-permute-start(f32[104,128]{1,0:T(8,128)S(1)} %get-tuple-element.68), channel_id=1, source_target_pairs={{0,2},{1,3},{2,0},{3,1},{4,6},{5,7},{6,4},{7,5},{8,10},{9,11},{10,... | collective-permute-start | bytes 159752 | tf_op jit(solution)/shard_map/ppermute | solution.py:547
  10.7 4.5 %collective-permute-start.3 = (f32[104,128]{1,0:T(8,128)S(1)}, f32[104,128]{1,0:T(8,128)S(1)}, u32[]{:S(2)}, u32[]{:S(2)}) collective-permute-start(f32[104,128]{1,0:T(8,128)S(1)} %get-tuple-element.69), channel_id=1, source_target_pairs={{0,2},{1,3},{2,0},{3,1},{4,6},{5,7},{6,4},{7,5},{8,10},{9,11},{10,... | collective-permute-start | bytes 159752 | tf_op jit(solution)/shard_map/ppermute | solution.py:547
  12.9 5.0 %collective-permute-start.2 = (f32[104,128]{1,0:T(8,128)S(1)}, f32[104,128]{1,0:T(8,128)S(1)}, u32[]{:S(2)}, u32[]{:S(2)}) collective-permute-start(f32[104,128]{1,0:T(8,128)S(1)} %add.22.left_ref), channel_id=1, source_target_pairs={{0,4},{1,5},{2,6},{3,7},{4,0},{5,1},{6,2},{7,3},{8,12},{9,13},{10,... | collective-permute-start | bytes 159752 | tf_op jit(solution)/shard_map/ppermute | solution.py:547
  15.2 5.4 %collective-permute-start.5 = (f32[104,128]{1,0:T(8,128)S(1)}, f32[104,128]{1,0:T(8,128)S(1)}, u32[]{:S(2)}, u32[]{:S(2)}) collective-permute-start(f32[104,128]{1,0:T(8,128)S(1)} %add.23.left_ref), channel_id=1, source_target_pairs={{0,4},{1,5},{2,6},{3,7},{4,0},{5,1},{6,2},{7,3},{8,12},{9,13},{10,... | collective-permute-start | bytes 159752 | tf_op jit(solution)/shard_map/ppermute | solution.py:547
  17.8 6.5 %collective-permute-start.4 = (f32[104,128]{1,0:T(8,128)S(1)}, f32[104,128]{1,0:T(8,128)S(1)}, u32[]{:S(2)}, u32[]{:S(2)}) collective-permute-start(f32[104,128]{1,0:T(8,128)S(1)} %add.24.left_ref), channel_id=1, source_target_pairs={{0,8},{1,9},{2,10},{3,11},{4,12},{5,13},{6,14},{7,15},{8,0},{9,1},... | collective-permute-start | bytes 159752 | tf_op jit(solution)/shard_map/ppermute | solution.py:547
  20.7 5.2 %collective-permute-start.7 = (f32[104,128]{1,0:T(8,128)S(1)}, f32[104,128]{1,0:T(8,128)S(1)}, u32[]{:S(2)}, u32[]{:S(2)}) collective-permute-start(f32[104,128]{1,0:T(8,128)S(1)} %add.25.left_ref), channel_id=1, source_target_pairs={{0,8},{1,9},{2,10},{3,11},{4,12},{5,13},{6,14},{7,15},{8,0},{9,1},... | collective-permute-start | bytes 159752 | tf_op jit(solution)/shard_map/ppermute | solution.py:547
  24.4 5.0 %collective-permute-start.6 = (f32[104,128]{1,0:T(8,128)S(1)}, f32[104,128]{1,0:T(8,128)S(1)}, u32[]{:S(2)}, u32[]{:S(2)}) collective-permute-start(f32[104,128]{1,0:T(8,128)S(1)} %add.26), channel_id=1, source_target_pairs={{0,2},{1,3},{2,0},{3,1},{4,6},{5,7},{6,4},{7,5},{8,10},{9,11},{10,... | collective-permute-start | bytes 159752 | tf_op jit(solution)/shard_map/ppermute | solution.py:547
  25.9 4.2 %collective-permute-start.9 = (f32[104,128]{1,0:T(8,128)S(1)}, f32[104,128]{1,0:T(8,128)S(1)}, u32[]{:S(2)}, u32[]{:S(2)}) collective-permute-start(f32[104,128]{1,0:T(8,128)S(1)} %add.27), channel_id=1, source_target_pairs={{0,2},{1,3},{2,0},{3,1},{4,6},{5,7},{6,4},{7,5},{8,10},{9,11},{10,... | collective-permute-start | bytes 159752 | tf_op jit(solution)/shard_map/ppermute | solution.py:547
  29.4 1.7 %collective-permute-start.8 = (f32[208,128]{1,0:T(8,128)S(1)}, f32[208,128]{1,0:T(8,128)S(1)}, u32[]{:S(2)}, u32[]{:S(2)}) collective-permute-start(f32[208,128]{1,0:T(8,128)S(1)} %pad_maximum_fusion.2), channel_id=1, source_target_pairs={{0,1},{1,0},{2,3},{3,2},{4,5},{5,4},{6,7},{7,6},{8,9},{9,8},{10,11... | collective-permute-start | bytes 319496 | tf_op jit(solution)/shard_map/ppermute | solution.py:547
  30.1 1.4 %collective-permute-start.10 = (f32[208,128]{1,0:T(8,128)S(1)}, f32[208,128]{1,0:T(8,128)S(1)}, u32[]{:S(2)}, u32[]{:S(2)}) collective-permute-start(f32[208,128]{1,0:T(8,128)S(1)} %pad_maximum_fusion.3), channel_id=1, source_target_pairs={{0,1},{1,0},{2,3},{3,2},{4,5},{5,4},{6,7},{7,6},{8,9},{9,8},{10,11... | collective-permute-start | bytes 319496 | tf_op jit(solution)/shard_map/ppermute | solution.py:547
  35.6 1.5 %collective-permute-start.11 = (f32[416,128]{1,0:T(8,128)S(1)}, f32[416,128]{1,0:T(8,128)S(1)}, u32[]{:S(2)}, u32[]{:S(2)}) collective-permute-start(f32[416,128]{1,0:T(8,128)S(1)} %slice_select_fusion), channel_id=1, source_target_pairs={{0,1},{1,0},{2,3},{3,2},{4,5},{5,4},{6,7},{7,6},{8,9},{9,8},{10,11... | collective-permute-start | bytes 638984 | tf_op jit(solution)/shard_map/ppermute | solution.py:547
  37.2 4.4 %collective-permute-start.12 = (f32[104,128]{1,0:T(8,128)S(1)}, f32[104,128]{1,0:T(8,128)S(1)}, u32[]{:S(2)}, u32[]{:S(2)}) collective-permute-start(f32[104,128]{1,0:T(8,128)S(1)} %get-tuple-element.95), channel_id=1, source_target_pairs={{0,2},{1,3},{2,0},{3,1},{4,6},{5,7},{6,4},{7,5},{8,10},{9,11},{10,... | collective-permute-start | bytes 159752 | tf_op jit(solution)/shard_map/ppermute | solution.py:547
  38.8 4.1 %collective-permute-start.14 = (f32[104,128]{1,0:T(8,128)S(1)}, f32[104,128]{1,0:T(8,128)S(1)}, u32[]{:S(2)}, u32[]{:S(2)}) collective-permute-start(f32[104,128]{1,0:T(8,128)S(1)} %get-tuple-element.96), channel_id=1, source_target_pairs={{0,2},{1,3},{2,0},{3,1},{4,6},{5,7},{6,4},{7,5},{8,10},{9,11},{10,... | collective-permute-start | bytes 159752 | tf_op jit(solution)/shard_map/ppermute | solution.py:547
  41.6 4.3 %collective-permute-start.13 = (f32[104,128]{1,0:T(8,128)S(1)}, f32[104,128]{1,0:T(8,128)S(1)}, u32[]{:S(2)}, u32[]{:S(2)}) collective-permute-start(f32[104,128]{1,0:T(8,128)S(1)} %add.28.left_ref), channel_id=1, source_target_pairs={{0,4},{1,5},{2,6},{3,7},{4,0},{5,1},{6,2},{7,3},{8,12},{9,13},{10,... | collective-permute-start | bytes 159752 | tf_op jit(solution)/shard_map/ppermute | solution.py:547
  42.9 5.2 %collective-permute-start.16 = (f32[104,128]{1,0:T(8,128)S(1)}, f32[104,128]{1,0:T(8,128)S(1)}, u32[]{:S(2)}, u32[]{:S(2)}) collective-permute-start(f32[104,128]{1,0:T(8,128)S(1)} %add.29.left_ref), channel_id=1, source_target_pairs={{0,4},{1,5},{2,6},{3,7},{4,0},{5,1},{6,2},{7,3},{8,12},{9,13},{10,... | collective-permute-start | bytes 159752 | tf_op jit(solution)/shard_map/ppermute | solution.py:547
  46.0 6.1 %collective-permute-start.15 = (f32[104,128]{1,0:T(8,128)S(1)}, f32[104,128]{1,0:T(8,128)S(1)}, u32[]{:S(2)}, u32[]{:S(2)}) collective-permute-start(f32[104,128]{1,0:T(8,128)S(1)} %add.30.left_ref), channel_id=1, source_target_pairs={{0,8},{1,9},{2,10},{3,11},{4,12},{5,13},{6,14},{7,15},{8,0},{9,1},... | collective-permute-start | bytes 159752 | tf_op jit(solution)/shard_map/ppermute | solution.py:547
  48.1 5.1 %collective-permute-start.18 = (f32[104,128]{1,0:T(8,128)S(1)}, f32[104,128]{1,0:T(8,128)S(1)}, u32[]{:S(2)}, u32[]{:S(2)}) collective-permute-start(f32[104,128]{1,0:T(8,128)S(1)} %add.31.left_ref), channel_id=1, source_target_pairs={{0,8},{1,9},{2,10},{3,11},{4,12},{5,13},{6,14},{7,15},{8,0},{9,1},... | collective-permute-start | bytes 159752 | tf_op jit(solution)/shard_map/ppermute | solution.py:547
  52.1 4.9 %collective-permute-start.17 = (f32[104,128]{1,0:T(8,128)S(1)}, f32[104,128]{1,0:T(8,128)S(1)}, u32[]{:S(2)}, u32[]{:S(2)}) collective-permute-start(f32[104,128]{1,0:T(8,128)S(1)} %add.32), channel_id=1, source_target_pairs={{0,2},{1,3},{2,0},{3,1},{4,6},{5,7},{6,4},{7,5},{8,10},{9,11},{10,... | collective-permute-start | bytes 159752 | tf_op jit(solution)/shard_map/ppermute | solution.py:547
  53.2 4.2 %collective-permute-start.20 = (f32[104,128]{1,0:T(8,128)S(1)}, f32[104,128]{1,0:T(8,128)S(1)}, u32[]{:S(2)}, u32[]{:S(2)}) collective-permute-start(f32[104,128]{1,0:T(8,128)S(1)} %add.33), channel_id=1, source_target_pairs={{0,2},{1,3},{2,0},{3,1},{4,6},{5,7},{6,4},{7,5},{8,10},{9,11},{10,... | collective-permute-start | bytes 159752 | tf_op jit(solution)/shard_map/ppermute | solution.py:547
  57.4 1.7 %collective-permute-start.19 = (f32[208,128]{1,0:T(8,128)S(1)}, f32[208,128]{1,0:T(8,128)S(1)}, u32[]{:S(2)}, u32[]{:S(2)}) collective-permute-start(f32[208,128]{1,0:T(8,128)S(1)} %pad_maximum_fusion.4), channel_id=1, source_target_pairs={{0,1},{1,0},{2,3},{3,2},{4,5},{5,4},{6,7},{7,6},{8,9},{9,8},{10,11... | collective-permute-start | bytes 319496 | tf_op jit(solution)/shard_map/ppermute | solution.py:547
  57.5 1.6 %collective-permute-start.21 = (f32[208,128]{1,0:T(8,128)S(1)}, f32[208,128]{1,0:T(8,128)S(1)}, u32[]{:S(2)}, u32[]{:S(2)}) collective-permute-start(f32[208,128]{1,0:T(8,128)S(1)} %pad_maximum_fusion.5), channel_id=1, source_target_pairs={{0,1},{1,0},{2,3},{3,2},{4,5},{5,4},{6,7},{7,6},{8,9},{9,8},{10,11... | collective-permute-start | bytes 319496 | tf_op jit(solution)/shard_map/ppermute | solution.py:547

commit v9 on v8

--- a/solution.py
+++ b/solution.py
@@ -125,13 +125,17 @@
     return jnp.concatenate(high + low, axis=0)
 
 
-def in_turn(front, back, tiles):
-    made = front(0)
+def tile_cells(tile):
+    return pl.ds(pl.multiple_of(tile * TILE, TILE), TILE)
+
+
+def in_turn(front, back, first, tiles):
+    made = front(first)
     for tile in range(1, tiles):
-        upcoming = front(tile)
-        back(tile - 1, made)
+        upcoming = front(first + tile)
+        back(first + tile - 1, made)
         made = upcoming
-    back(tiles - 1, made)
+    back(first + tiles - 1, made)
 
 
 def start_kernel(
@@ -155,16 +159,15 @@
     ]
     for copy in small:
         copy.start()
-    copies = [
-        pltpu.make_async_copy(
-            deviation_hbm.at[:, pl.ds(chunk * width, width)],
-            deviation_ref.at[:, pl.ds(chunk * width, width)],
-            sems.at[chunk],
+
+    def arrival(chunk):
+        there = pl.ds(pl.multiple_of(chunk * width, width), width)
+        return pltpu.make_async_copy(
+            deviation_hbm.at[:, there], deviation_ref.at[:, there], sems.at[chunk]
         )
-        for chunk in range(CHUNKS)
-    ]
-    for copy in copies:
-        copy.start()
+
+    for chunk in range(CHUNKS):
+        arrival(chunk).start()
     small[0].wait()
     exponent_table, polynomial_table, table = make_tables(vel_ref[...], total_count)
     exponent_ref[...] = exponent_table
@@ -174,7 +177,7 @@
     for copy in small[1:]:
         copy.wait()
     def front(tile):
-        here = pl.ds(tile * TILE, TILE)
+        here = tile_cells(tile)
         density, flow, thermal = density_ref[:, here], flow_ref[:, here], thermal_ref[:, here]
         rate = (0.5 * LOG2E) / thermal
         speed_sq = flow[0:1] * flow[0:1] + flow[1:2] * flow[1:2] + flow[2:3] * flow[2:3]
@@ -189,14 +192,14 @@
         return store_tile(f_ref, here, f_ref.shape[0], values_of)
 
     def back(tile, split):
-        store_moments(moments_ref, table, split, tile, cells // LANES)
-
-    def front_when_here(tile):
-        if tile * TILE % width == 0:
-            copies[tile * TILE // width].wait()
-        return front(tile)
-
-    in_turn(front_when_here, back, cells // TILE)
+        store_moments(moments_ref, table_ref[...], split, tile, cells // LANES)
+
+    def step(chunk, carry):
+        arrival(chunk).wait()
+        in_turn(front, back, chunk * (width // TILE), width // TILE)
+        return carry
+
+    lax.fori_loop(0, CHUNKS, step, 0)
 
 
 def start_call(velocities, density, flow, thermal, deviation, total_count):
@@ -432,7 +435,7 @@
 def relaxed(g_refs, here, coef_ref, exponent_ref, polynomial_ref, tile):
     per_tile = TILE // LANES
     parts = [
-        coef_ref[pl.ds((tile * per_tile + part) * COEF, COEF), :]
+        coef_ref[pl.ds(pl.multiple_of((tile * per_tile + part) * COEF, 8), COEF), :]
         for part in range(per_tile)
     ]
     coefficients = jnp.concatenate(parts, axis=1)
@@ -456,14 +459,18 @@
     cells = f_ref.shape[1]
 
     def front(tile):
-        here = pl.ds(tile * TILE, TILE)
+        here = tile_cells(tile)
         values_of = relaxed(g_refs, here, coef_ref, exponent_ref, polynomial_ref, tile)
         return store_tile(f_ref, here, f_ref.shape[0], values_of)
 
     def back(tile, split):
         store_moments(moments_ref, table_ref[...], split, tile, cells // LANES)
 
-    in_turn(front, back, cells // TILE)
+    def step(chunk, carry):
+        in_turn(front, back, chunk * (cells // CHUNKS // TILE), cells // CHUNKS // TILE)
+        return carry
+
+    lax.fori_loop(0, CHUNKS, step, 0)
 
 
 def update_call(g, coefficients, tables, table):
@@ -486,22 +493,29 @@
     coef_ref, macro_ref, exponent_ref, polynomial_ref, f_ref, fields_ref, held, sems = refs[PARTS:]
     cells = held.shape[1]
     width = cells // CHUNKS
-    copies = []
-    for chunk in range(CHUNKS):
+
+    def departure(chunk):
+        there = pl.ds(pl.multiple_of(chunk * width, width), width)
+        return pltpu.make_async_copy(held.at[:, there], f_ref.at[:, there], sems.at[chunk])
+
+    def step(chunk, carry):
         for local in range(width // TILE):
             tile = chunk * (width // TILE) + local
-            here = pl.ds(tile * TILE, TILE)
+            here = tile_cells(tile)
             values_of = relaxed(g_refs, here, coef_ref, exponent_ref, polynomial_ref, tile)
             for first in range(0, held.shape[0], ROWS):
                 held[pl.ds(first, ROWS), here] = values_of(pl.ds(first, ROWS))
-            for block in range(tile * TILE // LANES, (tile + 1) * TILE // LANES):
-                fields_ref[:, pl.ds(block * LANES, LANES)] = macro_ref[pl.ds(block * 8, 8), :]
-        there = pl.ds(chunk * width, width)
-        copy = pltpu.make_async_copy(held.at[:, there], f_ref.at[:, there], sems.at[chunk])
-        copy.start()
-        copies.append(copy)
-    for copy in copies:
-        copy.wait()
+            for part in range(TILE // LANES):
+                block = tile * (TILE // LANES) + part
+                fields_ref[:, pl.ds(pl.multiple_of(block * LANES, LANES), LANES)] = macro_ref[
+                    pl.ds(pl.multiple_of(block * 8, 8), 8), :
+                ]
+        departure(chunk).start()
+        return carry
+
+    lax.fori_loop(0, CHUNKS, step, 0)
+    for chunk in range(CHUNKS):
+        departure(chunk).wait()
 
 
 def finish_call(g, coefficients, macro, tables):

time: 63.5 us -> 65.6 us (1.033)
  Pallas kernels: 29.4 us -> 31.7 us
    pallas_call x1, Pallas kernels: 3.2 us -> 4.66 us  [update_call(): pl.pallas_call(update_kernel, out_shape=(pltpu.VMEM((rows * PARTS, cells)...]
    pallas_call x1, Pallas kernels: 3.06 us -> 3.9 us  [finish_call(): pl.pallas_call(finish_kernel, out_shape=(jax.ShapeDtypeStruct((rows * PAR...]
where the time goes in v9:
time: 65.6 us; the launch traced here: 65.5 us
  Pallas kernels  31.7 us (48%)
  starting transfers between devices  27 us (41%)
  waiting for transfers between devices  5.29 us (8%)
  between operations  1.02 us (2%)
    ppermute x22, starting transfers between devices, swap(): lax.ppermute(values, 'vel', [(device, device ^ stride) for device in rang...  27 us
    pallas_call x16, Pallas kernels, transport_call(): pl.pallas_call(functools.partial(transport_kernel, part * rows), out_shap...  15.9 us
    pallas_call x1, Pallas kernels, start_call(): pl.pallas_call(functools.partial(start_kernel, total_count), out_shape=(p...  5.4 us
    ppermute x22, waiting for transfers between devices, swap(): lax.ppermute(values, 'vel', [(device, device ^ stride) for device in rang...  5.29 us
    pallas_call x1, Pallas kernels, update_call(): pl.pallas_call(update_kernel, out_shape=(pltpu.VMEM((rows * PARTS, cells)...  4.66 us
    pallas_call x1, Pallas kernels, finish_call(): pl.pallas_call(finish_kernel, out_shape=(jax.ShapeDtypeStruct((rows * PAR...  3.9 us
    pallas_call x2, Pallas kernels, fluid_call(): pl.pallas_call(fluid_kernel, out_shape=shapes, in_specs=[WHOLE], out_spec...  1.71 us
  transfers between devices with their start and end apart: 22, of which 12 were waited for; matrix products, arithmetic and copies ran while one was open for 0% of the time, Pallas kernels for 25%

profile of v9, /device:TPU:0, one launch (start us, length us, event | category | flops | bytes accessed | tf_op | source)
XLA Modules:
  0.0 65.5 jit_solution(7750486405515338496)
XLA Ops:
  0.6 5.4 %start.1 = (f32[128,8192]{1,0:T(8,128)S(1)}, f32[832,128]{1,0:T(8,128)S(1)}, bf16[128,48]{1,0:T(8,128)(2,1)S(1)}, bf16[128,48]{1,0:T(8,128)(2,1)S(1)}, bf16[32,2...) custom-call(f32[3,128]{1,0:T(4,128)} %vel_hbm, f32[1,8192]{1,0:T(1,128)} %bitcast.2, f32[3,8192]{1,0:T(4,128)} %flow_hbm.1, ...), custom_call_target="tpu_custom_call" | custom-call | tf_op jit(solution)/shard_map/start/pallas_call | solution.py:207
  7.8 3.0 %collective-permute-start.1 = (f32[104,128]{1,0:T(8,128)S(1)}, f32[104,128]{1,0:T(8,128)S(1)}, u32[]{:S(2)}, u32[]{:S(2)}) collective-permute-start(f32[104,128]{1,0:T(8,128)S(1)} %get-tuple-element.68), channel_id=1, source_target_pairs={{0,2},{1,3},{2,0},{3,1},{4,6},{5,7},{6,4},{7,5},{8,10},{9,11},{10,... | collective-permute-start | bytes 159752 | tf_op jit(solution)/shard_map/ppermute | solution.py:561
  11.8 1.0 %transport.17.refs_1_ = f32[16,8192]{1,0:T(8,128)S(1)} custom-call(f32[128,128]{1,0:T(8,128)S(1)} %get-tuple-element.62.stream_ref, f32[128,8192]{1,0:T(8,128)S(1)} %get-tuple-element.84.f_ref), custom_call_target="tpu_custom_call" | custom-call | tf_op jit(solution)/shard_map/transport/pallas_call | solution.py:298
  12.9 2.4 %collective-permute-start.2 = (f32[104,128]{1,0:T(8,128)S(1)}, f32[104,128]{1,0:T(8,128)S(1)}, u32[]{:S(2)}, u32[]{:S(2)}) collective-permute-start(f32[104,128]{1,0:T(8,128)S(1)} %add.22.left_ref), channel_id=1, source_target_pairs={{0,4},{1,5},{2,6},{3,7},{4,0},{5,1},{6,2},{7,3},{8,12},{9,13},{10,... | collective-permute-start | bytes 159752 | tf_op jit(solution)/shard_map/ppermute | solution.py:561
  15.2 1.3 %collective-permute-start.5 = (f32[104,128]{1,0:T(8,128)S(1)}, f32[104,128]{1,0:T(8,128)S(1)}, u32[]{:S(2)}, u32[]{:S(2)}) collective-permute-start(f32[104,128]{1,0:T(8,128)S(1)} %add.23.left_ref), channel_id=1, source_target_pairs={{0,4},{1,5},{2,6},{3,7},{4,0},{5,1},{6,2},{7,3},{8,12},{9,13},{10,... | collective-permute-start | bytes 159752 | tf_op jit(solution)/shard_map/ppermute | solution.py:561
  17.8 2.8 %collective-permute-start.4 = (f32[104,128]{1,0:T(8,128)S(1)}, f32[104,128]{1,0:T(8,128)S(1)}, u32[]{:S(2)}, u32[]{:S(2)}) collective-permute-start(f32[104,128]{1,0:T(8,128)S(1)} %add.24.left_ref), channel_id=1, source_target_pairs={{0,8},{1,9},{2,10},{3,11},{4,12},{5,13},{6,14},{7,15},{8,0},{9,1},... | collective-permute-start | bytes 159752 | tf_op jit(solution)/shard_map/ppermute | solution.py:561
  20.7 1.6 %collective-permute-start.7 = (f32[104,128]{1,0:T(8,128)S(1)}, f32[104,128]{1,0:T(8,128)S(1)}, u32[]{:S(2)}, u32[]{:S(2)}) collective-permute-start(f32[104,128]{1,0:T(8,128)S(1)} %add.25.left_ref), channel_id=1, source_target_pairs={{0,8},{1,9},{2,10},{3,11},{4,12},{5,13},{6,14},{7,15},{8,0},{9,1},... | collective-permute-start | bytes 159752 | tf_op jit(solution)/shard_map/ppermute | solution.py:561
  22.2 1.0 %transport.20.refs_4_ = f32[16,8192]{1,0:T(8,128)S(1)} custom-call(f32[128,128]{1,0:T(8,128)S(1)} %get-tuple-element.62.stream_ref, f32[128,8192]{1,0:T(8,128)S(1)} %get-tuple-element.84.f_ref), custom_call_target="tpu_custom_call" | custom-call | tf_op jit(solution)/shard_map/transport/pallas_call | solution.py:298
  23.2 1.1 %collective-permute-done.4.right_ref = f32[104,128]{1,0:T(8,128)S(1)} collective-permute-done((f32[104,128]{1,0:T(8,128)S(1)}, f32[104,128]{1,0:T(8,128)S(1)}, u32[]{:S(2)}, u32[]{:S(2)}) %collective-permute-start.4) | collective-permute-done | bytes 53280 | tf_op jit(solution)/shard_map/ppermute | solution.py:561
  24.4 1.5 %collective-permute-start.6 = (f32[104,128]{1,0:T(8,128)S(1)}, f32[104,128]{1,0:T(8,128)S(1)}, u32[]{:S(2)}, u32[]{:S(2)}) collective-permute-start(f32[104,128]{1,0:T(8,128)S(1)} %add.26), channel_id=1, source_target_pairs={{0,2},{1,3},{2,0},{3,1},{4,6},{5,7},{6,4},{7,5},{8,10},{9,11},{10,... | collective-permute-start | bytes 159752 | tf_op jit(solution)/shard_map/ppermute | solution.py:561
  25.9 1.5 %collective-permute-start.9 = (f32[104,128]{1,0:T(8,128)S(1)}, f32[104,128]{1,0:T(8,128)S(1)}, u32[]{:S(2)}, u32[]{:S(2)}) collective-permute-start(f32[104,128]{1,0:T(8,128)S(1)} %add.27), channel_id=1, source_target_pairs={{0,2},{1,3},{2,0},{3,1},{4,6},{5,7},{6,4},{7,5},{8,10},{9,11},{10,... | collective-permute-start | bytes 159752 | tf_op jit(solution)/shard_map/ppermute | solution.py:561
  28.4 1.0 %transport.21.refs_5_ = f32[16,8192]{1,0:T(8,128)S(1)} custom-call(f32[128,128]{1,0:T(8,128)S(1)} %get-tuple-element.62.stream_ref, f32[128,8192]{1,0:T(8,128)S(1)} %get-tuple-element.84.f_ref), custom_call_target="tpu_custom_call" | custom-call | tf_op jit(solution)/shard_map/transport/pallas_call | solution.py:298
  30.2 1.0 %transport.23.refs_7_ = f32[16,8192]{1,0:T(8,128)S(1)} custom-call(f32[128,128]{1,0:T(8,128)S(1)} %get-tuple-element.62.stream_ref, f32[128,8192]{1,0:T(8,128)S(1)} %get-tuple-element.84.f_ref), custom_call_target="tpu_custom_call" | custom-call | tf_op jit(solution)/shard_map/transport/pallas_call | solution.py:298
  32.4 4.7 %update.1 = (f32[128,8192]{1,0:T(8,128)S(1)}, f32[832,128]{1,0:T(8,128)S(1)}) custom-call(f32[16,8192]{1,0:T(8,128)S(1)} %transport.16.refs_0_, f32[16,8192]{1,0:T(8,128)S(1)} %transport.17.refs_1_, f32[16,8192]{1,0:T(8,128)S(1)} %transport.18.refs_2_, f32[16,8192]{1,0:T(8,128)S(1)} %transport.19.refs_3_, f32[16,8192]{1,0:T(8,128)S(1)} %transport.20.refs_4_, ...), custom_call_target="tpu_custom_call" | custom-call | tf_op jit(solution)/shard_map/update/pallas_call | solution.py:478
  38.7 1.5 %collective-permute-start.12 = (f32[104,128]{1,0:T(8,128)S(1)}, f32[104,128]{1,0:T(8,128)S(1)}, u32[]{:S(2)}, u32[]{:S(2)}) collective-permute-start(f32[104,128]{1,0:T(8,128)S(1)} %get-tuple-element.95), channel_id=1, source_target_pairs={{0,2},{1,3},{2,0},{3,1},{4,6},{5,7},{6,4},{7,5},{8,10},{9,11},{10,... | collective-permute-start | bytes 159752 | tf_op jit(solution)/shard_map/ppermute | solution.py:561
  40.8 1.0 %transport.26.refs_2_ = f32[16,8192]{1,0:T(8,128)S(1)} custom-call(f32[128,128]{1,0:T(8,128)S(1)} %get-tuple-element.62.stream_ref, f32[128,8192]{1,0:T(8,128)S(1)} %get-tuple-element.111.f_ref), custom_call_target="tpu_custom_call" | custom-call | tf_op jit(solution)/shard_map/transport/pallas_call | solution.py:298
  41.8 1.0 %transport.25.refs_1_ = f32[16,8192]{1,0:T(8,128)S(1)} custom-call(f32[128,128]{1,0:T(8,128)S(1)} %get-tuple-element.62.stream_ref, f32[128,8192]{1,0:T(8,128)S(1)} %get-tuple-element.111.f_ref), custom_call_target="tpu_custom_call" | custom-call | tf_op jit(solution)/shard_map/transport/pallas_call | solution.py:298
  43.1 1.2 %collective-permute-start.13 = (f32[104,128]{1,0:T(8,128)S(1)}, f32[104,128]{1,0:T(8,128)S(1)}, u32[]{:S(2)}, u32[]{:S(2)}) collective-permute-start(f32[104,128]{1,0:T(8,128)S(1)} %add.28.left_ref), channel_id=1, source_target_pairs={{0,4},{1,5},{2,6},{3,7},{4,0},{5,1},{6,2},{7,3},{8,12},{9,13},{10,... | collective-permute-start | bytes 159752 | tf_op jit(solution)/shard_map/ppermute | solution.py:561
  44.4 1.5 %collective-permute-start.16 = (f32[104,128]{1,0:T(8,128)S(1)}, f32[104,128]{1,0:T(8,128)S(1)}, u32[]{:S(2)}, u32[]{:S(2)}) collective-permute-start(f32[104,128]{1,0:T(8,128)S(1)} %add.29.left_ref), channel_id=1, source_target_pairs={{0,4},{1,5},{2,6},{3,7},{4,0},{5,1},{6,2},{7,3},{8,12},{9,13},{10,... | collective-permute-start | bytes 159752 | tf_op jit(solution)/shard_map/ppermute | solution.py:561
  47.4 2.1 %collective-permute-start.15 = (f32[104,128]{1,0:T(8,128)S(1)}, f32[104,128]{1,0:T(8,128)S(1)}, u32[]{:S(2)}, u32[]{:S(2)}) collective-permute-start(f32[104,128]{1,0:T(8,128)S(1)} %add.30.left_ref), channel_id=1, source_target_pairs={{0,8},{1,9},{2,10},{3,11},{4,12},{5,13},{6,14},{7,15},{8,0},{9,1},... | collective-permute-start | bytes 159752 | tf_op jit(solution)/shard_map/ppermute | solution.py:561
  49.6 2.1 %collective-permute-start.18 = (f32[104,128]{1,0:T(8,128)S(1)}, f32[104,128]{1,0:T(8,128)S(1)}, u32[]{:S(2)}, u32[]{:S(2)}) collective-permute-start(f32[104,128]{1,0:T(8,128)S(1)} %add.31.left_ref), channel_id=1, source_target_pairs={{0,8},{1,9},{2,10},{3,11},{4,12},{5,13},{6,14},{7,15},{8,0},{9,1},... | collective-permute-start | bytes 159752 | tf_op jit(solution)/shard_map/ppermute | solution.py:561
  54.7 1.7 %collective-permute-start.20 = (f32[104,128]{1,0:T(8,128)S(1)}, f32[104,128]{1,0:T(8,128)S(1)}, u32[]{:S(2)}, u32[]{:S(2)}) collective-permute-start(f32[104,128]{1,0:T(8,128)S(1)} %add.33), channel_id=1, source_target_pairs={{0,2},{1,3},{2,0},{3,1},{4,6},{5,7},{6,4},{7,5},{8,10},{9,11},{10,... | collective-permute-start | bytes 159752 | tf_op jit(solution)/shard_map/ppermute | solution.py:561
  57.4 1.0 %transport.29.refs_5_ = f32[16,8192]{1,0:T(8,128)S(1)} custom-call(f32[128,128]{1,0:T(8,128)S(1)} %get-tuple-element.62.stream_ref, f32[128,8192]{1,0:T(8,128)S(1)} %get-tuple-element.111.f_ref), custom_call_target="tpu_custom_call" | custom-call | tf_op jit(solution)/shard_map/transport/pallas_call | solution.py:298
  61.6 3.9 %finish.1 = (f32[128,8192]{1,0:T(8,128)}, f32[8,8192]{1,0:T(8,128)}) custom-call(f32[16,8192]{1,0:T(8,128)S(1)} %transport.24.refs_0_, f32[16,8192]{1,0:T(8,128)S(1)} %transport.25.refs_1_, f32[16,8192]{1,0:T(8,128)S(1)} %transport.26.refs_2_, f32[16,8192]{1,0:T(8,128)S(1)} %transport.27.refs_3_, f32[16,8192]{1,0:T(8,128)S(1)} %transport.28.refs_4_, ...), custom_call_target="tpu_custom_call" | custom-call | tf_op jit(solution)/shard_map/finish/pallas_call | solution.py:523
  (72 shorter events, 18.3 us)
Async XLA Ops:
  6.1 1.6 %collective-permute-start = (f32[416,128]{1,0:T(8,128)S(1)}, f32[416,128]{1,0:T(8,128)S(1)}, u32[]{:S(2)}, u32[]{:S(2)}) collective-permute-start(f32[416,128]{1,0:T(8,128)S(1)} %slice_select_fusion.1), channel_id=1, source_target_pairs={{0,1},{1,0},{2,3},{3,2},{4,5},{5,4},{6,7},{7,6},{8,9},{9,8},{10,11... | collective-permute-start | bytes 638984 | tf_op jit(solution)/shard_map/ppermute | solution.py:561
  7.8 5.1 %collective-permute-start.1 = (f32[104,128]{1,0:T(8,128)S(1)}, f32[104,128]{1,0:T(8,128)S(1)}, u32[]{:S(2)}, u32[]{:S(2)}) collective-permute-start(f32[104,128]{1,0:T(8,128)S(1)} %get-tuple-element.68), channel_id=1, source_target_pairs={{0,2},{1,3},{2,0},{3,1},{4,6},{5,7},{6,4},{7,5},{8,10},{9,11},{10,... | collective-permute-start | bytes 159752 | tf_op jit(solution)/shard_map/ppermute | solution.py:561
  10.7 4.5 %collective-permute-start.3 = (f32[104,128]{1,0:T(8,128)S(1)}, f32[104,128]{1,0:T(8,128)S(1)}, u32[]{:S(2)}, u32[]{:S(2)}) collective-permute-start(f32[104,128]{1,0:T(8,128)S(1)} %get-tuple-element.69), channel_id=1, source_target_pairs={{0,2},{1,3},{2,0},{3,1},{4,6},{5,7},{6,4},{7,5},{8,10},{9,11},{10,... | collective-permute-start | bytes 159752 | tf_op jit(solution)/shard_map/ppermute | solution.py:561
  12.9 5.0 %collective-permute-start.2 = (f32[104,128]{1,0:T(8,128)S(1)}, f32[104,128]{1,0:T(8,128)S(1)}, u32[]{:S(2)}, u32[]{:S(2)}) collective-permute-start(f32[104,128]{1,0:T(8,128)S(1)} %add.22.left_ref), channel_id=1, source_target_pairs={{0,4},{1,5},{2,6},{3,7},{4,0},{5,1},{6,2},{7,3},{8,12},{9,13},{10,... | collective-permute-start | bytes 159752 | tf_op jit(solution)/shard_map/ppermute | solution.py:561
  15.2 5.4 %collective-permute-start.5 = (f32[104,128]{1,0:T(8,128)S(1)}, f32[104,128]{1,0:T(8,128)S(1)}, u32[]{:S(2)}, u32[]{:S(2)}) collective-permute-start(f32[104,128]{1,0:T(8,128)S(1)} %add.23.left_ref), channel_id=1, source_target_pairs={{0,4},{1,5},{2,6},{3,7},{4,0},{5,1},{6,2},{7,3},{8,12},{9,13},{10,... | collective-permute-start | bytes 159752 | tf_op jit(solution)/shard_map/ppermute | solution.py:561
  17.8 6.5 %collective-permute-start.4 = (f32[104,128]{1,0:T(8,128)S(1)}, f32[104,128]{1,0:T(8,128)S(1)}, u32[]{:S(2)}, u32[]{:S(2)}) collective-permute-start(f32[104,128]{1,0:T(8,128)S(1)} %add.24.left_ref), channel_id=1, source_target_pairs={{0,8},{1,9},{2,10},{3,11},{4,12},{5,13},{6,14},{7,15},{8,0},{9,1},... | collective-permute-start | bytes 159752 | tf_op jit(solution)/shard_map/ppermute | solution.py:561
  20.7 5.2 %collective-permute-start.7 = (f32[104,128]{1,0:T(8,128)S(1)}, f32[104,128]{1,0:T(8,128)S(1)}, u32[]{:S(2)}, u32[]{:S(2)}) collective-permute-start(f32[104,128]{1,0:T(8,128)S(1)} %add.25.left_ref), channel_id=1, source_target_pairs={{0,8},{1,9},{2,10},{3,11},{4,12},{5,13},{6,14},{7,15},{8,0},{9,1},... | collective-permute-start | bytes 159752 | tf_op jit(solution)/shard_map/ppermute | solution.py:561
  24.4 5.0 %collective-permute-start.6 = (f32[104,128]{1,0:T(8,128)S(1)}, f32[104,128]{1,0:T(8,128)S(1)}, u32[]{:S(2)}, u32[]{:S(2)}) collective-permute-start(f32[104,128]{1,0:T(8,128)S(1)} %add.26), channel_id=1, source_target_pairs={{0,2},{1,3},{2,0},{3,1},{4,6},{5,7},{6,4},{7,5},{8,10},{9,11},{10,... | collective-permute-start | bytes 159752 | tf_op jit(solution)/shard_map/ppermute | solution.py:561
  25.9 4.2 %collective-permute-start.9 = (f32[104,128]{1,0:T(8,128)S(1)}, f32[104,128]{1,0:T(8,128)S(1)}, u32[]{:S(2)}, u32[]{:S(2)}) collective-permute-start(f32[104,128]{1,0:T(8,128)S(1)} %add.27), channel_id=1, source_target_pairs={{0,2},{1,3},{2,0},{3,1},{4,6},{5,7},{6,4},{7,5},{8,10},{9,11},{10,... | collective-permute-start | bytes 159752 | tf_op jit(solution)/shard_map/ppermute | solution.py:561
  29.4 1.7 %collective-permute-start.8 = (f32[208,128]{1,0:T(8,128)S(1)}, f32[208,128]{1,0:T(8,128)S(1)}, u32[]{:S(2)}, u32[]{:S(2)}) collective-permute-start(f32[208,128]{1,0:T(8,128)S(1)} %pad_maximum_fusion.2), channel_id=1, source_target_pairs={{0,1},{1,0},{2,3},{3,2},{4,5},{5,4},{6,7},{7,6},{8,9},{9,8},{10,11... | collective-permute-start | bytes 319496 | tf_op jit(solution)/shard_map/ppermute | solution.py:561
  30.1 1.4 %collective-permute-start.10 = (f32[208,128]{1,0:T(8,128)S(1)}, f32[208,128]{1,0:T(8,128)S(1)}, u32[]{:S(2)}, u32[]{:S(2)}) collective-permute-start(f32[208,128]{1,0:T(8,128)S(1)} %pad_maximum_fusion.3), channel_id=1, source_target_pairs={{0,1},{1,0},{2,3},{3,2},{4,5},{5,4},{6,7},{7,6},{8,9},{9,8},{10,11... | collective-permute-start | bytes 319496 | tf_op jit(solution)/shard_map/ppermute | solution.py:561
  37.1 1.5 %collective-permute-start.11 = (f32[416,128]{1,0:T(8,128)S(1)}, f32[416,128]{1,0:T(8,128)S(1)}, u32[]{:S(2)}, u32[]{:S(2)}) collective-permute-start(f32[416,128]{1,0:T(8,128)S(1)} %slice_select_fusion), channel_id=1, source_target_pairs={{0,1},{1,0},{2,3},{3,2},{4,5},{5,4},{6,7},{7,6},{8,9},{9,8},{10,11... | collective-permute-start | bytes 638984 | tf_op jit(solution)/shard_map/ppermute | solution.py:561
  38.7 4.4 %collective-permute-start.12 = (f32[104,128]{1,0:T(8,128)S(1)}, f32[104,128]{1,0:T(8,128)S(1)}, u32[]{:S(2)}, u32[]{:S(2)}) collective-permute-start(f32[104,128]{1,0:T(8,128)S(1)} %get-tuple-element.95), channel_id=1, source_target_pairs={{0,2},{1,3},{2,0},{3,1},{4,6},{5,7},{6,4},{7,5},{8,10},{9,11},{10,... | collective-permute-start | bytes 159752 | tf_op jit(solution)/shard_map/ppermute | solution.py:561
  40.2 4.1 %collective-permute-start.14 = (f32[104,128]{1,0:T(8,128)S(1)}, f32[104,128]{1,0:T(8,128)S(1)}, u32[]{:S(2)}, u32[]{:S(2)}) collective-permute-start(f32[104,128]{1,0:T(8,128)S(1)} %get-tuple-element.96), channel_id=1, source_target_pairs={{0,2},{1,3},{2,0},{3,1},{4,6},{5,7},{6,4},{7,5},{8,10},{9,11},{10,... | collective-permute-start | bytes 159752 | tf_op jit(solution)/shard_map/ppermute | solution.py:561
  43.1 4.3 %collective-permute-start.13 = (f32[104,128]{1,0:T(8,128)S(1)}, f32[104,128]{1,0:T(8,128)S(1)}, u32[]{:S(2)}, u32[]{:S(2)}) collective-permute-start(f32[104,128]{1,0:T(8,128)S(1)} %add.28.left_ref), channel_id=1, source_target_pairs={{0,4},{1,5},{2,6},{3,7},{4,0},{5,1},{6,2},{7,3},{8,12},{9,13},{10,... | collective-permute-start | bytes 159752 | tf_op jit(solution)/shard_map/ppermute | solution.py:561
  44.4 5.2 %collective-permute-start.16 = (f32[104,128]{1,0:T(8,128)S(1)}, f32[104,128]{1,0:T(8,128)S(1)}, u32[]{:S(2)}, u32[]{:S(2)}) collective-permute-start(f32[104,128]{1,0:T(8,128)S(1)} %add.29.left_ref), channel_id=1, source_target_pairs={{0,4},{1,5},{2,6},{3,7},{4,0},{5,1},{6,2},{7,3},{8,12},{9,13},{10,... | collective-permute-start | bytes 159752 | tf_op jit(solution)/shard_map/ppermute | solution.py:561
  47.4 6.1 %collective-permute-start.15 = (f32[104,128]{1,0:T(8,128)S(1)}, f32[104,128]{1,0:T(8,128)S(1)}, u32[]{:S(2)}, u32[]{:S(2)}) collective-permute-start(f32[104,128]{1,0:T(8,128)S(1)} %add.30.left_ref), channel_id=1, source_target_pairs={{0,8},{1,9},{2,10},{3,11},{4,12},{5,13},{6,14},{7,15},{8,0},{9,1},... | collective-permute-start | bytes 159752 | tf_op jit(solution)/shard_map/ppermute | solution.py:561
  49.6 5.1 %collective-permute-start.18 = (f32[104,128]{1,0:T(8,128)S(1)}, f32[104,128]{1,0:T(8,128)S(1)}, u32[]{:S(2)}, u32[]{:S(2)}) collective-permute-start(f32[104,128]{1,0:T(8,128)S(1)} %add.31.left_ref), channel_id=1, source_target_pairs={{0,8},{1,9},{2,10},{3,11},{4,12},{5,13},{6,14},{7,15},{8,0},{9,1},... | collective-permute-start | bytes 159752 | tf_op jit(solution)/shard_map/ppermute | solution.py:561
  53.5 4.9 %collective-permute-start.17 = (f32[104,128]{1,0:T(8,128)S(1)}, f32[104,128]{1,0:T(8,128)S(1)}, u32[]{:S(2)}, u32[]{:S(2)}) collective-permute-start(f32[104,128]{1,0:T(8,128)S(1)} %add.32), channel_id=1, source_target_pairs={{0,2},{1,3},{2,0},{3,1},{4,6},{5,7},{6,4},{7,5},{8,10},{9,11},{10,... | collective-permute-start | bytes 159752 | tf_op jit(solution)/shard_map/ppermute | solution.py:561
  54.7 4.2 %collective-permute-start.20 = (f32[104,128]{1,0:T(8,128)S(1)}, f32[104,128]{1,0:T(8,128)S(1)}, u32[]{:S(2)}, u32[]{:S(2)}) collective-permute-start(f32[104,128]{1,0:T(8,128)S(1)} %add.33), channel_id=1, source_target_pairs={{0,2},{1,3},{2,0},{3,1},{4,6},{5,7},{6,4},{7,5},{8,10},{9,11},{10,... | collective-permute-start | bytes 159752 | tf_op jit(solution)/shard_map/ppermute | solution.py:561
  58.9 1.7 %collective-permute-start.19 = (f32[208,128]{1,0:T(8,128)S(1)}, f32[208,128]{1,0:T(8,128)S(1)}, u32[]{:S(2)}, u32[]{:S(2)}) collective-permute-start(f32[208,128]{1,0:T(8,128)S(1)} %pad_maximum_fusion.4), channel_id=1, source_target_pairs={{0,1},{1,0},{2,3},{3,2},{4,5},{5,4},{6,7},{7,6},{8,9},{9,8},{10,11... | collective-permute-start | bytes 319496 | tf_op jit(solution)/shard_map/ppermute | solution.py:561
  59.0 1.6 %collective-permute-start.21 = (f32[208,128]{1,0:T(8,128)S(1)}, f32[208,128]{1,0:T(8,128)S(1)}, u32[]{:S(2)}, u32[]{:S(2)}) collective-permute-start(f32[208,128]{1,0:T(8,128)S(1)} %pad_maximum_fusion.5), channel_id=1, source_target_pairs={{0,1},{1,0},{2,3},{3,2},{4,5},{5,4},{6,7},{7,6},{8,9},{9,8},{10,11... | collective-permute-start | bytes 319496 | tf_op jit(solution)/shard_map/ppermute | solution.py:561

commit v10 on v8

--- a/solution.py
+++ b/solution.py
@@ -27,7 +27,7 @@
 ROWS = 64
 CHUNKS = 8
 PARTS = 8
-BESIDE = (1, 2, 1, 1, 2, 1)
+BESIDE = (1, 2, 2, 2, 1)
 MIB = 1024 * 1024
 
 WHOLE = pl.BlockSpec(memory_space=pltpu.VMEM)
@@ -538,21 +538,17 @@
     )(near(left), near(right))
 
 
-def plan(count):
-    strides = [1 << bit for bit in range(count.bit_length() - 1)]
-    return strides[:2], strides[2:]
-
-
 def swap(values, count, stride):
     return lax.ppermute(values, "vel", [(device, device ^ stride) for device in range(count)])
 
 
-def staged_sum(values, count, sides, f, tasks):
-    splits, sums = plan(count)
+def staged_sum(values, count, even, f, tasks):
+    strides = [1 << bit for bit in range(1, count.bit_length() - 1)]
+    orders = (strides, strides[1:] + strides[:1])
     results, waiting, portions = [], list(tasks), list(BESIDE)
 
-    def exchange(chunks, stride):
-        got = [swap(chunk, count, stride) for chunk in chunks]
+    def exchange(chunks, chosen):
+        got = [swap(chunk, count, stride) for chunk, stride in zip(chunks, chosen)]
         portion = portions.pop(0) if portions else 0
         if portion:
             _, held = lax.optimization_barrier((chunks[-1], f))
@@ -562,46 +558,24 @@
             results.extend(made)
         return got
 
-    def split(chunks, stride, lower_side):
-        kept, sent = [], []
-        for chunk in chunks:
-            half = chunk.shape[0] // 2
-            first, second = chunk[:half], chunk[half:]
-            kept.append(jnp.where(lower_side, first, second))
-            sent.append(jnp.where(lower_side, second, first))
-        sent = lax.optimization_barrier(sent)
-        got = exchange(sent, stride)
-        if len(chunks) == 1:
-            return [kept[0] + got[0]]
-        return [add_call(own, other) for own, other in zip(kept, got)]
-
-    def join(chunks, stride, lower_side):
-        out = []
-        for own, got in zip(chunks, exchange(chunks, stride)):
-            lower = jnp.where(lower_side, own, got)
-            upper = jnp.where(lower_side, got, own)
-            out.append((lower, upper))
-        return out
-
-    (block,) = split([values], splits[0], sides[0])
-    half = block.shape[0] // 2
-    chunks = [block[:half], block[half:]]
-    for stride, lower_side in zip(splits[1:], sides[1:]):
-        chunks = split(chunks, stride, lower_side)
-    for stride in sums:
-        chunks = [add_call(own, got) for own, got in zip(chunks, exchange(chunks, stride))]
-    for stride, lower_side in reversed(list(zip(splits[1:], sides[1:]))):
-        chunks = [jnp.concatenate(both, axis=0) for both in join(chunks, stride, lower_side)]
-    lowers, uppers = zip(*join(chunks, splits[0], sides[0]))
+    half = values.shape[0] // 2
+    first, second = values[:half], values[half:]
+    kept, sent = jnp.where(even, first, second), jnp.where(even, second, first)
+    (got,) = exchange([sent], [1])
+    block = kept + got
+    chunks = lax.optimization_barrier([block[: half // 2], block[half // 2 :]])
+    for chosen in zip(*orders):
+        chunks = [add_call(own, got) for own, got in zip(chunks, exchange(chunks, chosen))]
+    got = exchange(chunks, [1, 1])
     results.extend(task(f) for task in waiting)
-    return jnp.concatenate(lowers + uppers, axis=0), results
+    lower = [jnp.where(even, own, other) for own, other in zip(chunks, got)]
+    upper = [jnp.where(even, other, own) for own, other in zip(chunks, got)]
+    return jnp.concatenate(lower + upper, axis=0), results
 
 
 def on_device(velocities, density, flow, thermal, deviation):
     count = lax.axis_size("vel")
-    place = lax.axis_index("vel")
-    sides = [place & stride == 0 for stride in plan(count)[0]]
-    velocities, sides = lax.optimization_barrier((velocities, sides))
+    velocities, even = lax.optimization_barrier((velocities, lax.axis_index("vel") & 1 == 0))
     f, moments, *tables, table, stream = start_call(
         velocities, density, flow, thermal, deviation, velocities.shape[1] * count
     )
@@ -610,7 +584,7 @@
             functools.partial(lambda held, part: transport_call(stream, held, part), part=part)
             for part in range(PARTS)
         ]
-        summed, g = staged_sum(moments, count, sides, f, tasks)
+        summed, g = staged_sum(moments, count, even, f, tasks)
         last = iteration == ITERS - 1
         coefficients, *macro = fluid_call(summed, last)
         if not last:

time: 63.5 us -> 63.5 us (level)
  waiting for transfers between devices: 5.27 us -> 7.63 us
  starting transfers between devices: 27 us -> 24.8 us
    ppermute x22 -> x18, waiting for transfers between devices: 5.27 us -> 7.63 us  [swap(): lax.ppermute(values, 'vel', [(device, device ^ stride) for device in rang...]
    ppermute x22 -> x18, starting transfers between devices: 27 us -> 24.8 us  [swap(): lax.ppermute(values, 'vel', [(device, device ^ stride) for device in rang...]
  transfers between devices with their start and end apart: 22 -> 18, of which waited for: 12 -> 10; matrix products, arithmetic and copies ran while one was open for 0% -> 0% of each run, Pallas kernels for 25% -> 25%
where the time goes in v10:
time: 63.5 us; the launch traced here: 63.4 us
  Pallas kernels  29.5 us (46%)
  starting transfers between devices  24.8 us (39%)
  waiting for transfers between devices  7.63 us (12%)
  between operations  1.16 us (2%)
    ppermute x18, starting transfers between devices, swap(): lax.ppermute(values, 'vel', [(device, device ^ stride) for device in rang...  24.8 us
    pallas_call x16, Pallas kernels, transport_call(): pl.pallas_call(functools.partial(transport_kernel, part * rows), out_shap...  16 us
    ppermute x18, waiting for transfers between devices, swap(): lax.ppermute(values, 'vel', [(device, device ^ stride) for device in rang...  7.63 us
    pallas_call x1, Pallas kernels, start_call(): pl.pallas_call(functools.partial(start_kernel, total_count), out_shape=(p...  5.4 us
    pallas_call x1, Pallas kernels, update_call(): pl.pallas_call(update_kernel, out_shape=(pltpu.VMEM((rows * PARTS, cells)...  3.2 us
    pallas_call x1, Pallas kernels, finish_call(): pl.pallas_call(finish_kernel, out_shape=(jax.ShapeDtypeStruct((rows * PAR...  3.06 us
    pallas_call x2, Pallas kernels, fluid_call(): pl.pallas_call(fluid_kernel, out_shape=shapes, in_specs=[WHOLE], out_spec...  1.71 us
  transfers between devices with their start and end apart: 18, of which 10 were waited for; matrix products, arithmetic and copies ran while one was open for 0% of the time, Pallas kernels for 25%

profile of v10, /device:TPU:0, one launch (start us, length us, event | category | flops | bytes accessed | tf_op | source)
XLA Modules:
  0.0 63.4 jit_solution(14189167450825271927)
XLA Ops:
  0.6 5.4 %start.1 = (f32[128,8192]{1,0:T(8,128)S(1)}, f32[832,128]{1,0:T(8,128)S(1)}, bf16[128,48]{1,0:T(8,128)(2,1)S(1)}, bf16[128,48]{1,0:T(8,128)(2,1)S(1)}, bf16[32,2...) custom-call(f32[3,128]{1,0:T(4,128)} %vel_hbm, f32[1,8192]{1,0:T(1,128)} %bitcast.2, f32[3,8192]{1,0:T(4,128)} %flow_hbm.1, ...), custom_call_target="tpu_custom_call" | custom-call | tf_op jit(solution)/shard_map/start/pallas_call | solution.py:204
  7.7 3.0 %collective-permute-start.1 = (f32[208,128]{1,0:T(8,128)S(1)}, f32[208,128]{1,0:T(8,128)S(1)}, u32[]{:S(2)}, u32[]{:S(2)}) collective-permute-start(f32[208,128]{1,0:T(8,128)S(1)} %get-tuple-element.62.left_ref), channel_id=1, source_target_pairs={{0,2},{1,3},{2,0},{3,1},{4,6},{5,7},{6,4},{7,5},{8,10},{9,11},{10,... | collective-permute-start | bytes 319496 | tf_op jit(solution)/shard_map/ppermute | solution.py:542
  10.7 1.6 %collective-permute-start.3 = (f32[208,128]{1,0:T(8,128)S(1)}, f32[208,128]{1,0:T(8,128)S(1)}, u32[]{:S(2)}, u32[]{:S(2)}) collective-permute-start(f32[208,128]{1,0:T(8,128)S(1)} %get-tuple-element.63.left_ref), channel_id=1, source_target_pairs={{0,4},{1,5},{2,6},{3,7},{4,0},{5,1},{6,2},{7,3},{8,12},{9,13},{10,... | collective-permute-start | bytes 319496 | tf_op jit(solution)/shard_map/ppermute | solution.py:542
  13.3 1.0 %transport.17.refs_1_ = f32[16,8192]{1,0:T(8,128)S(1)} custom-call(f32[128,128]{1,0:T(8,128)S(1)} %get-tuple-element.57.stream_ref, f32[128,8192]{1,0:T(8,128)S(1)} %get-tuple-element.76.f_ref), custom_call_target="tpu_custom_call" | custom-call | tf_op jit(solution)/shard_map/transport/pallas_call | solution.py:295
  14.3 1.5 %collective-permute-start.2 = (f32[208,128]{1,0:T(8,128)S(1)}, f32[208,128]{1,0:T(8,128)S(1)}, u32[]{:S(2)}, u32[]{:S(2)}) collective-permute-start(f32[208,128]{1,0:T(8,128)S(1)} %add.22.left_ref), channel_id=1, source_target_pairs={{0,4},{1,5},{2,6},{3,7},{4,0},{5,1},{6,2},{7,3},{8,12},{9,13},{10,... | collective-permute-start | bytes 319496 | tf_op jit(solution)/shard_map/ppermute | solution.py:542
  15.9 2.7 %collective-permute-start.5 = (f32[208,128]{1,0:T(8,128)S(1)}, f32[208,128]{1,0:T(8,128)S(1)}, u32[]{:S(2)}, u32[]{:S(2)}) collective-permute-start(f32[208,128]{1,0:T(8,128)S(1)} %add.23.left_ref), channel_id=1, source_target_pairs={{0,8},{1,9},{2,10},{3,11},{4,12},{5,13},{6,14},{7,15},{8,0},{9,1},... | collective-permute-start | bytes 319496 | tf_op jit(solution)/shard_map/ppermute | solution.py:542
  19.5 1.0 %transport.19.refs_3_ = f32[16,8192]{1,0:T(8,128)S(1)} custom-call(f32[128,128]{1,0:T(8,128)S(1)} %get-tuple-element.57.stream_ref, f32[128,8192]{1,0:T(8,128)S(1)} %get-tuple-element.76.f_ref), custom_call_target="tpu_custom_call" | custom-call | tf_op jit(solution)/shard_map/transport/pallas_call | solution.py:295
  20.6 2.1 %collective-permute-start.4 = (f32[208,128]{1,0:T(8,128)S(1)}, f32[208,128]{1,0:T(8,128)S(1)}, u32[]{:S(2)}, u32[]{:S(2)}) collective-permute-start(f32[208,128]{1,0:T(8,128)S(1)} %add.24.left_ref), channel_id=1, source_target_pairs={{0,8},{1,9},{2,10},{3,11},{4,12},{5,13},{6,14},{7,15},{8,0},{9,1},... | collective-permute-start | bytes 319496 | tf_op jit(solution)/shard_map/ppermute | solution.py:542
  23.4 2.5 %collective-permute-start.7 = (f32[208,128]{1,0:T(8,128)S(1)}, f32[208,128]{1,0:T(8,128)S(1)}, u32[]{:S(2)}, u32[]{:S(2)}) collective-permute-start(f32[208,128]{1,0:T(8,128)S(1)} %add.25.left_ref), channel_id=1, source_target_pairs={{0,2},{1,3},{2,0},{3,1},{4,6},{5,7},{6,4},{7,5},{8,10},{9,11},{10,... | collective-permute-start | bytes 319496 | tf_op jit(solution)/shard_map/ppermute | solution.py:542
  26.9 1.0 %transport.21.refs_5_ = f32[16,8192]{1,0:T(8,128)S(1)} custom-call(f32[128,128]{1,0:T(8,128)S(1)} %get-tuple-element.57.stream_ref, f32[128,8192]{1,0:T(8,128)S(1)} %get-tuple-element.76.f_ref), custom_call_target="tpu_custom_call" | custom-call | tf_op jit(solution)/shard_map/transport/pallas_call | solution.py:295
  28.6 1.0 %transport.23.refs_7_ = f32[16,8192]{1,0:T(8,128)S(1)} custom-call(f32[128,128]{1,0:T(8,128)S(1)} %get-tuple-element.57.stream_ref, f32[128,8192]{1,0:T(8,128)S(1)} %get-tuple-element.76.f_ref), custom_call_target="tpu_custom_call" | custom-call | tf_op jit(solution)/shard_map/transport/pallas_call | solution.py:295
  30.9 3.2 %update.1 = (f32[128,8192]{1,0:T(8,128)S(1)}, f32[832,128]{1,0:T(8,128)S(1)}) custom-call(f32[16,8192]{1,0:T(8,128)S(1)} %transport.16.refs_0_, f32[16,8192]{1,0:T(8,128)S(1)} %transport.17.refs_1_, f32[16,8192]{1,0:T(8,128)S(1)} %transport.18.refs_2_, f32[16,8192]{1,0:T(8,128)S(1)} %transport.19.refs_3_, f32[16,8192]{1,0:T(8,128)S(1)} %transport.20.refs_4_, ...), custom_call_target="tpu_custom_call" | custom-call | tf_op jit(solution)/shard_map/update/pallas_call | solution.py:471
  35.7 2.1 %collective-permute-start.10 = (f32[208,128]{1,0:T(8,128)S(1)}, f32[208,128]{1,0:T(8,128)S(1)}, u32[]{:S(2)}, u32[]{:S(2)}) collective-permute-start(f32[208,128]{1,0:T(8,128)S(1)} %get-tuple-element.87.left_ref), channel_id=1, source_target_pairs={{0,2},{1,3},{2,0},{3,1},{4,6},{5,7},{6,4},{7,5},{8,10},{9,11},{10,... | collective-permute-start | bytes 319496 | tf_op jit(solution)/shard_map/ppermute | solution.py:542
  39.3 1.0 %transport.25.refs_1_ = f32[16,8192]{1,0:T(8,128)S(1)} custom-call(f32[128,128]{1,0:T(8,128)S(1)} %get-tuple-element.57.stream_ref, f32[128,8192]{1,0:T(8,128)S(1)} %get-tuple-element.101.f_ref), custom_call_target="tpu_custom_call" | custom-call | tf_op jit(solution)/shard_map/transport/pallas_call | solution.py:295
  41.2 1.4 %collective-permute-start.11 = (f32[208,128]{1,0:T(8,128)S(1)}, f32[208,128]{1,0:T(8,128)S(1)}, u32[]{:S(2)}, u32[]{:S(2)}) collective-permute-start(f32[208,128]{1,0:T(8,128)S(1)} %add.28.left_ref), channel_id=1, source_target_pairs={{0,4},{1,5},{2,6},{3,7},{4,0},{5,1},{6,2},{7,3},{8,12},{9,13},{10,... | collective-permute-start | bytes 319496 | tf_op jit(solution)/shard_map/ppermute | solution.py:542
  42.7 4.6 %collective-permute-start.14 = (f32[208,128]{1,0:T(8,128)S(1)}, f32[208,128]{1,0:T(8,128)S(1)}, u32[]{:S(2)}, u32[]{:S(2)}) collective-permute-start(f32[208,128]{1,0:T(8,128)S(1)} %add.29.left_ref), channel_id=1, source_target_pairs={{0,8},{1,9},{2,10},{3,11},{4,12},{5,13},{6,14},{7,15},{8,0},{9,1},... | collective-permute-start | bytes 319496 | tf_op jit(solution)/shard_map/ppermute | solution.py:542
  48.2 1.0 %transport.27.refs_3_ = f32[16,8192]{1,0:T(8,128)S(1)} custom-call(f32[128,128]{1,0:T(8,128)S(1)} %get-tuple-element.57.stream_ref, f32[128,8192]{1,0:T(8,128)S(1)} %get-tuple-element.101.f_ref), custom_call_target="tpu_custom_call" | custom-call | tf_op jit(solution)/shard_map/transport/pallas_call | solution.py:295
  49.3 1.7 %collective-permute-start.13 = (f32[208,128]{1,0:T(8,128)S(1)}, f32[208,128]{1,0:T(8,128)S(1)}, u32[]{:S(2)}, u32[]{:S(2)}) collective-permute-start(f32[208,128]{1,0:T(8,128)S(1)} %add.30.left_ref), channel_id=1, source_target_pairs={{0,8},{1,9},{2,10},{3,11},{4,12},{5,13},{6,14},{7,15},{8,0},{9,1},... | collective-permute-start | bytes 319496 | tf_op jit(solution)/shard_map/ppermute | solution.py:542
  50.9 2.1 %collective-permute-done.14.right_ref = f32[208,128]{1,0:T(8,128)S(1)} collective-permute-done((f32[208,128]{1,0:T(8,128)S(1)}, f32[208,128]{1,0:T(8,128)S(1)}, u32[]{:S(2)}, u32[]{:S(2)}) %collective-permute-start.14) | collective-permute-done | bytes 106528 | tf_op jit(solution)/shard_map/ppermute | solution.py:542
  53.1 1.0 %transport.30.refs_6_ = f32[16,8192]{1,0:T(8,128)S(1)} custom-call(f32[128,128]{1,0:T(8,128)S(1)} %get-tuple-element.57.stream_ref, f32[128,8192]{1,0:T(8,128)S(1)} %get-tuple-element.101.f_ref), custom_call_target="tpu_custom_call" | custom-call | tf_op jit(solution)/shard_map/transport/pallas_call | solution.py:295
  54.1 1.0 %transport.29.refs_5_ = f32[16,8192]{1,0:T(8,128)S(1)} custom-call(f32[128,128]{1,0:T(8,128)S(1)} %get-tuple-element.57.stream_ref, f32[128,8192]{1,0:T(8,128)S(1)} %get-tuple-element.101.f_ref), custom_call_target="tpu_custom_call" | custom-call | tf_op jit(solution)/shard_map/transport/pallas_call | solution.py:295
  55.1 1.2 %collective-permute-done.13.right_ref = f32[208,128]{1,0:T(8,128)S(1)} collective-permute-done((f32[208,128]{1,0:T(8,128)S(1)}, f32[208,128]{1,0:T(8,128)S(1)}, u32[]{:S(2)}, u32[]{:S(2)}) %collective-permute-start.13) | collective-permute-done | bytes 106528 | tf_op jit(solution)/shard_map/ppermute | solution.py:542
  56.5 1.4 %collective-permute-done.16.right_ref = f32[208,128]{1,0:T(8,128)S(1)} collective-permute-done((f32[208,128]{1,0:T(8,128)S(1)}, f32[208,128]{1,0:T(8,128)S(1)}, u32[]{:S(2)}, u32[]{:S(2)}) %collective-permute-start.16) | collective-permute-done | bytes 106528 | tf_op jit(solution)/shard_map/ppermute | solution.py:542
  60.1 3.1 %finish.1 = (f32[128,8192]{1,0:T(8,128)}, f32[8,8192]{1,0:T(8,128)}) custom-call(f32[16,8192]{1,0:T(8,128)S(1)} %transport.24.refs_0_, f32[16,8192]{1,0:T(8,128)S(1)} %transport.25.refs_1_, f32[16,8192]{1,0:T(8,128)S(1)} %transport.26.refs_2_, f32[16,8192]{1,0:T(8,128)S(1)} %transport.27.refs_3_, f32[16,8192]{1,0:T(8,128)S(1)} %transport.28.refs_4_, ...), custom_call_target="tpu_custom_call" | custom-call | tf_op jit(solution)/shard_map/finish/pallas_call | solution.py:509
  (57 shorter events, 14.8 us)
Async XLA Ops:
  6.1 1.6 %collective-permute-start = (f32[416,128]{1,0:T(8,128)S(1)}, f32[416,128]{1,0:T(8,128)S(1)}, u32[]{:S(2)}, u32[]{:S(2)}) collective-permute-start(f32[416,128]{1,0:T(8,128)S(1)} %slice_select_fusion.1), channel_id=1, source_target_pairs={{0,1},{1,0},{2,3},{3,2},{4,5},{5,4},{6,7},{7,6},{8,9},{9,8},{10,11... | collective-permute-start | bytes 638984 | tf_op jit(solution)/shard_map/ppermute | solution.py:542
  7.7 6.5 %collective-permute-start.1 = (f32[208,128]{1,0:T(8,128)S(1)}, f32[208,128]{1,0:T(8,128)S(1)}, u32[]{:S(2)}, u32[]{:S(2)}) collective-permute-start(f32[208,128]{1,0:T(8,128)S(1)} %get-tuple-element.62.left_ref), channel_id=1, source_target_pairs={{0,2},{1,3},{2,0},{3,1},{4,6},{5,7},{6,4},{7,5},{8,10},{9,11},{10,... | collective-permute-start | bytes 319496 | tf_op jit(solution)/shard_map/ppermute | solution.py:542
  10.7 5.2 %collective-permute-start.3 = (f32[208,128]{1,0:T(8,128)S(1)}, f32[208,128]{1,0:T(8,128)S(1)}, u32[]{:S(2)}, u32[]{:S(2)}) collective-permute-start(f32[208,128]{1,0:T(8,128)S(1)} %get-tuple-element.63.left_ref), channel_id=1, source_target_pairs={{0,4},{1,5},{2,6},{3,7},{4,0},{5,1},{6,2},{7,3},{8,12},{9,13},{10,... | collective-permute-start | bytes 319496 | tf_op jit(solution)/shard_map/ppermute | solution.py:542
  14.3 6.2 %collective-permute-start.2 = (f32[208,128]{1,0:T(8,128)S(1)}, f32[208,128]{1,0:T(8,128)S(1)}, u32[]{:S(2)}, u32[]{:S(2)}) collective-permute-start(f32[208,128]{1,0:T(8,128)S(1)} %add.22.left_ref), channel_id=1, source_target_pairs={{0,4},{1,5},{2,6},{3,7},{4,0},{5,1},{6,2},{7,3},{8,12},{9,13},{10,... | collective-permute-start | bytes 319496 | tf_op jit(solution)/shard_map/ppermute | solution.py:542
  15.9 7.5 %collective-permute-start.5 = (f32[208,128]{1,0:T(8,128)S(1)}, f32[208,128]{1,0:T(8,128)S(1)}, u32[]{:S(2)}, u32[]{:S(2)}) collective-permute-start(f32[208,128]{1,0:T(8,128)S(1)} %add.23.left_ref), channel_id=1, source_target_pairs={{0,8},{1,9},{2,10},{3,11},{4,12},{5,13},{6,14},{7,15},{8,0},{9,1},... | collective-permute-start | bytes 319496 | tf_op jit(solution)/shard_map/ppermute | solution.py:542
  20.6 7.3 %collective-permute-start.4 = (f32[208,128]{1,0:T(8,128)S(1)}, f32[208,128]{1,0:T(8,128)S(1)}, u32[]{:S(2)}, u32[]{:S(2)}) collective-permute-start(f32[208,128]{1,0:T(8,128)S(1)} %add.24.left_ref), channel_id=1, source_target_pairs={{0,8},{1,9},{2,10},{3,11},{4,12},{5,13},{6,14},{7,15},{8,0},{9,1},... | collective-permute-start | bytes 319496 | tf_op jit(solution)/shard_map/ppermute | solution.py:542
  23.4 5.2 %collective-permute-start.7 = (f32[208,128]{1,0:T(8,128)S(1)}, f32[208,128]{1,0:T(8,128)S(1)}, u32[]{:S(2)}, u32[]{:S(2)}) collective-permute-start(f32[208,128]{1,0:T(8,128)S(1)} %add.25.left_ref), channel_id=1, source_target_pairs={{0,2},{1,3},{2,0},{3,1},{4,6},{5,7},{6,4},{7,5},{8,10},{9,11},{10,... | collective-permute-start | bytes 319496 | tf_op jit(solution)/shard_map/ppermute | solution.py:542
  27.9 1.7 %collective-permute-start.6 = (f32[208,128]{1,0:T(8,128)S(1)}, f32[208,128]{1,0:T(8,128)S(1)}, u32[]{:S(2)}, u32[]{:S(2)}) collective-permute-start(f32[208,128]{1,0:T(8,128)S(1)} %add.26), channel_id=1, source_target_pairs={{0,1},{1,0},{2,3},{3,2},{4,5},{5,4},{6,7},{7,6},{8,9},{9,8},{10,11... | collective-permute-start | bytes 319496 | tf_op jit(solution)/shard_map/ppermute | solution.py:542
  28.6 1.4 %collective-permute-start.8 = (f32[208,128]{1,0:T(8,128)S(1)}, f32[208,128]{1,0:T(8,128)S(1)}, u32[]{:S(2)}, u32[]{:S(2)}) collective-permute-start(f32[208,128]{1,0:T(8,128)S(1)} %add.27), channel_id=1, source_target_pairs={{0,1},{1,0},{2,3},{3,2},{4,5},{5,4},{6,7},{7,6},{8,9},{9,8},{10,11... | collective-permute-start | bytes 319496 | tf_op jit(solution)/shard_map/ppermute | solution.py:542
  34.1 1.5 %collective-permute-start.9 = (f32[416,128]{1,0:T(8,128)S(1)}, f32[416,128]{1,0:T(8,128)S(1)}, u32[]{:S(2)}, u32[]{:S(2)}) collective-permute-start(f32[416,128]{1,0:T(8,128)S(1)} %slice_select_fusion), channel_id=1, source_target_pairs={{0,1},{1,0},{2,3},{3,2},{4,5},{5,4},{6,7},{7,6},{8,9},{9,8},{10,11... | collective-permute-start | bytes 638984 | tf_op jit(solution)/shard_map/ppermute | solution.py:542
  35.7 5.5 %collective-permute-start.10 = (f32[208,128]{1,0:T(8,128)S(1)}, f32[208,128]{1,0:T(8,128)S(1)}, u32[]{:S(2)}, u32[]{:S(2)}) collective-permute-start(f32[208,128]{1,0:T(8,128)S(1)} %get-tuple-element.87.left_ref), channel_id=1, source_target_pairs={{0,2},{1,3},{2,0},{3,1},{4,6},{5,7},{6,4},{7,5},{8,10},{9,11},{10,... | collective-permute-start | bytes 319496 | tf_op jit(solution)/shard_map/ppermute | solution.py:542
  37.8 4.9 %collective-permute-start.12 = (f32[208,128]{1,0:T(8,128)S(1)}, f32[208,128]{1,0:T(8,128)S(1)}, u32[]{:S(2)}, u32[]{:S(2)}) collective-permute-start(f32[208,128]{1,0:T(8,128)S(1)} %get-tuple-element.88.left_ref), channel_id=1, source_target_pairs={{0,4},{1,5},{2,6},{3,7},{4,0},{5,1},{6,2},{7,3},{8,12},{9,13},{10,... | collective-permute-start | bytes 319496 | tf_op jit(solution)/shard_map/ppermute | solution.py:542
  41.2 8.0 %collective-permute-start.11 = (f32[208,128]{1,0:T(8,128)S(1)}, f32[208,128]{1,0:T(8,128)S(1)}, u32[]{:S(2)}, u32[]{:S(2)}) collective-permute-start(f32[208,128]{1,0:T(8,128)S(1)} %add.28.left_ref), channel_id=1, source_target_pairs={{0,4},{1,5},{2,6},{3,7},{4,0},{5,1},{6,2},{7,3},{8,12},{9,13},{10,... | collective-permute-start | bytes 319496 | tf_op jit(solution)/shard_map/ppermute | solution.py:542
  42.7 10.4 %collective-permute-start.14 = (f32[208,128]{1,0:T(8,128)S(1)}, f32[208,128]{1,0:T(8,128)S(1)}, u32[]{:S(2)}, u32[]{:S(2)}) collective-permute-start(f32[208,128]{1,0:T(8,128)S(1)} %add.29.left_ref), channel_id=1, source_target_pairs={{0,8},{1,9},{2,10},{3,11},{4,12},{5,13},{6,14},{7,15},{8,0},{9,1},... | collective-permute-start | bytes 319496 | tf_op jit(solution)/shard_map/ppermute | solution.py:542
  49.3 7.1 %collective-permute-start.13 = (f32[208,128]{1,0:T(8,128)S(1)}, f32[208,128]{1,0:T(8,128)S(1)}, u32[]{:S(2)}, u32[]{:S(2)}) collective-permute-start(f32[208,128]{1,0:T(8,128)S(1)} %add.30.left_ref), channel_id=1, source_target_pairs={{0,8},{1,9},{2,10},{3,11},{4,12},{5,13},{6,14},{7,15},{8,0},{9,1},... | collective-permute-start | bytes 319496 | tf_op jit(solution)/shard_map/ppermute | solution.py:542
  53.1 4.8 %collective-permute-start.16 = (f32[208,128]{1,0:T(8,128)S(1)}, f32[208,128]{1,0:T(8,128)S(1)}, u32[]{:S(2)}, u32[]{:S(2)}) collective-permute-start(f32[208,128]{1,0:T(8,128)S(1)} %add.31.left_ref), channel_id=1, source_target_pairs={{0,2},{1,3},{2,0},{3,1},{4,6},{5,7},{6,4},{7,5},{8,10},{9,11},{10,... | collective-permute-start | bytes 319496 | tf_op jit(solution)/shard_map/ppermute | solution.py:542
  56.4 2.5 %collective-permute-start.15 = (f32[208,128]{1,0:T(8,128)S(1)}, f32[208,128]{1,0:T(8,128)S(1)}, u32[]{:S(2)}, u32[]{:S(2)}) collective-permute-start(f32[208,128]{1,0:T(8,128)S(1)} %add.32), channel_id=1, source_target_pairs={{0,1},{1,0},{2,3},{3,2},{4,5},{5,4},{6,7},{7,6},{8,9},{9,8},{10,11... | collective-permute-start | bytes 319496 | tf_op jit(solution)/shard_map/ppermute | solution.py:542
  57.8 1.4 %collective-permute-start.17 = (f32[208,128]{1,0:T(8,128)S(1)}, f32[208,128]{1,0:T(8,128)S(1)}, u32[]{:S(2)}, u32[]{:S(2)}) collective-permute-start(f32[208,128]{1,0:T(8,128)S(1)} %add.33), channel_id=1, source_target_pairs={{0,1},{1,0},{2,3},{3,2},{4,5},{5,4},{6,7},{7,6},{8,9},{9,8},{10,11... | collective-permute-start | bytes 319496 | tf_op jit(solution)/shard_map/ppermute | solution.py:542

commit v11 on v8

--- a/solution.py
+++ b/solution.py
@@ -26,6 +26,7 @@
 DAMP = 13
 ROWS = 64
 CHUNKS = 8
+DEPARTURES = 16
 PARTS = 8
 BESIDE = (1, 2, 1, 1, 2, 1)
 MIB = 1024 * 1024
@@ -483,21 +484,23 @@
 
 def finish_kernel(*refs):
     g_refs = refs[:PARTS]
-    coef_ref, macro_ref, exponent_ref, polynomial_ref, f_ref, fields_ref, held, sems = refs[PARTS:]
+    coef_ref, macro_ref, exponent_ref, polynomial_ref, f_hbm, fields_hbm = refs[PARTS : PARTS + 6]
+    held, fields, sems = refs[PARTS + 6 :]
     cells = held.shape[1]
-    width = cells // CHUNKS
-    copies = []
-    for chunk in range(CHUNKS):
+    width = cells // DEPARTURES
+    for block in range(cells // LANES):
+        fields[:, block * LANES : (block + 1) * LANES] = macro_ref[block * 8 : (block + 1) * 8, :]
+    copies = [pltpu.make_async_copy(fields, fields_hbm, sems.at[DEPARTURES])]
+    copies[0].start()
+    for chunk in range(DEPARTURES):
         for local in range(width // TILE):
             tile = chunk * (width // TILE) + local
             here = pl.ds(tile * TILE, TILE)
             values_of = relaxed(g_refs, here, coef_ref, exponent_ref, polynomial_ref, tile)
             for first in range(0, held.shape[0], ROWS):
                 held[pl.ds(first, ROWS), here] = values_of(pl.ds(first, ROWS))
-            for block in range(tile * TILE // LANES, (tile + 1) * TILE // LANES):
-                fields_ref[:, pl.ds(block * LANES, LANES)] = macro_ref[pl.ds(block * 8, 8), :]
         there = pl.ds(chunk * width, width)
-        copy = pltpu.make_async_copy(held.at[:, there], f_ref.at[:, there], sems.at[chunk])
+        copy = pltpu.make_async_copy(held.at[:, there], f_hbm.at[:, there], sems.at[chunk])
         copy.start()
         copies.append(copy)
     for copy in copies:
@@ -513,10 +516,11 @@
             jax.ShapeDtypeStruct((8, cells), jnp.float32),
         ),
         in_specs=[WHOLE] * (PARTS + 4),
-        out_specs=(OUTSIDE, WHOLE),
+        out_specs=(OUTSIDE, OUTSIDE),
         scratch_shapes=[
             pltpu.VMEM((rows * PARTS, cells), jnp.float32),
-            pltpu.SemaphoreType.DMA((CHUNKS,)),
+            pltpu.VMEM((8, cells), jnp.float32),
+            pltpu.SemaphoreType.DMA((DEPARTURES + 1,)),
         ],
         compiler_params=params(16),
         name="finish",

time: 63.5 us -> 62.8 us (0.989)
    pallas_call x1, Pallas kernels: 3.06 us -> 2.4 us  [finish_call(): pl.pallas_call(finish_kernel, out_shape=(jax.ShapeDtypeStruct((rows * PAR...]
  transfers between devices with their start and end apart: 22 -> 22, of which waited for: 12 -> 12; matrix products, arithmetic and copies ran while one was open for 0% -> 0% of each run, Pallas kernels for 25% -> 26%
where the time goes in v11:
time: 62.8 us; the launch traced here: 62.6 us
  Pallas kernels  28.8 us (46%)
  starting transfers between devices  27 us (43%)
  waiting for transfers between devices  5.27 us (8%)
  between operations  1.18 us (2%)
    ppermute x22, starting transfers between devices, swap(): lax.ppermute(values, 'vel', [(device, device ^ stride) for device in rang...  27 us
    pallas_call x16, Pallas kernels, transport_call(): pl.pallas_call(functools.partial(transport_kernel, part * rows), out_shap...  15.9 us
    pallas_call x1, Pallas kernels, start_call(): pl.pallas_call(functools.partial(start_kernel, total_count), out_shape=(p...  5.41 us
    ppermute x22, waiting for transfers between devices, swap(): lax.ppermute(values, 'vel', [(device, device ^ stride) for device in rang...  5.27 us
    pallas_call x1, Pallas kernels, update_call(): pl.pallas_call(update_kernel, out_shape=(pltpu.VMEM((rows * PARTS, cells)...  3.2 us
    pallas_call x1, Pallas kernels, finish_call(): pl.pallas_call(finish_kernel, out_shape=(jax.ShapeDtypeStruct((rows * PAR...  2.4 us
    pallas_call x2, Pallas kernels, fluid_call(): pl.pallas_call(fluid_kernel, out_shape=shapes, in_specs=[WHOLE], out_spec...  1.71 us
  transfers between devices with their start and end apart: 22, of which 12 were waited for; matrix products, arithmetic and copies ran while one was open for 0% of the time, Pallas kernels for 26%

profile of v11, /device:TPU:0, one launch (start us, length us, event | category | flops | bytes accessed | tf_op | source)
XLA Modules:
  0.0 62.6 jit_solution(10998461210833265169)
XLA Ops:
  0.6 5.4 %start.1 = (f32[128,8192]{1,0:T(8,128)S(1)}, f32[832,128]{1,0:T(8,128)S(1)}, bf16[128,48]{1,0:T(8,128)(2,1)S(1)}, bf16[128,48]{1,0:T(8,128)(2,1)S(1)}, bf16[32,2...) custom-call(f32[3,128]{1,0:T(4,128)} %vel_hbm, f32[1,8192]{1,0:T(1,128)} %bitcast.2, f32[3,8192]{1,0:T(4,128)} %flow_hbm.1, ...), custom_call_target="tpu_custom_call" | custom-call | tf_op jit(solution)/shard_map/start/pallas_call | solution.py:205
  6.6 1.0 %transport.16.refs_0_ = f32[16,8192]{1,0:T(8,128)S(1)} custom-call(f32[128,128]{1,0:T(8,128)S(1)} %get-tuple-element.62.stream_ref, f32[128,8192]{1,0:T(8,128)S(1)} %get-tuple-element.84.f_ref), custom_call_target="tpu_custom_call" | custom-call | tf_op jit(solution)/shard_map/transport/pallas_call | solution.py:296
  7.8 3.0 %collective-permute-start.1 = (f32[104,128]{1,0:T(8,128)S(1)}, f32[104,128]{1,0:T(8,128)S(1)}, u32[]{:S(2)}, u32[]{:S(2)}) collective-permute-start(f32[104,128]{1,0:T(8,128)S(1)} %get-tuple-element.68), channel_id=1, source_target_pairs={{0,2},{1,3},{2,0},{3,1},{4,6},{5,7},{6,4},{7,5},{8,10},{9,11},{10,... | collective-permute-start | bytes 159752 | tf_op jit(solution)/shard_map/ppermute | solution.py:551
  10.8 1.0 %transport.18.refs_2_ = f32[16,8192]{1,0:T(8,128)S(1)} custom-call(f32[128,128]{1,0:T(8,128)S(1)} %get-tuple-element.62.stream_ref, f32[128,8192]{1,0:T(8,128)S(1)} %get-tuple-element.84.f_ref), custom_call_target="tpu_custom_call" | custom-call | tf_op jit(solution)/shard_map/transport/pallas_call | solution.py:296
  11.8 1.0 %transport.17.refs_1_ = f32[16,8192]{1,0:T(8,128)S(1)} custom-call(f32[128,128]{1,0:T(8,128)S(1)} %get-tuple-element.62.stream_ref, f32[128,8192]{1,0:T(8,128)S(1)} %get-tuple-element.84.f_ref), custom_call_target="tpu_custom_call" | custom-call | tf_op jit(solution)/shard_map/transport/pallas_call | solution.py:296
  12.9 2.4 %collective-permute-start.2 = (f32[104,128]{1,0:T(8,128)S(1)}, f32[104,128]{1,0:T(8,128)S(1)}, u32[]{:S(2)}, u32[]{:S(2)}) collective-permute-start(f32[104,128]{1,0:T(8,128)S(1)} %add.22.left_ref), channel_id=1, source_target_pairs={{0,4},{1,5},{2,6},{3,7},{4,0},{5,1},{6,2},{7,3},{8,12},{9,13},{10,... | collective-permute-start | bytes 159752 | tf_op jit(solution)/shard_map/ppermute | solution.py:551
  15.2 1.3 %collective-permute-start.5 = (f32[104,128]{1,0:T(8,128)S(1)}, f32[104,128]{1,0:T(8,128)S(1)}, u32[]{:S(2)}, u32[]{:S(2)}) collective-permute-start(f32[104,128]{1,0:T(8,128)S(1)} %add.23.left_ref), channel_id=1, source_target_pairs={{0,4},{1,5},{2,6},{3,7},{4,0},{5,1},{6,2},{7,3},{8,12},{9,13},{10,... | collective-permute-start | bytes 159752 | tf_op jit(solution)/shard_map/ppermute | solution.py:551
  17.8 2.8 %collective-permute-start.4 = (f32[104,128]{1,0:T(8,128)S(1)}, f32[104,128]{1,0:T(8,128)S(1)}, u32[]{:S(2)}, u32[]{:S(2)}) collective-permute-start(f32[104,128]{1,0:T(8,128)S(1)} %add.24.left_ref), channel_id=1, source_target_pairs={{0,8},{1,9},{2,10},{3,11},{4,12},{5,13},{6,14},{7,15},{8,0},{9,1},... | collective-permute-start | bytes 159752 | tf_op jit(solution)/shard_map/ppermute | solution.py:551
  20.7 1.6 %collective-permute-start.7 = (f32[104,128]{1,0:T(8,128)S(1)}, f32[104,128]{1,0:T(8,128)S(1)}, u32[]{:S(2)}, u32[]{:S(2)}) collective-permute-start(f32[104,128]{1,0:T(8,128)S(1)} %add.25.left_ref), channel_id=1, source_target_pairs={{0,8},{1,9},{2,10},{3,11},{4,12},{5,13},{6,14},{7,15},{8,0},{9,1},... | collective-permute-start | bytes 159752 | tf_op jit(solution)/shard_map/ppermute | solution.py:551
  23.2 1.1 %collective-permute-done.4.right_ref = f32[104,128]{1,0:T(8,128)S(1)} collective-permute-done((f32[104,128]{1,0:T(8,128)S(1)}, f32[104,128]{1,0:T(8,128)S(1)}, u32[]{:S(2)}, u32[]{:S(2)}) %collective-permute-start.4) | collective-permute-done | bytes 53280 | tf_op jit(solution)/shard_map/ppermute | solution.py:551
  24.4 1.5 %collective-permute-start.6 = (f32[104,128]{1,0:T(8,128)S(1)}, f32[104,128]{1,0:T(8,128)S(1)}, u32[]{:S(2)}, u32[]{:S(2)}) collective-permute-start(f32[104,128]{1,0:T(8,128)S(1)} %add.26), channel_id=1, source_target_pairs={{0,2},{1,3},{2,0},{3,1},{4,6},{5,7},{6,4},{7,5},{8,10},{9,11},{10,... | collective-permute-start | bytes 159752 | tf_op jit(solution)/shard_map/ppermute | solution.py:551
  25.9 1.5 %collective-permute-start.9 = (f32[104,128]{1,0:T(8,128)S(1)}, f32[104,128]{1,0:T(8,128)S(1)}, u32[]{:S(2)}, u32[]{:S(2)}) collective-permute-start(f32[104,128]{1,0:T(8,128)S(1)} %add.27), channel_id=1, source_target_pairs={{0,2},{1,3},{2,0},{3,1},{4,6},{5,7},{6,4},{7,5},{8,10},{9,11},{10,... | collective-permute-start | bytes 159752 | tf_op jit(solution)/shard_map/ppermute | solution.py:551
  28.4 1.0 %transport.21.refs_5_ = f32[16,8192]{1,0:T(8,128)S(1)} custom-call(f32[128,128]{1,0:T(8,128)S(1)} %get-tuple-element.62.stream_ref, f32[128,8192]{1,0:T(8,128)S(1)} %get-tuple-element.84.f_ref), custom_call_target="tpu_custom_call" | custom-call | tf_op jit(solution)/shard_map/transport/pallas_call | solution.py:296
  30.2 1.0 %transport.23.refs_7_ = f32[16,8192]{1,0:T(8,128)S(1)} custom-call(f32[128,128]{1,0:T(8,128)S(1)} %get-tuple-element.62.stream_ref, f32[128,8192]{1,0:T(8,128)S(1)} %get-tuple-element.84.f_ref), custom_call_target="tpu_custom_call" | custom-call | tf_op jit(solution)/shard_map/transport/pallas_call | solution.py:296
  32.4 3.2 %update.1 = (f32[128,8192]{1,0:T(8,128)S(1)}, f32[832,128]{1,0:T(8,128)S(1)}) custom-call(f32[16,8192]{1,0:T(8,128)S(1)} %transport.16.refs_0_, f32[16,8192]{1,0:T(8,128)S(1)} %transport.17.refs_1_, f32[16,8192]{1,0:T(8,128)S(1)} %transport.18.refs_2_, f32[16,8192]{1,0:T(8,128)S(1)} %transport.19.refs_3_, f32[16,8192]{1,0:T(8,128)S(1)} %transport.20.refs_4_, ...), custom_call_target="tpu_custom_call" | custom-call | tf_op jit(solution)/shard_map/update/pallas_call | solution.py:472
  37.2 1.5 %collective-permute-start.12 = (f32[104,128]{1,0:T(8,128)S(1)}, f32[104,128]{1,0:T(8,128)S(1)}, u32[]{:S(2)}, u32[]{:S(2)}) collective-permute-start(f32[104,128]{1,0:T(8,128)S(1)} %get-tuple-element.95), channel_id=1, source_target_pairs={{0,2},{1,3},{2,0},{3,1},{4,6},{5,7},{6,4},{7,5},{8,10},{9,11},{10,... | collective-permute-start | bytes 159752 | tf_op jit(solution)/shard_map/ppermute | solution.py:551
  40.3 1.0 %transport.25.refs_1_ = f32[16,8192]{1,0:T(8,128)S(1)} custom-call(f32[128,128]{1,0:T(8,128)S(1)} %get-tuple-element.62.stream_ref, f32[128,8192]{1,0:T(8,128)S(1)} %get-tuple-element.111.f_ref), custom_call_target="tpu_custom_call" | custom-call | tf_op jit(solution)/shard_map/transport/pallas_call | solution.py:296
  41.6 1.2 %collective-permute-start.13 = (f32[104,128]{1,0:T(8,128)S(1)}, f32[104,128]{1,0:T(8,128)S(1)}, u32[]{:S(2)}, u32[]{:S(2)}) collective-permute-start(f32[104,128]{1,0:T(8,128)S(1)} %add.28.left_ref), channel_id=1, source_target_pairs={{0,4},{1,5},{2,6},{3,7},{4,0},{5,1},{6,2},{7,3},{8,12},{9,13},{10,... | collective-permute-start | bytes 159752 | tf_op jit(solution)/shard_map/ppermute | solution.py:551
  42.9 1.5 %collective-permute-start.16 = (f32[104,128]{1,0:T(8,128)S(1)}, f32[104,128]{1,0:T(8,128)S(1)}, u32[]{:S(2)}, u32[]{:S(2)}) collective-permute-start(f32[104,128]{1,0:T(8,128)S(1)} %add.29.left_ref), channel_id=1, source_target_pairs={{0,4},{1,5},{2,6},{3,7},{4,0},{5,1},{6,2},{7,3},{8,12},{9,13},{10,... | collective-permute-start | bytes 159752 | tf_op jit(solution)/shard_map/ppermute | solution.py:551
  46.0 2.1 %collective-permute-start.15 = (f32[104,128]{1,0:T(8,128)S(1)}, f32[104,128]{1,0:T(8,128)S(1)}, u32[]{:S(2)}, u32[]{:S(2)}) collective-permute-start(f32[104,128]{1,0:T(8,128)S(1)} %add.30.left_ref), channel_id=1, source_target_pairs={{0,8},{1,9},{2,10},{3,11},{4,12},{5,13},{6,14},{7,15},{8,0},{9,1},... | collective-permute-start | bytes 159752 | tf_op jit(solution)/shard_map/ppermute | solution.py:551
  48.1 2.1 %collective-permute-start.18 = (f32[104,128]{1,0:T(8,128)S(1)}, f32[104,128]{1,0:T(8,128)S(1)}, u32[]{:S(2)}, u32[]{:S(2)}) collective-permute-start(f32[104,128]{1,0:T(8,128)S(1)} %add.31.left_ref), channel_id=1, source_target_pairs={{0,8},{1,9},{2,10},{3,11},{4,12},{5,13},{6,14},{7,15},{8,0},{9,1},... | collective-permute-start | bytes 159752 | tf_op jit(solution)/shard_map/ppermute | solution.py:551
  53.2 1.7 %collective-permute-start.20 = (f32[104,128]{1,0:T(8,128)S(1)}, f32[104,128]{1,0:T(8,128)S(1)}, u32[]{:S(2)}, u32[]{:S(2)}) collective-permute-start(f32[104,128]{1,0:T(8,128)S(1)} %add.33), channel_id=1, source_target_pairs={{0,2},{1,3},{2,0},{3,1},{4,6},{5,7},{6,4},{7,5},{8,10},{9,11},{10,... | collective-permute-start | bytes 159752 | tf_op jit(solution)/shard_map/ppermute | solution.py:551
  55.9 1.0 %transport.29.refs_5_ = f32[16,8192]{1,0:T(8,128)S(1)} custom-call(f32[128,128]{1,0:T(8,128)S(1)} %get-tuple-element.62.stream_ref, f32[128,8192]{1,0:T(8,128)S(1)} %get-tuple-element.111.f_ref), custom_call_target="tpu_custom_call" | custom-call | tf_op jit(solution)/shard_map/transport/pallas_call | solution.py:296
  60.1 2.4 %finish.1 = (f32[128,8192]{1,0:T(8,128)}, f32[8,8192]{1,0:T(8,128)}) custom-call(f32[16,8192]{1,0:T(8,128)S(1)} %transport.24.refs_0_, f32[16,8192]{1,0:T(8,128)S(1)} %transport.25.refs_1_, f32[16,8192]{1,0:T(8,128)S(1)} %transport.26.refs_2_, f32[16,8192]{1,0:T(8,128)S(1)} %transport.27.refs_3_, f32[16,8192]{1,0:T(8,128)S(1)} %transport.28.refs_4_, ...), custom_call_target="tpu_custom_call" | custom-call | tf_op jit(solution)/shard_map/finish/pallas_call | solution.py:512
  (72 shorter events, 18.3 us)
Async XLA Ops:
  6.1 1.6 %collective-permute-start = (f32[416,128]{1,0:T(8,128)S(1)}, f32[416,128]{1,0:T(8,128)S(1)}, u32[]{:S(2)}, u32[]{:S(2)}) collective-permute-start(f32[416,128]{1,0:T(8,128)S(1)} %slice_select_fusion.1), channel_id=1, source_target_pairs={{0,1},{1,0},{2,3},{3,2},{4,5},{5,4},{6,7},{7,6},{8,9},{9,8},{10,11... | collective-permute-start | bytes 638984 | tf_op jit(solution)/shard_map/ppermute | solution.py:551
  7.8 5.1 %collective-permute-start.1 = (f32[104,128]{1,0:T(8,128)S(1)}, f32[104,128]{1,0:T(8,128)S(1)}, u32[]{:S(2)}, u32[]{:S(2)}) collective-permute-start(f32[104,128]{1,0:T(8,128)S(1)} %get-tuple-element.68), channel_id=1, source_target_pairs={{0,2},{1,3},{2,0},{3,1},{4,6},{5,7},{6,4},{7,5},{8,10},{9,11},{10,... | collective-permute-start | bytes 159752 | tf_op jit(solution)/shard_map/ppermute | solution.py:551
  10.7 4.5 %collective-permute-start.3 = (f32[104,128]{1,0:T(8,128)S(1)}, f32[104,128]{1,0:T(8,128)S(1)}, u32[]{:S(2)}, u32[]{:S(2)}) collective-permute-start(f32[104,128]{1,0:T(8,128)S(1)} %get-tuple-element.69), channel_id=1, source_target_pairs={{0,2},{1,3},{2,0},{3,1},{4,6},{5,7},{6,4},{7,5},{8,10},{9,11},{10,... | collective-permute-start | bytes 159752 | tf_op jit(solution)/shard_map/ppermute | solution.py:551
  12.9 5.0 %collective-permute-start.2 = (f32[104,128]{1,0:T(8,128)S(1)}, f32[104,128]{1,0:T(8,128)S(1)}, u32[]{:S(2)}, u32[]{:S(2)}) collective-permute-start(f32[104,128]{1,0:T(8,128)S(1)} %add.22.left_ref), channel_id=1, source_target_pairs={{0,4},{1,5},{2,6},{3,7},{4,0},{5,1},{6,2},{7,3},{8,12},{9,13},{10,... | collective-permute-start | bytes 159752 | tf_op jit(solution)/shard_map/ppermute | solution.py:551
  15.2 5.4 %collective-permute-start.5 = (f32[104,128]{1,0:T(8,128)S(1)}, f32[104,128]{1,0:T(8,128)S(1)}, u32[]{:S(2)}, u32[]{:S(2)}) collective-permute-start(f32[104,128]{1,0:T(8,128)S(1)} %add.23.left_ref), channel_id=1, source_target_pairs={{0,4},{1,5},{2,6},{3,7},{4,0},{5,1},{6,2},{7,3},{8,12},{9,13},{10,... | collective-permute-start | bytes 159752 | tf_op jit(solution)/shard_map/ppermute | solution.py:551
  17.8 6.5 %collective-permute-start.4 = (f32[104,128]{1,0:T(8,128)S(1)}, f32[104,128]{1,0:T(8,128)S(1)}, u32[]{:S(2)}, u32[]{:S(2)}) collective-permute-start(f32[104,128]{1,0:T(8,128)S(1)} %add.24.left_ref), channel_id=1, source_target_pairs={{0,8},{1,9},{2,10},{3,11},{4,12},{5,13},{6,14},{7,15},{8,0},{9,1},... | collective-permute-start | bytes 159752 | tf_op jit(solution)/shard_map/ppermute | solution.py:551
  20.7 5.2 %collective-permute-start.7 = (f32[104,128]{1,0:T(8,128)S(1)}, f32[104,128]{1,0:T(8,128)S(1)}, u32[]{:S(2)}, u32[]{:S(2)}) collective-permute-start(f32[104,128]{1,0:T(8,128)S(1)} %add.25.left_ref), channel_id=1, source_target_pairs={{0,8},{1,9},{2,10},{3,11},{4,12},{5,13},{6,14},{7,15},{8,0},{9,1},... | collective-permute-start | bytes 159752 | tf_op jit(solution)/shard_map/ppermute | solution.py:551
  24.4 5.0 %collective-permute-start.6 = (f32[104,128]{1,0:T(8,128)S(1)}, f32[104,128]{1,0:T(8,128)S(1)}, u32[]{:S(2)}, u32[]{:S(2)}) collective-permute-start(f32[104,128]{1,0:T(8,128)S(1)} %add.26), channel_id=1, source_target_pairs={{0,2},{1,3},{2,0},{3,1},{4,6},{5,7},{6,4},{7,5},{8,10},{9,11},{10,... | collective-permute-start | bytes 159752 | tf_op jit(solution)/shard_map/ppermute | solution.py:551
  25.9 4.2 %collective-permute-start.9 = (f32[104,128]{1,0:T(8,128)S(1)}, f32[104,128]{1,0:T(8,128)S(1)}, u32[]{:S(2)}, u32[]{:S(2)}) collective-permute-start(f32[104,128]{1,0:T(8,128)S(1)} %add.27), channel_id=1, source_target_pairs={{0,2},{1,3},{2,0},{3,1},{4,6},{5,7},{6,4},{7,5},{8,10},{9,11},{10,... | collective-permute-start | bytes 159752 | tf_op jit(solution)/shard_map/ppermute | solution.py:551
  29.4 1.7 %collective-permute-start.8 = (f32[208,128]{1,0:T(8,128)S(1)}, f32[208,128]{1,0:T(8,128)S(1)}, u32[]{:S(2)}, u32[]{:S(2)}) collective-permute-start(f32[208,128]{1,0:T(8,128)S(1)} %pad_maximum_fusion.2), channel_id=1, source_target_pairs={{0,1},{1,0},{2,3},{3,2},{4,5},{5,4},{6,7},{7,6},{8,9},{9,8},{10,11... | collective-permute-start | bytes 319496 | tf_op jit(solution)/shard_map/ppermute | solution.py:551
  30.1 1.4 %collective-permute-start.10 = (f32[208,128]{1,0:T(8,128)S(1)}, f32[208,128]{1,0:T(8,128)S(1)}, u32[]{:S(2)}, u32[]{:S(2)}) collective-permute-start(f32[208,128]{1,0:T(8,128)S(1)} %pad_maximum_fusion.3), channel_id=1, source_target_pairs={{0,1},{1,0},{2,3},{3,2},{4,5},{5,4},{6,7},{7,6},{8,9},{9,8},{10,11... | collective-permute-start | bytes 319496 | tf_op jit(solution)/shard_map/ppermute | solution.py:551
  35.6 1.5 %collective-permute-start.11 = (f32[416,128]{1,0:T(8,128)S(1)}, f32[416,128]{1,0:T(8,128)S(1)}, u32[]{:S(2)}, u32[]{:S(2)}) collective-permute-start(f32[416,128]{1,0:T(8,128)S(1)} %slice_select_fusion), channel_id=1, source_target_pairs={{0,1},{1,0},{2,3},{3,2},{4,5},{5,4},{6,7},{7,6},{8,9},{9,8},{10,11... | collective-permute-start | bytes 638984 | tf_op jit(solution)/shard_map/ppermute | solution.py:551
  37.2 4.4 %collective-permute-start.12 = (f32[104,128]{1,0:T(8,128)S(1)}, f32[104,128]{1,0:T(8,128)S(1)}, u32[]{:S(2)}, u32[]{:S(2)}) collective-permute-start(f32[104,128]{1,0:T(8,128)S(1)} %get-tuple-element.95), channel_id=1, source_target_pairs={{0,2},{1,3},{2,0},{3,1},{4,6},{5,7},{6,4},{7,5},{8,10},{9,11},{10,... | collective-permute-start | bytes 159752 | tf_op jit(solution)/shard_map/ppermute | solution.py:551
  38.8 4.1 %collective-permute-start.14 = (f32[104,128]{1,0:T(8,128)S(1)}, f32[104,128]{1,0:T(8,128)S(1)}, u32[]{:S(2)}, u32[]{:S(2)}) collective-permute-start(f32[104,128]{1,0:T(8,128)S(1)} %get-tuple-element.96), channel_id=1, source_target_pairs={{0,2},{1,3},{2,0},{3,1},{4,6},{5,7},{6,4},{7,5},{8,10},{9,11},{10,... | collective-permute-start | bytes 159752 | tf_op jit(solution)/shard_map/ppermute | solution.py:551
  41.6 4.3 %collective-permute-start.13 = (f32[104,128]{1,0:T(8,128)S(1)}, f32[104,128]{1,0:T(8,128)S(1)}, u32[]{:S(2)}, u32[]{:S(2)}) collective-permute-start(f32[104,128]{1,0:T(8,128)S(1)} %add.28.left_ref), channel_id=1, source_target_pairs={{0,4},{1,5},{2,6},{3,7},{4,0},{5,1},{6,2},{7,3},{8,12},{9,13},{10,... | collective-permute-start | bytes 159752 | tf_op jit(solution)/shard_map/ppermute | solution.py:551
  42.9 5.2 %collective-permute-start.16 = (f32[104,128]{1,0:T(8,128)S(1)}, f32[104,128]{1,0:T(8,128)S(1)}, u32[]{:S(2)}, u32[]{:S(2)}) collective-permute-start(f32[104,128]{1,0:T(8,128)S(1)} %add.29.left_ref), channel_id=1, source_target_pairs={{0,4},{1,5},{2,6},{3,7},{4,0},{5,1},{6,2},{7,3},{8,12},{9,13},{10,... | collective-permute-start | bytes 159752 | tf_op jit(solution)/shard_map/ppermute | solution.py:551
  46.0 6.1 %collective-permute-start.15 = (f32[104,128]{1,0:T(8,128)S(1)}, f32[104,128]{1,0:T(8,128)S(1)}, u32[]{:S(2)}, u32[]{:S(2)}) collective-permute-start(f32[104,128]{1,0:T(8,128)S(1)} %add.30.left_ref), channel_id=1, source_target_pairs={{0,8},{1,9},{2,10},{3,11},{4,12},{5,13},{6,14},{7,15},{8,0},{9,1},... | collective-permute-start | bytes 159752 | tf_op jit(solution)/shard_map/ppermute | solution.py:551
  48.1 5.1 %collective-permute-start.18 = (f32[104,128]{1,0:T(8,128)S(1)}, f32[104,128]{1,0:T(8,128)S(1)}, u32[]{:S(2)}, u32[]{:S(2)}) collective-permute-start(f32[104,128]{1,0:T(8,128)S(1)} %add.31.left_ref), channel_id=1, source_target_pairs={{0,8},{1,9},{2,10},{3,11},{4,12},{5,13},{6,14},{7,15},{8,0},{9,1},... | collective-permute-start | bytes 159752 | tf_op jit(solution)/shard_map/ppermute | solution.py:551
  52.1 4.9 %collective-permute-start.17 = (f32[104,128]{1,0:T(8,128)S(1)}, f32[104,128]{1,0:T(8,128)S(1)}, u32[]{:S(2)}, u32[]{:S(2)}) collective-permute-start(f32[104,128]{1,0:T(8,128)S(1)} %add.32), channel_id=1, source_target_pairs={{0,2},{1,3},{2,0},{3,1},{4,6},{5,7},{6,4},{7,5},{8,10},{9,11},{10,... | collective-permute-start | bytes 159752 | tf_op jit(solution)/shard_map/ppermute | solution.py:551
  53.2 4.2 %collective-permute-start.20 = (f32[104,128]{1,0:T(8,128)S(1)}, f32[104,128]{1,0:T(8,128)S(1)}, u32[]{:S(2)}, u32[]{:S(2)}) collective-permute-start(f32[104,128]{1,0:T(8,128)S(1)} %add.33), channel_id=1, source_target_pairs={{0,2},{1,3},{2,0},{3,1},{4,6},{5,7},{6,4},{7,5},{8,10},{9,11},{10,... | collective-permute-start | bytes 159752 | tf_op jit(solution)/shard_map/ppermute | solution.py:551
  57.4 1.7 %collective-permute-start.19 = (f32[208,128]{1,0:T(8,128)S(1)}, f32[208,128]{1,0:T(8,128)S(1)}, u32[]{:S(2)}, u32[]{:S(2)}) collective-permute-start(f32[208,128]{1,0:T(8,128)S(1)} %pad_maximum_fusion.4), channel_id=1, source_target_pairs={{0,1},{1,0},{2,3},{3,2},{4,5},{5,4},{6,7},{7,6},{8,9},{9,8},{10,11... | collective-permute-start | bytes 319496 | tf_op jit(solution)/shard_map/ppermute | solution.py:551
  57.5 1.6 %collective-permute-start.21 = (f32[208,128]{1,0:T(8,128)S(1)}, f32[208,128]{1,0:T(8,128)S(1)}, u32[]{:S(2)}, u32[]{:S(2)}) collective-permute-start(f32[208,128]{1,0:T(8,128)S(1)} %pad_maximum_fusion.5), channel_id=1, source_target_pairs={{0,1},{1,0},{2,3},{3,2},{4,5},{5,4},{6,7},{7,6},{8,9},{9,8},{10,11... | collective-permute-start | bytes 319496 | tf_op jit(solution)/shard_map/ppermute | solution.py:551

commit v12 on v11

--- a/solution.py
+++ b/solution.py
@@ -29,6 +29,7 @@
 DEPARTURES = 16
 PARTS = 8
 BESIDE = (1, 2, 1, 1, 2, 1)
+BESIDE_ROUNDS = (1, 2, 2, 2, 1)
 MIB = 1024 * 1024
 
 WHOLE = pl.BlockSpec(memory_space=pltpu.VMEM)
@@ -72,14 +73,19 @@
     return high, middle, values - high - middle
 
 
+def polynomial_table_of(velocities):
+    high, middle, _ = parts_of(phi_rows(velocities)[0])
+    wide = jnp.zeros((128 - 3 * BASIS, velocities.shape[1]), jnp.float32)
+    rows = jnp.concatenate([high, high, middle, wide], axis=0)
+    return rows.T[:, : 3 * BASIS].astype(jnp.bfloat16)
+
+
 def make_tables(velocities, total_count):
     phi, sq = phi_rows(velocities)
     high, middle, low = parts_of(phi)
     three = [high[:8], high[:8], high[:8], middle[:8], middle[:8], low[:8]]
     wide = jnp.zeros((128 - 6 * 8, phi.shape[1]), jnp.float32)
     exponent = jnp.concatenate(three + [wide], axis=0).T[:, : 6 * 8].astype(jnp.bfloat16)
-    two = [high, high, middle]
-    polynomial = jnp.concatenate(two + [wide], axis=0).T[:, : 3 * BASIS].astype(jnp.bfloat16)
     weighted = phi * (SPREAD_SCALE**3 * jnp.exp(sq / (2.0 * SPREAD_SCALE**2)) / total_count)
     top = rounded(weighted)
     rest = weighted - top
@@ -90,7 +96,7 @@
         ],
         axis=0,
     ).astype(jnp.bfloat16)
-    return exponent, polynomial, moments
+    return exponent, moments
 
 
 def expand_exponent(rows):
@@ -167,11 +173,9 @@
     for copy in copies:
         copy.start()
     small[0].wait()
-    exponent_table, polynomial_table, table = make_tables(vel_ref[...], total_count)
+    exponent_table, table = make_tables(vel_ref[...], total_count)
     exponent_ref[...] = exponent_table
-    polynomial_ref[...] = polynomial_table
     table_ref[...] = table
-    stream_ref[...] = jnp.broadcast_to(vel_ref[0:1, :], (LANES, vel_ref.shape[1])).T
     for copy in small[1:]:
         copy.wait()
     def front(tile):
@@ -191,6 +195,9 @@
 
     def back(tile, split):
         store_moments(moments_ref, table, split, tile, cells // LANES)
+        if tile == 1:
+            polynomial_ref[...] = polynomial_table_of(vel_ref[...])
+            stream_ref[...] = jnp.broadcast_to(vel_ref[0:1, :], (LANES, vel_ref.shape[1])).T
 
     def front_when_here(tile):
         if tile * TILE % width == 0:
@@ -601,6 +608,37 @@
     return jnp.concatenate(lowers + uppers, axis=0), results
 
 
+def rounds_sum(values, count, even, f, tasks):
+    strides = [1 << bit for bit in range(1, count.bit_length() - 1)]
+    orders = (strides, strides[1:] + strides[:1])
+    results, waiting, portions = [], list(tasks), list(BESIDE_ROUNDS)
+
+    def exchange(chunks, chosen):
+        got = [swap(chunk, count, stride) for chunk, stride in zip(chunks, chosen)]
+        portion = portions.pop(0) if portions else 0
+        if portion:
+            _, held = lax.optimization_barrier((chunks[-1], f))
+            made = [task(held) for task in waiting[:portion]]
+            del waiting[:portion]
+            got[0], made = lax.optimization_barrier((got[0], made))
+            results.extend(made)
+        return got
+
+    half = values.shape[0] // 2
+    first, second = values[:half], values[half:]
+    kept, sent = jnp.where(even, first, second), jnp.where(even, second, first)
+    (got,) = exchange([sent], [1])
+    block = kept + got
+    chunks = lax.optimization_barrier([block[: half // 2], block[half // 2 :]])
+    for chosen in zip(*orders):
+        chunks = [add_call(own, got) for own, got in zip(chunks, exchange(chunks, chosen))]
+    got = exchange(chunks, [1, 1])
+    results.extend(task(f) for task in waiting)
+    lower = [jnp.where(even, own, other) for own, other in zip(chunks, got)]
+    upper = [jnp.where(even, other, own) for own, other in zip(chunks, got)]
+    return jnp.concatenate(lower + upper, axis=0), results
+
+
 def on_device(velocities, density, flow, thermal, deviation):
     count = lax.axis_size("vel")
     place = lax.axis_index("vel")
@@ -614,7 +652,10 @@
             functools.partial(lambda held, part: transport_call(stream, held, part), part=part)
             for part in range(PARTS)
         ]
-        summed, g = staged_sum(moments, count, sides, f, tasks)
+        if iteration == 0:
+            summed, g = rounds_sum(moments, count, sides[0], f, tasks)
+        else:
+            summed, g = staged_sum(moments, count, sides, f, tasks)
         last = iteration == ITERS - 1
         coefficients, *macro = fluid_call(summed, last)
         if not last:

time: 62.8 us -> 64 us (1.019)
  waiting for transfers between devices: 5.27 us -> 6.58 us
    ppermute x22 -> x20, waiting for transfers between devices: 5.27 us -> 6.58 us  [swap(): lax.ppermute(values, 'vel', [(device, device ^ stride) for device in rang...]
    ppermute x22 -> x20, starting transfers between devices: 27 us -> 26.9 us  [swap(): lax.ppermute(values, 'vel', [(device, device ^ stride) for device in rang...]
  transfers between devices with their start and end apart: 22 -> 20, of which waited for: 12 -> 10; matrix products, arithmetic and copies ran while one was open for 0% -> 0% of each run, Pallas kernels for 26% -> 25%
where the time goes in v12:
time: 64 us; the launch traced here: 63.8 us
  Pallas kernels  28.8 us (45%)
  starting transfers between devices  26.9 us (42%)
  waiting for transfers between devices  6.58 us (10%)
  between operations  1.17 us (2%)
    ppermute x20, starting transfers between devices, swap(): lax.ppermute(values, 'vel', [(device, device ^ stride) for device in rang...  26.9 us
    pallas_call x16, Pallas kernels, transport_call(): pl.pallas_call(functools.partial(transport_kernel, part * rows), out_shap...  16 us
    ppermute x20, waiting for transfers between devices, swap(): lax.ppermute(values, 'vel', [(device, device ^ stride) for device in rang...  6.58 us
    pallas_call x1, Pallas kernels, start_call(): pl.pallas_call(functools.partial(start_kernel, total_count), out_shape=(p...  5.41 us
    pallas_call x1, Pallas kernels, update_call(): pl.pallas_call(update_kernel, out_shape=(pltpu.VMEM((rows * PARTS, cells)...  3.2 us
    pallas_call x1, Pallas kernels, finish_call(): pl.pallas_call(finish_kernel, out_shape=(jax.ShapeDtypeStruct((rows * PAR...  2.4 us
    pallas_call x2, Pallas kernels, fluid_call(): pl.pallas_call(fluid_kernel, out_shape=shapes, in_specs=[WHOLE], out_spec...  1.71 us
  transfers between devices with their start and end apart: 20, of which 10 were waited for; matrix products, arithmetic and copies ran while one was open for 0% of the time, Pallas kernels for 25%

profile of v12, /device:TPU:0, one launch (start us, length us, event | category | flops | bytes accessed | tf_op | source)
XLA Modules:
  0.0 63.8 jit_solution(3793495584317643844)
XLA Ops:
  0.6 5.4 %start.1 = (f32[128,8192]{1,0:T(8,128)S(1)}, f32[832,128]{1,0:T(8,128)S(1)}, bf16[128,48]{1,0:T(8,128)(2,1)S(1)}, bf16[128,48]{1,0:T(8,128)(2,1)S(1)}, bf16[32,2...) custom-call(f32[3,128]{1,0:T(4,128)} %vel_hbm, f32[1,8192]{1,0:T(1,128)} %bitcast.2, f32[3,8192]{1,0:T(4,128)} %flow_hbm.1, ...), custom_call_target="tpu_custom_call" | custom-call | tf_op jit(solution)/shard_map/start/pallas_call | solution.py:212
  6.6 1.0 %transport.16.refs_0_ = f32[16,8192]{1,0:T(8,128)S(1)} custom-call(f32[128,128]{1,0:T(8,128)S(1)} %get-tuple-element.60.stream_ref, f32[128,8192]{1,0:T(8,128)S(1)} %get-tuple-element.79.f_ref), custom_call_target="tpu_custom_call" | custom-call | tf_op jit(solution)/shard_map/transport/pallas_call | solution.py:303
  7.7 3.0 %collective-permute-start.1 = (f32[208,128]{1,0:T(8,128)S(1)}, f32[208,128]{1,0:T(8,128)S(1)}, u32[]{:S(2)}, u32[]{:S(2)}) collective-permute-start(f32[208,128]{1,0:T(8,128)S(1)} %get-tuple-element.65.left_ref), channel_id=1, source_target_pairs={{0,2},{1,3},{2,0},{3,1},{4,6},{5,7},{6,4},{7,5},{8,10},{9,11},{10,... | collective-permute-start | bytes 319496 | tf_op jit(solution)/shard_map/ppermute | solution.py:558
  10.7 1.6 %collective-permute-start.3 = (f32[208,128]{1,0:T(8,128)S(1)}, f32[208,128]{1,0:T(8,128)S(1)}, u32[]{:S(2)}, u32[]{:S(2)}) collective-permute-start(f32[208,128]{1,0:T(8,128)S(1)} %get-tuple-element.66.left_ref), channel_id=1, source_target_pairs={{0,4},{1,5},{2,6},{3,7},{4,0},{5,1},{6,2},{7,3},{8,12},{9,13},{10,... | collective-permute-start | bytes 319496 | tf_op jit(solution)/shard_map/ppermute | solution.py:558
  12.3 1.0 %transport.18.refs_2_ = f32[16,8192]{1,0:T(8,128)S(1)} custom-call(f32[128,128]{1,0:T(8,128)S(1)} %get-tuple-element.60.stream_ref, f32[128,8192]{1,0:T(8,128)S(1)} %get-tuple-element.79.f_ref), custom_call_target="tpu_custom_call" | custom-call | tf_op jit(solution)/shard_map/transport/pallas_call | solution.py:303
  13.3 1.0 %transport.17.refs_1_ = f32[16,8192]{1,0:T(8,128)S(1)} custom-call(f32[128,128]{1,0:T(8,128)S(1)} %get-tuple-element.60.stream_ref, f32[128,8192]{1,0:T(8,128)S(1)} %get-tuple-element.79.f_ref), custom_call_target="tpu_custom_call" | custom-call | tf_op jit(solution)/shard_map/transport/pallas_call | solution.py:303
  14.3 1.5 %collective-permute-start.2 = (f32[208,128]{1,0:T(8,128)S(1)}, f32[208,128]{1,0:T(8,128)S(1)}, u32[]{:S(2)}, u32[]{:S(2)}) collective-permute-start(f32[208,128]{1,0:T(8,128)S(1)} %add.22.left_ref), channel_id=1, source_target_pairs={{0,4},{1,5},{2,6},{3,7},{4,0},{5,1},{6,2},{7,3},{8,12},{9,13},{10,... | collective-permute-start | bytes 319496 | tf_op jit(solution)/shard_map/ppermute | solution.py:558
  15.9 2.7 %collective-permute-start.5 = (f32[208,128]{1,0:T(8,128)S(1)}, f32[208,128]{1,0:T(8,128)S(1)}, u32[]{:S(2)}, u32[]{:S(2)}) collective-permute-start(f32[208,128]{1,0:T(8,128)S(1)} %add.23.left_ref), channel_id=1, source_target_pairs={{0,8},{1,9},{2,10},{3,11},{4,12},{5,13},{6,14},{7,15},{8,0},{9,1},... | collective-permute-start | bytes 319496 | tf_op jit(solution)/shard_map/ppermute | solution.py:558
  19.5 1.0 %transport.19.refs_3_ = f32[16,8192]{1,0:T(8,128)S(1)} custom-call(f32[128,128]{1,0:T(8,128)S(1)} %get-tuple-element.60.stream_ref, f32[128,8192]{1,0:T(8,128)S(1)} %get-tuple-element.79.f_ref), custom_call_target="tpu_custom_call" | custom-call | tf_op jit(solution)/shard_map/transport/pallas_call | solution.py:303
  20.6 2.1 %collective-permute-start.4 = (f32[208,128]{1,0:T(8,128)S(1)}, f32[208,128]{1,0:T(8,128)S(1)}, u32[]{:S(2)}, u32[]{:S(2)}) collective-permute-start(f32[208,128]{1,0:T(8,128)S(1)} %add.24.left_ref), channel_id=1, source_target_pairs={{0,8},{1,9},{2,10},{3,11},{4,12},{5,13},{6,14},{7,15},{8,0},{9,1},... | collective-permute-start | bytes 319496 | tf_op jit(solution)/shard_map/ppermute | solution.py:558
  23.4 2.5 %collective-permute-start.7 = (f32[208,128]{1,0:T(8,128)S(1)}, f32[208,128]{1,0:T(8,128)S(1)}, u32[]{:S(2)}, u32[]{:S(2)}) collective-permute-start(f32[208,128]{1,0:T(8,128)S(1)} %add.25.left_ref), channel_id=1, source_target_pairs={{0,2},{1,3},{2,0},{3,1},{4,6},{5,7},{6,4},{7,5},{8,10},{9,11},{10,... | collective-permute-start | bytes 319496 | tf_op jit(solution)/shard_map/ppermute | solution.py:558
  26.9 1.0 %transport.21.refs_5_ = f32[16,8192]{1,0:T(8,128)S(1)} custom-call(f32[128,128]{1,0:T(8,128)S(1)} %get-tuple-element.60.stream_ref, f32[128,8192]{1,0:T(8,128)S(1)} %get-tuple-element.79.f_ref), custom_call_target="tpu_custom_call" | custom-call | tf_op jit(solution)/shard_map/transport/pallas_call | solution.py:303
  28.6 1.0 %transport.23.refs_7_ = f32[16,8192]{1,0:T(8,128)S(1)} custom-call(f32[128,128]{1,0:T(8,128)S(1)} %get-tuple-element.60.stream_ref, f32[128,8192]{1,0:T(8,128)S(1)} %get-tuple-element.79.f_ref), custom_call_target="tpu_custom_call" | custom-call | tf_op jit(solution)/shard_map/transport/pallas_call | solution.py:303
  30.9 3.2 %update.1 = (f32[128,8192]{1,0:T(8,128)S(1)}, f32[832,128]{1,0:T(8,128)S(1)}) custom-call(f32[16,8192]{1,0:T(8,128)S(1)} %transport.16.refs_0_, f32[16,8192]{1,0:T(8,128)S(1)} %transport.17.refs_1_, f32[16,8192]{1,0:T(8,128)S(1)} %transport.18.refs_2_, f32[16,8192]{1,0:T(8,128)S(1)} %transport.19.refs_3_, f32[16,8192]{1,0:T(8,128)S(1)} %transport.20.refs_4_, ...), custom_call_target="tpu_custom_call" | custom-call | tf_op jit(solution)/shard_map/update/pallas_call | solution.py:479
  35.7 2.1 %collective-permute-start.10 = (f32[104,128]{1,0:T(8,128)S(1)}, f32[104,128]{1,0:T(8,128)S(1)}, u32[]{:S(2)}, u32[]{:S(2)}) collective-permute-start(f32[104,128]{1,0:T(8,128)S(1)} %get-tuple-element.91), channel_id=1, source_target_pairs={{0,2},{1,3},{2,0},{3,1},{4,6},{5,7},{6,4},{7,5},{8,10},{9,11},{10,... | collective-permute-start | bytes 159752 | tf_op jit(solution)/shard_map/ppermute | solution.py:558
  38.9 1.0 %transport.25.refs_1_ = f32[16,8192]{1,0:T(8,128)S(1)} custom-call(f32[128,128]{1,0:T(8,128)S(1)} %get-tuple-element.60.stream_ref, f32[128,8192]{1,0:T(8,128)S(1)} %get-tuple-element.107.f_ref), custom_call_target="tpu_custom_call" | custom-call | tf_op jit(solution)/shard_map/transport/pallas_call | solution.py:303
  40.0 2.1 %collective-permute-start.11 = (f32[104,128]{1,0:T(8,128)S(1)}, f32[104,128]{1,0:T(8,128)S(1)}, u32[]{:S(2)}, u32[]{:S(2)}) collective-permute-start(f32[104,128]{1,0:T(8,128)S(1)} %add.28.left_ref), channel_id=1, source_target_pairs={{0,4},{1,5},{2,6},{3,7},{4,0},{5,1},{6,2},{7,3},{8,12},{9,13},{10,... | collective-permute-start | bytes 159752 | tf_op jit(solution)/shard_map/ppermute | solution.py:558
  43.7 1.1 %collective-permute-done.11.right_ref = f32[104,128]{1,0:T(8,128)S(1)} collective-permute-done((f32[104,128]{1,0:T(8,128)S(1)}, f32[104,128]{1,0:T(8,128)S(1)}, u32[]{:S(2)}, u32[]{:S(2)}) %collective-permute-start.11) | collective-permute-done | bytes 53280 | tf_op jit(solution)/shard_map/ppermute | solution.py:558
  44.8 4.5 %collective-permute-start.13 = (f32[104,128]{1,0:T(8,128)S(1)}, f32[104,128]{1,0:T(8,128)S(1)}, u32[]{:S(2)}, u32[]{:S(2)}) collective-permute-start(f32[104,128]{1,0:T(8,128)S(1)} %add.30.left_ref), channel_id=1, source_target_pairs={{0,8},{1,9},{2,10},{3,11},{4,12},{5,13},{6,14},{7,15},{8,0},{9,1},... | collective-permute-start | bytes 159752 | tf_op jit(solution)/shard_map/ppermute | solution.py:558
  49.3 1.6 %collective-permute-start.16 = (f32[104,128]{1,0:T(8,128)S(1)}, f32[104,128]{1,0:T(8,128)S(1)}, u32[]{:S(2)}, u32[]{:S(2)}) collective-permute-start(f32[104,128]{1,0:T(8,128)S(1)} %add.31.left_ref), channel_id=1, source_target_pairs={{0,8},{1,9},{2,10},{3,11},{4,12},{5,13},{6,14},{7,15},{8,0},{9,1},... | collective-permute-start | bytes 159752 | tf_op jit(solution)/shard_map/ppermute | solution.py:558
  51.9 1.1 %collective-permute-done.13.right_ref = f32[104,128]{1,0:T(8,128)S(1)} collective-permute-done((f32[104,128]{1,0:T(8,128)S(1)}, f32[104,128]{1,0:T(8,128)S(1)}, u32[]{:S(2)}, u32[]{:S(2)}) %collective-permute-start.13) | collective-permute-done | bytes 53280 | tf_op jit(solution)/shard_map/ppermute | solution.py:558
  56.2 1.0 %transport.29.refs_5_ = f32[16,8192]{1,0:T(8,128)S(1)} custom-call(f32[128,128]{1,0:T(8,128)S(1)} %get-tuple-element.60.stream_ref, f32[128,8192]{1,0:T(8,128)S(1)} %get-tuple-element.107.f_ref), custom_call_target="tpu_custom_call" | custom-call | tf_op jit(solution)/shard_map/transport/pallas_call | solution.py:303
  57.2 1.4 %collective-permute-done.18 = f32[104,128]{1,0:T(8,128)S(1)} collective-permute-done((f32[104,128]{1,0:T(8,128)S(1)}, f32[104,128]{1,0:T(8,128)S(1)}, u32[]{:S(2)}, u32[]{:S(2)}) %collective-permute-start.18) | collective-permute-done | bytes 53280 | tf_op jit(solution)/shard_map/ppermute | solution.py:558
  61.3 2.4 %finish.1 = (f32[128,8192]{1,0:T(8,128)}, f32[8,8192]{1,0:T(8,128)}) custom-call(f32[16,8192]{1,0:T(8,128)S(1)} %transport.24.refs_0_, f32[16,8192]{1,0:T(8,128)S(1)} %transport.25.refs_1_, f32[16,8192]{1,0:T(8,128)S(1)} %transport.26.refs_2_, f32[16,8192]{1,0:T(8,128)S(1)} %transport.27.refs_3_, f32[16,8192]{1,0:T(8,128)S(1)} %transport.28.refs_4_, ...), custom_call_target="tpu_custom_call" | custom-call | tf_op jit(solution)/shard_map/finish/pallas_call | solution.py:519
  (64 shorter events, 16.6 us)
Async XLA Ops:
  6.1 1.6 %collective-permute-start = (f32[416,128]{1,0:T(8,128)S(1)}, f32[416,128]{1,0:T(8,128)S(1)}, u32[]{:S(2)}, u32[]{:S(2)}) collective-permute-start(f32[416,128]{1,0:T(8,128)S(1)} %slice_select_fusion.1), channel_id=1, source_target_pairs={{0,1},{1,0},{2,3},{3,2},{4,5},{5,4},{6,7},{7,6},{8,9},{9,8},{10,11... | collective-permute-start | bytes 638984 | tf_op jit(solution)/shard_map/ppermute | solution.py:558
  7.7 6.5 %collective-permute-start.1 = (f32[208,128]{1,0:T(8,128)S(1)}, f32[208,128]{1,0:T(8,128)S(1)}, u32[]{:S(2)}, u32[]{:S(2)}) collective-permute-start(f32[208,128]{1,0:T(8,128)S(1)} %get-tuple-element.65.left_ref), channel_id=1, source_target_pairs={{0,2},{1,3},{2,0},{3,1},{4,6},{5,7},{6,4},{7,5},{8,10},{9,11},{10,... | collective-permute-start | bytes 319496 | tf_op jit(solution)/shard_map/ppermute | solution.py:558
  10.7 5.2 %collective-permute-start.3 = (f32[208,128]{1,0:T(8,128)S(1)}, f32[208,128]{1,0:T(8,128)S(1)}, u32[]{:S(2)}, u32[]{:S(2)}) collective-permute-start(f32[208,128]{1,0:T(8,128)S(1)} %get-tuple-element.66.left_ref), channel_id=1, source_target_pairs={{0,4},{1,5},{2,6},{3,7},{4,0},{5,1},{6,2},{7,3},{8,12},{9,13},{10,... | collective-permute-start | bytes 319496 | tf_op jit(solution)/shard_map/ppermute | solution.py:558
  14.3 6.2 %collective-permute-start.2 = (f32[208,128]{1,0:T(8,128)S(1)}, f32[208,128]{1,0:T(8,128)S(1)}, u32[]{:S(2)}, u32[]{:S(2)}) collective-permute-start(f32[208,128]{1,0:T(8,128)S(1)} %add.22.left_ref), channel_id=1, source_target_pairs={{0,4},{1,5},{2,6},{3,7},{4,0},{5,1},{6,2},{7,3},{8,12},{9,13},{10,... | collective-permute-start | bytes 319496 | tf_op jit(solution)/shard_map/ppermute | solution.py:558
  15.9 7.5 %collective-permute-start.5 = (f32[208,128]{1,0:T(8,128)S(1)}, f32[208,128]{1,0:T(8,128)S(1)}, u32[]{:S(2)}, u32[]{:S(2)}) collective-permute-start(f32[208,128]{1,0:T(8,128)S(1)} %add.23.left_ref), channel_id=1, source_target_pairs={{0,8},{1,9},{2,10},{3,11},{4,12},{5,13},{6,14},{7,15},{8,0},{9,1},... | collective-permute-start | bytes 319496 | tf_op jit(solution)/shard_map/ppermute | solution.py:558
  20.6 7.3 %collective-permute-start.4 = (f32[208,128]{1,0:T(8,128)S(1)}, f32[208,128]{1,0:T(8,128)S(1)}, u32[]{:S(2)}, u32[]{:S(2)}) collective-permute-start(f32[208,128]{1,0:T(8,128)S(1)} %add.24.left_ref), channel_id=1, source_target_pairs={{0,8},{1,9},{2,10},{3,11},{4,12},{5,13},{6,14},{7,15},{8,0},{9,1},... | collective-permute-start | bytes 319496 | tf_op jit(solution)/shard_map/ppermute | solution.py:558
  23.4 5.2 %collective-permute-start.7 = (f32[208,128]{1,0:T(8,128)S(1)}, f32[208,128]{1,0:T(8,128)S(1)}, u32[]{:S(2)}, u32[]{:S(2)}) collective-permute-start(f32[208,128]{1,0:T(8,128)S(1)} %add.25.left_ref), channel_id=1, source_target_pairs={{0,2},{1,3},{2,0},{3,1},{4,6},{5,7},{6,4},{7,5},{8,10},{9,11},{10,... | collective-permute-start | bytes 319496 | tf_op jit(solution)/shard_map/ppermute | solution.py:558
  27.9 1.7 %collective-permute-start.6 = (f32[208,128]{1,0:T(8,128)S(1)}, f32[208,128]{1,0:T(8,128)S(1)}, u32[]{:S(2)}, u32[]{:S(2)}) collective-permute-start(f32[208,128]{1,0:T(8,128)S(1)} %add.26), channel_id=1, source_target_pairs={{0,1},{1,0},{2,3},{3,2},{4,5},{5,4},{6,7},{7,6},{8,9},{9,8},{10,11... | collective-permute-start | bytes 319496 | tf_op jit(solution)/shard_map/ppermute | solution.py:558
  28.6 1.4 %collective-permute-start.8 = (f32[208,128]{1,0:T(8,128)S(1)}, f32[208,128]{1,0:T(8,128)S(1)}, u32[]{:S(2)}, u32[]{:S(2)}) collective-permute-start(f32[208,128]{1,0:T(8,128)S(1)} %add.27), channel_id=1, source_target_pairs={{0,1},{1,0},{2,3},{3,2},{4,5},{5,4},{6,7},{7,6},{8,9},{9,8},{10,11... | collective-permute-start | bytes 319496 | tf_op jit(solution)/shard_map/ppermute | solution.py:558
  34.1 1.5 %collective-permute-start.9 = (f32[416,128]{1,0:T(8,128)S(1)}, f32[416,128]{1,0:T(8,128)S(1)}, u32[]{:S(2)}, u32[]{:S(2)}) collective-permute-start(f32[416,128]{1,0:T(8,128)S(1)} %slice_select_fusion), channel_id=1, source_target_pairs={{0,1},{1,0},{2,3},{3,2},{4,5},{5,4},{6,7},{7,6},{8,9},{9,8},{10,11... | collective-permute-start | bytes 638984 | tf_op jit(solution)/shard_map/ppermute | solution.py:558
  35.7 4.3 %collective-permute-start.10 = (f32[104,128]{1,0:T(8,128)S(1)}, f32[104,128]{1,0:T(8,128)S(1)}, u32[]{:S(2)}, u32[]{:S(2)}) collective-permute-start(f32[104,128]{1,0:T(8,128)S(1)} %get-tuple-element.91), channel_id=1, source_target_pairs={{0,2},{1,3},{2,0},{3,1},{4,6},{5,7},{6,4},{7,5},{8,10},{9,11},{10,... | collective-permute-start | bytes 159752 | tf_op jit(solution)/shard_map/ppermute | solution.py:558
  37.8 4.3 %collective-permute-start.12 = (f32[104,128]{1,0:T(8,128)S(1)}, f32[104,128]{1,0:T(8,128)S(1)}, u32[]{:S(2)}, u32[]{:S(2)}) collective-permute-start(f32[104,128]{1,0:T(8,128)S(1)} %get-tuple-element.92), channel_id=1, source_target_pairs={{0,2},{1,3},{2,0},{3,1},{4,6},{5,7},{6,4},{7,5},{8,10},{9,11},{10,... | collective-permute-start | bytes 159752 | tf_op jit(solution)/shard_map/ppermute | solution.py:558
  40.0 4.7 %collective-permute-start.11 = (f32[104,128]{1,0:T(8,128)S(1)}, f32[104,128]{1,0:T(8,128)S(1)}, u32[]{:S(2)}, u32[]{:S(2)}) collective-permute-start(f32[104,128]{1,0:T(8,128)S(1)} %add.28.left_ref), channel_id=1, source_target_pairs={{0,4},{1,5},{2,6},{3,7},{4,0},{5,1},{6,2},{7,3},{8,12},{9,13},{10,... | collective-permute-start | bytes 159752 | tf_op jit(solution)/shard_map/ppermute | solution.py:558
  42.1 7.2 %collective-permute-start.14 = (f32[104,128]{1,0:T(8,128)S(1)}, f32[104,128]{1,0:T(8,128)S(1)}, u32[]{:S(2)}, u32[]{:S(2)}) collective-permute-start(f32[104,128]{1,0:T(8,128)S(1)} %add.29.left_ref), channel_id=1, source_target_pairs={{0,4},{1,5},{2,6},{3,7},{4,0},{5,1},{6,2},{7,3},{8,12},{9,13},{10,... | collective-permute-start | bytes 159752 | tf_op jit(solution)/shard_map/ppermute | solution.py:558
  44.8 8.2 %collective-permute-start.13 = (f32[104,128]{1,0:T(8,128)S(1)}, f32[104,128]{1,0:T(8,128)S(1)}, u32[]{:S(2)}, u32[]{:S(2)}) collective-permute-start(f32[104,128]{1,0:T(8,128)S(1)} %add.30.left_ref), channel_id=1, source_target_pairs={{0,8},{1,9},{2,10},{3,11},{4,12},{5,13},{6,14},{7,15},{8,0},{9,1},... | collective-permute-start | bytes 159752 | tf_op jit(solution)/shard_map/ppermute | solution.py:558
  49.3 5.1 %collective-permute-start.16 = (f32[104,128]{1,0:T(8,128)S(1)}, f32[104,128]{1,0:T(8,128)S(1)}, u32[]{:S(2)}, u32[]{:S(2)}) collective-permute-start(f32[104,128]{1,0:T(8,128)S(1)} %add.31.left_ref), channel_id=1, source_target_pairs={{0,8},{1,9},{2,10},{3,11},{4,12},{5,13},{6,14},{7,15},{8,0},{9,1},... | collective-permute-start | bytes 159752 | tf_op jit(solution)/shard_map/ppermute | solution.py:558
  53.0 4.2 %collective-permute-start.15 = (f32[104,128]{1,0:T(8,128)S(1)}, f32[104,128]{1,0:T(8,128)S(1)}, u32[]{:S(2)}, u32[]{:S(2)}) collective-permute-start(f32[104,128]{1,0:T(8,128)S(1)} %add.32), channel_id=1, source_target_pairs={{0,2},{1,3},{2,0},{3,1},{4,6},{5,7},{6,4},{7,5},{8,10},{9,11},{10,... | collective-permute-start | bytes 159752 | tf_op jit(solution)/shard_map/ppermute | solution.py:558
  54.4 4.2 %collective-permute-start.18 = (f32[104,128]{1,0:T(8,128)S(1)}, f32[104,128]{1,0:T(8,128)S(1)}, u32[]{:S(2)}, u32[]{:S(2)}) collective-permute-start(f32[104,128]{1,0:T(8,128)S(1)} %add.33), channel_id=1, source_target_pairs={{0,2},{1,3},{2,0},{3,1},{4,6},{5,7},{6,4},{7,5},{8,10},{9,11},{10,... | collective-permute-start | bytes 159752 | tf_op jit(solution)/shard_map/ppermute | solution.py:558
  58.6 1.7 %collective-permute-start.17 = (f32[208,128]{1,0:T(8,128)S(1)}, f32[208,128]{1,0:T(8,128)S(1)}, u32[]{:S(2)}, u32[]{:S(2)}) collective-permute-start(f32[208,128]{1,0:T(8,128)S(1)} %pad_maximum_fusion.2), channel_id=1, source_target_pairs={{0,1},{1,0},{2,3},{3,2},{4,5},{5,4},{6,7},{7,6},{8,9},{9,8},{10,11... | collective-permute-start | bytes 319496 | tf_op jit(solution)/shard_map/ppermute | solution.py:558
  58.7 1.6 %collective-permute-start.19 = (f32[208,128]{1,0:T(8,128)S(1)}, f32[208,128]{1,0:T(8,128)S(1)}, u32[]{:S(2)}, u32[]{:S(2)}) collective-permute-start(f32[208,128]{1,0:T(8,128)S(1)} %pad_maximum_fusion.3), channel_id=1, source_target_pairs={{0,1},{1,0},{2,3},{3,2},{4,5},{5,4},{6,7},{7,6},{8,9},{9,8},{10,11... | collective-permute-start | bytes 319496 | tf_op jit(solution)/shard_map/ppermute | solution.py:558

commit v13 on v11

--- a/solution.py
+++ b/solution.py
@@ -19,12 +19,12 @@
 
 LOG2E = 1.4426950408889634
 LANES = 128
-TILE = 256
+TILE = 512
 BASIS = 16
 SENT = 13
 COEF = 24
 DAMP = 13
-ROWS = 64
+ROWS = 32
 CHUNKS = 8
 DEPARTURES = 16
 PARTS = 8

time: 62.8 us -> 61.7 us (0.982)
  Pallas kernels: 28.8 us -> 27.6 us
    pallas_call x1, Pallas kernels: 3.2 us -> 2.41 us  [update_call(): pl.pallas_call(update_kernel, out_shape=(pltpu.VMEM((rows * PARTS, cells)...]
where the time goes in v13:
time: 61.7 us; the launch traced here: 61.5 us
  Pallas kernels  27.6 us (45%)
  starting transfers between devices  27 us (44%)
  waiting for transfers between devices  5.36 us (9%)
  between operations  1.19 us (2%)
    ppermute x22, starting transfers between devices, swap(): lax.ppermute(values, 'vel', [(device, device ^ stride) for device in rang...  27 us
    pallas_call x16, Pallas kernels, transport_call(): pl.pallas_call(functools.partial(transport_kernel, part * rows), out_shap...  15.9 us
    ppermute x22, waiting for transfers between devices, swap(): lax.ppermute(values, 'vel', [(device, device ^ stride) for device in rang...  5.36 us
    pallas_call x1, Pallas kernels, start_call(): pl.pallas_call(functools.partial(start_kernel, total_count), out_shape=(p...  5.04 us
    pallas_call x1, Pallas kernels, finish_call(): pl.pallas_call(finish_kernel, out_shape=(jax.ShapeDtypeStruct((rows * PAR...  2.41 us
    pallas_call x1, Pallas kernels, update_call(): pl.pallas_call(update_kernel, out_shape=(pltpu.VMEM((rows * PARTS, cells)...  2.41 us
    pallas_call x2, Pallas kernels, fluid_call(): pl.pallas_call(fluid_kernel, out_shape=shapes, in_specs=[WHOLE], out_spec...  1.71 us
  transfers between devices with their start and end apart: 22, of which 12 were waited for; matrix products, arithmetic and copies ran while one was open for 0% of the time, Pallas kernels for 26%

profile of v13, /device:TPU:0, one launch (start us, length us, event | category | flops | bytes accessed | tf_op | source)
XLA Modules:
  0.0 61.5 jit_solution(10115843637206277437)
XLA Ops:
  0.6 5.0 %start.1 = (f32[128,8192]{1,0:T(8,128)S(1)}, f32[832,128]{1,0:T(8,128)S(1)}, bf16[128,48]{1,0:T(8,128)(2,1)S(1)}, bf16[128,48]{1,0:T(8,128)(2,1)S(1)}, bf16[32,2...) custom-call(f32[3,128]{1,0:T(4,128)} %vel_hbm, f32[1,8192]{1,0:T(1,128)} %bitcast.2, f32[3,8192]{1,0:T(4,128)} %flow_hbm.1, ...), custom_call_target="tpu_custom_call" | custom-call | tf_op jit(solution)/shard_map/start/pallas_call | solution.py:205
  6.2 1.0 %transport.16.refs_0_ = f32[16,8192]{1,0:T(8,128)S(1)} custom-call(f32[128,128]{1,0:T(8,128)S(1)} %get-tuple-element.62.stream_ref, f32[128,8192]{1,0:T(8,128)S(1)} %get-tuple-element.84.f_ref), custom_call_target="tpu_custom_call" | custom-call | tf_op jit(solution)/shard_map/transport/pallas_call | solution.py:296
  7.4 2.9 %collective-permute-start.1 = (f32[104,128]{1,0:T(8,128)S(1)}, f32[104,128]{1,0:T(8,128)S(1)}, u32[]{:S(2)}, u32[]{:S(2)}) collective-permute-start(f32[104,128]{1,0:T(8,128)S(1)} %get-tuple-element.68), channel_id=1, source_target_pairs={{0,2},{1,3},{2,0},{3,1},{4,6},{5,7},{6,4},{7,5},{8,10},{9,11},{10,... | collective-permute-start | bytes 159752 | tf_op jit(solution)/shard_map/ppermute | solution.py:551
  10.4 1.0 %transport.18.refs_2_ = f32[16,8192]{1,0:T(8,128)S(1)} custom-call(f32[128,128]{1,0:T(8,128)S(1)} %get-tuple-element.62.stream_ref, f32[128,8192]{1,0:T(8,128)S(1)} %get-tuple-element.84.f_ref), custom_call_target="tpu_custom_call" | custom-call | tf_op jit(solution)/shard_map/transport/pallas_call | solution.py:296
  11.4 1.0 %transport.17.refs_1_ = f32[16,8192]{1,0:T(8,128)S(1)} custom-call(f32[128,128]{1,0:T(8,128)S(1)} %get-tuple-element.62.stream_ref, f32[128,8192]{1,0:T(8,128)S(1)} %get-tuple-element.84.f_ref), custom_call_target="tpu_custom_call" | custom-call | tf_op jit(solution)/shard_map/transport/pallas_call | solution.py:296
  12.5 2.4 %collective-permute-start.2 = (f32[104,128]{1,0:T(8,128)S(1)}, f32[104,128]{1,0:T(8,128)S(1)}, u32[]{:S(2)}, u32[]{:S(2)}) collective-permute-start(f32[104,128]{1,0:T(8,128)S(1)} %add.22.left_ref), channel_id=1, source_target_pairs={{0,4},{1,5},{2,6},{3,7},{4,0},{5,1},{6,2},{7,3},{8,12},{9,13},{10,... | collective-permute-start | bytes 159752 | tf_op jit(solution)/shard_map/ppermute | solution.py:551
  14.9 1.3 %collective-permute-start.5 = (f32[104,128]{1,0:T(8,128)S(1)}, f32[104,128]{1,0:T(8,128)S(1)}, u32[]{:S(2)}, u32[]{:S(2)}) collective-permute-start(f32[104,128]{1,0:T(8,128)S(1)} %add.23.left_ref), channel_id=1, source_target_pairs={{0,4},{1,5},{2,6},{3,7},{4,0},{5,1},{6,2},{7,3},{8,12},{9,13},{10,... | collective-permute-start | bytes 159752 | tf_op jit(solution)/shard_map/ppermute | solution.py:551
  17.5 2.8 %collective-permute-start.4 = (f32[104,128]{1,0:T(8,128)S(1)}, f32[104,128]{1,0:T(8,128)S(1)}, u32[]{:S(2)}, u32[]{:S(2)}) collective-permute-start(f32[104,128]{1,0:T(8,128)S(1)} %add.24.left_ref), channel_id=1, source_target_pairs={{0,8},{1,9},{2,10},{3,11},{4,12},{5,13},{6,14},{7,15},{8,0},{9,1},... | collective-permute-start | bytes 159752 | tf_op jit(solution)/shard_map/ppermute | solution.py:551
  20.3 1.6 %collective-permute-start.7 = (f32[104,128]{1,0:T(8,128)S(1)}, f32[104,128]{1,0:T(8,128)S(1)}, u32[]{:S(2)}, u32[]{:S(2)}) collective-permute-start(f32[104,128]{1,0:T(8,128)S(1)} %add.25.left_ref), channel_id=1, source_target_pairs={{0,8},{1,9},{2,10},{3,11},{4,12},{5,13},{6,14},{7,15},{8,0},{9,1},... | collective-permute-start | bytes 159752 | tf_op jit(solution)/shard_map/ppermute | solution.py:551
  22.9 1.1 %collective-permute-done.4.right_ref = f32[104,128]{1,0:T(8,128)S(1)} collective-permute-done((f32[104,128]{1,0:T(8,128)S(1)}, f32[104,128]{1,0:T(8,128)S(1)}, u32[]{:S(2)}, u32[]{:S(2)}) %collective-permute-start.4) | collective-permute-done | bytes 53280 | tf_op jit(solution)/shard_map/ppermute | solution.py:551
  24.0 1.5 %collective-permute-start.6 = (f32[104,128]{1,0:T(8,128)S(1)}, f32[104,128]{1,0:T(8,128)S(1)}, u32[]{:S(2)}, u32[]{:S(2)}) collective-permute-start(f32[104,128]{1,0:T(8,128)S(1)} %add.26), channel_id=1, source_target_pairs={{0,2},{1,3},{2,0},{3,1},{4,6},{5,7},{6,4},{7,5},{8,10},{9,11},{10,... | collective-permute-start | bytes 159752 | tf_op jit(solution)/shard_map/ppermute | solution.py:551
  25.5 1.5 %collective-permute-start.9 = (f32[104,128]{1,0:T(8,128)S(1)}, f32[104,128]{1,0:T(8,128)S(1)}, u32[]{:S(2)}, u32[]{:S(2)}) collective-permute-start(f32[104,128]{1,0:T(8,128)S(1)} %add.27), channel_id=1, source_target_pairs={{0,2},{1,3},{2,0},{3,1},{4,6},{5,7},{6,4},{7,5},{8,10},{9,11},{10,... | collective-permute-start | bytes 159752 | tf_op jit(solution)/shard_map/ppermute | solution.py:551
  28.0 1.0 %transport.21.refs_5_ = f32[16,8192]{1,0:T(8,128)S(1)} custom-call(f32[128,128]{1,0:T(8,128)S(1)} %get-tuple-element.62.stream_ref, f32[128,8192]{1,0:T(8,128)S(1)} %get-tuple-element.84.f_ref), custom_call_target="tpu_custom_call" | custom-call | tf_op jit(solution)/shard_map/transport/pallas_call | solution.py:296
  29.8 1.0 %transport.23.refs_7_ = f32[16,8192]{1,0:T(8,128)S(1)} custom-call(f32[128,128]{1,0:T(8,128)S(1)} %get-tuple-element.62.stream_ref, f32[128,8192]{1,0:T(8,128)S(1)} %get-tuple-element.84.f_ref), custom_call_target="tpu_custom_call" | custom-call | tf_op jit(solution)/shard_map/transport/pallas_call | solution.py:296
  32.0 2.4 %update.1 = (f32[128,8192]{1,0:T(8,128)S(1)}, f32[832,128]{1,0:T(8,128)S(1)}) custom-call(f32[16,8192]{1,0:T(8,128)S(1)} %transport.16.refs_0_, f32[16,8192]{1,0:T(8,128)S(1)} %transport.17.refs_1_, f32[16,8192]{1,0:T(8,128)S(1)} %transport.18.refs_2_, f32[16,8192]{1,0:T(8,128)S(1)} %transport.19.refs_3_, f32[16,8192]{1,0:T(8,128)S(1)} %transport.20.refs_4_, ...), custom_call_target="tpu_custom_call" | custom-call | tf_op jit(solution)/shard_map/update/pallas_call | solution.py:472
  36.1 1.5 %collective-permute-start.12 = (f32[104,128]{1,0:T(8,128)S(1)}, f32[104,128]{1,0:T(8,128)S(1)}, u32[]{:S(2)}, u32[]{:S(2)}) collective-permute-start(f32[104,128]{1,0:T(8,128)S(1)} %get-tuple-element.95), channel_id=1, source_target_pairs={{0,2},{1,3},{2,0},{3,1},{4,6},{5,7},{6,4},{7,5},{8,10},{9,11},{10,... | collective-permute-start | bytes 159752 | tf_op jit(solution)/shard_map/ppermute | solution.py:551
  39.2 1.0 %transport.25.refs_1_ = f32[16,8192]{1,0:T(8,128)S(1)} custom-call(f32[128,128]{1,0:T(8,128)S(1)} %get-tuple-element.62.stream_ref, f32[128,8192]{1,0:T(8,128)S(1)} %get-tuple-element.111.f_ref), custom_call_target="tpu_custom_call" | custom-call | tf_op jit(solution)/shard_map/transport/pallas_call | solution.py:296
  40.5 1.1 %collective-permute-start.13 = (f32[104,128]{1,0:T(8,128)S(1)}, f32[104,128]{1,0:T(8,128)S(1)}, u32[]{:S(2)}, u32[]{:S(2)}) collective-permute-start(f32[104,128]{1,0:T(8,128)S(1)} %add.28.left_ref), channel_id=1, source_target_pairs={{0,4},{1,5},{2,6},{3,7},{4,0},{5,1},{6,2},{7,3},{8,12},{9,13},{10,... | collective-permute-start | bytes 159752 | tf_op jit(solution)/shard_map/ppermute | solution.py:551
  41.7 1.5 %collective-permute-start.16 = (f32[104,128]{1,0:T(8,128)S(1)}, f32[104,128]{1,0:T(8,128)S(1)}, u32[]{:S(2)}, u32[]{:S(2)}) collective-permute-start(f32[104,128]{1,0:T(8,128)S(1)} %add.29.left_ref), channel_id=1, source_target_pairs={{0,4},{1,5},{2,6},{3,7},{4,0},{5,1},{6,2},{7,3},{8,12},{9,13},{10,... | collective-permute-start | bytes 159752 | tf_op jit(solution)/shard_map/ppermute | solution.py:551
  44.8 2.1 %collective-permute-start.15 = (f32[104,128]{1,0:T(8,128)S(1)}, f32[104,128]{1,0:T(8,128)S(1)}, u32[]{:S(2)}, u32[]{:S(2)}) collective-permute-start(f32[104,128]{1,0:T(8,128)S(1)} %add.30.left_ref), channel_id=1, source_target_pairs={{0,8},{1,9},{2,10},{3,11},{4,12},{5,13},{6,14},{7,15},{8,0},{9,1},... | collective-permute-start | bytes 159752 | tf_op jit(solution)/shard_map/ppermute | solution.py:551
  47.0 2.1 %collective-permute-start.18 = (f32[104,128]{1,0:T(8,128)S(1)}, f32[104,128]{1,0:T(8,128)S(1)}, u32[]{:S(2)}, u32[]{:S(2)}) collective-permute-start(f32[104,128]{1,0:T(8,128)S(1)} %add.31.left_ref), channel_id=1, source_target_pairs={{0,8},{1,9},{2,10},{3,11},{4,12},{5,13},{6,14},{7,15},{8,0},{9,1},... | collective-permute-start | bytes 159752 | tf_op jit(solution)/shard_map/ppermute | solution.py:551
  52.1 1.7 %collective-permute-start.20 = (f32[104,128]{1,0:T(8,128)S(1)}, f32[104,128]{1,0:T(8,128)S(1)}, u32[]{:S(2)}, u32[]{:S(2)}) collective-permute-start(f32[104,128]{1,0:T(8,128)S(1)} %add.33), channel_id=1, source_target_pairs={{0,2},{1,3},{2,0},{3,1},{4,6},{5,7},{6,4},{7,5},{8,10},{9,11},{10,... | collective-permute-start | bytes 159752 | tf_op jit(solution)/shard_map/ppermute | solution.py:551
  54.8 1.0 %transport.29.refs_5_ = f32[16,8192]{1,0:T(8,128)S(1)} custom-call(f32[128,128]{1,0:T(8,128)S(1)} %get-tuple-element.62.stream_ref, f32[128,8192]{1,0:T(8,128)S(1)} %get-tuple-element.111.f_ref), custom_call_target="tpu_custom_call" | custom-call | tf_op jit(solution)/shard_map/transport/pallas_call | solution.py:296
  58.9 2.4 %finish.1 = (f32[128,8192]{1,0:T(8,128)}, f32[8,8192]{1,0:T(8,128)}) custom-call(f32[16,8192]{1,0:T(8,128)S(1)} %transport.24.refs_0_, f32[16,8192]{1,0:T(8,128)S(1)} %transport.25.refs_1_, f32[16,8192]{1,0:T(8,128)S(1)} %transport.26.refs_2_, f32[16,8192]{1,0:T(8,128)S(1)} %transport.27.refs_3_, f32[16,8192]{1,0:T(8,128)S(1)} %transport.28.refs_4_, ...), custom_call_target="tpu_custom_call" | custom-call | tf_op jit(solution)/shard_map/finish/pallas_call | solution.py:512
  (72 shorter events, 18.3 us)
Async XLA Ops:
  5.7 1.6 %collective-permute-start = (f32[416,128]{1,0:T(8,128)S(1)}, f32[416,128]{1,0:T(8,128)S(1)}, u32[]{:S(2)}, u32[]{:S(2)}) collective-permute-start(f32[416,128]{1,0:T(8,128)S(1)} %slice_select_fusion.1), channel_id=1, source_target_pairs={{0,1},{1,0},{2,3},{3,2},{4,5},{5,4},{6,7},{7,6},{8,9},{9,8},{10,11... | collective-permute-start | bytes 638984 | tf_op jit(solution)/shard_map/ppermute | solution.py:551
  7.4 5.1 %collective-permute-start.1 = (f32[104,128]{1,0:T(8,128)S(1)}, f32[104,128]{1,0:T(8,128)S(1)}, u32[]{:S(2)}, u32[]{:S(2)}) collective-permute-start(f32[104,128]{1,0:T(8,128)S(1)} %get-tuple-element.68), channel_id=1, source_target_pairs={{0,2},{1,3},{2,0},{3,1},{4,6},{5,7},{6,4},{7,5},{8,10},{9,11},{10,... | collective-permute-start | bytes 159752 | tf_op jit(solution)/shard_map/ppermute | solution.py:551
  10.3 4.5 %collective-permute-start.3 = (f32[104,128]{1,0:T(8,128)S(1)}, f32[104,128]{1,0:T(8,128)S(1)}, u32[]{:S(2)}, u32[]{:S(2)}) collective-permute-start(f32[104,128]{1,0:T(8,128)S(1)} %get-tuple-element.69), channel_id=1, source_target_pairs={{0,2},{1,3},{2,0},{3,1},{4,6},{5,7},{6,4},{7,5},{8,10},{9,11},{10,... | collective-permute-start | bytes 159752 | tf_op jit(solution)/shard_map/ppermute | solution.py:551
  12.5 5.0 %collective-permute-start.2 = (f32[104,128]{1,0:T(8,128)S(1)}, f32[104,128]{1,0:T(8,128)S(1)}, u32[]{:S(2)}, u32[]{:S(2)}) collective-permute-start(f32[104,128]{1,0:T(8,128)S(1)} %add.22.left_ref), channel_id=1, source_target_pairs={{0,4},{1,5},{2,6},{3,7},{4,0},{5,1},{6,2},{7,3},{8,12},{9,13},{10,... | collective-permute-start | bytes 159752 | tf_op jit(solution)/shard_map/ppermute | solution.py:551
  14.9 5.4 %collective-permute-start.5 = (f32[104,128]{1,0:T(8,128)S(1)}, f32[104,128]{1,0:T(8,128)S(1)}, u32[]{:S(2)}, u32[]{:S(2)}) collective-permute-start(f32[104,128]{1,0:T(8,128)S(1)} %add.23.left_ref), channel_id=1, source_target_pairs={{0,4},{1,5},{2,6},{3,7},{4,0},{5,1},{6,2},{7,3},{8,12},{9,13},{10,... | collective-permute-start | bytes 159752 | tf_op jit(solution)/shard_map/ppermute | solution.py:551
  17.5 6.5 %collective-permute-start.4 = (f32[104,128]{1,0:T(8,128)S(1)}, f32[104,128]{1,0:T(8,128)S(1)}, u32[]{:S(2)}, u32[]{:S(2)}) collective-permute-start(f32[104,128]{1,0:T(8,128)S(1)} %add.24.left_ref), channel_id=1, source_target_pairs={{0,8},{1,9},{2,10},{3,11},{4,12},{5,13},{6,14},{7,15},{8,0},{9,1},... | collective-permute-start | bytes 159752 | tf_op jit(solution)/shard_map/ppermute | solution.py:551
  20.3 5.2 %collective-permute-start.7 = (f32[104,128]{1,0:T(8,128)S(1)}, f32[104,128]{1,0:T(8,128)S(1)}, u32[]{:S(2)}, u32[]{:S(2)}) collective-permute-start(f32[104,128]{1,0:T(8,128)S(1)} %add.25.left_ref), channel_id=1, source_target_pairs={{0,8},{1,9},{2,10},{3,11},{4,12},{5,13},{6,14},{7,15},{8,0},{9,1},... | collective-permute-start | bytes 159752 | tf_op jit(solution)/shard_map/ppermute | solution.py:551
  24.0 5.0 %collective-permute-start.6 = (f32[104,128]{1,0:T(8,128)S(1)}, f32[104,128]{1,0:T(8,128)S(1)}, u32[]{:S(2)}, u32[]{:S(2)}) collective-permute-start(f32[104,128]{1,0:T(8,128)S(1)} %add.26), channel_id=1, source_target_pairs={{0,2},{1,3},{2,0},{3,1},{4,6},{5,7},{6,4},{7,5},{8,10},{9,11},{10,... | collective-permute-start | bytes 159752 | tf_op jit(solution)/shard_map/ppermute | solution.py:551
  25.5 4.2 %collective-permute-start.9 = (f32[104,128]{1,0:T(8,128)S(1)}, f32[104,128]{1,0:T(8,128)S(1)}, u32[]{:S(2)}, u32[]{:S(2)}) collective-permute-start(f32[104,128]{1,0:T(8,128)S(1)} %add.27), channel_id=1, source_target_pairs={{0,2},{1,3},{2,0},{3,1},{4,6},{5,7},{6,4},{7,5},{8,10},{9,11},{10,... | collective-permute-start | bytes 159752 | tf_op jit(solution)/shard_map/ppermute | solution.py:551
  29.1 1.7 %collective-permute-start.8 = (f32[208,128]{1,0:T(8,128)S(1)}, f32[208,128]{1,0:T(8,128)S(1)}, u32[]{:S(2)}, u32[]{:S(2)}) collective-permute-start(f32[208,128]{1,0:T(8,128)S(1)} %pad_maximum_fusion.2), channel_id=1, source_target_pairs={{0,1},{1,0},{2,3},{3,2},{4,5},{5,4},{6,7},{7,6},{8,9},{9,8},{10,11... | collective-permute-start | bytes 319496 | tf_op jit(solution)/shard_map/ppermute | solution.py:551
  29.7 1.4 %collective-permute-start.10 = (f32[208,128]{1,0:T(8,128)S(1)}, f32[208,128]{1,0:T(8,128)S(1)}, u32[]{:S(2)}, u32[]{:S(2)}) collective-permute-start(f32[208,128]{1,0:T(8,128)S(1)} %pad_maximum_fusion.3), channel_id=1, source_target_pairs={{0,1},{1,0},{2,3},{3,2},{4,5},{5,4},{6,7},{7,6},{8,9},{9,8},{10,11... | collective-permute-start | bytes 319496 | tf_op jit(solution)/shard_map/ppermute | solution.py:551
  34.5 1.5 %collective-permute-start.11 = (f32[416,128]{1,0:T(8,128)S(1)}, f32[416,128]{1,0:T(8,128)S(1)}, u32[]{:S(2)}, u32[]{:S(2)}) collective-permute-start(f32[416,128]{1,0:T(8,128)S(1)} %slice_select_fusion), channel_id=1, source_target_pairs={{0,1},{1,0},{2,3},{3,2},{4,5},{5,4},{6,7},{7,6},{8,9},{9,8},{10,11... | collective-permute-start | bytes 638984 | tf_op jit(solution)/shard_map/ppermute | solution.py:551
  36.1 4.4 %collective-permute-start.12 = (f32[104,128]{1,0:T(8,128)S(1)}, f32[104,128]{1,0:T(8,128)S(1)}, u32[]{:S(2)}, u32[]{:S(2)}) collective-permute-start(f32[104,128]{1,0:T(8,128)S(1)} %get-tuple-element.95), channel_id=1, source_target_pairs={{0,2},{1,3},{2,0},{3,1},{4,6},{5,7},{6,4},{7,5},{8,10},{9,11},{10,... | collective-permute-start | bytes 159752 | tf_op jit(solution)/shard_map/ppermute | solution.py:551
  37.6 4.1 %collective-permute-start.14 = (f32[104,128]{1,0:T(8,128)S(1)}, f32[104,128]{1,0:T(8,128)S(1)}, u32[]{:S(2)}, u32[]{:S(2)}) collective-permute-start(f32[104,128]{1,0:T(8,128)S(1)} %get-tuple-element.96), channel_id=1, source_target_pairs={{0,2},{1,3},{2,0},{3,1},{4,6},{5,7},{6,4},{7,5},{8,10},{9,11},{10,... | collective-permute-start | bytes 159752 | tf_op jit(solution)/shard_map/ppermute | solution.py:551
  40.5 4.3 %collective-permute-start.13 = (f32[104,128]{1,0:T(8,128)S(1)}, f32[104,128]{1,0:T(8,128)S(1)}, u32[]{:S(2)}, u32[]{:S(2)}) collective-permute-start(f32[104,128]{1,0:T(8,128)S(1)} %add.28.left_ref), channel_id=1, source_target_pairs={{0,4},{1,5},{2,6},{3,7},{4,0},{5,1},{6,2},{7,3},{8,12},{9,13},{10,... | collective-permute-start | bytes 159752 | tf_op jit(solution)/shard_map/ppermute | solution.py:551
  41.7 5.2 %collective-permute-start.16 = (f32[104,128]{1,0:T(8,128)S(1)}, f32[104,128]{1,0:T(8,128)S(1)}, u32[]{:S(2)}, u32[]{:S(2)}) collective-permute-start(f32[104,128]{1,0:T(8,128)S(1)} %add.29.left_ref), channel_id=1, source_target_pairs={{0,4},{1,5},{2,6},{3,7},{4,0},{5,1},{6,2},{7,3},{8,12},{9,13},{10,... | collective-permute-start | bytes 159752 | tf_op jit(solution)/shard_map/ppermute | solution.py:551
  44.8 6.1 %collective-permute-start.15 = (f32[104,128]{1,0:T(8,128)S(1)}, f32[104,128]{1,0:T(8,128)S(1)}, u32[]{:S(2)}, u32[]{:S(2)}) collective-permute-start(f32[104,128]{1,0:T(8,128)S(1)} %add.30.left_ref), channel_id=1, source_target_pairs={{0,8},{1,9},{2,10},{3,11},{4,12},{5,13},{6,14},{7,15},{8,0},{9,1},... | collective-permute-start | bytes 159752 | tf_op jit(solution)/shard_map/ppermute | solution.py:551
  47.0 5.1 %collective-permute-start.18 = (f32[104,128]{1,0:T(8,128)S(1)}, f32[104,128]{1,0:T(8,128)S(1)}, u32[]{:S(2)}, u32[]{:S(2)}) collective-permute-start(f32[104,128]{1,0:T(8,128)S(1)} %add.31.left_ref), channel_id=1, source_target_pairs={{0,8},{1,9},{2,10},{3,11},{4,12},{5,13},{6,14},{7,15},{8,0},{9,1},... | collective-permute-start | bytes 159752 | tf_op jit(solution)/shard_map/ppermute | solution.py:551
  50.9 4.8 %collective-permute-start.17 = (f32[104,128]{1,0:T(8,128)S(1)}, f32[104,128]{1,0:T(8,128)S(1)}, u32[]{:S(2)}, u32[]{:S(2)}) collective-permute-start(f32[104,128]{1,0:T(8,128)S(1)} %add.32), channel_id=1, source_target_pairs={{0,2},{1,3},{2,0},{3,1},{4,6},{5,7},{6,4},{7,5},{8,10},{9,11},{10,... | collective-permute-start | bytes 159752 | tf_op jit(solution)/shard_map/ppermute | solution.py:551
  52.1 4.2 %collective-permute-start.20 = (f32[104,128]{1,0:T(8,128)S(1)}, f32[104,128]{1,0:T(8,128)S(1)}, u32[]{:S(2)}, u32[]{:S(2)}) collective-permute-start(f32[104,128]{1,0:T(8,128)S(1)} %add.33), channel_id=1, source_target_pairs={{0,2},{1,3},{2,0},{3,1},{4,6},{5,7},{6,4},{7,5},{8,10},{9,11},{10,... | collective-permute-start | bytes 159752 | tf_op jit(solution)/shard_map/ppermute | solution.py:551
  56.3 1.7 %collective-permute-start.19 = (f32[208,128]{1,0:T(8,128)S(1)}, f32[208,128]{1,0:T(8,128)S(1)}, u32[]{:S(2)}, u32[]{:S(2)}) collective-permute-start(f32[208,128]{1,0:T(8,128)S(1)} %pad_maximum_fusion.4), channel_id=1, source_target_pairs={{0,1},{1,0},{2,3},{3,2},{4,5},{5,4},{6,7},{7,6},{8,9},{9,8},{10,11... | collective-permute-start | bytes 319496 | tf_op jit(solution)/shard_map/ppermute | solution.py:551
  56.4 1.6 %collective-permute-start.21 = (f32[208,128]{1,0:T(8,128)S(1)}, f32[208,128]{1,0:T(8,128)S(1)}, u32[]{:S(2)}, u32[]{:S(2)}) collective-permute-start(f32[208,128]{1,0:T(8,128)S(1)} %pad_maximum_fusion.5), channel_id=1, source_target_pairs={{0,1},{1,0},{2,3},{3,2},{4,5},{5,4},{6,7},{7,6},{8,9},{9,8},{10,11... | collective-permute-start | bytes 319496 | tf_op jit(solution)/shard_map/ppermute | solution.py:551

commit v14 on v13

--- a/solution.py
+++ b/solution.py
@@ -19,14 +19,14 @@
 
 LOG2E = 1.4426950408889634
 LANES = 128
-TILE = 512
+TILE = 1024
 BASIS = 16
 SENT = 13
 COEF = 24
 DAMP = 13
 ROWS = 32
 CHUNKS = 8
-DEPARTURES = 16
+DEPARTURES = 8
 PARTS = 8
 BESIDE = (1, 2, 1, 1, 2, 1)
 MIB = 1024 * 1024

time: 61.7 us -> 61.3 us (level)
  no operation moved by 1% of the time
where the time goes in v14:
time: 61.3 us; the launch traced here: 61.2 us
  Pallas kernels  27.3 us (45%)
  starting transfers between devices  27 us (44%)
  waiting for transfers between devices  5.28 us (9%)
  between operations  1.19 us (2%)
    ppermute x22, starting transfers between devices, swap(): lax.ppermute(values, 'vel', [(device, device ^ stride) for device in rang...  27 us
    pallas_call x16, Pallas kernels, transport_call(): pl.pallas_call(functools.partial(transport_kernel, part * rows), out_shap...  15.9 us
    ppermute x22, waiting for transfers between devices, swap(): lax.ppermute(values, 'vel', [(device, device ^ stride) for device in rang...  5.28 us
    pallas_call x1, Pallas kernels, start_call(): pl.pallas_call(functools.partial(start_kernel, total_count), out_shape=(p...  4.81 us
    pallas_call x1, Pallas kernels, finish_call(): pl.pallas_call(finish_kernel, out_shape=(jax.ShapeDtypeStruct((rows * PAR...  2.43 us
    pallas_call x1, Pallas kernels, update_call(): pl.pallas_call(update_kernel, out_shape=(pltpu.VMEM((rows * PARTS, cells)...  2.28 us
    pallas_call x2, Pallas kernels, fluid_call(): pl.pallas_call(fluid_kernel, out_shape=shapes, in_specs=[WHOLE], out_spec...  1.71 us
  transfers between devices with their start and end apart: 22, of which 12 were waited for; matrix products, arithmetic and copies ran while one was open for 0% of the time, Pallas kernels for 26%

profile of v14, /device:TPU:0, one launch (start us, length us, event | category | flops | bytes accessed | tf_op | source)
XLA Modules:
  0.0 61.2 jit_solution(2541615063572551832)
XLA Ops:
  0.6 4.8 %start.1 = (f32[128,8192]{1,0:T(8,128)S(1)}, f32[832,128]{1,0:T(8,128)S(1)}, bf16[128,48]{1,0:T(8,128)(2,1)S(1)}, bf16[128,48]{1,0:T(8,128)(2,1)S(1)}, bf16[32,2...) custom-call(f32[3,128]{1,0:T(4,128)} %vel_hbm, f32[1,8192]{1,0:T(1,128)} %bitcast.2, f32[3,8192]{1,0:T(4,128)} %flow_hbm.1, ...), custom_call_target="tpu_custom_call" | custom-call | tf_op jit(solution)/shard_map/start/pallas_call | solution.py:205
  6.0 1.0 %transport.16.refs_0_ = f32[16,8192]{1,0:T(8,128)S(1)} custom-call(f32[128,128]{1,0:T(8,128)S(1)} %get-tuple-element.62.stream_ref, f32[128,8192]{1,0:T(8,128)S(1)} %get-tuple-element.84.f_ref), custom_call_target="tpu_custom_call" | custom-call | tf_op jit(solution)/shard_map/transport/pallas_call | solution.py:296
  7.2 3.0 %collective-permute-start.1 = (f32[104,128]{1,0:T(8,128)S(1)}, f32[104,128]{1,0:T(8,128)S(1)}, u32[]{:S(2)}, u32[]{:S(2)}) collective-permute-start(f32[104,128]{1,0:T(8,128)S(1)} %get-tuple-element.68), channel_id=1, source_target_pairs={{0,2},{1,3},{2,0},{3,1},{4,6},{5,7},{6,4},{7,5},{8,10},{9,11},{10,... | collective-permute-start | bytes 159752 | tf_op jit(solution)/shard_map/ppermute | solution.py:551
  10.2 1.0 %transport.18.refs_2_ = f32[16,8192]{1,0:T(8,128)S(1)} custom-call(f32[128,128]{1,0:T(8,128)S(1)} %get-tuple-element.62.stream_ref, f32[128,8192]{1,0:T(8,128)S(1)} %get-tuple-element.84.f_ref), custom_call_target="tpu_custom_call" | custom-call | tf_op jit(solution)/shard_map/transport/pallas_call | solution.py:296
  11.2 1.0 %transport.17.refs_1_ = f32[16,8192]{1,0:T(8,128)S(1)} custom-call(f32[128,128]{1,0:T(8,128)S(1)} %get-tuple-element.62.stream_ref, f32[128,8192]{1,0:T(8,128)S(1)} %get-tuple-element.84.f_ref), custom_call_target="tpu_custom_call" | custom-call | tf_op jit(solution)/shard_map/transport/pallas_call | solution.py:296
  12.3 2.4 %collective-permute-start.2 = (f32[104,128]{1,0:T(8,128)S(1)}, f32[104,128]{1,0:T(8,128)S(1)}, u32[]{:S(2)}, u32[]{:S(2)}) collective-permute-start(f32[104,128]{1,0:T(8,128)S(1)} %add.22.left_ref), channel_id=1, source_target_pairs={{0,4},{1,5},{2,6},{3,7},{4,0},{5,1},{6,2},{7,3},{8,12},{9,13},{10,... | collective-permute-start | bytes 159752 | tf_op jit(solution)/shard_map/ppermute | solution.py:551
  14.6 1.3 %collective-permute-start.5 = (f32[104,128]{1,0:T(8,128)S(1)}, f32[104,128]{1,0:T(8,128)S(1)}, u32[]{:S(2)}, u32[]{:S(2)}) collective-permute-start(f32[104,128]{1,0:T(8,128)S(1)} %add.23.left_ref), channel_id=1, source_target_pairs={{0,4},{1,5},{2,6},{3,7},{4,0},{5,1},{6,2},{7,3},{8,12},{9,13},{10,... | collective-permute-start | bytes 159752 | tf_op jit(solution)/shard_map/ppermute | solution.py:551
  17.2 2.8 %collective-permute-start.4 = (f32[104,128]{1,0:T(8,128)S(1)}, f32[104,128]{1,0:T(8,128)S(1)}, u32[]{:S(2)}, u32[]{:S(2)}) collective-permute-start(f32[104,128]{1,0:T(8,128)S(1)} %add.24.left_ref), channel_id=1, source_target_pairs={{0,8},{1,9},{2,10},{3,11},{4,12},{5,13},{6,14},{7,15},{8,0},{9,1},... | collective-permute-start | bytes 159752 | tf_op jit(solution)/shard_map/ppermute | solution.py:551
  20.1 1.6 %collective-permute-start.7 = (f32[104,128]{1,0:T(8,128)S(1)}, f32[104,128]{1,0:T(8,128)S(1)}, u32[]{:S(2)}, u32[]{:S(2)}) collective-permute-start(f32[104,128]{1,0:T(8,128)S(1)} %add.25.left_ref), channel_id=1, source_target_pairs={{0,8},{1,9},{2,10},{3,11},{4,12},{5,13},{6,14},{7,15},{8,0},{9,1},... | collective-permute-start | bytes 159752 | tf_op jit(solution)/shard_map/ppermute | solution.py:551
  22.7 1.1 %collective-permute-done.4.right_ref = f32[104,128]{1,0:T(8,128)S(1)} collective-permute-done((f32[104,128]{1,0:T(8,128)S(1)}, f32[104,128]{1,0:T(8,128)S(1)}, u32[]{:S(2)}, u32[]{:S(2)}) %collective-permute-start.4) | collective-permute-done | bytes 53280 | tf_op jit(solution)/shard_map/ppermute | solution.py:551
  23.8 1.5 %collective-permute-start.6 = (f32[104,128]{1,0:T(8,128)S(1)}, f32[104,128]{1,0:T(8,128)S(1)}, u32[]{:S(2)}, u32[]{:S(2)}) collective-permute-start(f32[104,128]{1,0:T(8,128)S(1)} %add.26), channel_id=1, source_target_pairs={{0,2},{1,3},{2,0},{3,1},{4,6},{5,7},{6,4},{7,5},{8,10},{9,11},{10,... | collective-permute-start | bytes 159752 | tf_op jit(solution)/shard_map/ppermute | solution.py:551
  25.3 1.5 %collective-permute-start.9 = (f32[104,128]{1,0:T(8,128)S(1)}, f32[104,128]{1,0:T(8,128)S(1)}, u32[]{:S(2)}, u32[]{:S(2)}) collective-permute-start(f32[104,128]{1,0:T(8,128)S(1)} %add.27), channel_id=1, source_target_pairs={{0,2},{1,3},{2,0},{3,1},{4,6},{5,7},{6,4},{7,5},{8,10},{9,11},{10,... | collective-permute-start | bytes 159752 | tf_op jit(solution)/shard_map/ppermute | solution.py:551
  27.8 1.0 %transport.21.refs_5_ = f32[16,8192]{1,0:T(8,128)S(1)} custom-call(f32[128,128]{1,0:T(8,128)S(1)} %get-tuple-element.62.stream_ref, f32[128,8192]{1,0:T(8,128)S(1)} %get-tuple-element.84.f_ref), custom_call_target="tpu_custom_call" | custom-call | tf_op jit(solution)/shard_map/transport/pallas_call | solution.py:296
  29.6 1.0 %transport.23.refs_7_ = f32[16,8192]{1,0:T(8,128)S(1)} custom-call(f32[128,128]{1,0:T(8,128)S(1)} %get-tuple-element.62.stream_ref, f32[128,8192]{1,0:T(8,128)S(1)} %get-tuple-element.84.f_ref), custom_call_target="tpu_custom_call" | custom-call | tf_op jit(solution)/shard_map/transport/pallas_call | solution.py:296
  31.8 2.3 %update.1 = (f32[128,8192]{1,0:T(8,128)S(1)}, f32[832,128]{1,0:T(8,128)S(1)}) custom-call(f32[16,8192]{1,0:T(8,128)S(1)} %transport.16.refs_0_, f32[16,8192]{1,0:T(8,128)S(1)} %transport.17.refs_1_, f32[16,8192]{1,0:T(8,128)S(1)} %transport.18.refs_2_, f32[16,8192]{1,0:T(8,128)S(1)} %transport.19.refs_3_, f32[16,8192]{1,0:T(8,128)S(1)} %transport.20.refs_4_, ...), custom_call_target="tpu_custom_call" | custom-call | tf_op jit(solution)/shard_map/update/pallas_call | solution.py:472
  35.7 1.5 %collective-permute-start.12 = (f32[104,128]{1,0:T(8,128)S(1)}, f32[104,128]{1,0:T(8,128)S(1)}, u32[]{:S(2)}, u32[]{:S(2)}) collective-permute-start(f32[104,128]{1,0:T(8,128)S(1)} %get-tuple-element.95), channel_id=1, source_target_pairs={{0,2},{1,3},{2,0},{3,1},{4,6},{5,7},{6,4},{7,5},{8,10},{9,11},{10,... | collective-permute-start | bytes 159752 | tf_op jit(solution)/shard_map/ppermute | solution.py:551
  38.8 1.0 %transport.25.refs_1_ = f32[16,8192]{1,0:T(8,128)S(1)} custom-call(f32[128,128]{1,0:T(8,128)S(1)} %get-tuple-element.62.stream_ref, f32[128,8192]{1,0:T(8,128)S(1)} %get-tuple-element.111.f_ref), custom_call_target="tpu_custom_call" | custom-call | tf_op jit(solution)/shard_map/transport/pallas_call | solution.py:296
  40.1 1.2 %collective-permute-start.13 = (f32[104,128]{1,0:T(8,128)S(1)}, f32[104,128]{1,0:T(8,128)S(1)}, u32[]{:S(2)}, u32[]{:S(2)}) collective-permute-start(f32[104,128]{1,0:T(8,128)S(1)} %add.28.left_ref), channel_id=1, source_target_pairs={{0,4},{1,5},{2,6},{3,7},{4,0},{5,1},{6,2},{7,3},{8,12},{9,13},{10,... | collective-permute-start | bytes 159752 | tf_op jit(solution)/shard_map/ppermute | solution.py:551
  41.4 1.5 %collective-permute-start.16 = (f32[104,128]{1,0:T(8,128)S(1)}, f32[104,128]{1,0:T(8,128)S(1)}, u32[]{:S(2)}, u32[]{:S(2)}) collective-permute-start(f32[104,128]{1,0:T(8,128)S(1)} %add.29.left_ref), channel_id=1, source_target_pairs={{0,4},{1,5},{2,6},{3,7},{4,0},{5,1},{6,2},{7,3},{8,12},{9,13},{10,... | collective-permute-start | bytes 159752 | tf_op jit(solution)/shard_map/ppermute | solution.py:551
  44.5 2.1 %collective-permute-start.15 = (f32[104,128]{1,0:T(8,128)S(1)}, f32[104,128]{1,0:T(8,128)S(1)}, u32[]{:S(2)}, u32[]{:S(2)}) collective-permute-start(f32[104,128]{1,0:T(8,128)S(1)} %add.30.left_ref), channel_id=1, source_target_pairs={{0,8},{1,9},{2,10},{3,11},{4,12},{5,13},{6,14},{7,15},{8,0},{9,1},... | collective-permute-start | bytes 159752 | tf_op jit(solution)/shard_map/ppermute | solution.py:551
  46.6 2.1 %collective-permute-start.18 = (f32[104,128]{1,0:T(8,128)S(1)}, f32[104,128]{1,0:T(8,128)S(1)}, u32[]{:S(2)}, u32[]{:S(2)}) collective-permute-start(f32[104,128]{1,0:T(8,128)S(1)} %add.31.left_ref), channel_id=1, source_target_pairs={{0,8},{1,9},{2,10},{3,11},{4,12},{5,13},{6,14},{7,15},{8,0},{9,1},... | collective-permute-start | bytes 159752 | tf_op jit(solution)/shard_map/ppermute | solution.py:551
  51.7 1.7 %collective-permute-start.20 = (f32[104,128]{1,0:T(8,128)S(1)}, f32[104,128]{1,0:T(8,128)S(1)}, u32[]{:S(2)}, u32[]{:S(2)}) collective-permute-start(f32[104,128]{1,0:T(8,128)S(1)} %add.33), channel_id=1, source_target_pairs={{0,2},{1,3},{2,0},{3,1},{4,6},{5,7},{6,4},{7,5},{8,10},{9,11},{10,... | collective-permute-start | bytes 159752 | tf_op jit(solution)/shard_map/ppermute | solution.py:551
  54.4 1.0 %transport.29.refs_5_ = f32[16,8192]{1,0:T(8,128)S(1)} custom-call(f32[128,128]{1,0:T(8,128)S(1)} %get-tuple-element.62.stream_ref, f32[128,8192]{1,0:T(8,128)S(1)} %get-tuple-element.111.f_ref), custom_call_target="tpu_custom_call" | custom-call | tf_op jit(solution)/shard_map/transport/pallas_call | solution.py:296
  58.6 2.4 %finish.1 = (f32[128,8192]{1,0:T(8,128)}, f32[8,8192]{1,0:T(8,128)}) custom-call(f32[16,8192]{1,0:T(8,128)S(1)} %transport.24.refs_0_, f32[16,8192]{1,0:T(8,128)S(1)} %transport.25.refs_1_, f32[16,8192]{1,0:T(8,128)S(1)} %transport.26.refs_2_, f32[16,8192]{1,0:T(8,128)S(1)} %transport.27.refs_3_, f32[16,8192]{1,0:T(8,128)S(1)} %transport.28.refs_4_, ...), custom_call_target="tpu_custom_call" | custom-call | tf_op jit(solution)/shard_map/finish/pallas_call | solution.py:512
  (72 shorter events, 18.3 us)
Async XLA Ops:
  5.5 1.6 %collective-permute-start = (f32[416,128]{1,0:T(8,128)S(1)}, f32[416,128]{1,0:T(8,128)S(1)}, u32[]{:S(2)}, u32[]{:S(2)}) collective-permute-start(f32[416,128]{1,0:T(8,128)S(1)} %slice_select_fusion.1), channel_id=1, source_target_pairs={{0,1},{1,0},{2,3},{3,2},{4,5},{5,4},{6,7},{7,6},{8,9},{9,8},{10,11... | collective-permute-start | bytes 638984 | tf_op jit(solution)/shard_map/ppermute | solution.py:551
  7.2 5.1 %collective-permute-start.1 = (f32[104,128]{1,0:T(8,128)S(1)}, f32[104,128]{1,0:T(8,128)S(1)}, u32[]{:S(2)}, u32[]{:S(2)}) collective-permute-start(f32[104,128]{1,0:T(8,128)S(1)} %get-tuple-element.68), channel_id=1, source_target_pairs={{0,2},{1,3},{2,0},{3,1},{4,6},{5,7},{6,4},{7,5},{8,10},{9,11},{10,... | collective-permute-start | bytes 159752 | tf_op jit(solution)/shard_map/ppermute | solution.py:551
  10.1 4.5 %collective-permute-start.3 = (f32[104,128]{1,0:T(8,128)S(1)}, f32[104,128]{1,0:T(8,128)S(1)}, u32[]{:S(2)}, u32[]{:S(2)}) collective-permute-start(f32[104,128]{1,0:T(8,128)S(1)} %get-tuple-element.69), channel_id=1, source_target_pairs={{0,2},{1,3},{2,0},{3,1},{4,6},{5,7},{6,4},{7,5},{8,10},{9,11},{10,... | collective-permute-start | bytes 159752 | tf_op jit(solution)/shard_map/ppermute | solution.py:551
  12.3 5.0 %collective-permute-start.2 = (f32[104,128]{1,0:T(8,128)S(1)}, f32[104,128]{1,0:T(8,128)S(1)}, u32[]{:S(2)}, u32[]{:S(2)}) collective-permute-start(f32[104,128]{1,0:T(8,128)S(1)} %add.22.left_ref), channel_id=1, source_target_pairs={{0,4},{1,5},{2,6},{3,7},{4,0},{5,1},{6,2},{7,3},{8,12},{9,13},{10,... | collective-permute-start | bytes 159752 | tf_op jit(solution)/shard_map/ppermute | solution.py:551
  14.6 5.4 %collective-permute-start.5 = (f32[104,128]{1,0:T(8,128)S(1)}, f32[104,128]{1,0:T(8,128)S(1)}, u32[]{:S(2)}, u32[]{:S(2)}) collective-permute-start(f32[104,128]{1,0:T(8,128)S(1)} %add.23.left_ref), channel_id=1, source_target_pairs={{0,4},{1,5},{2,6},{3,7},{4,0},{5,1},{6,2},{7,3},{8,12},{9,13},{10,... | collective-permute-start | bytes 159752 | tf_op jit(solution)/shard_map/ppermute | solution.py:551
  17.2 6.5 %collective-permute-start.4 = (f32[104,128]{1,0:T(8,128)S(1)}, f32[104,128]{1,0:T(8,128)S(1)}, u32[]{:S(2)}, u32[]{:S(2)}) collective-permute-start(f32[104,128]{1,0:T(8,128)S(1)} %add.24.left_ref), channel_id=1, source_target_pairs={{0,8},{1,9},{2,10},{3,11},{4,12},{5,13},{6,14},{7,15},{8,0},{9,1},... | collective-permute-start | bytes 159752 | tf_op jit(solution)/shard_map/ppermute | solution.py:551
  20.1 5.2 %collective-permute-start.7 = (f32[104,128]{1,0:T(8,128)S(1)}, f32[104,128]{1,0:T(8,128)S(1)}, u32[]{:S(2)}, u32[]{:S(2)}) collective-permute-start(f32[104,128]{1,0:T(8,128)S(1)} %add.25.left_ref), channel_id=1, source_target_pairs={{0,8},{1,9},{2,10},{3,11},{4,12},{5,13},{6,14},{7,15},{8,0},{9,1},... | collective-permute-start | bytes 159752 | tf_op jit(solution)/shard_map/ppermute | solution.py:551
  23.8 5.0 %collective-permute-start.6 = (f32[104,128]{1,0:T(8,128)S(1)}, f32[104,128]{1,0:T(8,128)S(1)}, u32[]{:S(2)}, u32[]{:S(2)}) collective-permute-start(f32[104,128]{1,0:T(8,128)S(1)} %add.26), channel_id=1, source_target_pairs={{0,2},{1,3},{2,0},{3,1},{4,6},{5,7},{6,4},{7,5},{8,10},{9,11},{10,... | collective-permute-start | bytes 159752 | tf_op jit(solution)/shard_map/ppermute | solution.py:551
  25.3 4.2 %collective-permute-start.9 = (f32[104,128]{1,0:T(8,128)S(1)}, f32[104,128]{1,0:T(8,128)S(1)}, u32[]{:S(2)}, u32[]{:S(2)}) collective-permute-start(f32[104,128]{1,0:T(8,128)S(1)} %add.27), channel_id=1, source_target_pairs={{0,2},{1,3},{2,0},{3,1},{4,6},{5,7},{6,4},{7,5},{8,10},{9,11},{10,... | collective-permute-start | bytes 159752 | tf_op jit(solution)/shard_map/ppermute | solution.py:551
  28.8 1.7 %collective-permute-start.8 = (f32[208,128]{1,0:T(8,128)S(1)}, f32[208,128]{1,0:T(8,128)S(1)}, u32[]{:S(2)}, u32[]{:S(2)}) collective-permute-start(f32[208,128]{1,0:T(8,128)S(1)} %pad_maximum_fusion.2), channel_id=1, source_target_pairs={{0,1},{1,0},{2,3},{3,2},{4,5},{5,4},{6,7},{7,6},{8,9},{9,8},{10,11... | collective-permute-start | bytes 319496 | tf_op jit(solution)/shard_map/ppermute | solution.py:551
  29.5 1.4 %collective-permute-start.10 = (f32[208,128]{1,0:T(8,128)S(1)}, f32[208,128]{1,0:T(8,128)S(1)}, u32[]{:S(2)}, u32[]{:S(2)}) collective-permute-start(f32[208,128]{1,0:T(8,128)S(1)} %pad_maximum_fusion.3), channel_id=1, source_target_pairs={{0,1},{1,0},{2,3},{3,2},{4,5},{5,4},{6,7},{7,6},{8,9},{9,8},{10,11... | collective-permute-start | bytes 319496 | tf_op jit(solution)/shard_map/ppermute | solution.py:551
  34.1 1.5 %collective-permute-start.11 = (f32[416,128]{1,0:T(8,128)S(1)}, f32[416,128]{1,0:T(8,128)S(1)}, u32[]{:S(2)}, u32[]{:S(2)}) collective-permute-start(f32[416,128]{1,0:T(8,128)S(1)} %slice_select_fusion), channel_id=1, source_target_pairs={{0,1},{1,0},{2,3},{3,2},{4,5},{5,4},{6,7},{7,6},{8,9},{9,8},{10,11... | collective-permute-start | bytes 638984 | tf_op jit(solution)/shard_map/ppermute | solution.py:551
  35.7 4.4 %collective-permute-start.12 = (f32[104,128]{1,0:T(8,128)S(1)}, f32[104,128]{1,0:T(8,128)S(1)}, u32[]{:S(2)}, u32[]{:S(2)}) collective-permute-start(f32[104,128]{1,0:T(8,128)S(1)} %get-tuple-element.95), channel_id=1, source_target_pairs={{0,2},{1,3},{2,0},{3,1},{4,6},{5,7},{6,4},{7,5},{8,10},{9,11},{10,... | collective-permute-start | bytes 159752 | tf_op jit(solution)/shard_map/ppermute | solution.py:551
  37.2 4.1 %collective-permute-start.14 = (f32[104,128]{1,0:T(8,128)S(1)}, f32[104,128]{1,0:T(8,128)S(1)}, u32[]{:S(2)}, u32[]{:S(2)}) collective-permute-start(f32[104,128]{1,0:T(8,128)S(1)} %get-tuple-element.96), channel_id=1, source_target_pairs={{0,2},{1,3},{2,0},{3,1},{4,6},{5,7},{6,4},{7,5},{8,10},{9,11},{10,... | collective-permute-start | bytes 159752 | tf_op jit(solution)/shard_map/ppermute | solution.py:551
  40.1 4.3 %collective-permute-start.13 = (f32[104,128]{1,0:T(8,128)S(1)}, f32[104,128]{1,0:T(8,128)S(1)}, u32[]{:S(2)}, u32[]{:S(2)}) collective-permute-start(f32[104,128]{1,0:T(8,128)S(1)} %add.28.left_ref), channel_id=1, source_target_pairs={{0,4},{1,5},{2,6},{3,7},{4,0},{5,1},{6,2},{7,3},{8,12},{9,13},{10,... | collective-permute-start | bytes 159752 | tf_op jit(solution)/shard_map/ppermute | solution.py:551
  41.4 5.2 %collective-permute-start.16 = (f32[104,128]{1,0:T(8,128)S(1)}, f32[104,128]{1,0:T(8,128)S(1)}, u32[]{:S(2)}, u32[]{:S(2)}) collective-permute-start(f32[104,128]{1,0:T(8,128)S(1)} %add.29.left_ref), channel_id=1, source_target_pairs={{0,4},{1,5},{2,6},{3,7},{4,0},{5,1},{6,2},{7,3},{8,12},{9,13},{10,... | collective-permute-start | bytes 159752 | tf_op jit(solution)/shard_map/ppermute | solution.py:551
  44.5 6.1 %collective-permute-start.15 = (f32[104,128]{1,0:T(8,128)S(1)}, f32[104,128]{1,0:T(8,128)S(1)}, u32[]{:S(2)}, u32[]{:S(2)}) collective-permute-start(f32[104,128]{1,0:T(8,128)S(1)} %add.30.left_ref), channel_id=1, source_target_pairs={{0,8},{1,9},{2,10},{3,11},{4,12},{5,13},{6,14},{7,15},{8,0},{9,1},... | collective-permute-start | bytes 159752 | tf_op jit(solution)/shard_map/ppermute | solution.py:551
  46.6 5.1 %collective-permute-start.18 = (f32[104,128]{1,0:T(8,128)S(1)}, f32[104,128]{1,0:T(8,128)S(1)}, u32[]{:S(2)}, u32[]{:S(2)}) collective-permute-start(f32[104,128]{1,0:T(8,128)S(1)} %add.31.left_ref), channel_id=1, source_target_pairs={{0,8},{1,9},{2,10},{3,11},{4,12},{5,13},{6,14},{7,15},{8,0},{9,1},... | collective-permute-start | bytes 159752 | tf_op jit(solution)/shard_map/ppermute | solution.py:551
  50.6 4.9 %collective-permute-start.17 = (f32[104,128]{1,0:T(8,128)S(1)}, f32[104,128]{1,0:T(8,128)S(1)}, u32[]{:S(2)}, u32[]{:S(2)}) collective-permute-start(f32[104,128]{1,0:T(8,128)S(1)} %add.32), channel_id=1, source_target_pairs={{0,2},{1,3},{2,0},{3,1},{4,6},{5,7},{6,4},{7,5},{8,10},{9,11},{10,... | collective-permute-start | bytes 159752 | tf_op jit(solution)/shard_map/ppermute | solution.py:551
  51.7 4.2 %collective-permute-start.20 = (f32[104,128]{1,0:T(8,128)S(1)}, f32[104,128]{1,0:T(8,128)S(1)}, u32[]{:S(2)}, u32[]{:S(2)}) collective-permute-start(f32[104,128]{1,0:T(8,128)S(1)} %add.33), channel_id=1, source_target_pairs={{0,2},{1,3},{2,0},{3,1},{4,6},{5,7},{6,4},{7,5},{8,10},{9,11},{10,... | collective-permute-start | bytes 159752 | tf_op jit(solution)/shard_map/ppermute | solution.py:551
  55.9 1.7 %collective-permute-start.19 = (f32[208,128]{1,0:T(8,128)S(1)}, f32[208,128]{1,0:T(8,128)S(1)}, u32[]{:S(2)}, u32[]{:S(2)}) collective-permute-start(f32[208,128]{1,0:T(8,128)S(1)} %pad_maximum_fusion.4), channel_id=1, source_target_pairs={{0,1},{1,0},{2,3},{3,2},{4,5},{5,4},{6,7},{7,6},{8,9},{9,8},{10,11... | collective-permute-start | bytes 319496 | tf_op jit(solution)/shard_map/ppermute | solution.py:551
  56.0 1.6 %collective-permute-start.21 = (f32[208,128]{1,0:T(8,128)S(1)}, f32[208,128]{1,0:T(8,128)S(1)}, u32[]{:S(2)}, u32[]{:S(2)}) collective-permute-start(f32[208,128]{1,0:T(8,128)S(1)} %pad_maximum_fusion.5), channel_id=1, source_target_pairs={{0,1},{1,0},{2,3},{3,2},{4,5},{5,4},{6,7},{7,6},{8,9},{9,8},{10,11... | collective-permute-start | bytes 319496 | tf_op jit(solution)/shard_map/ppermute | solution.py:551
